TPU v7x, 256 devices: a whole 4x4x8 slice. The times are simulated.
256 devices in a mesh: grp: 32 (over x, y, z_lo), mem: 8 (over z_hi, core).
Axes of the slice: x: 4, y: 4, z: 8 (z_hi: 4, z_lo: 2; z = z_hi * 2 + z_lo), core: 2. Of those that a mesh axis runs over, the one named last changes fastest.
Arguments:
- embeddings: float32 [98304, 256], P(('grp', 'mem')), may hold values from -30 to 30
- positive: int32 [98304], P(('grp', 'mem')), may hold values from 0 to 98303, as said below
- pairing: int32 [2, 32], replicated, may hold values from 0 to 31, as said below
Outputs:
- loss: float32 [98304], P(('grp', 'mem'))
- grad_embed: float32 [98304, 256], P(('grp', 'mem'))
Inputs may be any that keep to these rules, and one draw needn't show every extreme that they name: positive[i] lies in the same block of 3072 views as i, differs from i, and positive[positive[i]] = i. Each row is a pairing of the 32 blocks into partners (pairing[r, pairing[r, b]] = b, never b itself); no two blocks are partners in two rounds.
All inputs are finite; a program needn't handle non-finite values.
Results may differ from a plain program's by a relative error of at most 0.0003.
Values sent between devices are 32-bit elements; how exact they have to be, the bound alone decides.
No kernel may reach another device: no remote copies, remote signals or barrier semaphores. Data moves between devices by JAX's collectives and lax.ppermute only.
A program may use at most 128 MiB of HBM per device.

v0:
```python
import math

import jax
import jax.numpy as jnp
from jax import lax
from jax.sharding import PartitionSpec as P

logit_divisor = 0.1
epsilon = 1e-06


def unit_rows(values):
    radius = jnp.sqrt(jnp.sum(values * values, axis=-1, keepdims=True) + epsilon)
    return (values / radius, radius)


def tile_pass(row_data, col_data, self_start, inv_rows, inv_cols):
    count, width_all = col_data.shape
    width = math.gcd(count, 512)
    pieces = count // width
    col_blocks = col_data.reshape(pieces, width, width_all)
    row_ids = jnp.arange(row_data.shape[0], dtype=jnp.int32)
    weighted_pass = inv_cols is not None
    items = (jnp.arange(pieces, dtype=jnp.int32), col_blocks)
    if weighted_pass:
        items = items + (inv_cols.reshape(pieces, width),)

    def advance(carry, item):
        totals, weighted = carry
        index = item[0]
        col_piece = item[1]
        cosine_logits = jnp.dot(
            row_data,
            col_piece.T,
            precision=lax.Precision.HIGHEST,
            preferred_element_type=jnp.float32,
        )
        exponent_logit = jnp.exp(cosine_logits / logit_divisor)
        if self_start is not None:
            col_ids = index * width + jnp.arange(width, dtype=jnp.int32)
            exponent_logit = jnp.where(
                row_ids[:, None] + self_start == col_ids[None, :], 0.0, exponent_logit
            )
        totals = totals + jnp.sum(exponent_logit, axis=1)
        if weighted_pass:
            factor = exponent_logit * (inv_rows[:, None] + item[2][None, :])
            weighted = weighted + jnp.dot(
                factor,
                col_piece,
                precision=lax.Precision.HIGHEST,
                preferred_element_type=jnp.float32,
            )
        return ((totals, weighted), None)

    start = (jnp.zeros((row_data.shape[0],), jnp.float32), jnp.zeros(row_data.shape, jnp.float32))
    result, _ = lax.scan(advance, start, items)
    return result


def local(embeddings, positive, pairing):
    slice_rows = embeddings.shape[0]
    members = lax.axis_size("mem")
    block_rows = slice_rows * members
    rounds = pairing.shape[0]
    group = lax.axis_index("grp")
    member = lax.axis_index("mem")
    sphere_embedding_matrix, radius = unit_rows(embeddings)
    partners = pairing[:, group]

    def pick_rows(carry, piece):
        length = piece.shape[0]
        global_ids = jnp.arange(length, dtype=jnp.int32)
        source = global_ids // slice_rows
        within = global_ids % slice_rows
        for which_round in range(rounds):
            chosen = (source == partners[which_round]).reshape((length,) + (1,) * (piece.ndim - 1))
            carry = carry.at[which_round, within].add(jnp.where(chosen, piece, 0.0))
        return carry

    own_block = lax.all_gather(sphere_embedding_matrix, "mem", axis=0, tiled=True)
    part_slices = pick_rows(
        jnp.zeros((rounds,) + sphere_embedding_matrix.shape, jnp.float32),
        lax.all_gather(sphere_embedding_matrix, "grp", axis=0, tiled=True),
    )
    self_start = member * slice_rows
    diag_totals, _ = tile_pass(sphere_embedding_matrix, own_block, self_start, None, None)
    part_blocks = lax.all_gather(part_slices, "mem", axis=1, tiled=True)
    denom = diag_totals
    for which_round in range(rounds):
        extra, _ = tile_pass(sphere_embedding_matrix, part_blocks[which_round], None, None, None)
        denom = denom + extra
    part_denom = pick_rows(
        jnp.zeros((rounds, slice_rows), jnp.float32),
        lax.all_gather(denom, "grp", axis=0, tiled=True),
    )
    own_denom_blk, part_denom_blk = (
        lax.all_gather(denom, "mem", axis=0, tiled=True),
        lax.all_gather(part_denom, "mem", axis=1, tiled=True),
    )
    inv_own = 1.0 / denom
    _, running_aggregate = tile_pass(
        sphere_embedding_matrix, own_block, self_start, inv_own, 1.0 / own_denom_blk
    )
    for which_round in range(rounds):
        _, extra_sum = tile_pass(
            sphere_embedding_matrix,
            part_blocks[which_round],
            None,
            inv_own,
            1.0 / part_denom_blk[which_round],
        )
        running_aggregate = running_aggregate + extra_sum
    local_pos = positive - group * block_rows
    rival_entries = own_block[local_pos]
    matched_logit = jnp.sum(sphere_embedding_matrix * rival_entries, axis=-1) / logit_divisor
    loss = jnp.log(denom) - matched_logit
    sphere_derivative = (running_aggregate - 2.0 * rival_entries) / logit_divisor
    grad_embed = (
        sphere_derivative
        - sphere_embedding_matrix
        * jnp.sum(sphere_embedding_matrix * sphere_derivative, axis=-1, keepdims=True)
    ) / radius
    return (loss, grad_embed)


def solution(mesh):
    placed = (P(("grp", "mem"), None), P(("grp", "mem")), P())
    return jax.shard_map(
        local,
        mesh=mesh,
        in_specs=placed,
        out_specs=(P(("grp", "mem")), P(("grp", "mem"), None)),
        check_vma=False,
    )
```

profile of v0, /device:TPU:8, one launch (start us, length us, event | category | flops | bytes accessed | tf_op | source)
XLA Modules:
  0.0 915.5 jit_solution(5464673663584020801)
XLA Ops:
  16.1 273.8 %all-gather.8.cloned.1.call-done = f32[12288,256]{1,0:T(8,128)} async-done(((f32[384,256]{1,0:T(8,128)}), f32[12288,256]{1,0:T(8,128)}) %all-gather.8.cloned.1.call-update) | async-done | bytes 12582928 | tf_op jit(solution)/shard_map/all_gather | solution.py:83
  289.9 73.8 %scatter_custom_fusion = f32[768,256]{1,0:T(8,128)S(1)} fusion(s32[12288]{0:T(1024)S(1)} %get-tuple-element.410, f32[12288,256]{1,0:T(8,128)} %all-gather.8.cloned.1.call-done, f32[]{:T(128)} %constant.123.clone.1, pred[12288]{0:T(1024)(128)(4,1)S(1)} %broadcast_compare_fusion.1), kind=kCustom, calls=%fused_computation.73 | custom fusion | flops 6291456 | bytes 13382656
  363.7 73.9 %scatter_custom_fusion.1 = f32[768,256]{1,0:T(8,128)S(1)} fusion(f32[768,256]{1,0:T(8,128)S(1)} %scatter_custom_fusion, s32[12288]{0:T(1024)S(1)} %get-tuple-element.409, f32[12288,256]{1,0:T(8,128)} %all-gather.8.cloned.1.call-done, f32[]{:T(128)} %constant.123.clone.1, pred[12288]{0:T(1024)(128)(4,1)S(1)} %broadcast_compare_fusion), kind=kCustom, calls=%fused_computation.71 | custom fusion | flops 6291456 | bytes 13381636
  438.7 4.1 gather_fusion
  442.8 20.5 %while.66 = (s32[]{:T(128)}, f32[384]{0:T(512)S(1)}, s32[]{:T(128)}, s32[6]{0:T(128)S(1)}, f32[6,512,256]{2,1,0:T(8,128)}, /*index=5*/f32[384,256]{1,0:T(8,128)S(1)}, s32[]{:T(128)}, s32[1]{0:T(128)}, s32[]{:T(128)}) while((s32[]{:T(128)}, f32[384]{0:T(512)S(1)}, s32[]{:T(128)}, s32[6]{0:T(128)S(1)}, f32[6,512,256]{2,1,0:T(8,128)}, ...), condition=%wide.region_3.4_spmd.clone, body=%wide.region_1.3_spmd.clone.sunk | while | flops 604767488 | bytes 931463 | solution.py:56
  463.9 39.8 %all-gather.10.cloned.1.call-done = f32[2,3072,256]{2,1,0:T(8,128)} async-done(((f32[2,384,256]{2,1,0:T(8,128)}), f32[2,3072,256]{2,1,0:T(8,128)}) %all-gather.10.cloned.1.call-update) | async-done | bytes 6291472 | tf_op jit(solution)/shard_map/all_gather | solution.py:87
  503.6 4.9 fusion.66
  508.6 12.6 %while.67 = (s32[]{:T(128)}, f32[384]{0:T(512)S(1)}, f32[6,512,256]{2,1,0:T(8,128)}, f32[384,256]{1,0:T(8,128)S(1)}, s32[]{:T(128)}, /*index=5*/s32[]{:T(128)}) while((s32[]{:T(128)}, f32[384]{0:T(512)S(1)}, f32[6,512,256]{2,1,0:T(8,128)}, f32[384,256]{1,0:T(8,128)S(1)}, s32[]{:T(128)}, /*index=5*/s32[]{:T(128)}) %tuple.153), condition=%wide.region_8.9_spmd.clone, body=%wide.region_6.8_spmd.clone.sunk | while | flops 604373376 | bytes 924239 | solution.py:56
  521.2 6.4 while.68
  529.2 83.2 %all-gather.1 = f32[32,1,384]{2,1,0:T(1,128)S(1)} all-gather(f32[1,1,384]{2,1,0:T(1,128)S(1)} %reshape.155), channel_id=1, replica_groups=mesh['grp'=32,'mem'=8] {'grp'}, dimensions={0}, use_global_device_ids=true | all-gather | bytes 50688 | tf_op jit(solution)/shard_map/all_gather | solution.py:94
  612.5 14.2 %all-gather = f32[8,1,384]{2,1,0:T(1,128)} all-gather(f32[1,1,384]{2,1,0:T(1,128)S(1)} %reshape.155), channel_id=1, replica_groups=mesh['grp'=32,'mem'=8] {'mem'}, dimensions={0}, use_global_device_ids=true | all-gather | bytes 13824 | tf_op jit(solution)/shard_map/all_gather | solution.py:97
  628.7 85.4 %scatter_custom_fusion.2 = f32[768]{0:T(1024)S(1)} fusion(s32[12288]{0:T(1024)} %copy-done.11, f32[12288]{0:T(1024)} %get-tuple-element.406, f32[]{:T(128)} %constant.123.clone.1), kind=kCustom, calls=%fused_computation.113 | custom fusion | flops 12288 | bytes 3584
  714.0 85.5 %scatter_fusion = f32[768]{0:T(1024)S(1)} fusion(f32[768]{0:T(1024)S(1)} %scatter_custom_fusion.2, s32[12288]{0:T(1024)} %copy-done.9, f32[12288]{0:T(1024)} %get-tuple-element.405), kind=kCustom, calls=%fused_computation.4 | custom fusion | flops 12288 | bytes 196608
  799.6 14.6 %all_gather.23 = f32[2,3072]{1,0:T(2,128)S(1)} all-gather(f32[2,384]{1,0:T(2,128)S(1)} %reshape.119), channel_id=1, replica_groups=mesh['grp'=32,'mem'=8] {'mem'}, dimensions={1}, use_global_device_ids=true | all-gather | bytes 27648 | tf_op jit(solution)/shard_map/all_gather | solution.py:98
  814.3 28.3 %while.70 = (s32[]{:T(128)}, f32[384,256]{1,0:T(8,128)S(1)}, f32[6,512,256]{2,1,0:T(8,128)}, f32[384,256]{1,0:T(8,128)S(1)}, f32[384]{0:T(512)S(1)}, /*index=5*/f32[6,512]{1,0:T(8,128)S(1)}, s32[]{:T(128)}, s32[]{:T(128)}) while((s32[]{:T(128)}, f32[384,256]{1,0:T(8,128)S(1)}, f32[6,512,256]{2,1,0:T(8,128)}, ...), condition=%wide.region_18.19_spmd.clone, body=%wide.region_17.18_spmd.clone.sunk | while | flops 1208745984 | bytes 3809891 | solution.py:56
  816.5 2.6 convolution_add_fusion.7
  842.7 36.1 %while.69 = (s32[]{:T(128)}, f32[384,256]{1,0:T(8,128)S(1)}, s32[]{:T(128)}, s32[6]{0:T(128)S(1)}, f32[6,512,256]{2,1,0:T(8,128)}, /*index=5*/f32[384,256]{1,0:T...) while((s32[]{:T(128)}, f32[384,256]{1,0:T(8,128)S(1)}, ...), condition=%wide.region_14.15_spmd.clone, body=%wide.region_13.14_spmd.clone.sunk | while | flops 1209140096 | bytes 3817115 | solution.py:56
  846.1 2.6 convolution_add_fusion.6
  858.1 2.6 convolution_add_fusion.6
  870.2 2.6 convolution_add_fusion.6
  876.2 2.6 convolution_add_fusion.6
  878.8 28.3 %while.71 = (s32[]{:T(128)}, f32[384,256]{1,0:T(8,128)S(1)}, f32[6,512,256]{2,1,0:T(8,128)}, f32[384,256]{1,0:T(8,128)S(1)}, f32[384]{0:T(512)S(1)}, /*index=5*/f32[6,512]{1,0:T(8,128)S(1)}, s32[]{:T(128)}, s32[]{:T(128)}) while((s32[]{:T(128)}, f32[384,256]{1,0:T(8,128)S(1)}, f32[6,512,256]{2,1,0:T(8,128)}, ...), condition=%wide.region_20.21_spmd.clone, body=%wide.region_19.20_spmd.clone.sunk | while | flops 1208745984 | bytes 3809891 | solution.py:56
  881.0 2.6 convolution_add_fusion.8
  904.5 2.6 convolution_add_fusion.8
  (195 shorter events, 121.2 us)
Async XLA Ops:
  7.2 4.5 copy-start
  7.2 282.7 %all-gather.8.cloned.1.call-start = ((), (), s32[]{:S(2)}) async-start(), calls=%async_computation.1 | async-start | bytes 12976128 | tf_op jit(solution)/shard_map/all_gather | solution.py:83
  8.4 0.6 copy-start.13
  10.9 427.8 %all-gather.6.cloned.1.call-start = ((), (), s32[]{:S(2)}) async-start(), calls=%async_computation | async-start | bytes 3538944 | tf_op jit(solution)/shard_map/all_gather | solution.py:80
  11.6 492.0 %all-gather.10.cloned.1.call-start = ((), (), s32[]{:S(2)}) async-start(), calls=%async_computation.2 | async-start | bytes 7077888 | tf_op jit(solution)/shard_map/all_gather | solution.py:87
  16.1 347.6 %copy-start.11 = (s32[12288]{0:T(1024)}, s32[12288]{0:T(1024)S(1)}, u32[]{:S(2)}) copy-start(s32[12288]{0:T(1024)S(1)} %get-tuple-element.410) | copy-start | bytes 147460
  16.1 347.6 %copy-start.9 = (s32[12288]{0:T(1024)}, s32[12288]{0:T(1024)S(1)}, u32[]{:S(2)}) copy-start(s32[12288]{0:T(1024)S(1)} %get-tuple-element.409) | copy-start | bytes 147460
  363.7 74.9 %copy-start.17 = (s32[384]{0:T(512)S(1)}, s32[384]{0:T(512)}, u32[]{:S(2)}) copy-start(s32[384]{0:T(512)} %param.16) | copy-start | bytes 4612
  437.6 0.9 copy-start.7
  437.6 5.1 copy-start.1
  463.3 0.6 copy-start.10
  527.6 101.1 %copy-start.2 = (f32[6,512,256]{2,1,0:T(8,128)}, f32[6,512,256]{2,1,0:T(8,128)S(1)}, u32[]{:S(2)}) copy-start(f32[6,512,256]{2,1,0:T(8,128)S(1)} %get-tuple-element.778) | copy-start | bytes 9437188
  528.3 0.9 copy-start.15
  714.0 100.2 %copy-start.5 = (f32[384,256]{1,0:T(8,128)S(1)}, f32[384,256]{1,0:T(8,128)}, u32[]{:S(2)}) copy-start(f32[384,256]{1,0:T(8,128)} %custom-call.4) | copy-start | bytes 1179652
  814.3 28.3 %copy-start.12 = (f32[8,1,384]{2,1,0:T(1,128)S(1)}, f32[8,1,384]{2,1,0:T(1,128)}, u32[]{:S(2)}) copy-start(f32[8,1,384]{2,1,0:T(1,128)} %all-gather) | copy-start | bytes 36868
  814.3 28.4 %copy-start.4 = (f32[384,256]{1,0:T(8,128)S(1)}, f32[384,256]{1,0:T(8,128)}, u32[]{:S(2)}) copy-start(f32[384,256]{1,0:T(8,128)} %custom-call.3) | copy-start | bytes 1179652
  842.7 36.1 %copy-start.3 = (f32[384,256]{1,0:T(8,128)S(1)}, f32[384,256]{1,0:T(8,128)}, u32[]{:S(2)}) copy-start(f32[384,256]{1,0:T(8,128)} %custom-call.5) | copy-start | bytes 1179652
  878.8 28.4 %copy-start.6 = (f32[384,256]{1,0:T(8,128)S(1)}, f32[384,256]{1,0:T(8,128)}, u32[]{:S(2)}) copy-start(f32[384,256]{1,0:T(8,128)} %param.15) | copy-start | bytes 1179652
  878.8 28.4 %copy-start.8 = (f32[384,256]{1,0:T(8,128)S(1)}, f32[384,256]{1,0:T(8,128)}, u32[]{:S(2)}) copy-start(f32[384,256]{1,0:T(8,128)} %gather_fusion) | copy-start | bytes 1179652
  878.8 28.4 %copy-start.14 = (f32[384]{0:T(512)S(1)}, f32[384]{0:T(512)}, u32[]{:S(2)}) copy-start(f32[384]{0:T(512)} %copy-done.13) | copy-start | bytes 4612
  878.8 28.6 %copy-start.16 = (f32[384]{0:T(512)S(1)}, f32[384]{0:T(512)}, u32[]{:S(2)}) copy-start(f32[384]{0:T(512)} %copy-done.15) | copy-start | bytes 4612
Sparse Core Ops, SparseCore 0:
  11.0 278.8 all-gather.7
  292.3 45.2 all-gather.5
  438.7 64.9 all-gather.9
where the time goes:
time: 924 us; the launch traced here: 915 us
  other arithmetic  330 us (36%)
  waiting for transfers between devices  314 us (34%)
  matrix products  116 us (13%)
  blocking collectives  112 us (12%)
  local copies, waits for them, and re-layouts  19.9 us (2%)
  between operations  14.2 us (2%)
    unnamed x13, other arithmetic  321 us
    all_gather x1, waiting for transfers between devices, local(): lax.all_gather(sphere_embedding_matrix, 'grp', axis=0, tiled=True)  274 us
    all_gather x1, blocking collectives, local(): lax.all_gather(denom, 'grp', axis=0, tiled=True)  83.2 us
    dot_general x36, matrix products, advance(): jnp.dot(row_data, col_piece.T, precision=lax.Precision.HIGHEST, preferred...  69.7 us
    dot_general x18, matrix products, advance(): jnp.dot(factor, col_piece, precision=lax.Precision.HIGHEST, preferred_ele...  45.9 us
    all_gather x1, waiting for transfers between devices, local(): part_blocks = lax.all_gather(part_slices, 'mem', axis=1, tiled=True)  39.8 us
  transfers between devices with their start and end apart: 3, of which 2 were waited for; matrix products, arithmetic and copies ran while one was open for 19% of the time, Pallas kernels for 0%

commit v1 on v0

v1 whole, which is shorter than its diff:
```python
import functools

import jax
import jax.numpy as jnp
from jax import lax
from jax.experimental import pallas as pl
from jax.experimental.pallas import tpu as pltpu
from jax.sharding import PartitionSpec as P

LOGIT_DIVISOR = 0.1
EPSILON = 1e-06
SLICE = 384
WIDTH = 256
SELF = 2
VMEM = 16 * 1024 * 1024
VMEM_LARGE = 40 * 1024 * 1024
HBM = pl.BlockSpec(memory_space=pltpu.HBM)
SMEM = pl.BlockSpec(memory_space=pltpu.SMEM)


def split(values):
    hi = values.astype(jnp.bfloat16)
    lo = (values - hi.astype(jnp.float32)).astype(jnp.bfloat16)
    return hi, lo


def rows_of(tiles):
    pairs = tiles.reshape(tiles.shape[0] // 2, 2, 8, 128)
    rows = tiles.shape[0] * 4
    return jnp.concatenate([pairs[:, 0].reshape(rows, 128), pairs[:, 1].reshape(rows, 128)], axis=1)


def radius_of(values):
    return jnp.sqrt(jnp.sum(values * values, axis=-1, keepdims=True) + EPSILON)


def as_column(line):
    return jnp.broadcast_to(line, (128, line.shape[1])).T


def in_hbm(value):
    return pltpu.with_memory_space_constraint(value, pltpu.HBM)


def params(limit=VMEM):
    return pltpu.CompilerParams(vmem_limit_bytes=limit)


def tile_kernel(emb_ref, tile_ref):
    rows = emb_ref.shape[0]
    for half in range(2):
        tile_ref[:, half] = emb_ref[:, half * 128 : half * 128 + 128].reshape(rows // 8, 8, 128)


def as_tiles(embeddings):
    rows, _ = embeddings.shape
    return pl.pallas_call(
        tile_kernel,
        out_shape=jax.ShapeDtypeStruct((rows // 8, 2, 8, 128), jnp.float32),
        compiler_params=params(),
        name="as_tiles",
    )(embeddings)


def forward_kernel(first, order, pieces, *refs):
    rows, refs = refs[:pieces], list(refs[pieces:])
    if first:
        sib, got, got_sib = refs[:3]
        refs = refs[3:]
    else:
        c_in = refs.pop(0)
    pos_ref, e_out, refs = refs[0], refs[1], refs[2:]
    if first:
        c_out = refs.pop(0)
    line_refs, (left_ref, e_buf, c_buf, tot_ref, e_sem, c_sem) = refs[:-6], refs[-6:]
    slices, _, count = e_buf.shape
    height, wide = slices * SLICE, 2 * SLICE

    copies, col_copies = [], []
    for base in range(0, count, wide):
        view, sem = (pl.ds(base, wide),), c_sem.at[base // wide]
        if first:
            col_copies.append(pltpu.make_async_copy(c_buf.at[view], c_out.at[view], sem))
        else:
            col_copies.append(pltpu.make_async_copy(c_in.at[view], c_buf.at[view], sem))
            col_copies[-1].start()
    at = 0
    for ref in rows:
        values = ref[...]
        hi, lo = split(values * (1.0 / (radius_of(values) * LOGIT_DIVISOR)))
        left_ref[at : at + hi.shape[0]] = jnp.concatenate([hi, lo, hi], axis=1)
        at += hi.shape[0]

    for base in range(0, count, wide):
        if first:
            half = got.shape[1] // 2
            tiles = got.shape[0] * half // 8
            for which, ref in enumerate((rows[0], sib) if base == 0 else (got, got_sib)):
                if base == 0:
                    piece = ref[...]
                else:
                    begin = (base // wide - 1) * half
                    piece = rows_of(ref[:, begin : begin + half].reshape(tiles, 8, 128))
                hi, lo = split(piece * (1.0 / radius_of(piece)))
                c_buf[base + which * SLICE : base + which * SLICE + SLICE] = jnp.concatenate([hi, lo], axis=1)
            col_copies[base // wide].start()
        else:
            col_copies[base // wide].wait()
        col = c_buf[base : base + wide]
        hi, lo = col[:, :WIDTH], col[:, WIDTH:]
        scores = lax.dot_general(
            left_ref[...],
            jnp.concatenate([hi, hi, lo], axis=1),
            (((1,), (1,)), ((), ())),
            preferred_element_type=jnp.float32,
        )
        total = jnp.zeros((height, 128), jnp.float32) if base == 0 else tot_ref[0]
        if base == 0:
            match = jnp.zeros((height, 128), jnp.float32)
            row_ids = lax.broadcasted_iota(jnp.int32, (height, 128), 0) + order * SLICE
            lane_ids = lax.broadcasted_iota(jnp.int32, (height, 128), 1)
        for k in range(0, wide, 128):
            score = scores[:, k : k + 128]
            e = jnp.exp(score)
            if base == 0:
                match = match + jnp.where(row_ids == pos_ref[:, k : k + 128], score, 0.0)
                if order == SELF and k < SLICE:
                    e = jnp.where(row_ids - SELF * SLICE == lane_ids + k, 0.0, e)
            total = total + e
            e_buf[:, :, base + k : base + k + 128] = e.reshape(slices, SLICE, 128)
        tot_ref[0] = total
        if base == 0:
            tot_ref[1] = match
        view = (slice(None), slice(None), pl.ds(base, wide))
        copies.append(pltpu.make_async_copy(e_buf.at[view], e_out.at[view], e_sem.at[base // wide]))
        copies[-1].start()

    for kind in range(2):
        line = jnp.sum(tot_ref[kind].T, axis=0, keepdims=True)
        for which, ref in enumerate(line_refs):
            ref[kind : kind + 1] = line[:, which * SLICE : which * SLICE + SLICE]
    for copy in copies + (col_copies if first else []):
        copy.wait()


def forward(order, slices, rows, cols, pos):
    height, count = slices * SLICE, 6 * SLICE
    first = len(cols) > 1
    split_shape = pltpu.HBM((count, 2 * WIDTH), jnp.bfloat16)
    line_shape = jax.ShapeDtypeStruct((2, SLICE), jnp.float32)
    return pl.pallas_call(
        functools.partial(forward_kernel, first, order, len(rows)),
        in_specs=[pl.BlockSpec()] * len(rows)
        + ([pl.BlockSpec()] * len(cols) if first else [HBM])
        + [pl.BlockSpec()],
        out_specs=[HBM] * (1 + first) + [pl.BlockSpec()] * slices,
        out_shape=[pltpu.HBM((slices, SLICE, count), jnp.float32)]
        + [split_shape] * first
        + [line_shape] * slices,
        scratch_shapes=[
            pltpu.VMEM((height, 3 * WIDTH), jnp.bfloat16),
            pltpu.VMEM((slices, SLICE, count), jnp.float32),
            pltpu.VMEM((count, 2 * WIDTH), jnp.bfloat16),
            pltpu.VMEM((2, height, 128), jnp.float32),
            pltpu.SemaphoreType.DMA((3,)),
            pltpu.SemaphoreType.DMA((3,)),
        ],
        cost_estimate=pl.CostEstimate(
            flops=6 * height * count * WIDTH, bytes_accessed=4 * height * count, transcendentals=height * count
        ),
        compiler_params=params(VMEM_LARGE),
        name="forward_%d" % order,
    )(*rows, *(cols if first else map(in_hbm, cols)), pos)


def sum_kernel(a_ref, b_ref, c_ref, d_ref, out_ref):
    out_ref[...] = (a_ref[...] + b_ref[...]) + (c_ref[...] + d_ref[...])


def sum_lines(*lines):
    return pl.pallas_call(
        sum_kernel,
        out_shape=jax.ShapeDtypeStruct(lines[0].shape, jnp.float32),
        compiler_params=params(),
        name="sum_lines",
    )(*lines)


def spread_kernel(own_ref, sib_ref, out_ref):
    both = jnp.concatenate([own_ref[0:1], sib_ref[0:1]], axis=1)
    out_ref[...] = jnp.broadcast_to(both.reshape(1, 1, 2 * SLICE), out_ref.shape)


def spread(own, sib, groups):
    return pl.pallas_call(
        spread_kernel,
        out_shape=jax.ShapeDtypeStruct((groups, 1, 2 * SLICE), jnp.float32),
        compiler_params=params(),
        name="spread",
    )(own, sib)


def backward_kernel(order, row_refs, partner_ref, *refs):
    rows_den, refs = refs[:row_refs], refs[row_refs:]
    own_ref, sib_ref, everyone_ref, pos_ref, e_in, c_in = refs[:6]
    refs = refs[6:]
    out_refs, (run_ref, e_buf, c_buf, e_sem, c_sem) = refs[:-5], refs[-5:]
    slices = e_buf.shape[0]
    wide = 2 * SLICE
    copies = []
    for k in range(3):
        wanted = pl.ds(k * wide, wide)
        copies.append(
            pltpu.make_async_copy(
                e_in.at[:, :, wanted], e_buf.at[:, :, wanted], e_sem.at[k]
            )
        )
        copies.append(pltpu.make_async_copy(c_in.at[wanted], c_buf.at[wanted], c_sem.at[k]))
    for copy in copies:
        copy.start()

    rows = slices * SLICE
    row_inv = 1.0 / as_column(jnp.concatenate([ref[0:1] for ref in rows_den], axis=1))
    row_ids = lax.broadcasted_iota(jnp.int32, (rows, 128), 0) + order * SLICE
    for k in range(3):
        if k == 0:
            col_inv = 1.0 / jnp.concatenate([own_ref[0:1], sib_ref[0:1]], axis=1)
        else:
            col_inv = 1.0 / everyone_ref[partner_ref[k - 1]]
        copies[2 * k].wait()
        copies[2 * k + 1].wait()
        his, los = [], []
        for at in range(0, wide, 128):
            e = e_buf[:, :, k * wide + at : k * wide + at + 128].reshape(rows, 128)
            weight = e * (row_inv + col_inv[:, at : at + 128])
            if k == 0:
                weight = weight - jnp.where(row_ids == pos_ref[:, at : at + 128], 2.0, 0.0)
            hi, lo = split(weight)
            his.append(hi)
            los.append(lo)
        cols = c_buf[k * wide : k * wide + wide]
        c_hi, c_lo = cols[:, :WIDTH], cols[:, WIDTH:]
        part = jnp.dot(
            jnp.concatenate(his + his + los, axis=1),
            jnp.concatenate([c_hi, c_lo, c_hi], axis=0),
            preferred_element_type=jnp.float32,
        )
        if k == 0:
            run_ref[...] = part
        elif k == 1:
            run_ref[...] += part
        else:
            part = run_ref[...] + part
            size = rows // len(out_refs)
            for which, ref in enumerate(out_refs):
                ref[...] = part[which * size : which * size + size]


def backward(order, pieces, row_dens, e, partners, own, sib, everyone, pos, cols):
    slices = len(row_dens)
    count = 6 * SLICE
    return pl.pallas_call(
        functools.partial(backward_kernel, order, slices),
        in_specs=[SMEM] + [pl.BlockSpec()] * (slices + 4) + [HBM] * 2,
        out_shape=[jax.ShapeDtypeStruct((slices * SLICE // pieces, WIDTH), jnp.float32)] * pieces,
        scratch_shapes=[
            pltpu.VMEM((slices * SLICE, WIDTH), jnp.float32),
            pltpu.VMEM((slices, SLICE, count), jnp.float32),
            pltpu.VMEM((count, 2 * WIDTH), jnp.bfloat16),
            pltpu.SemaphoreType.DMA((3,)),
            pltpu.SemaphoreType.DMA((3,)),
        ],
        cost_estimate=pl.CostEstimate(
            flops=6 * slices * SLICE * count * WIDTH, bytes_accessed=4 * slices * SLICE * count, transcendentals=0
        ),
        compiler_params=params(VMEM_LARGE),
        name="backward_%d" % order,
    )(partners, *row_dens, own, sib, everyone, pos, in_hbm(e), in_hbm(cols))


def add_kernel(a_ref, b_ref, c_ref, d_ref, ab_ref, cd_ref):
    ab_ref[...] = a_ref[...] + b_ref[...]
    cd_ref[...] = c_ref[...] + d_ref[...]


def add_pairs(a, b, c, d):
    out = jax.ShapeDtypeStruct(a.shape, jnp.float32)
    return pl.pallas_call(add_kernel, out_shape=(out, out), compiler_params=params(), name="add_pairs")(
        a, b, c, d
    )


def finish_kernel(emb_ref, run_ref, low0, low1, high0, high1, line_ref, loss_ref, grad_ref):
    values = emb_ref[...]
    radius = radius_of(values)
    unit = values / radius
    low, high = low0[...] + low1[...], high0[...] + high1[...]
    slope = (run_ref[...] + jnp.concatenate([low, high], axis=0)) / LOGIT_DIVISOR
    grad_ref[...] = (slope - unit * jnp.sum(unit * slope, axis=-1, keepdims=True)) / radius
    loss_ref[...] = jnp.log(line_ref[0:1]) - line_ref[1:2]


def finish(embeddings, run, lows, highs, line):
    rows, width = embeddings.shape
    return pl.pallas_call(
        finish_kernel,
        out_shape=(
            jax.ShapeDtypeStruct((1, rows), jnp.float32),
            jax.ShapeDtypeStruct((rows, width), jnp.float32),
        ),
        compiler_params=params(),
        name="finish",
    )(embeddings, run, *lows, *highs, line)


def local(embeddings, positive, pairing):
    rows, width = embeddings.shape
    members = lax.axis_size("mem")
    groups = lax.axis_size("grp")
    block = rows * members
    rounds = pairing.shape[0]
    group = lax.axis_index("grp")
    member = lax.axis_index("mem")
    half = rows // 2

    def shift(value, by):
        return lax.ppermute(value, "mem", [(m, (m + by) % members) for m in range(members)])

    def swap(value):
        return lax.ppermute(value, "mem", [(m, m ^ 1) for m in range(members)])

    per = rows * width // (groups * 128)
    pieces = lax.all_to_all(as_tiles(embeddings).reshape(groups, per, 128), "grp", 0, 0, tiled=True)
    picked = pieces[pairing.T].reshape(groups, rounds * per, 128)
    got = lax.all_to_all(picked, "grp", 0, 0, tiled=True)
    left, right = shift(embeddings, 2), shift(embeddings, -2)
    sib, pos_sib = swap(embeddings), swap(positive)
    got, left, right, sib, pos_sib = lax.optimization_barrier((got, left, right, sib, pos_sib))
    far = (shift(left[:half], 2), shift(right[half:], -2))

    both = jnp.concatenate([positive, pos_sib]) - group * block
    owner = both // rows
    turn = (owner // 2 - member // 2) % (members // 2)
    order = jnp.where(turn == 0, SELF, jnp.where(turn == 3, 0, jnp.where(turn == 1, 1, 3)))
    pos = jnp.where(owner % 2 == member % 2, order * rows + both % rows, -1).reshape(1, 2 * rows)

    e_self, cols, line_self = forward(SELF, 1, (embeddings,), (sib, got, swap(got)), pos)
    e_sides, line_left, line_right = forward(0, 2, (left, right), (cols,), pos)
    e_far, line_far = forward(3, 1, far, (cols,), pos)

    line = sum_lines(line_self, shift(line_left, -2), shift(line_right, 2), shift(line_far, 4))
    line_sib = swap(line)
    everyone = lax.all_to_all(spread(line, line_sib, groups), "grp", 0, 0, tiled=True)
    at_left, at_right, at_far = shift(line, 2), shift(line, -2), shift(line, 4)

    shared = (pairing[:, group], line, line_sib, everyone, pos, cols)
    far_low, far_high = backward(3, 2, (at_far,), e_far, *shared)
    far_low, far_high = shift(far_low, 2), shift(far_high, -2)
    left_low, left_high, right_low, right_high = backward(0, 4, (at_left, at_right), e_sides, *shared)
    high0, low1 = shift(right_high, 2), shift(left_low, -2)
    right_low, left_high = add_pairs(right_low, far_low, left_high, far_high)
    low0, high1 = shift(right_low, 2), shift(left_high, -2)
    (run,) = backward(SELF, 1, (line,), e_self, *shared)
    loss, grad = finish(embeddings, run, (low0, low1), (high0, high1), line)
    return loss.reshape(rows), grad


def solution(mesh):
    placed = (P(("grp", "mem"), None), P(("grp", "mem")), P())
    return jax.shard_map(
        local,
        mesh=mesh,
        in_specs=placed,
        out_specs=(P(("grp", "mem")), P(("grp", "mem"), None)),
        check_vma=False,
    )
```

time: 924 us -> 143 us (0.15)
  other arithmetic: 330 us -> 1.36 us
  waiting for transfers between devices: 314 us -> 45.4 us
  matrix products: 116 us -> 0 us
  blocking collectives: 112 us -> 0 us
  starting transfers between devices: 0.12 us -> 55.5 us
  Pallas kernels: 0 us -> 34.1 us
  local copies, waits for them, and re-layouts: 19.9 us -> 2.95 us
  between operations: 14.2 us -> 0.85 us
    unnamed x13 -> x0, other arithmetic: 321 us -> none
    all_gather x3 -> x0, waiting for transfers between devices: 314 us -> none  [the longest x1 274 us: local(): lax.all_gather(sphere_embedding_matrix, 'grp', axis=0, tiled=True)]
    dot_general x54 -> x0, matrix products: 116 us -> none  [the longest x36 69.7 us: advance(): jnp.dot(row_data, col_piece.T, precision=lax.Precision.HIGHEST, preferred...]
    all_gather x3 -> x0, blocking collectives: 112 us -> none  [the longest x1 83.2 us: local(): lax.all_gather(denom, 'grp', axis=0, tiled=True)]
    ppermute x0 -> x20, waiting for transfers between devices: none -> 36.6 us  [the longest x16 34.2 us: shift(): lax.ppermute(value, 'mem', [(m, (m + by) % members) for m in range(member...]
    pallas_call x0 -> x11, Pallas kernels: none -> 34.1 us  [the longest x3 16.7 us: backward(): pl.pallas_call(functools.partial(backward_kernel, order, slices), in_spec...]
    ppermute x0 -> x20, starting transfers between devices: none -> 34.1 us  [the longest x16 33.5 us: shift(): lax.ppermute(value, 'mem', [(m, (m + by) % members) for m in range(member...]
    all_to_all x0 -> x3, starting transfers between devices: none -> 21.4 us  [the longest x1 8.89 us: local(): lax.all_to_all(as_tiles(embeddings).reshape(groups, per, 128), 'grp', 0,...]
  transfers between devices with their start and end apart: 3 -> 23, of which waited for: 2 -> 7; matrix products, arithmetic and copies ran while one was open for 19% -> 1% of each run, Pallas kernels for 0% -> 23%
where the time goes in v1:
time: 143 us; the launch traced here: 140 us
  starting transfers between devices  55.5 us (39%)
  waiting for transfers between devices  45.4 us (32%)
  Pallas kernels  34.1 us (24%)
  local copies, waits for them, and re-layouts  2.95 us (2%)
    ppermute x16, waiting for transfers between devices, shift(): lax.ppermute(value, 'mem', [(m, (m + by) % members) for m in range(member...  34.2 us
    ppermute x16, starting transfers between devices, shift(): lax.ppermute(value, 'mem', [(m, (m + by) % members) for m in range(member...  33.5 us
    pallas_call x3, Pallas kernels, backward(): pl.pallas_call(functools.partial(backward_kernel, order, slices), in_spec...  16.7 us
    pallas_call x3, Pallas kernels, forward(): pl.pallas_call(functools.partial(forward_kernel, first, order, len(rows))...  14.8 us
    all_to_all x1, starting transfers between devices, local(): lax.all_to_all(as_tiles(embeddings).reshape(groups, per, 128), 'grp', 0,...  8.89 us
    all_to_all x1, waiting for transfers between devices, local(): lax.all_to_all(as_tiles(embeddings).reshape(groups, per, 128), 'grp', 0,...  8.81 us
    all_to_all x1, starting transfers between devices, local(): lax.all_to_all(spread(line, line_sib, groups), 'grp', 0, 0, tiled=True)  7.49 us
    all_to_all x1, starting transfers between devices, local(): got = lax.all_to_all(picked, 'grp', 0, 0, tiled=True)  5.02 us
  transfers between devices with their start and end apart: 23, of which 7 were waited for; matrix products, arithmetic and copies ran while one was open for 1% of the time, Pallas kernels for 23%

profile of v1, /device:TPU:8, one launch (start us, length us, event | category | flops | bytes accessed | tf_op | source)
XLA Modules:
  0.0 140.1 jit_solution(16770848873878722302)
XLA Ops:
  2.4 8.9 %all-to-all-start = ((f32[32,24,128]{2,1,0:T(8,128)}), f32[32,24,128]{2,1,0:T(8,128)S(1)}, u32[]{:S(2)}, u32[]{:S(2)}) async-start(f32[32,24,128]{2,1,0:T(8,128)} %bitcast), calls=%async_computation | async-start | bytes 786432 | tf_op jit(solution)/shard_map/all_to_all | solution.py:333
  12.2 8.8 %all-to-all-done = f32[32,24,128]{2,1,0:T(8,128)S(1)} async-done(((f32[32,24,128]{2,1,0:T(8,128)}), f32[32,24,128]{2,1,0:T(8,128)S(1)}, u32[]{:S(2)}, u32[]{:S(2)}) %all-to-all-start) | async-done | bytes 393248 | tf_op jit(solution)/shard_map/all_to_all | solution.py:333
  22.5 5.0 %all-to-all-start.1 = ((f32[32,48,128]{2,1,0:T(8,128)}), f32[32,48,128]{2,1,0:T(8,128)S(1)}, u32[]{:S(2)}, u32[]{:S(2)}) async-start(f32[32,48,128]{2,1,0:T(8,128)} %bitcast.2), calls=%async_computation.1 | async-start | bytes 1572864 | tf_op jit(solution)/shard_map/all_to_all | solution.py:335
  27.6 3.3 %collective-permute-start = (f32[384,256]{1,0:T(8,128)S(1)}, f32[384,256]{1,0:T(8,128)S(1)}, u32[]{:S(2)}, u32[]{:S(2)}) collective-permute-start(f32[384,256]{1,0:T(8,128)S(1)} %copy-done.1), channel_id=1, source_target_pairs={{0,2},{1,3},{2,4},{3,5},{4,6},{5,7},{6,0},{7,1},{8,10},{9,11},{10,... | collective-permute-start | bytes 1179656 | tf_op jit(solution)/shard_map/ppermute | solution.py:327
  30.9 2.2 %collective-permute-start.1 = (f32[384,256]{1,0:T(8,128)S(1)}, f32[384,256]{1,0:T(8,128)S(1)}, u32[]{:S(2)}, u32[]{:S(2)}) collective-permute-start(f32[384,256]{1,0:T(8,128)S(1)} %copy-done.1), channel_id=1, source_target_pairs={{0,6},{1,7},{2,0},{3,1},{4,2},{5,3},{6,4},{7,5},{8,14},{9,15},{10,... | collective-permute-start | bytes 1179656 | tf_op jit(solution)/shard_map/ppermute | solution.py:327
  34.9 22.6 %collective-permute-done.refs_0_ = f32[384,256]{1,0:T(8,128)S(1)} collective-permute-done((f32[384,256]{1,0:T(8,128)S(1)}, f32[384,256]{1,0:T(8,128)S(1)}, u32[]{:S(2)}, u32[]{:S(2)}) %collective-permute-start) | collective-permute-done | bytes 393248 | tf_op jit(solution)/shard_map/ppermute | solution.py:327
  57.7 4.2 %collective-permute-start.8 = (f32[192,256]{1,0:T(8,128)S(1)}, f32[192,256]{1,0:T(8,128)S(1)}, u32[]{:S(2)}, u32[]{:S(2)}) collective-permute-start(f32[192,256]{1,0:T(8,128)S(1)} %slice.7), channel_id=1, source_target_pairs={{0,6},{1,7},{2,0},{3,1},{4,2},{5,3},{6,4},{7,5},{8,14},{9,15},{10,... | collective-permute-start | bytes 589832 | tf_op jit(solution)/shard_map/ppermute | solution.py:327
  62.0 3.5 %forward_2.1 = (f32[1,384,2304]{2,1,0:T(8,128)}, bf16[2304,512]{1,0:T(8,128)(2,1)}, f32[2,384]{1,0:T(2,128)S(1)}) custom-call(f32[384,256]{1,0:T(8,128)S(1)} %copy-done.1, f32[384,256]{1,0:T(8,128)S(1)} %collective-permute-done.2.refs_1_, f32[32,48,128]{2,1,0:T(8,128)S(1)} %all-to-all-done.1.refs_2_, f32[32,48,128]{2,1,0:T(8,128)S(1)} %collective-permute-done.4.refs_3_, ...), custom_call_target="tpu_custom_call" | custom-call | flops 1358954496 | bytes 3538944 | tf_op jit(solution)/shard_map/forward_2/pallas_call | solution.py:151
  65.6 6.8 %forward_0.1 = (f32[2,384,2304]{2,1,0:T(8,128)}, f32[2,384]{1,0:T(2,128)S(1)}, f32[2,384]{1,0:T(2,128)S(1)}) custom-call(f32[384,256]{1,0:T(8,128)S(1)} %collective-permute-done.refs_0_, f32[384,256]{1,0:T(8,128)S(1)} %collective-permute-done.1.refs_1_, bf16[2304,512]{1,0:T(8,128)(2,1)} %get-tuple-element.31.refs_2_.refs_6_.refs_7_, ...), custom_call_target="tpu_custom_call" | custom-call | flops 2717908992 | bytes 7077888 | tf_op jit(solution)/shard_map/forward_0/pallas_call | solution.py:151
  72.9 2.7 %collective-permute-start.6 = (f32[2,384]{1,0:T(2,128)S(1)}, f32[2,384]{1,0:T(2,128)S(1)}, u32[]{:S(2)}, u32[]{:S(2)}) collective-permute-start(f32[2,384]{1,0:T(2,128)S(1)} %get-tuple-element.33), channel_id=1, source_target_pairs={{0,2},{1,3},{2,4},{3,5},{4,6},{5,7},{6,0},{7,1},{8,10},{9,11},{10,... | collective-permute-start | bytes 9224 | tf_op jit(solution)/shard_map/ppermute | solution.py:327
  75.5 4.5 %forward_3.1 = (f32[1,384,2304]{2,1,0:T(8,128)}, f32[2,384]{1,0:T(2,128)S(1)}) custom-call(f32[192,256]{1,0:T(8,128)S(1)} %collective-permute-done.7.refs_0_, f32[192,256]{1,0:T(8,128)S(1)} %collective-permute-done.8.refs_1_, bf16[2304,512]{1,0:T(8,128)(2,1)} %get-tuple-element.31.refs_2_.refs_6_.refs_7_, ...), custom_call_target="tpu_custom_call" | custom-call | flops 1358954496 | bytes 3538944 | tf_op jit(solution)/shard_map/forward_3/pallas_call | solution.py:151
  81.6 6.1 %collective-permute-done.9.d_ref = f32[2,384]{1,0:T(2,128)S(1)} collective-permute-done((f32[2,384]{1,0:T(2,128)S(1)}, f32[2,384]{1,0:T(2,128)S(1)}, u32[]{:S(2)}, u32[]{:S(2)}) %collective-permute-start.9) | collective-permute-done | bytes 3104 | tf_op jit(solution)/shard_map/ppermute | solution.py:327
  89.5 7.5 %all-to-all-start.2 = ((f32[32,1,768]{2,1,0:T(1,128)}), f32[32,1,768]{2,1,0:T(1,128)S(1)}, u32[]{:S(2)}, u32[]{:S(2)}) async-start(f32[32,1,768]{2,1,0:T(1,128)} %spread.1), calls=%async_computation.2 | async-start | bytes 196608 | tf_op jit(solution)/shard_map/all_to_all | solution.py:353
  97.0 3.3 %collective-permute-start.13 = (f32[2,384]{1,0:T(2,128)S(1)}, f32[2,384]{1,0:T(2,128)S(1)}, u32[]{:S(2)}, u32[]{:S(2)}) collective-permute-start(f32[2,384]{1,0:T(2,128)S(1)} %sum_lines.1.own_ref.refs_0_.refs_1_.refs_2_.line_ref), channel_id=1, source_target_pairs={{0,4},{1,5},{2,6},{3,7},{4,0},{5,1},{6,2},{7,3},{8,12},{9,13},{10,... | collective-permute-start | bytes 9224 | tf_op jit(solution)/shard_map/ppermute | solution.py:327
  101.2 3.5 %collective-permute-start.12 = (f32[2,384]{1,0:T(2,128)S(1)}, f32[2,384]{1,0:T(2,128)S(1)}, u32[]{:S(2)}, u32[]{:S(2)}) collective-permute-start(f32[2,384]{1,0:T(2,128)S(1)} %sum_lines.1.own_ref.refs_0_.refs_1_.refs_2_.line_ref), channel_id=1, source_target_pairs={{0,6},{1,7},{2,0},{3,1},{4,2},{5,3},{6,4},{7,5},{8,14},{9,15},{10,... | collective-permute-start | bytes 9224 | tf_op jit(solution)/shard_map/ppermute | solution.py:327
  104.7 4.7 %backward_3.1 = (f32[192,256]{1,0:T(8,128)S(1)}, f32[192,256]{1,0:T(8,128)S(1)}) custom-call(s32[2]{0:T(128)S(1)} %dynamic-slice_reduce_fusion.partner_ref, f32[2,384]{1,0:T(2,128)S(1)} %collective-permute-done.13.refs_0_, f32[2,384]{1,0:T(2,128)S(1)} %sum_lines.1.own_ref.refs_0_.refs_1_.refs_2_.line_ref, ...), custom_call_target="tpu_custom_call" | custom-call | flops 1358954496 | bytes 3538944 | tf_op jit(solution)/shard_map/backward_3/pallas_call | solution.py:262
  109.4 2.2 %collective-permute-start.14 = (f32[192,256]{1,0:T(8,128)S(1)}, f32[192,256]{1,0:T(8,128)S(1)}, u32[]{:S(2)}, u32[]{:S(2)}) collective-permute-start(f32[192,256]{1,0:T(8,128)S(1)} %get-tuple-element.39), channel_id=1, source_target_pairs={{0,2},{1,3},{2,4},{3,5},{4,6},{5,7},{6,0},{7,1},{8,10},{9,11},{10,... | collective-permute-start | bytes 589832 | tf_op jit(solution)/shard_map/ppermute | solution.py:327
  111.6 2.0 %collective-permute-start.15 = (f32[192,256]{1,0:T(8,128)S(1)}, f32[192,256]{1,0:T(8,128)S(1)}, u32[]{:S(2)}, u32[]{:S(2)}) collective-permute-start(f32[192,256]{1,0:T(8,128)S(1)} %get-tuple-element.41), channel_id=1, source_target_pairs={{0,6},{1,7},{2,0},{3,1},{4,2},{5,3},{6,4},{7,5},{8,14},{9,15},{10,... | collective-permute-start | bytes 589832 | tf_op jit(solution)/shard_map/ppermute | solution.py:327
  113.6 7.3 %backward_0.1 = (f32[192,256]{1,0:T(8,128)S(1)}, f32[192,256]{1,0:T(8,128)S(1)}, f32[192,256]{1,0:T(8,128)S(1)}, f32[192,256]{1,0:T(8,128)S(1)}) custom-call(s32[2]{0:T(128)S(1)} %dynamic-slice_reduce_fusion.partner_ref, f32[2,384]{1,0:T(2,128)S(1)} %collective-permute-done.11.refs_0_, f32[2,384]{1,0:T(2,128)S(1)} %collective-permute-done.12.refs_1_, ...), custom_call_target="tpu_custom_call" | custom-call | flops 2717908992 | bytes 7077888 | tf_op jit(solution)/shard_map/backward_0/pallas_call | solution.py:262
  121.2 2.7 %collective-permute-start.18 = (f32[192,256]{1,0:T(8,128)S(1)}, f32[192,256]{1,0:T(8,128)S(1)}, u32[]{:S(2)}, u32[]{:S(2)}) collective-permute-start(f32[192,256]{1,0:T(8,128)S(1)} %get-tuple-element.44), channel_id=1, source_target_pairs={{0,2},{1,3},{2,4},{3,5},{4,6},{5,7},{6,0},{7,1},{8,10},{9,11},{10,... | collective-permute-start | bytes 589832 | tf_op jit(solution)/shard_map/ppermute | solution.py:327
  124.0 2.2 %collective-permute-start.16 = (f32[192,256]{1,0:T(8,128)S(1)}, f32[192,256]{1,0:T(8,128)S(1)}, u32[]{:S(2)}, u32[]{:S(2)}) collective-permute-start(f32[192,256]{1,0:T(8,128)S(1)} %get-tuple-element.42), channel_id=1, source_target_pairs={{0,2},{1,3},{2,4},{3,5},{4,6},{5,7},{6,0},{7,1},{8,10},{9,11},{10,... | collective-permute-start | bytes 589832 | tf_op jit(solution)/shard_map/ppermute | solution.py:327
  126.2 2.0 %collective-permute-start.19 = (f32[192,256]{1,0:T(8,128)S(1)}, f32[192,256]{1,0:T(8,128)S(1)}, u32[]{:S(2)}, u32[]{:S(2)}) collective-permute-start(f32[192,256]{1,0:T(8,128)S(1)} %get-tuple-element.45), channel_id=1, source_target_pairs={{0,6},{1,7},{2,0},{3,1},{4,2},{5,3},{6,4},{7,5},{8,14},{9,15},{10,... | collective-permute-start | bytes 589832 | tf_op jit(solution)/shard_map/ppermute | solution.py:327
  128.2 4.7 %backward_2.1.run_ref = f32[384,256]{1,0:T(8,128)S(1)} custom-call(s32[2]{0:T(128)S(1)} %dynamic-slice_reduce_fusion.partner_ref, f32[2,384]{1,0:T(2,128)S(1)} %sum_lines.1.own_ref.refs_0_.refs_1_.refs_2_.line_ref, f32[2,384]{1,0:T(2,128)S(1)} %sum_lines.1.own_ref.refs_0_.refs_1_.refs_2_.line_ref, ...), custom_call_target="tpu_custom_call" | custom-call | flops 1358954496 | bytes 3538944 | tf_op jit(solution)/shard_map/backward_2/pallas_call | solution.py:262
  133.5 5.0 %collective-permute-done.19.high1 = f32[192,256]{1,0:T(8,128)S(1)} collective-permute-done((f32[192,256]{1,0:T(8,128)S(1)}, f32[192,256]{1,0:T(8,128)S(1)}, u32[]{:S(2)}, u32[]{:S(2)}) %collective-permute-start.19) | collective-permute-done | bytes 196640 | tf_op jit(solution)/shard_map/ppermute | solution.py:327
  (53 shorter events, 13.5 us)
Async XLA Ops:
  1.6 31.5 %copy-start.3 = (s32[384]{0:T(512)S(1)}, s32[384]{0:T(512)}, u32[]{:S(2)}) copy-start(s32[384]{0:T(512)} %param.4) | copy-start | bytes 4612
  2.4 18.6 %all-to-all-start = ((f32[32,24,128]{2,1,0:T(8,128)}), f32[32,24,128]{2,1,0:T(8,128)S(1)}, u32[]{:S(2)}, u32[]{:S(2)}) async-start(f32[32,24,128]{2,1,0:T(8,128)} %bitcast), calls=%async_computation | async-start | bytes 786432 | tf_op jit(solution)/shard_map/all_to_all | solution.py:333
  22.5 34.9 %all-to-all-start.1 = ((f32[32,48,128]{2,1,0:T(8,128)}), f32[32,48,128]{2,1,0:T(8,128)S(1)}, u32[]{:S(2)}, u32[]{:S(2)}) async-start(f32[32,48,128]{2,1,0:T(8,128)} %bitcast.2), calls=%async_computation.1 | async-start | bytes 1572864 | tf_op jit(solution)/shard_map/all_to_all | solution.py:335
  27.6 29.9 %collective-permute-start = (f32[384,256]{1,0:T(8,128)S(1)}, f32[384,256]{1,0:T(8,128)S(1)}, u32[]{:S(2)}, u32[]{:S(2)}) collective-permute-start(f32[384,256]{1,0:T(8,128)S(1)} %copy-done.1), channel_id=1, source_target_pairs={{0,2},{1,3},{2,4},{3,5},{4,6},{5,7},{6,0},{7,1},{8,10},{9,11},{10,... | collective-permute-start | bytes 1179656 | tf_op jit(solution)/shard_map/ppermute | solution.py:327
  30.9 26.5 %collective-permute-start.1 = (f32[384,256]{1,0:T(8,128)S(1)}, f32[384,256]{1,0:T(8,128)S(1)}, u32[]{:S(2)}, u32[]{:S(2)}) collective-permute-start(f32[384,256]{1,0:T(8,128)S(1)} %copy-done.1), channel_id=1, source_target_pairs={{0,6},{1,7},{2,0},{3,1},{4,2},{5,3},{6,4},{7,5},{8,14},{9,15},{10,... | collective-permute-start | bytes 1179656 | tf_op jit(solution)/shard_map/ppermute | solution.py:327
  33.1 24.3 %collective-permute-start.2 = (f32[384,256]{1,0:T(8,128)S(1)}, f32[384,256]{1,0:T(8,128)S(1)}, u32[]{:S(2)}, u32[]{:S(2)}) collective-permute-start(f32[384,256]{1,0:T(8,128)S(1)} %copy-done.1), channel_id=1, source_target_pairs={{0,1},{1,0},{2,3},{3,2},{4,5},{5,4},{6,7},{7,6},{8,9},{9,8},{10,11... | collective-permute-start | bytes 1179656 | tf_op jit(solution)/shard_map/ppermute | solution.py:330
  33.1 1.7 %collective-permute-start.3 = (s32[384]{0:T(512)S(1)}, s32[384]{0:T(512)S(1)}, u32[]{:S(2)}, u32[]{:S(2)}) collective-permute-start(s32[384]{0:T(512)S(1)} %copy-done.3), channel_id=1, source_target_pairs={{0,1},{1,0},{2,3},{3,2},{4,5},{5,4},{6,7},{7,6},{8,9},{9,8},{10,11... | collective-permute-start | bytes 4616 | tf_op jit(solution)/shard_map/ppermute | solution.py:330
  57.5 4.6 %collective-permute-start.4 = (f32[32,48,128]{2,1,0:T(8,128)S(1)}, f32[32,48,128]{2,1,0:T(8,128)S(1)}, u32[]{:S(2)}, u32[]{:S(2)}) collective-permute-start(f32[32,48,128]{2,1,0:T(8,128)S(1)} %all-to-all-done.1.refs_2_), channel_id=1, source_target_pairs={{0,1},{1,0},{2,3},{3,2},{4,5},{5,4},{6,7},{7,6},{8,9},{9,8},{10,11... | collective-permute-start | bytes 2359304 | tf_op jit(solution)/shard_map/ppermute | solution.py:330
  57.6 17.9 %collective-permute-start.7 = (f32[192,256]{1,0:T(8,128)S(1)}, f32[192,256]{1,0:T(8,128)S(1)}, u32[]{:S(2)}, u32[]{:S(2)}) collective-permute-start(f32[192,256]{1,0:T(8,128)S(1)} %slice.6), channel_id=1, source_target_pairs={{0,2},{1,3},{2,4},{3,5},{4,6},{5,7},{6,0},{7,1},{8,10},{9,11},{10,... | collective-permute-start | bytes 589832 | tf_op jit(solution)/shard_map/ppermute | solution.py:327
  57.7 17.8 %collective-permute-start.8 = (f32[192,256]{1,0:T(8,128)S(1)}, f32[192,256]{1,0:T(8,128)S(1)}, u32[]{:S(2)}, u32[]{:S(2)}) collective-permute-start(f32[192,256]{1,0:T(8,128)S(1)} %slice.7), channel_id=1, source_target_pairs={{0,6},{1,7},{2,0},{3,1},{4,2},{5,3},{6,4},{7,5},{8,14},{9,15},{10,... | collective-permute-start | bytes 589832 | tf_op jit(solution)/shard_map/ppermute | solution.py:327
  72.4 9.2 %collective-permute-start.5 = (f32[2,384]{1,0:T(2,128)S(1)}, f32[2,384]{1,0:T(2,128)S(1)}, u32[]{:S(2)}, u32[]{:S(2)}) collective-permute-start(f32[2,384]{1,0:T(2,128)S(1)} %get-tuple-element.32), channel_id=1, source_target_pairs={{0,6},{1,7},{2,0},{3,1},{4,2},{5,3},{6,4},{7,5},{8,14},{9,15},{10,... | collective-permute-start | bytes 9224 | tf_op jit(solution)/shard_map/ppermute | solution.py:327
  72.9 8.8 %collective-permute-start.6 = (f32[2,384]{1,0:T(2,128)S(1)}, f32[2,384]{1,0:T(2,128)S(1)}, u32[]{:S(2)}, u32[]{:S(2)}) collective-permute-start(f32[2,384]{1,0:T(2,128)S(1)} %get-tuple-element.33), channel_id=1, source_target_pairs={{0,2},{1,3},{2,4},{3,5},{4,6},{5,7},{6,0},{7,1},{8,10},{9,11},{10,... | collective-permute-start | bytes 9224 | tf_op jit(solution)/shard_map/ppermute | solution.py:327
  80.1 7.6 %collective-permute-start.9 = (f32[2,384]{1,0:T(2,128)S(1)}, f32[2,384]{1,0:T(2,128)S(1)}, u32[]{:S(2)}, u32[]{:S(2)}) collective-permute-start(f32[2,384]{1,0:T(2,128)S(1)} %get-tuple-element.34), channel_id=1, source_target_pairs={{0,4},{1,5},{2,6},{3,7},{4,0},{5,1},{6,2},{7,3},{8,12},{9,13},{10,... | collective-permute-start | bytes 9224 | tf_op jit(solution)/shard_map/ppermute | solution.py:327
  87.7 1.2 collective-permute-start.10
  89.5 15.2 %all-to-all-start.2 = ((f32[32,1,768]{2,1,0:T(1,128)}), f32[32,1,768]{2,1,0:T(1,128)S(1)}, u32[]{:S(2)}, u32[]{:S(2)}) async-start(f32[32,1,768]{2,1,0:T(1,128)} %spread.1), calls=%async_computation.2 | async-start | bytes 196608 | tf_op jit(solution)/shard_map/all_to_all | solution.py:353
  97.0 7.7 %collective-permute-start.13 = (f32[2,384]{1,0:T(2,128)S(1)}, f32[2,384]{1,0:T(2,128)S(1)}, u32[]{:S(2)}, u32[]{:S(2)}) collective-permute-start(f32[2,384]{1,0:T(2,128)S(1)} %sum_lines.1.own_ref.refs_0_.refs_1_.refs_2_.line_ref), channel_id=1, source_target_pairs={{0,4},{1,5},{2,6},{3,7},{4,0},{5,1},{6,2},{7,3},{8,12},{9,13},{10,... | collective-permute-start | bytes 9224 | tf_op jit(solution)/shard_map/ppermute | solution.py:327
  100.4 13.1 %collective-permute-start.11 = (f32[2,384]{1,0:T(2,128)S(1)}, f32[2,384]{1,0:T(2,128)S(1)}, u32[]{:S(2)}, u32[]{:S(2)}) collective-permute-start(f32[2,384]{1,0:T(2,128)S(1)} %sum_lines.1.own_ref.refs_0_.refs_1_.refs_2_.line_ref), channel_id=1, source_target_pairs={{0,2},{1,3},{2,4},{3,5},{4,6},{5,7},{6,0},{7,1},{8,10},{9,11},{10,... | collective-permute-start | bytes 9224 | tf_op jit(solution)/shard_map/ppermute | solution.py:327
  101.2 12.4 %collective-permute-start.12 = (f32[2,384]{1,0:T(2,128)S(1)}, f32[2,384]{1,0:T(2,128)S(1)}, u32[]{:S(2)}, u32[]{:S(2)}) collective-permute-start(f32[2,384]{1,0:T(2,128)S(1)} %sum_lines.1.own_ref.refs_0_.refs_1_.refs_2_.line_ref), channel_id=1, source_target_pairs={{0,6},{1,7},{2,0},{3,1},{4,2},{5,3},{6,4},{7,5},{8,14},{9,15},{10,... | collective-permute-start | bytes 9224 | tf_op jit(solution)/shard_map/ppermute | solution.py:327
  109.4 14.6 %collective-permute-start.14 = (f32[192,256]{1,0:T(8,128)S(1)}, f32[192,256]{1,0:T(8,128)S(1)}, u32[]{:S(2)}, u32[]{:S(2)}) collective-permute-start(f32[192,256]{1,0:T(8,128)S(1)} %get-tuple-element.39), channel_id=1, source_target_pairs={{0,2},{1,3},{2,4},{3,5},{4,6},{5,7},{6,0},{7,1},{8,10},{9,11},{10,... | collective-permute-start | bytes 589832 | tf_op jit(solution)/shard_map/ppermute | solution.py:327
  111.6 12.3 %collective-permute-start.15 = (f32[192,256]{1,0:T(8,128)S(1)}, f32[192,256]{1,0:T(8,128)S(1)}, u32[]{:S(2)}, u32[]{:S(2)}) collective-permute-start(f32[192,256]{1,0:T(8,128)S(1)} %get-tuple-element.41), channel_id=1, source_target_pairs={{0,6},{1,7},{2,0},{3,1},{4,2},{5,3},{6,4},{7,5},{8,14},{9,15},{10,... | collective-permute-start | bytes 589832 | tf_op jit(solution)/shard_map/ppermute | solution.py:327
  120.9 12.5 %collective-permute-start.17 = (f32[192,256]{1,0:T(8,128)S(1)}, f32[192,256]{1,0:T(8,128)S(1)}, u32[]{:S(2)}, u32[]{:S(2)}) collective-permute-start(f32[192,256]{1,0:T(8,128)S(1)} %get-tuple-element.43), channel_id=1, source_target_pairs={{0,6},{1,7},{2,0},{3,1},{4,2},{5,3},{6,4},{7,5},{8,14},{9,15},{10,... | collective-permute-start | bytes 589832 | tf_op jit(solution)/shard_map/ppermute | solution.py:327
  121.2 12.2 %collective-permute-start.18 = (f32[192,256]{1,0:T(8,128)S(1)}, f32[192,256]{1,0:T(8,128)S(1)}, u32[]{:S(2)}, u32[]{:S(2)}) collective-permute-start(f32[192,256]{1,0:T(8,128)S(1)} %get-tuple-element.44), channel_id=1, source_target_pairs={{0,2},{1,3},{2,4},{3,5},{4,6},{5,7},{6,0},{7,1},{8,10},{9,11},{10,... | collective-permute-start | bytes 589832 | tf_op jit(solution)/shard_map/ppermute | solution.py:327
  124.0 9.5 %collective-permute-start.16 = (f32[192,256]{1,0:T(8,128)S(1)}, f32[192,256]{1,0:T(8,128)S(1)}, u32[]{:S(2)}, u32[]{:S(2)}) collective-permute-start(f32[192,256]{1,0:T(8,128)S(1)} %get-tuple-element.42), channel_id=1, source_target_pairs={{0,2},{1,3},{2,4},{3,5},{4,6},{5,7},{6,0},{7,1},{8,10},{9,11},{10,... | collective-permute-start | bytes 589832 | tf_op jit(solution)/shard_map/ppermute | solution.py:327
  126.2 12.2 %collective-permute-start.19 = (f32[192,256]{1,0:T(8,128)S(1)}, f32[192,256]{1,0:T(8,128)S(1)}, u32[]{:S(2)}, u32[]{:S(2)}) collective-permute-start(f32[192,256]{1,0:T(8,128)S(1)} %get-tuple-element.45), channel_id=1, source_target_pairs={{0,6},{1,7},{2,0},{3,1},{4,2},{5,3},{6,4},{7,5},{8,14},{9,15},{10,... | collective-permute-start | bytes 589832 | tf_op jit(solution)/shard_map/ppermute | solution.py:327
  (3 other events, 54.8 us)

commit v2 on v1

v2 whole, which is shorter than its diff:
```python
import functools

import jax
import jax.numpy as jnp
from jax import lax
from jax.experimental import pallas as pl
from jax.experimental.pallas import tpu as pltpu
from jax.sharding import PartitionSpec as P

LOGIT_DIVISOR = 0.1
EPSILON = 1e-06
SLICE = 384
WIDTH = 256
SELF = 2
VMEM = 16 * 1024 * 1024
VMEM_LARGE = 44 * 1024 * 1024
HBM = pl.BlockSpec(memory_space=pltpu.HBM)
SMEM = pl.BlockSpec(memory_space=pltpu.SMEM)


def split(values):
    hi = values.astype(jnp.bfloat16)
    lo = (values - hi.astype(jnp.float32)).astype(jnp.bfloat16)
    return hi, lo


def rows_of(tiles):
    pairs = tiles.reshape(tiles.shape[0] // 2, 2, 8, 128)
    rows = tiles.shape[0] * 4
    return jnp.concatenate([pairs[:, 0].reshape(rows, 128), pairs[:, 1].reshape(rows, 128)], axis=1)


def radius_of(values):
    return jnp.sqrt(jnp.sum(values * values, axis=-1, keepdims=True) + EPSILON)


def as_column(line):
    return jnp.broadcast_to(line, (128, line.shape[1])).T


def in_hbm(value):
    return pltpu.with_memory_space_constraint(value, pltpu.HBM)


def params(limit=VMEM):
    return pltpu.CompilerParams(vmem_limit_bytes=limit)


def tile_kernel(emb_ref, tile_ref):
    rows = emb_ref.shape[0]
    for half in range(2):
        tile_ref[:, half] = emb_ref[:, half * 128 : half * 128 + 128].reshape(rows // 8, 8, 128)


def as_tiles(embeddings):
    rows, _ = embeddings.shape
    return pl.pallas_call(
        tile_kernel,
        out_shape=jax.ShapeDtypeStruct((rows // 8, 2, 8, 128), jnp.float32),
        compiler_params=params(),
        name="as_tiles",
    )(embeddings)


def prepare_kernel(left, right, mine, out_ref):
    at = 0
    for ref in (left, right, mine):
        values = ref[...]
        hi, lo = split(values * (1.0 / (radius_of(values) * LOGIT_DIVISOR)))
        out_ref[at : at + hi.shape[0]] = jnp.concatenate([hi, lo, hi], axis=1)
        at += hi.shape[0]


def prepare(left, right, mine):
    shape = (3 * SLICE, 3 * WIDTH)
    return pl.pallas_call(
        prepare_kernel,
        out_shape=jax.ShapeDtypeStruct(shape, jnp.bfloat16),
        cost_estimate=pl.CostEstimate(flops=20 * 10**9, bytes_accessed=4 * shape[0] * WIDTH, transcendentals=0),
        compiler_params=params(),
        name="prepare",
    )(left, right, mine)


def forward_kernel(
    ready, mine, far0, far1, sib, got, got_sib, pos_ref, e_out, c_out, line_ref,
    left_ref, e_buf, c_buf, tot_ref, e_sem, c_sem, ready_sem,
):
    orders, _, count = e_buf.shape
    wide = 2 * SLICE

    at = ready.shape[0]
    ready_copy = pltpu.make_async_copy(ready, left_ref.at[pl.ds(0, at)], ready_sem)
    ready_copy.start()
    for ref in (far0, far1):
        values = ref[...]
        hi, lo = split(values * (1.0 / (radius_of(values) * LOGIT_DIVISOR)))
        left_ref[at : at + hi.shape[0]] = jnp.concatenate([hi, lo, hi], axis=1)
        at += hi.shape[0]
    half = got.shape[1] // 2
    tiles = got.shape[0] * half // 8

    copies = []
    for base in range(0, count, wide):
        for which, ref in enumerate((mine, sib) if base == 0 else (got, got_sib)):
            if base == 0:
                piece = ref[...]
            else:
                begin = (base // wide - 1) * half
                piece = rows_of(ref[:, begin : begin + half].reshape(tiles, 8, 128))
            hi, lo = split(piece * (1.0 / radius_of(piece)))
            c_buf[base + which * SLICE : base + which * SLICE + SLICE] = jnp.concatenate([hi, lo], axis=1)
        view = (pl.ds(base, wide),)
        copies.append(pltpu.make_async_copy(c_buf.at[view], c_out.at[view], c_sem.at[base // wide]))
        copies[-1].start()
        if base == 0:
            ready_copy.wait()
        for order in range(0, orders, 2):
            band = slice(order * SLICE, (order + 2) * SLICE)
            col = c_buf[base : base + wide]
            hi, lo = col[:, :WIDTH], col[:, WIDTH:]
            scores = lax.dot_general(
                left_ref[band],
                jnp.concatenate([hi, hi, lo], axis=1),
                (((1,), (1,)), ((), ())),
                preferred_element_type=jnp.float32,
            )
            total = jnp.zeros((wide, 128), jnp.float32) if base == 0 else tot_ref[0, band]
            if base == 0:
                match = jnp.zeros((wide, 128), jnp.float32)
                row_ids = lax.broadcasted_iota(jnp.int32, (wide, 128), 0) + order * SLICE
                lane_ids = lax.broadcasted_iota(jnp.int32, (wide, 128), 1)
            for k in range(0, wide, 128):
                score = scores[:, k : k + 128]
                e = jnp.exp(score)
                if base == 0:
                    match = match + jnp.where(row_ids == pos_ref[:, k : k + 128], score, 0.0)
                    if order == SELF and k < SLICE:
                        e = jnp.where(row_ids - SELF * SLICE == lane_ids + k, 0.0, e)
                total = total + e
                e_buf[order : order + 2, :, base + k : base + k + 128] = e.reshape(2, SLICE, 128)
            tot_ref[0, band] = total
            if base == 0:
                tot_ref[1, band] = match
            view = (pl.ds(order, 2), slice(None), pl.ds(base, wide))
            sem = e_sem.at[base // wide * 2 + order // 2]
            copies.append(pltpu.make_async_copy(e_buf.at[view], e_out.at[view], sem))
            copies[-1].start()

    line = jnp.concatenate([jnp.sum(tot_ref[k].T, axis=0, keepdims=True) for k in range(2)], axis=0)
    for member in range(line_ref.shape[0]):
        line_ref[member] = line
    for copy in copies:
        copy.wait()


def forward(operands, members):
    rows, count = 4 * SLICE, 6 * SLICE
    return pl.pallas_call(
        forward_kernel,
        in_specs=[HBM] + [pl.BlockSpec()] * (len(operands) - 1),
        out_specs=[HBM, HBM, pl.BlockSpec()],
        out_shape=(
            pltpu.HBM((4, SLICE, count), jnp.float32),
            pltpu.HBM((count, 2 * WIDTH), jnp.bfloat16),
            jax.ShapeDtypeStruct((members, 2, rows), jnp.float32),
        ),
        scratch_shapes=[
            pltpu.VMEM((rows, 3 * WIDTH), jnp.bfloat16),
            pltpu.VMEM((4, SLICE, count), jnp.float32),
            pltpu.VMEM((count, 2 * WIDTH), jnp.bfloat16),
            pltpu.VMEM((2, rows, 128), jnp.float32),
            pltpu.SemaphoreType.DMA((6,)),
            pltpu.SemaphoreType.DMA((3,)),
            pltpu.SemaphoreType.DMA,
        ],
        cost_estimate=pl.CostEstimate(
            flops=6 * rows * count * WIDTH, bytes_accessed=4 * rows * count, transcendentals=rows * count
        ),
        compiler_params=params(VMEM_LARGE),
        name="forward",
    )(in_hbm(operands[0]), *operands[1:])


def denominator_kernel(member_ref, all_ref, row_ref, own_ref, line_ref, spread_ref):
    member = member_ref[0]
    members = all_ref.shape[0]

    def summed(owner, kind):
        value = 0.0
        for by, order in ((0, SELF), (2, 0), (members - 2, 1), (4, 3)):
            held = all_ref[lax.rem(owner + by, members)]
            value = value + held[kind : kind + 1, order * SLICE : order * SLICE + SLICE]
        return value

    mate = member + 1 - 2 * lax.rem(member, 2)
    own = summed(member, 0)
    line_ref[0:1] = own
    line_ref[1:2] = summed(member, 1)
    both = jnp.concatenate([own, summed(mate, 0)], axis=1)
    own_ref[...] = both
    spread_ref[...] = jnp.broadcast_to(both.reshape(1, 1, 2 * SLICE), spread_ref.shape)
    for order, by in enumerate((members - 2, 2, 0, 4)):
        value = own if by == 0 else summed(lax.rem(member + by, members), 0)
        row_ref[:, order * SLICE : order * SLICE + SLICE] = value


def denominators(member, everything, groups):
    return pl.pallas_call(
        denominator_kernel,
        in_specs=[SMEM, pl.BlockSpec()],
        out_shape=(
            jax.ShapeDtypeStruct((1, 4 * SLICE), jnp.float32),
            jax.ShapeDtypeStruct((1, 2 * SLICE), jnp.float32),
            jax.ShapeDtypeStruct((2, SLICE), jnp.float32),
            jax.ShapeDtypeStruct((groups, 1, 2 * SLICE), jnp.float32),
        ),
        compiler_params=params(),
        name="denominators",
    )(member, everything)


def backward_kernel(
    order, partner_ref, row_ref, own_ref, everyone_ref, pos_ref, e_in, c_in, *refs
):
    out_refs, (run_ref, e_buf, c_buf, e_sem, c_sem) = refs[:-5], refs[-5:]
    slices = e_buf.shape[0]
    wide = 2 * SLICE
    copies = []
    for k in range(3):
        wanted = pl.ds(k * wide, wide)
        copies.append(
            pltpu.make_async_copy(
                e_in.at[pl.ds(order, slices), :, wanted], e_buf.at[:, :, wanted], e_sem.at[k]
            )
        )
        copies.append(pltpu.make_async_copy(c_in.at[wanted], c_buf.at[wanted], c_sem.at[k]))
    for copy in copies:
        copy.start()

    rows = slices * SLICE
    row_inv = 1.0 / as_column(row_ref[:, order * SLICE : order * SLICE + rows])
    row_ids = lax.broadcasted_iota(jnp.int32, (rows, 128), 0) + order * SLICE
    for k in range(3):
        col_inv = 1.0 / (own_ref[...] if k == 0 else everyone_ref[partner_ref[k - 1]])
        copies[2 * k].wait()
        copies[2 * k + 1].wait()
        his, los = [], []
        for at in range(0, wide, 128):
            e = e_buf[:, :, k * wide + at : k * wide + at + 128].reshape(rows, 128)
            weight = e * (row_inv + col_inv[:, at : at + 128])
            if k == 0:
                weight = weight - jnp.where(row_ids == pos_ref[:, at : at + 128], 2.0, 0.0)
            hi, lo = split(weight)
            his.append(hi)
            los.append(lo)
        cols = c_buf[k * wide : k * wide + wide]
        c_hi, c_lo = cols[:, :WIDTH], cols[:, WIDTH:]
        part = jnp.dot(
            jnp.concatenate(his + his + los, axis=1),
            jnp.concatenate([c_hi, c_lo, c_hi], axis=0),
            preferred_element_type=jnp.float32,
        )
        if k == 0:
            run_ref[...] = part
        elif k == 1:
            run_ref[...] += part
        else:
            part = run_ref[...] + part
            size = rows // len(out_refs)
            for which, ref in enumerate(out_refs):
                ref[...] = part[which * size : which * size + size]


def backward(order, slices, pieces, partners, row_den, own_den, everyone, pos, e, cols):
    count = 6 * SLICE
    return pl.pallas_call(
        functools.partial(backward_kernel, order),
        in_specs=[SMEM] + [pl.BlockSpec()] * 4 + [HBM] * 2,
        out_shape=[jax.ShapeDtypeStruct((slices * SLICE // pieces, WIDTH), jnp.float32)] * pieces,
        scratch_shapes=[
            pltpu.VMEM((slices * SLICE, WIDTH), jnp.float32),
            pltpu.VMEM((slices, SLICE, count), jnp.float32),
            pltpu.VMEM((count, 2 * WIDTH), jnp.bfloat16),
            pltpu.SemaphoreType.DMA((3,)),
            pltpu.SemaphoreType.DMA((3,)),
        ],
        cost_estimate=pl.CostEstimate(
            flops=6 * slices * SLICE * count * WIDTH, bytes_accessed=4 * slices * SLICE * count, transcendentals=0
        ),
        compiler_params=params(VMEM_LARGE),
        name="backward_%d" % order,
    )(partners, row_den, own_den, everyone, pos, in_hbm(e), in_hbm(cols))


def add_kernel(a_ref, b_ref, c_ref, d_ref, ab_ref, cd_ref):
    ab_ref[...] = a_ref[...] + b_ref[...]
    cd_ref[...] = c_ref[...] + d_ref[...]


def add_pairs(a, b, c, d):
    out = jax.ShapeDtypeStruct(a.shape, jnp.float32)
    return pl.pallas_call(add_kernel, out_shape=(out, out), compiler_params=params(), name="add_pairs")(
        a, b, c, d
    )


def finish_kernel(emb_ref, run_ref, low0, low1, high0, high1, line_ref, loss_ref, grad_ref):
    values = emb_ref[...]
    radius = radius_of(values)
    unit = values / radius
    low, high = low0[...] + low1[...], high0[...] + high1[...]
    slope = (run_ref[...] + jnp.concatenate([low, high], axis=0)) / LOGIT_DIVISOR
    grad_ref[...] = (slope - unit * jnp.sum(unit * slope, axis=-1, keepdims=True)) / radius
    loss_ref[...] = jnp.log(line_ref[0:1]) - line_ref[1:2]


def finish(embeddings, run, lows, highs, line):
    rows, width = embeddings.shape
    return pl.pallas_call(
        finish_kernel,
        out_shape=(
            jax.ShapeDtypeStruct((1, rows), jnp.float32),
            jax.ShapeDtypeStruct((rows, width), jnp.float32),
        ),
        compiler_params=params(),
        name="finish",
    )(embeddings, run, *lows, *highs, line)


def local(embeddings, positive, pairing):
    rows, width = embeddings.shape
    members = lax.axis_size("mem")
    groups = lax.axis_size("grp")
    block = rows * members
    rounds = pairing.shape[0]
    group = lax.axis_index("grp")
    member = lax.axis_index("mem")
    half = rows // 2

    def shift(value, by):
        return lax.ppermute(value, "mem", [(m, (m + by) % members) for m in range(members)])

    def swap(value):
        return lax.ppermute(value, "mem", [(m, m ^ 1) for m in range(members)])

    left, right = shift(embeddings, 2), shift(embeddings, -2)
    far = (shift(left[:half], 2), shift(right[half:], -2))
    per = rows * width // (groups * 128)
    pieces = lax.all_to_all(as_tiles(embeddings).reshape(groups, per, 128), "grp", 0, 0, tiled=True)
    picked = pieces[pairing.T].reshape(groups, rounds * per, 128)
    got = lax.all_to_all(picked, "grp", 0, 0, tiled=True)
    sib, pos_sib = swap(embeddings), swap(positive)
    ready = prepare(left, right, embeddings)
    got, ready, sib, pos_sib = lax.optimization_barrier((got, ready, sib, pos_sib))

    both = jnp.concatenate([positive, pos_sib]) - group * block
    owner = both // rows
    turn = (owner // 2 - member // 2) % (members // 2)
    order = jnp.where(turn == 0, SELF, jnp.where(turn == 3, 0, jnp.where(turn == 1, 1, 3)))
    pos = jnp.where(owner % 2 == member % 2, order * rows + both % rows, -1).reshape(1, 2 * rows)

    e, cols, line = forward((ready, embeddings, *far, sib, got, swap(got), pos), members)

    everything = lax.all_to_all(line, "mem", 0, 0, tiled=True)
    row_den, own_den, line, spread = denominators(jnp.reshape(member, (1,)), everything, groups)
    everyone = lax.all_to_all(spread, "grp", 0, 0, tiled=True)

    shared = (pairing[:, group], row_den, own_den, everyone, pos, e, cols)
    far_low, far_high = backward(3, 1, 2, *shared)
    far_low, far_high = shift(far_low, 2), shift(far_high, -2)
    left_low, left_high, right_low, right_high = backward(0, 2, 4, *shared)
    high0, low1 = shift(right_high, 2), shift(left_low, -2)
    right_low, left_high = add_pairs(right_low, far_low, left_high, far_high)
    low0, high1 = shift(right_low, 2), shift(left_high, -2)
    (run,) = backward(SELF, 1, 1, *shared)
    loss, grad = finish(embeddings, run, (low0, low1), (high0, high1), line)
    return loss.reshape(rows), grad


def solution(mesh):
    placed = (P(("grp", "mem"), None), P(("grp", "mem")), P())
    return jax.shard_map(
        local,
        mesh=mesh,
        in_specs=placed,
        out_specs=(P(("grp", "mem")), P(("grp", "mem"), None)),
        check_vma=False,
    )
```

time: 143 us -> 139 us (0.972); the launches traced: 140 us -> 138 us
  starting transfers between devices: 55.5 us -> 42 us
  blocking collectives: 0 us -> 11.7 us
  Pallas kernels: 34.1 us -> 29.4 us
  waiting for transfers between devices: 45.4 us -> 48.1 us
  local copies, waits for them, and re-layouts: 2.95 us -> 4.83 us
    ppermute x16 -> x10, waiting for transfers between devices: 34.2 us -> 19.5 us  [shift(): lax.ppermute(value, 'mem', [(m, (m + by) % members) for m in range(member...]
    all_to_all x0 -> x1, blocking collectives: none -> 11.7 us  [local(): everything = lax.all_to_all(line, 'mem', 0, 0, tiled=True)]
    ppermute x16 -> x10, starting transfers between devices: 33.5 us -> 22.1 us  [shift(): lax.ppermute(value, 'mem', [(m, (m + by) % members) for m in range(member...]
    all_to_all x1, waiting for transfers between devices: 0.01 us -> 8.87 us  [local(): got = lax.all_to_all(picked, 'grp', 0, 0, tiled=True)]
    all_to_all x1, waiting for transfers between devices: 0.01 us -> 7.13 us  [local(): everyone = lax.all_to_all(spread, 'grp', 0, 0, tiled=True)]
    pallas_call x8 -> x6, Pallas kernels: 32.2 us -> 27.5 us  [the longest x3 16.7 us: backward(): pl.pallas_call(functools.partial(backward_kernel, order), in_specs=[SMEM]...]
    all_to_all x1, waiting for transfers between devices: 8.81 us -> 12.6 us  [local(): lax.all_to_all(as_tiles(embeddings).reshape(groups, per, 128), 'grp', 0,...]
    ppermute x4 -> x3, waiting for transfers between devices: 2.37 us -> 0.01 us  [swap(): return lax.ppermute(value, 'mem', [(m, m ^ 1) for m in range(members)])]
  transfers between devices with their start and end apart: 23 -> 16, of which waited for: 7 -> 9; matrix products, arithmetic and copies ran while one was open for 1% -> 2% of each run, Pallas kernels for 23% -> 9%
where the time goes in v2:
time: 139 us; the launch traced here: 138 us
  waiting for transfers between devices  48.1 us (35%)
  starting transfers between devices  42 us (30%)
  Pallas kernels  29.4 us (21%)
  blocking collectives  11.7 us (8%)
  local copies, waits for them, and re-layouts  4.83 us (3%)
    ppermute x10, starting transfers between devices, shift(): lax.ppermute(value, 'mem', [(m, (m + by) % members) for m in range(member...  22.1 us
    ppermute x10, waiting for transfers between devices, shift(): lax.ppermute(value, 'mem', [(m, (m + by) % members) for m in range(member...  19.5 us
    pallas_call x3, Pallas kernels, backward(): pl.pallas_call(functools.partial(backward_kernel, order), in_specs=[SMEM]...  16.7 us
    all_to_all x1, waiting for transfers between devices, local(): lax.all_to_all(as_tiles(embeddings).reshape(groups, per, 128), 'grp', 0,...  12.6 us
    all_to_all x1, blocking collectives, local(): everything = lax.all_to_all(line, 'mem', 0, 0, tiled=True)  11.7 us
    pallas_call x1, Pallas kernels, forward(): pl.pallas_call(forward_kernel, in_specs=[HBM] + [pl.BlockSpec()] * (len(o...  9.6 us
    all_to_all x1, starting transfers between devices, local(): lax.all_to_all(as_tiles(embeddings).reshape(groups, per, 128), 'grp', 0,...  8.89 us
    all_to_all x1, waiting for transfers between devices, local(): got = lax.all_to_all(picked, 'grp', 0, 0, tiled=True)  8.87 us
  transfers between devices with their start and end apart: 16, of which 9 were waited for; matrix products, arithmetic and copies ran while one was open for 2% of the time, Pallas kernels for 9%

profile of v2, /device:TPU:8, one launch (start us, length us, event | category | flops | bytes accessed | tf_op | source)
XLA Modules:
  0.0 138.2 jit_solution(16377122728109862745)
XLA Ops:
  0.6 1.0 copy-done
  2.4 8.9 %all-to-all-start = ((f32[32,24,128]{2,1,0:T(8,128)}), f32[32,24,128]{2,1,0:T(8,128)S(1)}, u32[]{:S(2)}, u32[]{:S(2)}) async-start(f32[32,24,128]{2,1,0:T(8,128)} %bitcast.1), calls=%async_computation | async-start | bytes 786432 | tf_op jit(solution)/shard_map/all_to_all | solution.py:350
  11.3 5.5 %collective-permute-start.1 = (f32[384,256]{1,0:T(8,128)}, f32[384,256]{1,0:T(8,128)S(1)}, u32[]{:S(2)}, u32[]{:S(2)}) collective-permute-start(f32[384,256]{1,0:T(8,128)} %emb_ref.3), channel_id=1, source_target_pairs={{0,6},{1,7},{2,0},{3,1},{4,2},{5,3},{6,4},{7,5},{8,14},{9,15},{10,... | collective-permute-start | bytes 1179656 | tf_op jit(solution)/shard_map/ppermute | solution.py:342
  18.2 12.6 %all-to-all-done = f32[32,24,128]{2,1,0:T(8,128)S(1)} async-done(((f32[32,24,128]{2,1,0:T(8,128)}), f32[32,24,128]{2,1,0:T(8,128)S(1)}, u32[]{:S(2)}, u32[]{:S(2)}) %all-to-all-start) | async-done | bytes 393248 | tf_op jit(solution)/shard_map/all_to_all | solution.py:350
  30.8 1.5 %gather_fusion = f32[64,24,128]{2,1,0:T(8,128)} fusion(f32[32,24,128]{2,1,0:T(8,128)S(1)} %all-to-all-done, s32[1024]{0:T(1024)S(1)} %pad_clamp_fusion), kind=kCustom, calls=%fused_computation | custom fusion | bytes 1573120 | tf_op jit(solution)/shard_map/gather | solution.py:351
  32.3 5.0 %all-to-all-start.1 = ((f32[32,48,128]{2,1,0:T(8,128)}), f32[32,48,128]{2,1,0:T(8,128)S(1)}, u32[]{:S(2)}, u32[]{:S(2)}) async-start(f32[32,48,128]{2,1,0:T(8,128)} %bitcast.3), calls=%async_computation.1 | async-start | bytes 1572864 | tf_op jit(solution)/shard_map/all_to_all | solution.py:352
  38.5 1.2 copy-done.2
  39.7 8.9 %all-to-all-done.1.got = f32[32,48,128]{2,1,0:T(8,128)S(1)} async-done(((f32[32,48,128]{2,1,0:T(8,128)}), f32[32,48,128]{2,1,0:T(8,128)S(1)}, u32[]{:S(2)}, u32[]{:S(2)}) %all-to-all-start.1) | async-done | bytes 786464 | tf_op jit(solution)/shard_map/all_to_all | solution.py:352
  48.6 5.2 %collective-permute-start.5 = (f32[192,256]{1,0:T(8,128)S(1)}, f32[192,256]{1,0:T(8,128)S(1)}, u32[]{:S(2)}, u32[]{:S(2)}) collective-permute-start(f32[192,256]{1,0:T(8,128)S(1)} %slice.11), channel_id=1, source_target_pairs={{0,6},{1,7},{2,0},{3,1},{4,2},{5,3},{6,4},{7,5},{8,14},{9,15},{10,... | collective-permute-start | bytes 589832 | tf_op jit(solution)/shard_map/ppermute | solution.py:342
  54.7 6.9 %collective-permute-done.5.far1 = f32[192,256]{1,0:T(8,128)S(1)} collective-permute-done((f32[192,256]{1,0:T(8,128)S(1)}, f32[192,256]{1,0:T(8,128)S(1)}, u32[]{:S(2)}, u32[]{:S(2)}) %collective-permute-start.5) | collective-permute-done | bytes 196640 | tf_op jit(solution)/shard_map/ppermute | solution.py:342
  61.6 5.6 %collective-permute-done.4.far0 = f32[192,256]{1,0:T(8,128)S(1)} collective-permute-done((f32[192,256]{1,0:T(8,128)}, f32[192,256]{1,0:T(8,128)S(1)}, u32[]{:S(2)}, u32[]{:S(2)}) %collective-permute-start.4) | collective-permute-done | bytes 196640 | tf_op jit(solution)/shard_map/ppermute | solution.py:342
  67.1 9.6 %forward.1 = (f32[4,384,2304]{2,1,0:T(8,128)}, bf16[2304,512]{1,0:T(8,128)(2,1)}, f32[8,2,1536]{2,1,0:T(2,128)S(1)}) custom-call(bf16[1152,768]{1,0:T(8,128)(2,1)} %copy-done.2, f32[384,256]{1,0:T(8,128)S(1)} %copy-done.1, f32[192,256]{1,0:T(8,128)S(1)} %collective-permute-done.4.far0, f32[192,256]{1,0:T(8,128)S(1)} %collective-permute-done.5.far1, ...), custom_call_target="tpu_custom_call" | custom-call | flops 5435817984 | bytes 14155776 | tf_op jit(solution)/shard_map/forward/pallas_call | solution.py:159
  76.8 11.7 %all_to_all.20.all_ref = f32[8,2,1536]{2,1,0:T(2,128)S(1)} all-to-all(f32[8,2,1536]{2,1,0:T(2,128)S(1)} %get-tuple-element.27), channel_id=1, replica_groups=mesh['grp'=32,'mem'=8] {'mem'}, dimensions={0} | all-to-all | bytes 196608 | tf_op jit(solution)/shard_map/all_to_all | solution.py:365
  89.1 5.5 %all-to-all-start.3 = ((f32[32,1,768]{2,1,0:T(1,128)}), f32[32,1,768]{2,1,0:T(1,128)S(1)}, u32[]{:S(2)}, u32[]{:S(2)}) async-start(f32[32,1,768]{2,1,0:T(1,128)} %get-tuple-element.30), calls=%async_computation.3 | async-start | bytes 196608 | tf_op jit(solution)/shard_map/all_to_all | solution.py:367
  94.8 7.1 %all-to-all-done.3.everyone_ref = f32[32,1,768]{2,1,0:T(1,128)S(1)} async-done(((f32[32,1,768]{2,1,0:T(1,128)}), f32[32,1,768]{2,1,0:T(1,128)S(1)}, u32[]{:S(2)}, u32[]{:S(2)}) %all-to-all-start.3) | async-done | bytes 98336 | tf_op jit(solution)/shard_map/all_to_all | solution.py:367
  101.9 4.7 %backward_3.1 = (f32[192,256]{1,0:T(8,128)S(1)}, f32[192,256]{1,0:T(8,128)S(1)}) custom-call(s32[2]{0:T(128)S(1)} %dynamic-slice_reduce_fusion.partner_ref, f32[1,1536]{1,0:T(1,128)S(1)} %get-tuple-element.28.row_ref, f32[1,768]{1,0:T(1,128)S(1)} %get-tuple-element.29.own_ref, f32[32,1,768]{2,1,0:T(1,128)S(1)} %all-to-all-done.3.everyone_ref, ...), custom_call_target="tpu_custom_call" | custom-call | flops 1358954496 | bytes 3538944 | tf_op jit(solution)/shard_map/backward_3/pallas_call | solution.py:277
  107.1 3.7 %collective-permute-start.8 = (f32[192,256]{1,0:T(8,128)S(1)}, f32[192,256]{1,0:T(8,128)S(1)}, u32[]{:S(2)}, u32[]{:S(2)}) collective-permute-start(f32[192,256]{1,0:T(8,128)S(1)} %get-tuple-element.36), channel_id=1, source_target_pairs={{0,6},{1,7},{2,0},{3,1},{4,2},{5,3},{6,4},{7,5},{8,14},{9,15},{10,... | collective-permute-start | bytes 589832 | tf_op jit(solution)/shard_map/ppermute | solution.py:342
  110.8 7.3 %backward_0.1 = (f32[192,256]{1,0:T(8,128)S(1)}, f32[192,256]{1,0:T(8,128)S(1)}, f32[192,256]{1,0:T(8,128)S(1)}, f32[192,256]{1,0:T(8,128)S(1)}) custom-call(s32[2]{0:T(128)S(1)} %dynamic-slice_reduce_fusion.partner_ref, f32[1,1536]{1,0:T(1,128)S(1)} %get-tuple-element.28.row_ref, f32[1,768]{1,0:T(1,128)S(1)} %get-tuple-element.29.own_ref, ...), custom_call_target="tpu_custom_call" | custom-call | flops 2717908992 | bytes 7077888 | tf_op jit(solution)/shard_map/backward_0/pallas_call | solution.py:277
  118.3 2.9 %collective-permute-start.11 = (f32[192,256]{1,0:T(8,128)S(1)}, f32[192,256]{1,0:T(8,128)S(1)}, u32[]{:S(2)}, u32[]{:S(2)}) collective-permute-start(f32[192,256]{1,0:T(8,128)S(1)} %get-tuple-element.39), channel_id=1, source_target_pairs={{0,2},{1,3},{2,4},{3,5},{4,6},{5,7},{6,0},{7,1},{8,10},{9,11},{10,... | collective-permute-start | bytes 589832 | tf_op jit(solution)/shard_map/ppermute | solution.py:342
  121.8 3.7 %collective-permute-start.12 = (f32[192,256]{1,0:T(8,128)S(1)}, f32[192,256]{1,0:T(8,128)S(1)}, u32[]{:S(2)}, u32[]{:S(2)}) collective-permute-start(f32[192,256]{1,0:T(8,128)S(1)} %get-tuple-element.40), channel_id=1, source_target_pairs={{0,6},{1,7},{2,0},{3,1},{4,2},{5,3},{6,4},{7,5},{8,14},{9,15},{10,... | collective-permute-start | bytes 589832 | tf_op jit(solution)/shard_map/ppermute | solution.py:342
  125.5 4.7 %backward_2.1.run_ref = f32[384,256]{1,0:T(8,128)S(1)} custom-call(s32[2]{0:T(128)S(1)} %dynamic-slice_reduce_fusion.partner_ref, f32[1,1536]{1,0:T(1,128)S(1)} %get-tuple-element.28.row_ref, f32[1,768]{1,0:T(1,128)S(1)} %get-tuple-element.29.own_ref, f32[32,1,768]{2,1,0:T(1,128)S(1)} %all-to-all-done.3.everyone_ref, ...), custom_call_target="tpu_custom_call" | custom-call | flops 1358954496 | bytes 3538944 | tf_op jit(solution)/shard_map/backward_2/pallas_call | solution.py:277
  130.2 1.3 collective-permute-done.10.low1
  131.8 4.7 %collective-permute-done.9.low0 = f32[192,256]{1,0:T(8,128)S(1)} collective-permute-done((f32[192,256]{1,0:T(8,128)S(1)}, f32[192,256]{1,0:T(8,128)S(1)}, u32[]{:S(2)}, u32[]{:S(2)}) %collective-permute-start.9) | collective-permute-done | bytes 196640 | tf_op jit(solution)/shard_map/ppermute | solution.py:342
  136.5 1.1 finish.1
  (40 shorter events, 7.1 us)
Async XLA Ops:
  0.6 1.0 copy-start
  1.6 36.4 %copy-start.1 = (f32[384,256]{1,0:T(8,128)S(1)}, f32[384,256]{1,0:T(8,128)}, u32[]{:S(2)}) copy-start(f32[384,256]{1,0:T(8,128)} %emb_ref.3) | copy-start | bytes 1179652
  2.4 28.4 %all-to-all-start = ((f32[32,24,128]{2,1,0:T(8,128)}), f32[32,24,128]{2,1,0:T(8,128)S(1)}, u32[]{:S(2)}, u32[]{:S(2)}) async-start(f32[32,24,128]{2,1,0:T(8,128)} %bitcast.1), calls=%async_computation | async-start | bytes 786432 | tf_op jit(solution)/shard_map/all_to_all | solution.py:350
  11.3 26.0 %collective-permute-start.1 = (f32[384,256]{1,0:T(8,128)}, f32[384,256]{1,0:T(8,128)S(1)}, u32[]{:S(2)}, u32[]{:S(2)}) collective-permute-start(f32[384,256]{1,0:T(8,128)} %emb_ref.3), channel_id=1, source_target_pairs={{0,6},{1,7},{2,0},{3,1},{4,2},{5,3},{6,4},{7,5},{8,14},{9,15},{10,... | collective-permute-start | bytes 1179656 | tf_op jit(solution)/shard_map/ppermute | solution.py:342
  16.8 21.2 %collective-permute-start = (f32[384,256]{1,0:T(8,128)}, f32[384,256]{1,0:T(8,128)S(1)}, u32[]{:S(2)}, u32[]{:S(2)}) collective-permute-start(f32[384,256]{1,0:T(8,128)} %emb_ref.3), channel_id=1, source_target_pairs={{0,2},{1,3},{2,4},{3,5},{4,6},{5,7},{6,0},{7,1},{8,10},{9,11},{10,... | collective-permute-start | bytes 1179656 | tf_op jit(solution)/shard_map/ppermute | solution.py:342
  16.8 22.9 %collective-permute-start.2 = (f32[384,256]{1,0:T(8,128)}, f32[384,256]{1,0:T(8,128)S(1)}, u32[]{:S(2)}, u32[]{:S(2)}) collective-permute-start(f32[384,256]{1,0:T(8,128)} %emb_ref.3), channel_id=1, source_target_pairs={{0,1},{1,0},{2,3},{3,2},{4,5},{5,4},{6,7},{7,6},{8,9},{9,8},{10,11... | collective-permute-start | bytes 1179656 | tf_op jit(solution)/shard_map/ppermute | solution.py:345
  16.8 22.9 %collective-permute-start.3 = (s32[384]{0:T(512)}, s32[384]{0:T(512)S(1)}, u32[]{:S(2)}, u32[]{:S(2)}) collective-permute-start(s32[384]{0:T(512)} %param.4), channel_id=1, source_target_pairs={{0,1},{1,0},{2,3},{3,2},{4,5},{5,4},{6,7},{7,6},{8,9},{9,8},{10,11... | collective-permute-start | bytes 4616 | tf_op jit(solution)/shard_map/ppermute | solution.py:345
  32.3 16.3 %all-to-all-start.1 = ((f32[32,48,128]{2,1,0:T(8,128)}), f32[32,48,128]{2,1,0:T(8,128)S(1)}, u32[]{:S(2)}, u32[]{:S(2)}) async-start(f32[32,48,128]{2,1,0:T(8,128)} %bitcast.3), calls=%async_computation.1 | async-start | bytes 1572864 | tf_op jit(solution)/shard_map/all_to_all | solution.py:352
  37.3 17.2 %copy-start.4 = (s32[384]{0:T(512)S(1)}, s32[384]{0:T(512)}, u32[]{:S(2)}) copy-start(s32[384]{0:T(512)} %param.4) | copy-start | bytes 4612
  38.5 1.2 copy-start.2
  48.6 18.6 %collective-permute-start.6 = (f32[32,48,128]{2,1,0:T(8,128)S(1)}, f32[32,48,128]{2,1,0:T(8,128)S(1)}, u32[]{:S(2)}, u32[]{:S(2)}) collective-permute-start(f32[32,48,128]{2,1,0:T(8,128)S(1)} %all-to-all-done.1.got), channel_id=1, source_target_pairs={{0,1},{1,0},{2,3},{3,2},{4,5},{5,4},{6,7},{7,6},{8,9},{9,8},{10,11... | collective-permute-start | bytes 2359304 | tf_op jit(solution)/shard_map/ppermute | solution.py:345
  48.6 12.9 %collective-permute-start.5 = (f32[192,256]{1,0:T(8,128)S(1)}, f32[192,256]{1,0:T(8,128)S(1)}, u32[]{:S(2)}, u32[]{:S(2)}) collective-permute-start(f32[192,256]{1,0:T(8,128)S(1)} %slice.11), channel_id=1, source_target_pairs={{0,6},{1,7},{2,0},{3,1},{4,2},{5,3},{6,4},{7,5},{8,14},{9,15},{10,... | collective-permute-start | bytes 589832 | tf_op jit(solution)/shard_map/ppermute | solution.py:342
  54.5 12.6 %collective-permute-start.4 = (f32[192,256]{1,0:T(8,128)}, f32[192,256]{1,0:T(8,128)S(1)}, u32[]{:S(2)}, u32[]{:S(2)}) collective-permute-start(f32[192,256]{1,0:T(8,128)} %slice.10), channel_id=1, source_target_pairs={{0,2},{1,3},{2,4},{3,5},{4,6},{5,7},{6,0},{7,1},{8,10},{9,11},{10,... | collective-permute-start | bytes 589832 | tf_op jit(solution)/shard_map/ppermute | solution.py:342
  54.6 39.9 %copy-start.3 = (s32[2,32]{1,0:T(2,128)S(1)}, s32[2,32]{1,0:T(2,128)}, u32[]{:S(2)}) copy-start(s32[2,32]{1,0:T(2,128)} %param.5) | copy-start | bytes 772
  89.1 12.8 %all-to-all-start.3 = ((f32[32,1,768]{2,1,0:T(1,128)}), f32[32,1,768]{2,1,0:T(1,128)S(1)}, u32[]{:S(2)}, u32[]{:S(2)}) async-start(f32[32,1,768]{2,1,0:T(1,128)} %get-tuple-element.30), calls=%async_computation.3 | async-start | bytes 196608 | tf_op jit(solution)/shard_map/all_to_all | solution.py:367
  106.6 14.6 %collective-permute-start.7 = (f32[192,256]{1,0:T(8,128)S(1)}, f32[192,256]{1,0:T(8,128)S(1)}, u32[]{:S(2)}, u32[]{:S(2)}) collective-permute-start(f32[192,256]{1,0:T(8,128)S(1)} %get-tuple-element.34), channel_id=1, source_target_pairs={{0,2},{1,3},{2,4},{3,5},{4,6},{5,7},{6,0},{7,1},{8,10},{9,11},{10,... | collective-permute-start | bytes 589832 | tf_op jit(solution)/shard_map/ppermute | solution.py:342
  107.1 14.1 %collective-permute-start.8 = (f32[192,256]{1,0:T(8,128)S(1)}, f32[192,256]{1,0:T(8,128)S(1)}, u32[]{:S(2)}, u32[]{:S(2)}) collective-permute-start(f32[192,256]{1,0:T(8,128)S(1)} %get-tuple-element.36), channel_id=1, source_target_pairs={{0,6},{1,7},{2,0},{3,1},{4,2},{5,3},{6,4},{7,5},{8,14},{9,15},{10,... | collective-permute-start | bytes 589832 | tf_op jit(solution)/shard_map/ppermute | solution.py:342
  118.2 13.3 %collective-permute-start.10 = (f32[192,256]{1,0:T(8,128)S(1)}, f32[192,256]{1,0:T(8,128)S(1)}, u32[]{:S(2)}, u32[]{:S(2)}) collective-permute-start(f32[192,256]{1,0:T(8,128)S(1)} %get-tuple-element.38), channel_id=1, source_target_pairs={{0,6},{1,7},{2,0},{3,1},{4,2},{5,3},{6,4},{7,5},{8,14},{9,15},{10,... | collective-permute-start | bytes 589832 | tf_op jit(solution)/shard_map/ppermute | solution.py:342
  118.3 13.6 %collective-permute-start.11 = (f32[192,256]{1,0:T(8,128)S(1)}, f32[192,256]{1,0:T(8,128)S(1)}, u32[]{:S(2)}, u32[]{:S(2)}) collective-permute-start(f32[192,256]{1,0:T(8,128)S(1)} %get-tuple-element.39), channel_id=1, source_target_pairs={{0,2},{1,3},{2,4},{3,5},{4,6},{5,7},{6,0},{7,1},{8,10},{9,11},{10,... | collective-permute-start | bytes 589832 | tf_op jit(solution)/shard_map/ppermute | solution.py:342
  121.2 15.3 %collective-permute-start.9 = (f32[192,256]{1,0:T(8,128)S(1)}, f32[192,256]{1,0:T(8,128)S(1)}, u32[]{:S(2)}, u32[]{:S(2)}) collective-permute-start(f32[192,256]{1,0:T(8,128)S(1)} %get-tuple-element.37), channel_id=1, source_target_pairs={{0,2},{1,3},{2,4},{3,5},{4,6},{5,7},{6,0},{7,1},{8,10},{9,11},{10,... | collective-permute-start | bytes 589832 | tf_op jit(solution)/shard_map/ppermute | solution.py:342
  121.8 14.8 %collective-permute-start.12 = (f32[192,256]{1,0:T(8,128)S(1)}, f32[192,256]{1,0:T(8,128)S(1)}, u32[]{:S(2)}, u32[]{:S(2)}) collective-permute-start(f32[192,256]{1,0:T(8,128)S(1)} %get-tuple-element.40), channel_id=1, source_target_pairs={{0,6},{1,7},{2,0},{3,1},{4,2},{5,3},{6,4},{7,5},{8,14},{9,15},{10,... | collective-permute-start | bytes 589832 | tf_op jit(solution)/shard_map/ppermute | solution.py:342

commit v3 on v2

v3 whole, which is shorter than its diff:
```python
import functools

import jax
import jax.numpy as jnp
from jax import lax
from jax.experimental import pallas as pl
from jax.experimental.pallas import tpu as pltpu
from jax.sharding import PartitionSpec as P

LOGIT_DIVISOR = 0.1
EPSILON = 1e-06
SLICE = 384
WIDTH = 256
SELF = 2
VMEM = 16 * 1024 * 1024
VMEM_LARGE = 44 * 1024 * 1024
HBM = pl.BlockSpec(memory_space=pltpu.HBM)
SMEM = pl.BlockSpec(memory_space=pltpu.SMEM)


def split(values):
    hi = values.astype(jnp.bfloat16)
    lo = (values - hi.astype(jnp.float32)).astype(jnp.bfloat16)
    return hi, lo


def rows_of(tiles):
    pairs = tiles.reshape(tiles.shape[0] // 2, 2, 8, 128)
    rows = tiles.shape[0] * 4
    return jnp.concatenate([pairs[:, 0].reshape(rows, 128), pairs[:, 1].reshape(rows, 128)], axis=1)


def radius_of(values):
    return jnp.sqrt(jnp.sum(values * values, axis=-1, keepdims=True) + EPSILON)


def as_column(line):
    return jnp.broadcast_to(line, (128, line.shape[1])).T


def in_hbm(value):
    return pltpu.with_memory_space_constraint(value, pltpu.HBM)


def params(limit=VMEM):
    return pltpu.CompilerParams(vmem_limit_bytes=limit)


def tile_kernel(emb_ref, tile_ref):
    rows = emb_ref.shape[0]
    for half in range(2):
        tile_ref[:, half] = emb_ref[:, half * 128 : half * 128 + 128].reshape(rows // 8, 8, 128)


def as_tiles(embeddings):
    rows, _ = embeddings.shape
    return pl.pallas_call(
        tile_kernel,
        out_shape=jax.ShapeDtypeStruct((rows // 8, 2, 8, 128), jnp.float32),
        compiler_params=params(),
        name="as_tiles",
    )(embeddings)


def pick_kernel(pairing_ref, pieces_ref, out_ref):
    size = pieces_ref.shape[1]
    for which in range(out_ref.shape[1] // size):
        for group in range(out_ref.shape[0]):
            out_ref[group, which * size : which * size + size] = pieces_ref[pairing_ref[which, group]]


def pick(pairing, pieces):
    rounds, groups = pairing.shape
    return pl.pallas_call(
        pick_kernel,
        in_specs=[SMEM, pl.BlockSpec()],
        out_shape=jax.ShapeDtypeStruct((groups, rounds * pieces.shape[1], 128), jnp.float32),
        compiler_params=params(),
        name="pick",
    )(pairing, pieces)


def scaled_rows(refs, out_ref, at=0):
    for ref in refs:
        values = ref[...]
        hi, lo = split(values * (1.0 / (radius_of(values) * LOGIT_DIVISOR)))
        out_ref[at : at + hi.shape[0]] = jnp.concatenate([hi, lo, hi], axis=1)
        at += hi.shape[0]


def unit_parts(values):
    hi, lo = split(values * (1.0 / radius_of(values)))
    return jnp.concatenate([hi, lo], axis=1)


def product(left, cols):
    hi, lo = cols[:, :WIDTH], cols[:, WIDTH:]
    return lax.dot_general(
        left,
        jnp.concatenate([hi, hi, lo], axis=1),
        (((1,), (1,)), ((), ())),
        preferred_element_type=jnp.float32,
    )


def exponentials(scores, first_row, pos_ref, store):
    height = scores.shape[0]
    total = jnp.zeros((height, 128), jnp.float32)
    match = jnp.zeros((height, 128), jnp.float32)
    if first_row is not None:
        row_ids = lax.broadcasted_iota(jnp.int32, (height, 128), 0) + first_row
        lane_ids = lax.broadcasted_iota(jnp.int32, (height, 128), 1)
    for k in range(0, scores.shape[1], 128):
        score = scores[:, k : k + 128]
        e = jnp.exp(score)
        if first_row is not None:
            match = match + jnp.where(row_ids == pos_ref[:, k : k + 128], score, 0.0)
            if first_row <= SELF * SLICE < first_row + height and k < SLICE:
                e = jnp.where(row_ids - SELF * SLICE == lane_ids + k, 0.0, e)
        total = total + e
        store(k, e)
    return total, match


def as_line(total):
    return jnp.sum(total.T, axis=0, keepdims=True)


def own_kernel(
    ready, mine, sib, pos_ref, c_out, e_out, line_ref, left_ref, c_buf, e_buf, ready_sem, c_sem, e_sem
):
    ready_copy = pltpu.make_async_copy(ready, left_ref, ready_sem)
    ready_copy.start()
    c_buf[:SLICE] = unit_parts(mine[...])
    c_buf[SLICE:] = unit_parts(sib[...])
    copies = [pltpu.make_async_copy(c_buf, c_out, c_sem)]
    copies[0].start()
    ready_copy.wait()

    coming = product(left_ref[:SLICE], c_buf[...])
    totals, matches = [], []
    for order in range(3):
        scores = coming
        if order < 2:
            at = (order + 1) * SLICE
            coming = product(left_ref[at : at + SLICE], c_buf[...])

        def store(k, e):
            e_buf[order, :, k : k + 128] = e

        total, match = exponentials(scores, order * SLICE, pos_ref, store)
        totals.append(as_line(total))
        matches.append(as_line(match))
        copies.append(pltpu.make_async_copy(e_buf.at[order], e_out.at[order], e_sem.at[order]))
        copies[-1].start()
    line_ref[0:1] = jnp.concatenate(totals, axis=1)
    line_ref[1:2] = jnp.concatenate(matches, axis=1)
    for copy in copies:
        copy.wait()


def own_scores(ready, mine, sib, pos):
    rows, wide = 3 * SLICE, 2 * SLICE
    shapes = [((wide, 2 * WIDTH), jnp.bfloat16), ((3, SLICE, wide), jnp.float32)]
    return pl.pallas_call(
        own_kernel,
        in_specs=[HBM] + [pl.BlockSpec()] * 3,
        out_specs=[HBM] * 2 + [pl.BlockSpec()],
        out_shape=[pltpu.HBM(*shape) for shape in shapes] + [jax.ShapeDtypeStruct((2, rows), jnp.float32)],
        scratch_shapes=[pltpu.VMEM((rows, 3 * WIDTH), jnp.bfloat16)]
        + [pltpu.VMEM(*shape) for shape in shapes]
        + [pltpu.SemaphoreType.DMA, pltpu.SemaphoreType.DMA, pltpu.SemaphoreType.DMA((3,))],
        cost_estimate=pl.CostEstimate(
            flops=6 * rows * wide * WIDTH, bytes_accessed=4 * rows * wide, transcendentals=rows * wide
        ),
        compiler_params=params(VMEM_LARGE),
        name="own_scores",
    )(in_hbm(ready), mine, sib, pos)


def prepare_kernel(*refs):
    scaled_rows(refs[:-1], refs[-1])


def prepare(name, *pieces):
    rows = sum(piece.shape[0] for piece in pieces)
    return pl.pallas_call(
        prepare_kernel,
        out_shape=jax.ShapeDtypeStruct((rows, 3 * WIDTH), jnp.bfloat16),
        cost_estimate=pl.CostEstimate(flops=20 * 10**9, bytes_accessed=8 * rows * WIDTH, transcendentals=0),
        compiler_params=params(),
        name=name,
    )(*pieces)


def forward_kernel(
    ready, c_own, ready_far, line_in, got, got_sib, pos_ref, e0_out, e1_out, c_out, line_ref,
    left_ref, own_buf, c_buf, e0_buf, e1_buf, tot_ref, in_sem, c_sem, e0_sem, e1_sem,
):
    orders, _, count = e1_buf.shape
    wide = 2 * SLICE
    at = ready.shape[0]
    ready_copy = pltpu.make_async_copy(ready, left_ref.at[pl.ds(0, at)], in_sem.at[0])
    own_copy = pltpu.make_async_copy(c_own, own_buf, in_sem.at[1])
    own_copy.start()
    ready_copy.start()
    left_ref[at:] = ready_far[...]
    half = got.shape[1] // 2
    tiles = got.shape[0] * half // 8

    copies = []

    def columns(base):
        for which, ref in enumerate((got, got_sib)):
            begin = base // wide * half
            piece = rows_of(ref[:, begin : begin + half].reshape(tiles, 8, 128))
            c_buf[base + which * SLICE : base + which * SLICE + SLICE] = unit_parts(piece)
        view = (pl.ds(base, wide),)
        copies.append(pltpu.make_async_copy(c_buf.at[view], c_out.at[view], c_sem.at[base // wide]))
        copies[-1].start()

    def score(band, base):
        rows = left_ref[band * wide : band * wide + wide]
        return product(rows, c_buf[base : base + wide])

    columns(0)
    own_copy.wait()
    ready_copy.wait()
    scores = product(left_ref[at:], own_buf[...])
    coming = score(0, 0)

    def store_own(k, e):
        e0_buf[:, :, k : k + 128] = e.reshape(1, SLICE, 128)

    far_total, far_match = exponentials(scores, at, pos_ref, store_own)
    copies.append(pltpu.make_async_copy(e0_buf, e0_out, e0_sem))
    copies[-1].start()

    items = [(band, base) for base in range(0, count, wide) for band in range(orders // 2)]
    for turn, (band, base) in enumerate(items):
        scores = coming
        if turn + 1 < len(items):
            if items[turn + 1][1] != base:
                columns(items[turn + 1][1])
            coming = score(*items[turn + 1])

        def store(k, e):
            e1_buf[2 * band : 2 * band + 2, :, base + k : base + k + 128] = e.reshape(2, SLICE, 128)

        total, _ = exponentials(scores, None, pos_ref, store)
        if base == 0:
            tot_ref[band * wide : band * wide + wide] = total
        else:
            tot_ref[band * wide : band * wide + wide] += total
        view = (pl.ds(2 * band, 2), slice(None), pl.ds(base, wide))
        copies.append(pltpu.make_async_copy(e1_buf.at[view], e1_out.at[view], e1_sem.at[turn]))
        copies[-1].start()

    far = jnp.concatenate([as_line(far_total), as_line(far_match)], axis=0)
    line = jnp.concatenate([line_in[...], far], axis=1)
    total = as_line(tot_ref[...]) + line[0:1]
    for member in range(line_ref.shape[0]):
        line_ref[member, 0:1] = total
        line_ref[member, 1:2] = line[1:2]
    for copy in copies:
        copy.wait()


def forward(ready, c_own, ready_far, line, got, got_sib, pos, members):
    rows, wide, count = 4 * SLICE, 2 * SLICE, 4 * SLICE
    own_shape, part_shape = ((1, SLICE, wide), jnp.float32), ((4, SLICE, count), jnp.float32)
    col_shape = ((count, 2 * WIDTH), jnp.bfloat16)
    return pl.pallas_call(
        forward_kernel,
        in_specs=[HBM] * 2 + [pl.BlockSpec()] * 5,
        out_specs=[HBM] * 3 + [pl.BlockSpec()],
        out_shape=(
            pltpu.HBM(*own_shape),
            pltpu.HBM(*part_shape),
            pltpu.HBM(*col_shape),
            jax.ShapeDtypeStruct((members, 2, rows), jnp.float32),
        ),
        scratch_shapes=[
            pltpu.VMEM((rows, 3 * WIDTH), jnp.bfloat16),
            pltpu.VMEM((wide, 2 * WIDTH), jnp.bfloat16),
            pltpu.VMEM(*col_shape),
            pltpu.VMEM(*own_shape),
            pltpu.VMEM(*part_shape),
            pltpu.VMEM((rows, 128), jnp.float32),
            pltpu.SemaphoreType.DMA((2,)),
            pltpu.SemaphoreType.DMA((2,)),
            pltpu.SemaphoreType.DMA,
            pltpu.SemaphoreType.DMA((4,)),
        ],
        cost_estimate=pl.CostEstimate(
            flops=6 * rows * count * WIDTH, bytes_accessed=4 * rows * count, transcendentals=rows * count
        ),
        compiler_params=params(VMEM_LARGE),
        name="forward",
    )(in_hbm(ready), in_hbm(c_own), ready_far, line, got, got_sib, pos)


def denominator_kernel(member_ref, all_ref, row_ref, own_ref, line_ref, spread_ref):
    member = member_ref[0]
    members = all_ref.shape[0]

    def summed(owner, kind):
        value = 0.0
        for by, order in ((0, SELF), (2, 0), (members - 2, 1), (4, 3)):
            held = all_ref[lax.rem(owner + by, members)]
            value = value + held[kind : kind + 1, order * SLICE : order * SLICE + SLICE]
        return value

    mate = member + 1 - 2 * lax.rem(member, 2)
    own = summed(member, 0)
    line_ref[0:1] = own
    line_ref[1:2] = summed(member, 1)
    both = jnp.concatenate([own, summed(mate, 0)], axis=1)
    own_ref[...] = both
    spread_ref[...] = jnp.broadcast_to(both.reshape(1, 1, 2 * SLICE), spread_ref.shape)
    for order, by in enumerate((members - 2, 2, 0, 4)):
        value = own if by == 0 else summed(lax.rem(member + by, members), 0)
        row_ref[:, order * SLICE : order * SLICE + SLICE] = value


def denominators(member, everything, groups):
    return pl.pallas_call(
        denominator_kernel,
        in_specs=[SMEM, pl.BlockSpec()],
        out_shape=(
            jax.ShapeDtypeStruct((1, 4 * SLICE), jnp.float32),
            jax.ShapeDtypeStruct((1, 2 * SLICE), jnp.float32),
            jax.ShapeDtypeStruct((2, SLICE), jnp.float32),
            jax.ShapeDtypeStruct((groups, 1, 2 * SLICE), jnp.float32),
        ),
        compiler_params=params(),
        name="denominators",
    )(member, everything)


def backward_kernel(
    bands, partner_ref, row_ref, own_ref, everyone_ref, pos_ref, e0_in, e1_in, c0_in, c1_in, *refs
):
    out_refs, (run_ref, e_buf, c_buf, e_sem, c_sem) = refs[:-5], refs[-5:]
    wide = 2 * SLICE
    steps = e_buf.shape[1] // wide
    copies = []
    for k in range(steps):
        wanted = pl.ds(k * wide, wide)
        group = []
        at = 0
        for which, (order, begin, size) in enumerate(bands):
            rows = pl.ds(begin, size)
            if k == 0:
                src = e0_in.at[order if e0_in.shape[0] > 1 else 0, rows]
            else:
                src = e1_in.at[order, rows, pl.ds((k - 1) * wide, wide)]
            group.append(pltpu.make_async_copy(src, e_buf.at[pl.ds(at, size), wanted], e_sem.at[k, which]))
            at += size
        src = c0_in if k == 0 else c1_in.at[pl.ds((k - 1) * wide, wide)]
        group.append(pltpu.make_async_copy(src, c_buf.at[wanted], c_sem.at[k]))
        copies.append(group)
        for copy in group:
            copy.start()

    columns, places = [], []
    for order, begin, size in bands:
        column = as_column(row_ref[:, order * SLICE : order * SLICE + SLICE])
        columns.append(column[begin : begin + size])
        places.append(lax.broadcasted_iota(jnp.int32, (size, 128), 0) + (order * SLICE + begin))
    row_inv = 1.0 / jnp.concatenate(columns, axis=0)
    row_ids = jnp.concatenate(places, axis=0)
    for k in range(steps):
        col_inv = 1.0 / (own_ref[...] if k == 0 else everyone_ref[partner_ref[k - 1]])
        for copy in copies[k]:
            copy.wait()
        his, los = [], []
        for at in range(0, wide, 128):
            weight = e_buf[:, k * wide + at : k * wide + at + 128] * (row_inv + col_inv[:, at : at + 128])
            if k == 0:
                weight = weight - jnp.where(row_ids == pos_ref[:, at : at + 128], 2.0, 0.0)
            hi, lo = split(weight)
            his.append(hi)
            los.append(lo)
        cols = c_buf[k * wide : k * wide + wide]
        c_hi, c_lo = cols[:, :WIDTH], cols[:, WIDTH:]
        part = jnp.dot(
            jnp.concatenate(his + his + los, axis=1),
            jnp.concatenate([c_hi, c_lo, c_hi], axis=0),
            preferred_element_type=jnp.float32,
        )
        if k == 0:
            run_ref[...] = part
        elif k + 1 < steps:
            run_ref[...] += part
        else:
            part = run_ref[...] + part
            size = part.shape[0] // len(out_refs)
            for which, ref in enumerate(out_refs):
                ref[...] = part[which * size : which * size + size]


def backward(bands, pieces, e0, partners, row_den, own_den, everyone, pos, e1, c0, c1):
    count = 6 * SLICE
    return pl.pallas_call(
        functools.partial(backward_kernel, bands),
        in_specs=[SMEM] + [pl.BlockSpec()] * 4 + [HBM] * 4,
        out_shape=[jax.ShapeDtypeStruct((SLICE // pieces, WIDTH), jnp.float32)] * pieces,
        scratch_shapes=[
            pltpu.VMEM((SLICE, WIDTH), jnp.float32),
            pltpu.VMEM((SLICE, count), jnp.float32),
            pltpu.VMEM((count, 2 * WIDTH), jnp.bfloat16),
            pltpu.SemaphoreType.DMA((3, len(bands))),
            pltpu.SemaphoreType.DMA((3,)),
        ],
        cost_estimate=pl.CostEstimate(
            flops=6 * SLICE * count * WIDTH, bytes_accessed=4 * SLICE * count, transcendentals=0
        ),
        compiler_params=params(VMEM_LARGE),
        name="backward_%d_%d" % bands[0][:2],
    )(partners, row_den, own_den, everyone, pos, *map(in_hbm, (e0, e1, c0, c1)))


def add_kernel(a_ref, b_ref, c_ref, d_ref, ab_ref, cd_ref):
    ab_ref[...] = a_ref[...] + b_ref[...]
    cd_ref[...] = c_ref[...] + d_ref[...]


def add_pairs(a, b, c, d):
    out = jax.ShapeDtypeStruct(a.shape, jnp.float32)
    return pl.pallas_call(add_kernel, out_shape=(out, out), compiler_params=params(), name="add_pairs")(
        a, b, c, d
    )


def finish_kernel(emb_ref, run_ref, low0, low1, high0, high1, line_ref, loss_ref, grad_ref):
    values = emb_ref[...]
    radius = radius_of(values)
    unit = values / radius
    low, high = low0[...] + low1[...], high0[...] + high1[...]
    slope = (run_ref[...] + jnp.concatenate([low, high], axis=0)) / LOGIT_DIVISOR
    grad_ref[...] = (slope - unit * jnp.sum(unit * slope, axis=-1, keepdims=True)) / radius
    loss_ref[...] = (jnp.log(line_ref[0:1]) - line_ref[1:2]).reshape(loss_ref.shape)


def finish(embeddings, run, lows, highs, line):
    rows, width = embeddings.shape
    return pl.pallas_call(
        finish_kernel,
        out_shape=(
            jax.ShapeDtypeStruct((rows,), jnp.float32),
            jax.ShapeDtypeStruct((rows, width), jnp.float32),
        ),
        compiler_params=params(),
        name="finish",
    )(embeddings, run, *lows, *highs, line)


def local(embeddings, positive, pairing):
    rows, width = embeddings.shape
    members = lax.axis_size("mem")
    groups = lax.axis_size("grp")
    block = rows * members
    rounds = pairing.shape[0]
    group = lax.axis_index("grp")
    member = lax.axis_index("mem")
    half = rows // 2

    def shift(value, by):
        return lax.ppermute(value, "mem", [(m, (m + by) % members) for m in range(members)])

    def swap(value):
        return lax.ppermute(value, "mem", [(m, m ^ 1) for m in range(members)])

    left, right = shift(embeddings, 2), shift(embeddings, -2)
    far = (shift(left[:half], 2), shift(right[half:], -2))
    per = rows * width // (groups * 128)
    pieces = lax.all_to_all(as_tiles(embeddings).reshape(groups, per, 128), "grp", 0, 0, tiled=True)
    got = lax.all_to_all(pick(pairing, pieces), "grp", 0, 0, tiled=True)
    sib, pos_sib = swap(embeddings), swap(positive)

    both = jnp.concatenate([positive, pos_sib]) - group * block
    owner = both // rows
    turn = (owner // 2 - member // 2) % (members // 2)
    order = jnp.where(turn == 0, SELF, jnp.where(turn == 3, 0, jnp.where(turn == 1, 1, 3)))
    pos = jnp.where(owner % 2 == member % 2, order * rows + both % rows, -1).reshape(1, 2 * rows)

    ready = prepare("prepare", left, right, embeddings)
    c_own, e_own, line = own_scores(ready, embeddings, sib, pos)
    ready_far = prepare("prepare_far", *far)
    got, line, ready_far = lax.optimization_barrier((got, line, ready_far))
    e_far, e_part, c_part, line = forward(ready, c_own, ready_far, line, got, swap(got), pos, members)

    everything = lax.all_to_all(line, "mem", 0, 0, tiled=True)
    row_den, own_den, line, spread = denominators(jnp.reshape(member, (1,)), everything, groups)
    everyone = lax.all_to_all(spread, "grp", 0, 0, tiled=True)

    shared = (pairing[:, group], row_den, own_den, everyone, pos, e_part, c_own, c_part)
    far_low, far_high = backward(((3, 0, rows),), 2, e_far, *shared)
    far_low, far_high = shift(far_low, 2), shift(far_high, -2)
    left_low, right_high = backward(((0, 0, half), (1, half, half)), 2, e_own, *shared)
    high0, low1 = shift(right_high, 2), shift(left_low, -2)
    left_high, right_low = backward(((0, half, half), (1, 0, half)), 2, e_own, *shared)
    right_low, left_high = add_pairs(right_low, far_low, left_high, far_high)
    low0, high1 = shift(right_low, 2), shift(left_high, -2)
    (run,) = backward(((SELF, 0, rows),), 1, e_own, *shared)
    return finish(embeddings, run, (low0, low1), (high0, high1), line)


def solution(mesh):
    placed = (P(("grp", "mem"), None), P(("grp", "mem")), P())
    return jax.shard_map(
        local,
        mesh=mesh,
        in_specs=placed,
        out_specs=(P(("grp", "mem")), P(("grp", "mem"), None)),
        check_vma=False,
    )
```

time: 139 us -> 130 us (0.935)
  waiting for transfers between devices: 48.1 us -> 32.3 us
  Pallas kernels: 29.4 us -> 37.2 us
  blocking collectives: 11.7 us -> 13.6 us
  local copies, waits for them, and re-layouts: 4.83 us -> 3.1 us
    ppermute x10, waiting for transfers between devices: 19.5 us -> 8.48 us  [shift(): lax.ppermute(value, 'mem', [(m, (m + by) % members) for m in range(member...]
    all_to_all x1, waiting for transfers between devices: 12.6 us -> 1.69 us  [local(): lax.all_to_all(as_tiles(embeddings).reshape(groups, per, 128), 'grp', 0,...]
    pallas_call x6 -> x10, Pallas kernels: 27.9 us -> 35.7 us  [the longest x4 19.2 us: backward(): pl.pallas_call(functools.partial(backward_kernel, bands), in_specs=[SMEM]...]
    all_to_all x1, waiting for transfers between devices: 8.87 us -> 12.6 us  [local(): got = lax.all_to_all(pick(pairing, pieces), 'grp', 0, 0, tiled=True)]
    ppermute x3, waiting for transfers between devices: 0.01 us -> 2.29 us  [swap(): return lax.ppermute(value, 'mem', [(m, m ^ 1) for m in range(members)])]
    all_to_all x1, blocking collectives: 11.7 us -> 13.6 us  [local(): everything = lax.all_to_all(line, 'mem', 0, 0, tiled=True)]
    gather x1 -> x0, local copies, waits for them, and re-layouts: 1.51 us -> none  [local(): picked = pieces[pairing.T].reshape(groups, rounds * per, 128)]
  transfers between devices with their start and end apart: 16 -> 16, of which waited for: 9 -> 7; matrix products, arithmetic and copies ran while one was open for 2% -> 1% of each run, Pallas kernels for 9% -> 17%
where the time goes in v3:
time: 130 us; the launch traced here: 129 us
  starting transfers between devices  41.9 us (32%)
  Pallas kernels  37.2 us (29%)
  waiting for transfers between devices  32.3 us (25%)
  blocking collectives  13.6 us (10%)
  local copies, waits for them, and re-layouts  3.1 us (2%)
    ppermute x10, starting transfers between devices, shift(): lax.ppermute(value, 'mem', [(m, (m + by) % members) for m in range(member...  22.5 us
    pallas_call x4, Pallas kernels, backward(): pl.pallas_call(functools.partial(backward_kernel, bands), in_specs=[SMEM]...  19.2 us
    all_to_all x1, blocking collectives, local(): everything = lax.all_to_all(line, 'mem', 0, 0, tiled=True)  13.6 us
    all_to_all x1, waiting for transfers between devices, local(): got = lax.all_to_all(pick(pairing, pieces), 'grp', 0, 0, tiled=True)  12.6 us
    pallas_call x1, Pallas kernels, forward(): pl.pallas_call(forward_kernel, in_specs=[HBM] * 2 + [pl.BlockSpec()] * 5,...  8.66 us
    ppermute x10, waiting for transfers between devices, shift(): lax.ppermute(value, 'mem', [(m, (m + by) % members) for m in range(member...  8.48 us
    all_to_all x1, starting transfers between devices, local(): lax.all_to_all(as_tiles(embeddings).reshape(groups, per, 128), 'grp', 0,...  7.99 us
    all_to_all x1, waiting for transfers between devices, local(): everyone = lax.all_to_all(spread, 'grp', 0, 0, tiled=True)  7.25 us
  transfers between devices with their start and end apart: 16, of which 7 were waited for; matrix products, arithmetic and copies ran while one was open for 1% of the time, Pallas kernels for 17%

profile of v3, /device:TPU:8, one launch (start us, length us, event | category | flops | bytes accessed | tf_op | source)
XLA Modules:
  0.0 129.0 jit_solution(1984348722246333344)
XLA Ops:
  0.6 6.4 %collective-permute-start.1 = (f32[384,256]{1,0:T(8,128)}, f32[384,256]{1,0:T(8,128)S(1)}, u32[]{:S(2)}, u32[]{:S(2)}) collective-permute-start(f32[384,256]{1,0:T(8,128)} %emb_ref.3), channel_id=1, source_target_pairs={{0,6},{1,7},{2,0},{3,1},{4,2},{5,3},{6,4},{7,5},{8,14},{9,15},{10,... | collective-permute-start | bytes 1179656 | tf_op jit(solution)/shard_map/ppermute | solution.py:470
  9.3 8.0 %all-to-all-start = ((f32[32,24,128]{2,1,0:T(8,128)}), f32[32,24,128]{2,1,0:T(8,128)S(1)}, u32[]{:S(2)}, u32[]{:S(2)}) async-start(f32[32,24,128]{2,1,0:T(8,128)} %bitcast.1), calls=%async_computation | async-start | bytes 786432 | tf_op jit(solution)/shard_map/all_to_all | solution.py:478
  18.1 6.1 %collective-permute-done.1.refs_1_ = f32[384,256]{1,0:T(8,128)S(1)} collective-permute-done((f32[384,256]{1,0:T(8,128)}, f32[384,256]{1,0:T(8,128)S(1)}, u32[]{:S(2)}, u32[]{:S(2)}) %collective-permute-start.1) | collective-permute-done | bytes 393248 | tf_op jit(solution)/shard_map/ppermute | solution.py:470
  24.2 4.6 %collective-permute-start.5 = (f32[192,256]{1,0:T(8,128)S(1)}, f32[192,256]{1,0:T(8,128)S(1)}, u32[]{:S(2)}, u32[]{:S(2)}) collective-permute-start(f32[192,256]{1,0:T(8,128)S(1)} %slice.9), channel_id=1, source_target_pairs={{0,6},{1,7},{2,0},{3,1},{4,2},{5,3},{6,4},{7,5},{8,14},{9,15},{10,... | collective-permute-start | bytes 589832 | tf_op jit(solution)/shard_map/ppermute | solution.py:470
  29.4 1.2 copy-done.3
  30.6 4.5 %own_scores.1 = (bf16[768,512]{1,0:T(8,128)(2,1)}, f32[3,384,768]{2,1,0:T(8,128)}, f32[2,1152]{1,0:T(2,128)S(1)}) custom-call(bf16[1152,768]{1,0:T(8,128)(2,1)} %copy-done.3, f32[384,256]{1,0:T(8,128)S(1)} %copy-done.1, f32[384,256]{1,0:T(8,128)S(1)} %collective-permute-done.2.sib, s32[1,768]{1,0:T(1,128)S(1)} %compare_select_fusion.5.pos_ref), custom_call_target="tpu_custom_call" | custom-call | flops 1358954496 | bytes 3538944 | tf_op jit(solution)/shard_map/own_scores/pallas_call | solution.py:165
  35.2 1.7 %all-to-all-done.pieces_ref = f32[32,24,128]{2,1,0:T(8,128)S(1)} async-done(((f32[32,24,128]{2,1,0:T(8,128)}), f32[32,24,128]{2,1,0:T(8,128)S(1)}, u32[]{:S(2)}, u32[]{:S(2)}) %all-to-all-start) | async-done | bytes 393248 | tf_op jit(solution)/shard_map/all_to_all | solution.py:478
  36.9 1.5 %pick.1 = f32[32,48,128]{2,1,0:T(8,128)} custom-call(s32[2,32]{1,0:T(2,128)S(1)} %copy-done.2, f32[32,24,128]{2,1,0:T(8,128)S(1)} %all-to-all-done.pieces_ref), custom_call_target="tpu_custom_call" | custom-call | tf_op jit(solution)/shard_map/pick/pallas_call | solution.py:74
  38.4 5.9 %all-to-all-start.1 = ((f32[32,48,128]{2,1,0:T(8,128)}), f32[32,48,128]{2,1,0:T(8,128)S(1)}, u32[]{:S(2)}, u32[]{:S(2)}) async-start(f32[32,48,128]{2,1,0:T(8,128)} %pick.1), calls=%async_computation.1 | async-start | bytes 1572864 | tf_op jit(solution)/shard_map/all_to_all | solution.py:479
  44.5 12.6 %all-to-all-done.1.got = f32[32,48,128]{2,1,0:T(8,128)S(1)} async-done(((f32[32,48,128]{2,1,0:T(8,128)}), f32[32,48,128]{2,1,0:T(8,128)S(1)}, u32[]{:S(2)}, u32[]{:S(2)}) %all-to-all-start.1) | async-done | bytes 786464 | tf_op jit(solution)/shard_map/all_to_all | solution.py:479
  57.1 2.3 %collective-permute-done.6.got_sib = f32[32,48,128]{2,1,0:T(8,128)S(1)} collective-permute-done((f32[32,48,128]{2,1,0:T(8,128)S(1)}, f32[32,48,128]{2,1,0:T(8,128)S(1)}, u32[]{:S(2)}, u32[]{:S(2)}) %collective-permute-start.6) | collective-permute-done | bytes 786464 | tf_op jit(solution)/shard_map/ppermute | solution.py:473
  59.4 8.7 %forward.1 = (f32[1,384,768]{2,1,0:T(8,128)}, f32[4,384,1536]{2,1,0:T(8,128)}, bf16[1536,512]{1,0:T(8,128)(2,1)}, f32[8,2,1536]{2,1,0:T(2,128)S(1)}) custom-call(bf16[1152,768]{1,0:T(8,128)(2,1)} %copy-done.3, bf16[768,512]{1,0:T(8,128)(2,1)} %get-tuple-element.24.c_own.c0_in, bf16[384,768]{1,0:T(8,128)(2,1)S(1)} %prepare_far.1.ready_far, ...), custom_call_target="tpu_custom_call" | custom-call | flops 3623878656 | bytes 9437184 | tf_op jit(solution)/shard_map/forward/pallas_call | solution.py:273
  68.1 13.6 %all_to_all.20.all_ref = f32[8,2,1536]{2,1,0:T(2,128)S(1)} all-to-all(f32[8,2,1536]{2,1,0:T(2,128)S(1)} %get-tuple-element.29), channel_id=1, replica_groups=mesh['grp'=32,'mem'=8] {'mem'}, dimensions={0} | all-to-all | bytes 196608 | tf_op jit(solution)/shard_map/all_to_all | solution.py:494
  82.4 5.0 %all-to-all-start.3 = ((f32[32,1,768]{2,1,0:T(1,128)}), f32[32,1,768]{2,1,0:T(1,128)S(1)}, u32[]{:S(2)}, u32[]{:S(2)}) async-start(f32[32,1,768]{2,1,0:T(1,128)} %get-tuple-element.32), calls=%async_computation.3 | async-start | bytes 196608 | tf_op jit(solution)/shard_map/all_to_all | solution.py:496
  87.5 7.2 %all-to-all-done.3.everyone_ref = f32[32,1,768]{2,1,0:T(1,128)S(1)} async-done(((f32[32,1,768]{2,1,0:T(1,128)}), f32[32,1,768]{2,1,0:T(1,128)S(1)}, u32[]{:S(2)}, u32[]{:S(2)}) %all-to-all-start.3) | async-done | bytes 98336 | tf_op jit(solution)/shard_map/all_to_all | solution.py:496
  94.8 4.7 %backward_3_0.1 = (f32[192,256]{1,0:T(8,128)S(1)}, f32[192,256]{1,0:T(8,128)S(1)}) custom-call(s32[2]{0:T(128)S(1)} %dynamic-slice_reduce_fusion.partner_ref, f32[1,1536]{1,0:T(1,128)S(1)} %get-tuple-element.30.row_ref, f32[1,768]{1,0:T(1,128)S(1)} %get-tuple-element.31.own_ref, f32[32,1,768]{2,1,0:T(1,128)S(1)} %all-to-all-done.3.everyone_ref, ...), custom_call_target="tpu_custom_call" | custom-call | flops 1358954496 | bytes 3538944 | tf_op jit(solution)/shard_map/backward_3_0/pallas_call | solution.py:405
  100.5 3.2 %collective-permute-start.8 = (f32[192,256]{1,0:T(8,128)S(1)}, f32[192,256]{1,0:T(8,128)S(1)}, u32[]{:S(2)}, u32[]{:S(2)}) collective-permute-start(f32[192,256]{1,0:T(8,128)S(1)} %get-tuple-element.40), channel_id=1, source_target_pairs={{0,6},{1,7},{2,0},{3,1},{4,2},{5,3},{6,4},{7,5},{8,14},{9,15},{10,... | collective-permute-start | bytes 589832 | tf_op jit(solution)/shard_map/ppermute | solution.py:470
  103.7 4.9 %backward_0_0.1 = (f32[192,256]{1,0:T(8,128)S(1)}, f32[192,256]{1,0:T(8,128)S(1)}) custom-call(s32[2]{0:T(128)S(1)} %dynamic-slice_reduce_fusion.partner_ref, f32[1,1536]{1,0:T(1,128)S(1)} %get-tuple-element.30.row_ref, f32[1,768]{1,0:T(1,128)S(1)} %get-tuple-element.31.own_ref, f32[32,1,768]{2,1,0:T(1,128)S(1)} %all-to-all-done.3.everyone_ref, ...), custom_call_target="tpu_custom_call" | custom-call | flops 1358954496 | bytes 3538944 | tf_op jit(solution)/shard_map/backward_0_0/pallas_call | solution.py:405
  108.7 2.9 %collective-permute-start.11 = (f32[192,256]{1,0:T(8,128)S(1)}, f32[192,256]{1,0:T(8,128)S(1)}, u32[]{:S(2)}, u32[]{:S(2)}) collective-permute-start(f32[192,256]{1,0:T(8,128)S(1)} %get-tuple-element.43), channel_id=1, source_target_pairs={{0,2},{1,3},{2,4},{3,5},{4,6},{5,7},{6,0},{7,1},{8,10},{9,11},{10,... | collective-permute-start | bytes 589832 | tf_op jit(solution)/shard_map/ppermute | solution.py:470
  111.6 4.9 %backward_0_192.1 = (f32[192,256]{1,0:T(8,128)S(1)}, f32[192,256]{1,0:T(8,128)S(1)}) custom-call(s32[2]{0:T(128)S(1)} %dynamic-slice_reduce_fusion.partner_ref, f32[1,1536]{1,0:T(1,128)S(1)} %get-tuple-element.30.row_ref, f32[1,768]{1,0:T(1,128)S(1)} %get-tuple-element.31.own_ref, f32[32,1,768]{2,1,0:T(1,128)S(1)} %all-to-all-done.3.everyone_ref, ...), custom_call_target="tpu_custom_call" | custom-call | flops 1358954496 | bytes 3538944 | tf_op jit(solution)/shard_map/backward_0_192/pallas_call | solution.py:405
  117.6 3.2 %collective-permute-start.12 = (f32[192,256]{1,0:T(8,128)S(1)}, f32[192,256]{1,0:T(8,128)S(1)}, u32[]{:S(2)}, u32[]{:S(2)}) collective-permute-start(f32[192,256]{1,0:T(8,128)S(1)} %get-tuple-element.44), channel_id=1, source_target_pairs={{0,6},{1,7},{2,0},{3,1},{4,2},{5,3},{6,4},{7,5},{8,14},{9,15},{10,... | collective-permute-start | bytes 589832 | tf_op jit(solution)/shard_map/ppermute | solution.py:470
  120.8 4.7 %backward_2_0.1.run_ref = f32[384,256]{1,0:T(8,128)S(1)} custom-call(s32[2]{0:T(128)S(1)} %dynamic-slice_reduce_fusion.partner_ref, f32[1,1536]{1,0:T(1,128)S(1)} %get-tuple-element.30.row_ref, f32[1,768]{1,0:T(1,128)S(1)} %get-tuple-element.31.own_ref, f32[32,1,768]{2,1,0:T(1,128)S(1)} %all-to-all-done.3.everyone_ref, ...), custom_call_target="tpu_custom_call" | custom-call | flops 1358954496 | bytes 3538944 | tf_op jit(solution)/shard_map/backward_2_0/pallas_call | solution.py:405
  125.6 1.5 %collective-permute-done.9.low0 = f32[192,256]{1,0:T(8,128)S(1)} collective-permute-done((f32[192,256]{1,0:T(8,128)S(1)}, f32[192,256]{1,0:T(8,128)S(1)}, u32[]{:S(2)}, u32[]{:S(2)}) %collective-permute-start.9) | collective-permute-done | bytes 196640 | tf_op jit(solution)/shard_map/ppermute | solution.py:470
  127.9 1.1 finish.1
  (36 shorter events, 7.8 us)
Async XLA Ops:
  0.6 23.5 %collective-permute-start.1 = (f32[384,256]{1,0:T(8,128)}, f32[384,256]{1,0:T(8,128)S(1)}, u32[]{:S(2)}, u32[]{:S(2)}) collective-permute-start(f32[384,256]{1,0:T(8,128)} %emb_ref.3), channel_id=1, source_target_pairs={{0,6},{1,7},{2,0},{3,1},{4,2},{5,3},{6,4},{7,5},{8,14},{9,15},{10,... | collective-permute-start | bytes 1179656 | tf_op jit(solution)/shard_map/ppermute | solution.py:470
  7.0 21.8 %collective-permute-start = (f32[384,256]{1,0:T(8,128)}, f32[384,256]{1,0:T(8,128)S(1)}, u32[]{:S(2)}, u32[]{:S(2)}) collective-permute-start(f32[384,256]{1,0:T(8,128)} %emb_ref.3), channel_id=1, source_target_pairs={{0,2},{1,3},{2,4},{3,5},{4,6},{5,7},{6,0},{7,1},{8,10},{9,11},{10,... | collective-permute-start | bytes 1179656 | tf_op jit(solution)/shard_map/ppermute | solution.py:470
  7.0 23.6 %collective-permute-start.2 = (f32[384,256]{1,0:T(8,128)}, f32[384,256]{1,0:T(8,128)S(1)}, u32[]{:S(2)}, u32[]{:S(2)}) collective-permute-start(f32[384,256]{1,0:T(8,128)} %emb_ref.3), channel_id=1, source_target_pairs={{0,1},{1,0},{2,3},{3,2},{4,5},{5,4},{6,7},{7,6},{8,9},{9,8},{10,11... | collective-permute-start | bytes 1179656 | tf_op jit(solution)/shard_map/ppermute | solution.py:473
  7.0 11.0 %collective-permute-start.3 = (s32[384]{0:T(512)}, s32[384]{0:T(512)S(1)}, u32[]{:S(2)}, u32[]{:S(2)}) collective-permute-start(s32[384]{0:T(512)} %param.4), channel_id=1, source_target_pairs={{0,1},{1,0},{2,3},{3,2},{4,5},{5,4},{6,7},{7,6},{8,9},{9,8},{10,11... | collective-permute-start | bytes 4616 | tf_op jit(solution)/shard_map/ppermute | solution.py:473
  7.5 1.0 copy-start
  8.5 20.4 %copy-start.1 = (f32[384,256]{1,0:T(8,128)S(1)}, f32[384,256]{1,0:T(8,128)}, u32[]{:S(2)}) copy-start(f32[384,256]{1,0:T(8,128)} %emb_ref.3) | copy-start | bytes 1179652
  9.3 27.6 %all-to-all-start = ((f32[32,24,128]{2,1,0:T(8,128)}), f32[32,24,128]{2,1,0:T(8,128)S(1)}, u32[]{:S(2)}, u32[]{:S(2)}) async-start(f32[32,24,128]{2,1,0:T(8,128)} %bitcast.1), calls=%async_computation | async-start | bytes 786432 | tf_op jit(solution)/shard_map/all_to_all | solution.py:478
  24.2 20.1 %collective-permute-start.5 = (f32[192,256]{1,0:T(8,128)S(1)}, f32[192,256]{1,0:T(8,128)S(1)}, u32[]{:S(2)}, u32[]{:S(2)}) collective-permute-start(f32[192,256]{1,0:T(8,128)S(1)} %slice.9), channel_id=1, source_target_pairs={{0,6},{1,7},{2,0},{3,1},{4,2},{5,3},{6,4},{7,5},{8,14},{9,15},{10,... | collective-permute-start | bytes 589832 | tf_op jit(solution)/shard_map/ppermute | solution.py:470
  28.8 15.4 %collective-permute-start.4 = (f32[192,256]{1,0:T(8,128)S(1)}, f32[192,256]{1,0:T(8,128)S(1)}, u32[]{:S(2)}, u32[]{:S(2)}) collective-permute-start(f32[192,256]{1,0:T(8,128)S(1)} %slice.8), channel_id=1, source_target_pairs={{0,2},{1,3},{2,4},{3,5},{4,6},{5,7},{6,0},{7,1},{8,10},{9,11},{10,... | collective-permute-start | bytes 589832 | tf_op jit(solution)/shard_map/ppermute | solution.py:470
  29.4 1.2 copy-start.3
  30.6 6.2 %copy-start.2 = (s32[2,32]{1,0:T(2,128)S(1)}, s32[2,32]{1,0:T(2,128)}, u32[]{:S(2)}) copy-start(s32[2,32]{1,0:T(2,128)} %pairing_ref.1) | copy-start | bytes 772
  38.4 18.7 %all-to-all-start.1 = ((f32[32,48,128]{2,1,0:T(8,128)}), f32[32,48,128]{2,1,0:T(8,128)S(1)}, u32[]{:S(2)}, u32[]{:S(2)}) async-start(f32[32,48,128]{2,1,0:T(8,128)} %pick.1), calls=%async_computation.1 | async-start | bytes 1572864 | tf_op jit(solution)/shard_map/all_to_all | solution.py:479
  57.1 2.3 %collective-permute-start.6 = (f32[32,48,128]{2,1,0:T(8,128)S(1)}, f32[32,48,128]{2,1,0:T(8,128)S(1)}, u32[]{:S(2)}, u32[]{:S(2)}) collective-permute-start(f32[32,48,128]{2,1,0:T(8,128)S(1)} %all-to-all-done.1.got), channel_id=1, source_target_pairs={{0,1},{1,0},{2,3},{3,2},{4,5},{5,4},{6,7},{7,6},{8,9},{9,8},{10,11... | collective-permute-start | bytes 2359304 | tf_op jit(solution)/shard_map/ppermute | solution.py:473
  82.4 12.4 %all-to-all-start.3 = ((f32[32,1,768]{2,1,0:T(1,128)}), f32[32,1,768]{2,1,0:T(1,128)S(1)}, u32[]{:S(2)}, u32[]{:S(2)}) async-start(f32[32,1,768]{2,1,0:T(1,128)} %get-tuple-element.32), calls=%async_computation.3 | async-start | bytes 196608 | tf_op jit(solution)/shard_map/all_to_all | solution.py:496
  99.5 17.1 %collective-permute-start.7 = (f32[192,256]{1,0:T(8,128)S(1)}, f32[192,256]{1,0:T(8,128)S(1)}, u32[]{:S(2)}, u32[]{:S(2)}) collective-permute-start(f32[192,256]{1,0:T(8,128)S(1)} %get-tuple-element.38), channel_id=1, source_target_pairs={{0,2},{1,3},{2,4},{3,5},{4,6},{5,7},{6,0},{7,1},{8,10},{9,11},{10,... | collective-permute-start | bytes 589832 | tf_op jit(solution)/shard_map/ppermute | solution.py:470
  100.5 16.0 %collective-permute-start.8 = (f32[192,256]{1,0:T(8,128)S(1)}, f32[192,256]{1,0:T(8,128)S(1)}, u32[]{:S(2)}, u32[]{:S(2)}) collective-permute-start(f32[192,256]{1,0:T(8,128)S(1)} %get-tuple-element.40), channel_id=1, source_target_pairs={{0,6},{1,7},{2,0},{3,1},{4,2},{5,3},{6,4},{7,5},{8,14},{9,15},{10,... | collective-permute-start | bytes 589832 | tf_op jit(solution)/shard_map/ppermute | solution.py:470
  108.6 16.9 %collective-permute-start.10 = (f32[192,256]{1,0:T(8,128)S(1)}, f32[192,256]{1,0:T(8,128)S(1)}, u32[]{:S(2)}, u32[]{:S(2)}) collective-permute-start(f32[192,256]{1,0:T(8,128)S(1)} %get-tuple-element.42), channel_id=1, source_target_pairs={{0,6},{1,7},{2,0},{3,1},{4,2},{5,3},{6,4},{7,5},{8,14},{9,15},{10,... | collective-permute-start | bytes 589832 | tf_op jit(solution)/shard_map/ppermute | solution.py:470
  108.7 16.8 %collective-permute-start.11 = (f32[192,256]{1,0:T(8,128)S(1)}, f32[192,256]{1,0:T(8,128)S(1)}, u32[]{:S(2)}, u32[]{:S(2)}) collective-permute-start(f32[192,256]{1,0:T(8,128)S(1)} %get-tuple-element.43), channel_id=1, source_target_pairs={{0,2},{1,3},{2,4},{3,5},{4,6},{5,7},{6,0},{7,1},{8,10},{9,11},{10,... | collective-permute-start | bytes 589832 | tf_op jit(solution)/shard_map/ppermute | solution.py:470
  116.6 10.4 %collective-permute-start.9 = (f32[192,256]{1,0:T(8,128)S(1)}, f32[192,256]{1,0:T(8,128)S(1)}, u32[]{:S(2)}, u32[]{:S(2)}) collective-permute-start(f32[192,256]{1,0:T(8,128)S(1)} %get-tuple-element.41), channel_id=1, source_target_pairs={{0,2},{1,3},{2,4},{3,5},{4,6},{5,7},{6,0},{7,1},{8,10},{9,11},{10,... | collective-permute-start | bytes 589832 | tf_op jit(solution)/shard_map/ppermute | solution.py:470
  117.6 10.3 %collective-permute-start.12 = (f32[192,256]{1,0:T(8,128)S(1)}, f32[192,256]{1,0:T(8,128)S(1)}, u32[]{:S(2)}, u32[]{:S(2)}) collective-permute-start(f32[192,256]{1,0:T(8,128)S(1)} %get-tuple-element.44), channel_id=1, source_target_pairs={{0,6},{1,7},{2,0},{3,1},{4,2},{5,3},{6,4},{7,5},{8,14},{9,15},{10,... | collective-permute-start | bytes 589832 | tf_op jit(solution)/shard_map/ppermute | solution.py:470

commit v4 on v3

--- a/solution.py
+++ b/solution.py
@@ -179,14 +179,21 @@
 
 
 def prepare_kernel(*refs):
-    scaled_rows(refs[:-1], refs[-1])
+    pieces, (out_ref, buf, sem) = refs[:-3], refs[-3:]
+    scaled_rows(pieces, buf)
+    copy = pltpu.make_async_copy(buf, out_ref, sem)
+    copy.start()
+    copy.wait()
 
 
 def prepare(name, *pieces):
     rows = sum(piece.shape[0] for piece in pieces)
+    shape = ((rows, 3 * WIDTH), jnp.bfloat16)
     return pl.pallas_call(
         prepare_kernel,
-        out_shape=jax.ShapeDtypeStruct((rows, 3 * WIDTH), jnp.bfloat16),
+        out_specs=HBM,
+        out_shape=pltpu.HBM(*shape),
+        scratch_shapes=[pltpu.VMEM(*shape), pltpu.SemaphoreType.DMA],
         cost_estimate=pl.CostEstimate(flops=20 * 10**9, bytes_accessed=8 * rows * WIDTH, transcendentals=0),
         compiler_params=params(),
         name=name,
@@ -197,14 +204,14 @@
     ready, c_own, ready_far, line_in, got, got_sib, pos_ref, e0_out, e1_out, c_out, line_ref,
     left_ref, own_buf, c_buf, e0_buf, e1_buf, tot_ref, in_sem, c_sem, e0_sem, e1_sem,
 ):
-    orders, _, count = e1_buf.shape
-    wide = 2 * SLICE
+    chunks, orders, _, wide = e1_buf.shape
+    count = chunks * wide
     at = ready.shape[0]
     ready_copy = pltpu.make_async_copy(ready, left_ref.at[pl.ds(0, at)], in_sem.at[0])
     own_copy = pltpu.make_async_copy(c_own, own_buf, in_sem.at[1])
-    own_copy.start()
-    ready_copy.start()
-    left_ref[at:] = ready_far[...]
+    far_copy = pltpu.make_async_copy(ready_far, left_ref.at[pl.ds(at, SLICE)], in_sem.at[2])
+    for copy in (own_copy, far_copy, ready_copy):
+        copy.start()
     half = got.shape[1] // 2
     tiles = got.shape[0] * half // 8
 
@@ -224,8 +231,8 @@
         return product(rows, c_buf[base : base + wide])
 
     columns(0)
-    own_copy.wait()
-    ready_copy.wait()
+    for copy in (own_copy, far_copy, ready_copy):
+        copy.wait()
     scores = product(left_ref[at:], own_buf[...])
     coming = score(0, 0)
 
@@ -245,14 +252,14 @@
             coming = score(*items[turn + 1])
 
         def store(k, e):
-            e1_buf[2 * band : 2 * band + 2, :, base + k : base + k + 128] = e.reshape(2, SLICE, 128)
+            e1_buf[base // wide, 2 * band : 2 * band + 2, :, k : k + 128] = e.reshape(2, SLICE, 128)
 
         total, _ = exponentials(scores, None, pos_ref, store)
         if base == 0:
             tot_ref[band * wide : band * wide + wide] = total
         else:
             tot_ref[band * wide : band * wide + wide] += total
-        view = (pl.ds(2 * band, 2), slice(None), pl.ds(base, wide))
+        view = (base // wide, pl.ds(2 * band, 2))
         copies.append(pltpu.make_async_copy(e1_buf.at[view], e1_out.at[view], e1_sem.at[turn]))
         copies[-1].start()
 
@@ -268,11 +275,11 @@
 
 def forward(ready, c_own, ready_far, line, got, got_sib, pos, members):
     rows, wide, count = 4 * SLICE, 2 * SLICE, 4 * SLICE
-    own_shape, part_shape = ((1, SLICE, wide), jnp.float32), ((4, SLICE, count), jnp.float32)
+    own_shape, part_shape = ((1, SLICE, wide), jnp.float32), ((2, 4, SLICE, wide), jnp.float32)
     col_shape = ((count, 2 * WIDTH), jnp.bfloat16)
     return pl.pallas_call(
         forward_kernel,
-        in_specs=[HBM] * 2 + [pl.BlockSpec()] * 5,
+        in_specs=[HBM] * 3 + [pl.BlockSpec()] * 4,
         out_specs=[HBM] * 3 + [pl.BlockSpec()],
         out_shape=(
             pltpu.HBM(*own_shape),
@@ -287,7 +294,7 @@
             pltpu.VMEM(*own_shape),
             pltpu.VMEM(*part_shape),
             pltpu.VMEM((rows, 128), jnp.float32),
-            pltpu.SemaphoreType.DMA((2,)),
+            pltpu.SemaphoreType.DMA((3,)),
             pltpu.SemaphoreType.DMA((2,)),
             pltpu.SemaphoreType.DMA,
             pltpu.SemaphoreType.DMA((4,)),
@@ -297,7 +304,7 @@
         ),
         compiler_params=params(VMEM_LARGE),
         name="forward",
-    )(in_hbm(ready), in_hbm(c_own), ready_far, line, got, got_sib, pos)
+    )(*map(in_hbm, (ready, c_own, ready_far)), line, got, got_sib, pos)
 
 
 def denominator_kernel(member_ref, all_ref, row_ref, own_ref, line_ref, spread_ref):
@@ -343,7 +350,7 @@
 ):
     out_refs, (run_ref, e_buf, c_buf, e_sem, c_sem) = refs[:-5], refs[-5:]
     wide = 2 * SLICE
-    steps = e_buf.shape[1] // wide
+    steps = e_buf.shape[0]
     copies = []
     for k in range(steps):
         wanted = pl.ds(k * wide, wide)
@@ -354,8 +361,8 @@
             if k == 0:
                 src = e0_in.at[order if e0_in.shape[0] > 1 else 0, rows]
             else:
-                src = e1_in.at[order, rows, pl.ds((k - 1) * wide, wide)]
-            group.append(pltpu.make_async_copy(src, e_buf.at[pl.ds(at, size), wanted], e_sem.at[k, which]))
+                src = e1_in.at[k - 1, order, rows]
+            group.append(pltpu.make_async_copy(src, e_buf.at[k, pl.ds(at, size)], e_sem.at[k, which]))
             at += size
         src = c0_in if k == 0 else c1_in.at[pl.ds((k - 1) * wide, wide)]
         group.append(pltpu.make_async_copy(src, c_buf.at[wanted], c_sem.at[k]))
@@ -376,7 +383,7 @@
             copy.wait()
         his, los = [], []
         for at in range(0, wide, 128):
-            weight = e_buf[:, k * wide + at : k * wide + at + 128] * (row_inv + col_inv[:, at : at + 128])
+            weight = e_buf[k, :, at : at + 128] * (row_inv + col_inv[:, at : at + 128])
             if k == 0:
                 weight = weight - jnp.where(row_ids == pos_ref[:, at : at + 128], 2.0, 0.0)
             hi, lo = split(weight)
@@ -408,7 +415,7 @@
         out_shape=[jax.ShapeDtypeStruct((SLICE // pieces, WIDTH), jnp.float32)] * pieces,
         scratch_shapes=[
             pltpu.VMEM((SLICE, WIDTH), jnp.float32),
-            pltpu.VMEM((SLICE, count), jnp.float32),
+            pltpu.VMEM((3, SLICE, 2 * SLICE), jnp.float32),
             pltpu.VMEM((count, 2 * WIDTH), jnp.bfloat16),
             pltpu.SemaphoreType.DMA((3, len(bands))),
             pltpu.SemaphoreType.DMA((3,)),
@@ -476,7 +483,9 @@
     far = (shift(left[:half], 2), shift(right[half:], -2))
     per = rows * width // (groups * 128)
     pieces = lax.all_to_all(as_tiles(embeddings).reshape(groups, per, 128), "grp", 0, 0, tiled=True)
-    got = lax.all_to_all(pick(pairing, pieces), "grp", 0, 0, tiled=True)
+    ready = prepare("prepare", left, right, embeddings)
+    picked, ready = lax.optimization_barrier((pick(pairing, pieces), ready))
+    got = lax.all_to_all(picked, "grp", 0, 0, tiled=True)
     sib, pos_sib = swap(embeddings), swap(positive)
 
     both = jnp.concatenate([positive, pos_sib]) - group * block
@@ -485,7 +494,6 @@
     order = jnp.where(turn == 0, SELF, jnp.where(turn == 3, 0, jnp.where(turn == 1, 1, 3)))
     pos = jnp.where(owner % 2 == member % 2, order * rows + both % rows, -1).reshape(1, 2 * rows)
 
-    ready = prepare("prepare", left, right, embeddings)
     c_own, e_own, line = own_scores(ready, embeddings, sib, pos)
     ready_far = prepare("prepare_far", *far)
     got, line, ready_far = lax.optimization_barrier((got, line, ready_far))

time: 130 us -> 127 us (0.977)
  Pallas kernels: 37.2 us -> 39.1 us
  waiting for transfers between devices: 32.3 us -> 30.8 us
    all_to_all x1, waiting for transfers between devices: 12.6 us -> 6.53 us  [local(): got = lax.all_to_all(picked, 'grp', 0, 0, tiled=True)]
    all_to_all x1, waiting for transfers between devices: 1.69 us -> 6.22 us  [local(): lax.all_to_all(as_tiles(embeddings).reshape(groups, per, 128), 'grp', 0,...]
    pallas_call x3, Pallas kernels: 9.34 us -> 11.3 us  [the longest x1 8.55 us: forward(): pl.pallas_call(forward_kernel, in_specs=[HBM] * 3 + [pl.BlockSpec()] * 4,...]
  transfers between devices with their start and end apart: 16 -> 16, of which waited for: 7 -> 7; matrix products, arithmetic and copies ran while one was open for 1% -> 1% of each run, Pallas kernels for 17% -> 19%
where the time goes in v4:
time: 127 us; the launch traced here: 126 us
  starting transfers between devices  40.9 us (32%)
  Pallas kernels  39.1 us (31%)
  waiting for transfers between devices  30.8 us (24%)
  blocking collectives  12.4 us (10%)
  local copies, waits for them, and re-layouts  1.91 us (2%)
    ppermute x10, starting transfers between devices, shift(): lax.ppermute(value, 'mem', [(m, (m + by) % members) for m in range(member...  22.5 us
    pallas_call x4, Pallas kernels, backward(): pl.pallas_call(functools.partial(backward_kernel, bands), in_specs=[SMEM]...  19.2 us
    all_to_all x1, blocking collectives, local(): everything = lax.all_to_all(line, 'mem', 0, 0, tiled=True)  12.4 us
    pallas_call x1, Pallas kernels, forward(): pl.pallas_call(forward_kernel, in_specs=[HBM] * 3 + [pl.BlockSpec()] * 4,...  8.55 us
    ppermute x10, waiting for transfers between devices, shift(): lax.ppermute(value, 'mem', [(m, (m + by) % members) for m in range(member...  8.49 us
    all_to_all x1, starting transfers between devices, local(): lax.all_to_all(as_tiles(embeddings).reshape(groups, per, 128), 'grp', 0,...  7.99 us
    all_to_all x1, waiting for transfers between devices, local(): everyone = lax.all_to_all(spread, 'grp', 0, 0, tiled=True)  7.25 us
    all_to_all x1, waiting for transfers between devices, local(): got = lax.all_to_all(picked, 'grp', 0, 0, tiled=True)  6.53 us
  transfers between devices with their start and end apart: 16, of which 7 were waited for; matrix products, arithmetic and copies ran while one was open for 1% of the time, Pallas kernels for 19%

profile of v4, /device:TPU:8, one launch (start us, length us, event | category | flops | bytes accessed | tf_op | source)
XLA Modules:
  0.0 126.0 jit_solution(4216608324607925485)
XLA Ops:
  0.6 6.4 %collective-permute-start.1 = (f32[384,256]{1,0:T(8,128)}, f32[384,256]{1,0:T(8,128)S(1)}, u32[]{:S(2)}, u32[]{:S(2)}) collective-permute-start(f32[384,256]{1,0:T(8,128)} %emb_ref.3), channel_id=1, source_target_pairs={{0,6},{1,7},{2,0},{3,1},{4,2},{5,3},{6,4},{7,5},{8,14},{9,15},{10,... | collective-permute-start | bytes 1179656 | tf_op jit(solution)/shard_map/ppermute | solution.py:477
  9.3 8.0 %all-to-all-start = ((f32[32,24,128]{2,1,0:T(8,128)}), f32[32,24,128]{2,1,0:T(8,128)S(1)}, u32[]{:S(2)}, u32[]{:S(2)}) async-start(f32[32,24,128]{2,1,0:T(8,128)} %bitcast.1), calls=%async_computation | async-start | bytes 786432 | tf_op jit(solution)/shard_map/all_to_all | solution.py:485
  18.1 6.1 %collective-permute-done.1.refs_1_ = f32[384,256]{1,0:T(8,128)S(1)} collective-permute-done((f32[384,256]{1,0:T(8,128)}, f32[384,256]{1,0:T(8,128)S(1)}, u32[]{:S(2)}, u32[]{:S(2)}) %collective-permute-start.1) | collective-permute-done | bytes 393248 | tf_op jit(solution)/shard_map/ppermute | solution.py:477
  24.2 4.6 %collective-permute-start.5 = (f32[192,256]{1,0:T(8,128)S(1)}, f32[192,256]{1,0:T(8,128)S(1)}, u32[]{:S(2)}, u32[]{:S(2)}) collective-permute-start(f32[192,256]{1,0:T(8,128)S(1)} %slice.9), channel_id=1, source_target_pairs={{0,6},{1,7},{2,0},{3,1},{4,2},{5,3},{6,4},{7,5},{8,14},{9,15},{10,... | collective-permute-start | bytes 589832 | tf_op jit(solution)/shard_map/ppermute | solution.py:477
  28.9 1.7 %prepare.1.ready = bf16[1152,768]{1,0:T(8,128)(2,1)} custom-call(f32[384,256]{1,0:T(8,128)S(1)} %collective-permute-done.refs_0_, f32[384,256]{1,0:T(8,128)S(1)} %collective-permute-done.1.refs_1_, f32[384,256]{1,0:T(8,128)S(1)} %copy-done.1), custom_call_target="tpu_custom_call" | custom-call | flops 20000000000 | bytes 2359296 | tf_op jit(solution)/shard_map/prepare/pallas_call | solution.py:192
  30.6 6.2 %all-to-all-done.pieces_ref = f32[32,24,128]{2,1,0:T(8,128)S(1)} async-done(((f32[32,24,128]{2,1,0:T(8,128)}), f32[32,24,128]{2,1,0:T(8,128)S(1)}, u32[]{:S(2)}, u32[]{:S(2)}) %all-to-all-start) | async-done | bytes 393248 | tf_op jit(solution)/shard_map/all_to_all | solution.py:485
  36.9 1.5 %pick.1 = f32[32,48,128]{2,1,0:T(8,128)} custom-call(s32[2,32]{1,0:T(2,128)S(1)} %copy-done.2, f32[32,24,128]{2,1,0:T(8,128)S(1)} %all-to-all-done.pieces_ref), custom_call_target="tpu_custom_call" | custom-call | tf_op jit(solution)/shard_map/pick/pallas_call | solution.py:74
  38.4 4.9 %all-to-all-start.1 = ((f32[32,48,128]{2,1,0:T(8,128)}), f32[32,48,128]{2,1,0:T(8,128)S(1)}, u32[]{:S(2)}, u32[]{:S(2)}) async-start(f32[32,48,128]{2,1,0:T(8,128)} %pick.1), calls=%async_computation.1 | async-start | bytes 1572864 | tf_op jit(solution)/shard_map/all_to_all | solution.py:488
  44.4 4.5 %own_scores.1 = (bf16[768,512]{1,0:T(8,128)(2,1)}, f32[3,384,768]{2,1,0:T(8,128)}, f32[2,1152]{1,0:T(2,128)S(1)}) custom-call(bf16[1152,768]{1,0:T(8,128)(2,1)} %prepare.1.ready, f32[384,256]{1,0:T(8,128)S(1)} %copy-done.1, f32[384,256]{1,0:T(8,128)S(1)} %collective-permute-done.2.sib, s32[1,768]{1,0:T(1,128)S(1)} %compare_select_fusion.5.pos_ref), custom_call_target="tpu_custom_call" | custom-call | flops 1358954496 | bytes 3538944 | tf_op jit(solution)/shard_map/own_scores/pallas_call | solution.py:165
  48.9 6.5 %all-to-all-done.1.got = f32[32,48,128]{2,1,0:T(8,128)S(1)} async-done(((f32[32,48,128]{2,1,0:T(8,128)}), f32[32,48,128]{2,1,0:T(8,128)S(1)}, u32[]{:S(2)}, u32[]{:S(2)}) %all-to-all-start.1) | async-done | bytes 786464 | tf_op jit(solution)/shard_map/all_to_all | solution.py:488
  55.4 2.3 %collective-permute-done.6.got_sib = f32[32,48,128]{2,1,0:T(8,128)S(1)} collective-permute-done((f32[32,48,128]{2,1,0:T(8,128)S(1)}, f32[32,48,128]{2,1,0:T(8,128)S(1)}, u32[]{:S(2)}, u32[]{:S(2)}) %collective-permute-start.6) | collective-permute-done | bytes 786464 | tf_op jit(solution)/shard_map/ppermute | solution.py:480
  57.7 8.5 %forward.1 = (f32[1,384,768]{2,1,0:T(8,128)}, f32[2,4,384,768]{3,2,1,0:T(8,128)}, bf16[1536,512]{1,0:T(8,128)(2,1)}, f32[8,2,1536]{2,1,0:T(2,128)S(1)}) custom-call(bf16[1152,768]{1,0:T(8,128)(2,1)} %prepare.1.ready, bf16[768,512]{1,0:T(8,128)(2,1)} %get-tuple-element.27.c_own.c0_in, bf16[384,768]{1,0:T(8,128)(2,1)} %prepare_far.1.ready_far, ...), custom_call_target="tpu_custom_call" | custom-call | flops 3623878656 | bytes 9437184 | tf_op jit(solution)/shard_map/forward/pallas_call | solution.py:280
  66.3 12.4 %all_to_all.20.all_ref = f32[8,2,1536]{2,1,0:T(2,128)S(1)} all-to-all(f32[8,2,1536]{2,1,0:T(2,128)S(1)} %get-tuple-element.33), channel_id=1, replica_groups=mesh['grp'=32,'mem'=8] {'mem'}, dimensions={0} | all-to-all | bytes 196608 | tf_op jit(solution)/shard_map/all_to_all | solution.py:502
  79.3 5.0 %all-to-all-start.3 = ((f32[32,1,768]{2,1,0:T(1,128)}), f32[32,1,768]{2,1,0:T(1,128)S(1)}, u32[]{:S(2)}, u32[]{:S(2)}) async-start(f32[32,1,768]{2,1,0:T(1,128)} %get-tuple-element.36), calls=%async_computation.3 | async-start | bytes 196608 | tf_op jit(solution)/shard_map/all_to_all | solution.py:504
  84.5 7.2 %all-to-all-done.3.everyone_ref = f32[32,1,768]{2,1,0:T(1,128)S(1)} async-done(((f32[32,1,768]{2,1,0:T(1,128)}), f32[32,1,768]{2,1,0:T(1,128)S(1)}, u32[]{:S(2)}, u32[]{:S(2)}) %all-to-all-start.3) | async-done | bytes 98336 | tf_op jit(solution)/shard_map/all_to_all | solution.py:504
  91.7 4.7 %backward_3_0.1 = (f32[192,256]{1,0:T(8,128)S(1)}, f32[192,256]{1,0:T(8,128)S(1)}) custom-call(s32[2]{0:T(128)S(1)} %dynamic-slice_reduce_fusion.partner_ref, f32[1,1536]{1,0:T(1,128)S(1)} %get-tuple-element.34.row_ref, f32[1,768]{1,0:T(1,128)S(1)} %get-tuple-element.35.own_ref, f32[32,1,768]{2,1,0:T(1,128)S(1)} %all-to-all-done.3.everyone_ref, ...), custom_call_target="tpu_custom_call" | custom-call | flops 1358954496 | bytes 3538944 | tf_op jit(solution)/shard_map/backward_3_0/pallas_call | solution.py:412
  97.5 3.2 %collective-permute-start.8 = (f32[192,256]{1,0:T(8,128)S(1)}, f32[192,256]{1,0:T(8,128)S(1)}, u32[]{:S(2)}, u32[]{:S(2)}) collective-permute-start(f32[192,256]{1,0:T(8,128)S(1)} %get-tuple-element.44), channel_id=1, source_target_pairs={{0,6},{1,7},{2,0},{3,1},{4,2},{5,3},{6,4},{7,5},{8,14},{9,15},{10,... | collective-permute-start | bytes 589832 | tf_op jit(solution)/shard_map/ppermute | solution.py:477
  100.7 4.9 %backward_0_0.1 = (f32[192,256]{1,0:T(8,128)S(1)}, f32[192,256]{1,0:T(8,128)S(1)}) custom-call(s32[2]{0:T(128)S(1)} %dynamic-slice_reduce_fusion.partner_ref, f32[1,1536]{1,0:T(1,128)S(1)} %get-tuple-element.34.row_ref, f32[1,768]{1,0:T(1,128)S(1)} %get-tuple-element.35.own_ref, f32[32,1,768]{2,1,0:T(1,128)S(1)} %all-to-all-done.3.everyone_ref, ...), custom_call_target="tpu_custom_call" | custom-call | flops 1358954496 | bytes 3538944 | tf_op jit(solution)/shard_map/backward_0_0/pallas_call | solution.py:412
  105.7 2.9 %collective-permute-start.11 = (f32[192,256]{1,0:T(8,128)S(1)}, f32[192,256]{1,0:T(8,128)S(1)}, u32[]{:S(2)}, u32[]{:S(2)}) collective-permute-start(f32[192,256]{1,0:T(8,128)S(1)} %get-tuple-element.47), channel_id=1, source_target_pairs={{0,2},{1,3},{2,4},{3,5},{4,6},{5,7},{6,0},{7,1},{8,10},{9,11},{10,... | collective-permute-start | bytes 589832 | tf_op jit(solution)/shard_map/ppermute | solution.py:477
  108.6 4.9 %backward_0_192.1 = (f32[192,256]{1,0:T(8,128)S(1)}, f32[192,256]{1,0:T(8,128)S(1)}) custom-call(s32[2]{0:T(128)S(1)} %dynamic-slice_reduce_fusion.partner_ref, f32[1,1536]{1,0:T(1,128)S(1)} %get-tuple-element.34.row_ref, f32[1,768]{1,0:T(1,128)S(1)} %get-tuple-element.35.own_ref, f32[32,1,768]{2,1,0:T(1,128)S(1)} %all-to-all-done.3.everyone_ref, ...), custom_call_target="tpu_custom_call" | custom-call | flops 1358954496 | bytes 3538944 | tf_op jit(solution)/shard_map/backward_0_192/pallas_call | solution.py:412
  114.6 3.2 %collective-permute-start.12 = (f32[192,256]{1,0:T(8,128)S(1)}, f32[192,256]{1,0:T(8,128)S(1)}, u32[]{:S(2)}, u32[]{:S(2)}) collective-permute-start(f32[192,256]{1,0:T(8,128)S(1)} %get-tuple-element.48), channel_id=1, source_target_pairs={{0,6},{1,7},{2,0},{3,1},{4,2},{5,3},{6,4},{7,5},{8,14},{9,15},{10,... | collective-permute-start | bytes 589832 | tf_op jit(solution)/shard_map/ppermute | solution.py:477
  117.8 4.7 %backward_2_0.1.run_ref = f32[384,256]{1,0:T(8,128)S(1)} custom-call(s32[2]{0:T(128)S(1)} %dynamic-slice_reduce_fusion.partner_ref, f32[1,1536]{1,0:T(1,128)S(1)} %get-tuple-element.34.row_ref, f32[1,768]{1,0:T(1,128)S(1)} %get-tuple-element.35.own_ref, f32[32,1,768]{2,1,0:T(1,128)S(1)} %all-to-all-done.3.everyone_ref, ...), custom_call_target="tpu_custom_call" | custom-call | flops 1358954496 | bytes 3538944 | tf_op jit(solution)/shard_map/backward_2_0/pallas_call | solution.py:412
  122.5 1.5 %collective-permute-done.9.low0 = f32[192,256]{1,0:T(8,128)S(1)} collective-permute-done((f32[192,256]{1,0:T(8,128)S(1)}, f32[192,256]{1,0:T(8,128)S(1)}, u32[]{:S(2)}, u32[]{:S(2)}) %collective-permute-start.9) | collective-permute-done | bytes 196640 | tf_op jit(solution)/shard_map/ppermute | solution.py:477
  124.9 1.1 finish.1
  (34 shorter events, 8.2 us)
Async XLA Ops:
  0.6 23.5 %collective-permute-start.1 = (f32[384,256]{1,0:T(8,128)}, f32[384,256]{1,0:T(8,128)S(1)}, u32[]{:S(2)}, u32[]{:S(2)}) collective-permute-start(f32[384,256]{1,0:T(8,128)} %emb_ref.3), channel_id=1, source_target_pairs={{0,6},{1,7},{2,0},{3,1},{4,2},{5,3},{6,4},{7,5},{8,14},{9,15},{10,... | collective-permute-start | bytes 1179656 | tf_op jit(solution)/shard_map/ppermute | solution.py:477
  7.0 21.8 %collective-permute-start = (f32[384,256]{1,0:T(8,128)}, f32[384,256]{1,0:T(8,128)S(1)}, u32[]{:S(2)}, u32[]{:S(2)}) collective-permute-start(f32[384,256]{1,0:T(8,128)} %emb_ref.3), channel_id=1, source_target_pairs={{0,2},{1,3},{2,4},{3,5},{4,6},{5,7},{6,0},{7,1},{8,10},{9,11},{10,... | collective-permute-start | bytes 1179656 | tf_op jit(solution)/shard_map/ppermute | solution.py:477
  7.0 37.3 %collective-permute-start.2 = (f32[384,256]{1,0:T(8,128)}, f32[384,256]{1,0:T(8,128)S(1)}, u32[]{:S(2)}, u32[]{:S(2)}) collective-permute-start(f32[384,256]{1,0:T(8,128)} %emb_ref.3), channel_id=1, source_target_pairs={{0,1},{1,0},{2,3},{3,2},{4,5},{5,4},{6,7},{7,6},{8,9},{9,8},{10,11... | collective-permute-start | bytes 1179656 | tf_op jit(solution)/shard_map/ppermute | solution.py:480
  7.0 11.0 %collective-permute-start.3 = (s32[384]{0:T(512)}, s32[384]{0:T(512)S(1)}, u32[]{:S(2)}, u32[]{:S(2)}) collective-permute-start(s32[384]{0:T(512)} %param.4), channel_id=1, source_target_pairs={{0,1},{1,0},{2,3},{3,2},{4,5},{5,4},{6,7},{7,6},{8,9},{9,8},{10,11... | collective-permute-start | bytes 4616 | tf_op jit(solution)/shard_map/ppermute | solution.py:480
  7.5 1.0 copy-start
  8.5 20.4 %copy-start.1 = (f32[384,256]{1,0:T(8,128)S(1)}, f32[384,256]{1,0:T(8,128)}, u32[]{:S(2)}) copy-start(f32[384,256]{1,0:T(8,128)} %emb_ref.3) | copy-start | bytes 1179652
  9.3 27.6 %all-to-all-start = ((f32[32,24,128]{2,1,0:T(8,128)}), f32[32,24,128]{2,1,0:T(8,128)S(1)}, u32[]{:S(2)}, u32[]{:S(2)}) async-start(f32[32,24,128]{2,1,0:T(8,128)} %bitcast.1), calls=%async_computation | async-start | bytes 786432 | tf_op jit(solution)/shard_map/all_to_all | solution.py:485
  24.2 19.1 %collective-permute-start.5 = (f32[192,256]{1,0:T(8,128)S(1)}, f32[192,256]{1,0:T(8,128)S(1)}, u32[]{:S(2)}, u32[]{:S(2)}) collective-permute-start(f32[192,256]{1,0:T(8,128)S(1)} %slice.9), channel_id=1, source_target_pairs={{0,6},{1,7},{2,0},{3,1},{4,2},{5,3},{6,4},{7,5},{8,14},{9,15},{10,... | collective-permute-start | bytes 589832 | tf_op jit(solution)/shard_map/ppermute | solution.py:477
  28.8 8.0 %copy-start.2 = (s32[2,32]{1,0:T(2,128)S(1)}, s32[2,32]{1,0:T(2,128)}, u32[]{:S(2)}) copy-start(s32[2,32]{1,0:T(2,128)} %pairing_ref.1) | copy-start | bytes 772
  28.8 14.5 %collective-permute-start.4 = (f32[192,256]{1,0:T(8,128)S(1)}, f32[192,256]{1,0:T(8,128)S(1)}, u32[]{:S(2)}, u32[]{:S(2)}) collective-permute-start(f32[192,256]{1,0:T(8,128)S(1)} %slice.8), channel_id=1, source_target_pairs={{0,2},{1,3},{2,4},{3,5},{4,6},{5,7},{6,0},{7,1},{8,10},{9,11},{10,... | collective-permute-start | bytes 589832 | tf_op jit(solution)/shard_map/ppermute | solution.py:477
  38.4 17.1 %all-to-all-start.1 = ((f32[32,48,128]{2,1,0:T(8,128)}), f32[32,48,128]{2,1,0:T(8,128)S(1)}, u32[]{:S(2)}, u32[]{:S(2)}) async-start(f32[32,48,128]{2,1,0:T(8,128)} %pick.1), calls=%async_computation.1 | async-start | bytes 1572864 | tf_op jit(solution)/shard_map/all_to_all | solution.py:488
  55.4 2.3 %collective-permute-start.6 = (f32[32,48,128]{2,1,0:T(8,128)S(1)}, f32[32,48,128]{2,1,0:T(8,128)S(1)}, u32[]{:S(2)}, u32[]{:S(2)}) collective-permute-start(f32[32,48,128]{2,1,0:T(8,128)S(1)} %all-to-all-done.1.got), channel_id=1, source_target_pairs={{0,1},{1,0},{2,3},{3,2},{4,5},{5,4},{6,7},{7,6},{8,9},{9,8},{10,11... | collective-permute-start | bytes 2359304 | tf_op jit(solution)/shard_map/ppermute | solution.py:480
  79.3 12.4 %all-to-all-start.3 = ((f32[32,1,768]{2,1,0:T(1,128)}), f32[32,1,768]{2,1,0:T(1,128)S(1)}, u32[]{:S(2)}, u32[]{:S(2)}) async-start(f32[32,1,768]{2,1,0:T(1,128)} %get-tuple-element.36), calls=%async_computation.3 | async-start | bytes 196608 | tf_op jit(solution)/shard_map/all_to_all | solution.py:504
  96.4 17.1 %collective-permute-start.7 = (f32[192,256]{1,0:T(8,128)S(1)}, f32[192,256]{1,0:T(8,128)S(1)}, u32[]{:S(2)}, u32[]{:S(2)}) collective-permute-start(f32[192,256]{1,0:T(8,128)S(1)} %get-tuple-element.42), channel_id=1, source_target_pairs={{0,2},{1,3},{2,4},{3,5},{4,6},{5,7},{6,0},{7,1},{8,10},{9,11},{10,... | collective-permute-start | bytes 589832 | tf_op jit(solution)/shard_map/ppermute | solution.py:477
  97.5 16.0 %collective-permute-start.8 = (f32[192,256]{1,0:T(8,128)S(1)}, f32[192,256]{1,0:T(8,128)S(1)}, u32[]{:S(2)}, u32[]{:S(2)}) collective-permute-start(f32[192,256]{1,0:T(8,128)S(1)} %get-tuple-element.44), channel_id=1, source_target_pairs={{0,6},{1,7},{2,0},{3,1},{4,2},{5,3},{6,4},{7,5},{8,14},{9,15},{10,... | collective-permute-start | bytes 589832 | tf_op jit(solution)/shard_map/ppermute | solution.py:477
  105.6 16.9 %collective-permute-start.10 = (f32[192,256]{1,0:T(8,128)S(1)}, f32[192,256]{1,0:T(8,128)S(1)}, u32[]{:S(2)}, u32[]{:S(2)}) collective-permute-start(f32[192,256]{1,0:T(8,128)S(1)} %get-tuple-element.46), channel_id=1, source_target_pairs={{0,6},{1,7},{2,0},{3,1},{4,2},{5,3},{6,4},{7,5},{8,14},{9,15},{10,... | collective-permute-start | bytes 589832 | tf_op jit(solution)/shard_map/ppermute | solution.py:477
  105.7 16.8 %collective-permute-start.11 = (f32[192,256]{1,0:T(8,128)S(1)}, f32[192,256]{1,0:T(8,128)S(1)}, u32[]{:S(2)}, u32[]{:S(2)}) collective-permute-start(f32[192,256]{1,0:T(8,128)S(1)} %get-tuple-element.47), channel_id=1, source_target_pairs={{0,2},{1,3},{2,4},{3,5},{4,6},{5,7},{6,0},{7,1},{8,10},{9,11},{10,... | collective-permute-start | bytes 589832 | tf_op jit(solution)/shard_map/ppermute | solution.py:477
  113.6 10.4 %collective-permute-start.9 = (f32[192,256]{1,0:T(8,128)S(1)}, f32[192,256]{1,0:T(8,128)S(1)}, u32[]{:S(2)}, u32[]{:S(2)}) collective-permute-start(f32[192,256]{1,0:T(8,128)S(1)} %get-tuple-element.45), channel_id=1, source_target_pairs={{0,2},{1,3},{2,4},{3,5},{4,6},{5,7},{6,0},{7,1},{8,10},{9,11},{10,... | collective-permute-start | bytes 589832 | tf_op jit(solution)/shard_map/ppermute | solution.py:477
  114.6 10.3 %collective-permute-start.12 = (f32[192,256]{1,0:T(8,128)S(1)}, f32[192,256]{1,0:T(8,128)S(1)}, u32[]{:S(2)}, u32[]{:S(2)}) collective-permute-start(f32[192,256]{1,0:T(8,128)S(1)} %get-tuple-element.48), channel_id=1, source_target_pairs={{0,6},{1,7},{2,0},{3,1},{4,2},{5,3},{6,4},{7,5},{8,14},{9,15},{10,... | collective-permute-start | bytes 589832 | tf_op jit(solution)/shard_map/ppermute | solution.py:477

commit v5 on v4

--- a/solution.py
+++ b/solution.py
@@ -89,18 +89,14 @@
 
 
 def unit_parts(values):
-    hi, lo = split(values * (1.0 / radius_of(values)))
-    return jnp.concatenate([hi, lo], axis=1)
-
-
-def product(left, cols):
-    hi, lo = cols[:, :WIDTH], cols[:, WIDTH:]
-    return lax.dot_general(
-        left,
-        jnp.concatenate([hi, hi, lo], axis=1),
-        (((1,), (1,)), ((), ())),
-        preferred_element_type=jnp.float32,
-    )
+    unit = values * (1.0 / radius_of(values))
+    hi, lo = split(unit)
+    hi_t, lo_t = split(unit.T)
+    return jnp.concatenate([hi, lo], axis=1), jnp.concatenate([hi_t, hi_t, lo_t], axis=0)
+
+
+def product(left, right):
+    return jnp.dot(left, right, preferred_element_type=jnp.float32)
 
 
 def exponentials(scores, first_row, pos_ref, store):
@@ -127,23 +123,30 @@
 
 
 def own_kernel(
-    ready, mine, sib, pos_ref, c_out, e_out, line_ref, left_ref, c_buf, e_buf, ready_sem, c_sem, e_sem
+    ready, ready_far, mine, sib, pos_ref, c_out, e_out, line_ref, left_ref, c_buf, right_ref, e_buf, in_sem, c_sem, e_sem
 ):
-    ready_copy = pltpu.make_async_copy(ready, left_ref, ready_sem)
-    ready_copy.start()
-    c_buf[:SLICE] = unit_parts(mine[...])
-    c_buf[SLICE:] = unit_parts(sib[...])
+    at = ready.shape[0]
+    ready_copies = [
+        pltpu.make_async_copy(ready, left_ref.at[pl.ds(0, at)], in_sem.at[0]),
+        pltpu.make_async_copy(ready_far, left_ref.at[pl.ds(at, SLICE)], in_sem.at[1]),
+    ]
+    for copy in ready_copies:
+        copy.start()
+    for which, ref in enumerate((mine, sib)):
+        here = slice(which * SLICE, which * SLICE + SLICE)
+        c_buf[here], right_ref[:, here] = unit_parts(ref[...])
     copies = [pltpu.make_async_copy(c_buf, c_out, c_sem)]
     copies[0].start()
-    ready_copy.wait()
-
-    coming = product(left_ref[:SLICE], c_buf[...])
+    for copy in ready_copies:
+        copy.wait()
+
+    coming = product(left_ref[:SLICE], right_ref[...])
     totals, matches = [], []
-    for order in range(3):
+    for order in range(4):
         scores = coming
-        if order < 2:
+        if order < 3:
             at = (order + 1) * SLICE
-            coming = product(left_ref[at : at + SLICE], c_buf[...])
+            coming = product(left_ref[at : at + SLICE], right_ref[...])
 
         def store(k, e):
             e_buf[order, :, k : k + 128] = e
@@ -159,23 +162,29 @@
         copy.wait()
 
 
-def own_scores(ready, mine, sib, pos):
-    rows, wide = 3 * SLICE, 2 * SLICE
-    shapes = [((wide, 2 * WIDTH), jnp.bfloat16), ((3, SLICE, wide), jnp.float32)]
+def own_scores(ready, ready_far, mine, sib, pos):
+    rows, wide = 4 * SLICE, 2 * SLICE
+    shapes = [((wide, 2 * WIDTH), jnp.bfloat16), ((4, SLICE, wide), jnp.float32)]
     return pl.pallas_call(
         own_kernel,
-        in_specs=[HBM] + [pl.BlockSpec()] * 3,
+        in_specs=[HBM] * 2 + [pl.BlockSpec()] * 3,
         out_specs=[HBM] * 2 + [pl.BlockSpec()],
         out_shape=[pltpu.HBM(*shape) for shape in shapes] + [jax.ShapeDtypeStruct((2, rows), jnp.float32)],
-        scratch_shapes=[pltpu.VMEM((rows, 3 * WIDTH), jnp.bfloat16)]
-        + [pltpu.VMEM(*shape) for shape in shapes]
-        + [pltpu.SemaphoreType.DMA, pltpu.SemaphoreType.DMA, pltpu.SemaphoreType.DMA((3,))],
+        scratch_shapes=[
+            pltpu.VMEM((rows, 3 * WIDTH), jnp.bfloat16),
+            pltpu.VMEM(*shapes[0]),
+            pltpu.VMEM((3 * WIDTH, wide), jnp.bfloat16),
+            pltpu.VMEM(*shapes[1]),
+            pltpu.SemaphoreType.DMA((2,)),
+            pltpu.SemaphoreType.DMA,
+            pltpu.SemaphoreType.DMA((4,)),
+        ],
         cost_estimate=pl.CostEstimate(
             flops=6 * rows * wide * WIDTH, bytes_accessed=4 * rows * wide, transcendentals=rows * wide
         ),
         compiler_params=params(VMEM_LARGE),
         name="own_scores",
-    )(in_hbm(ready), mine, sib, pos)
+    )(in_hbm(ready), in_hbm(ready_far), mine, sib, pos)
 
 
 def prepare_kernel(*refs):
@@ -201,148 +210,127 @@
 
 
 def forward_kernel(
-    ready, c_own, ready_far, line_in, got, got_sib, pos_ref, e0_out, e1_out, c_out, line_ref,
-    left_ref, own_buf, c_buf, e0_buf, e1_buf, tot_ref, in_sem, c_sem, e0_sem, e1_sem,
+    ready, ready_far, line_in, got, got_sib, e_out, c_out, line_ref,
+    left_ref, c_buf, right_ref, e_buf, tot_ref, in_sem, c_sem, e_sem,
 ):
-    chunks, orders, _, wide = e1_buf.shape
-    count = chunks * wide
+    chunks, orders, _, wide = e_buf.shape
     at = ready.shape[0]
-    ready_copy = pltpu.make_async_copy(ready, left_ref.at[pl.ds(0, at)], in_sem.at[0])
-    own_copy = pltpu.make_async_copy(c_own, own_buf, in_sem.at[1])
-    far_copy = pltpu.make_async_copy(ready_far, left_ref.at[pl.ds(at, SLICE)], in_sem.at[2])
-    for copy in (own_copy, far_copy, ready_copy):
+    ready_copies = [
+        pltpu.make_async_copy(ready, left_ref.at[pl.ds(0, at)], in_sem.at[0]),
+        pltpu.make_async_copy(ready_far, left_ref.at[pl.ds(at, SLICE)], in_sem.at[1]),
+    ]
+    for copy in ready_copies:
         copy.start()
     half = got.shape[1] // 2
     tiles = got.shape[0] * half // 8
-
     copies = []
 
-    def columns(base):
+    def columns(chunk):
         for which, ref in enumerate((got, got_sib)):
-            begin = base // wide * half
-            piece = rows_of(ref[:, begin : begin + half].reshape(tiles, 8, 128))
-            c_buf[base + which * SLICE : base + which * SLICE + SLICE] = unit_parts(piece)
-        view = (pl.ds(base, wide),)
-        copies.append(pltpu.make_async_copy(c_buf.at[view], c_out.at[view], c_sem.at[base // wide]))
+            piece = rows_of(ref[:, chunk * half : chunk * half + half].reshape(tiles, 8, 128))
+            here = slice(which * SLICE, which * SLICE + SLICE)
+            c_buf[chunk, here], right_ref[chunk, :, here] = unit_parts(piece)
+        copies.append(pltpu.make_async_copy(c_buf.at[chunk], c_out.at[chunk], c_sem.at[chunk]))
         copies[-1].start()
 
-    def score(band, base):
-        rows = left_ref[band * wide : band * wide + wide]
-        return product(rows, c_buf[base : base + wide])
+    def scores_of(chunk, band):
+        return product(left_ref[band * wide : band * wide + wide], right_ref[chunk])
 
     columns(0)
-    for copy in (own_copy, far_copy, ready_copy):
+    for copy in ready_copies:
         copy.wait()
-    scores = product(left_ref[at:], own_buf[...])
-    coming = score(0, 0)
-
-    def store_own(k, e):
-        e0_buf[:, :, k : k + 128] = e.reshape(1, SLICE, 128)
-
-    far_total, far_match = exponentials(scores, at, pos_ref, store_own)
-    copies.append(pltpu.make_async_copy(e0_buf, e0_out, e0_sem))
-    copies[-1].start()
-
-    items = [(band, base) for base in range(0, count, wide) for band in range(orders // 2)]
-    for turn, (band, base) in enumerate(items):
+    items = [(chunk, band) for chunk in range(chunks) for band in range(orders // 2)]
+    coming = scores_of(*items[0])
+    for turn, (chunk, band) in enumerate(items):
         scores = coming
         if turn + 1 < len(items):
-            if items[turn + 1][1] != base:
-                columns(items[turn + 1][1])
-            coming = score(*items[turn + 1])
+            if items[turn + 1][0] != chunk:
+                columns(items[turn + 1][0])
+            coming = scores_of(*items[turn + 1])
 
         def store(k, e):
-            e1_buf[base // wide, 2 * band : 2 * band + 2, :, k : k + 128] = e.reshape(2, SLICE, 128)
-
-        total, _ = exponentials(scores, None, pos_ref, store)
-        if base == 0:
+            e_buf[chunk, 2 * band : 2 * band + 2, :, k : k + 128] = e.reshape(2, SLICE, 128)
+
+        total, _ = exponentials(scores, None, None, store)
+        if chunk == 0:
             tot_ref[band * wide : band * wide + wide] = total
         else:
             tot_ref[band * wide : band * wide + wide] += total
-        view = (base // wide, pl.ds(2 * band, 2))
-        copies.append(pltpu.make_async_copy(e1_buf.at[view], e1_out.at[view], e1_sem.at[turn]))
+        view = (chunk, pl.ds(2 * band, 2))
+        copies.append(pltpu.make_async_copy(e_buf.at[view], e_out.at[view], e_sem.at[turn]))
         copies[-1].start()
 
-    far = jnp.concatenate([as_line(far_total), as_line(far_match)], axis=0)
-    line = jnp.concatenate([line_in[...], far], axis=1)
-    total = as_line(tot_ref[...]) + line[0:1]
-    for member in range(line_ref.shape[0]):
-        line_ref[member, 0:1] = total
-        line_ref[member, 1:2] = line[1:2]
+    line_ref[0:1] = as_line(tot_ref[...]) + line_in[0:1]
+    line_ref[1:2] = line_in[1:2]
     for copy in copies:
         copy.wait()
 
 
-def forward(ready, c_own, ready_far, line, got, got_sib, pos, members):
-    rows, wide, count = 4 * SLICE, 2 * SLICE, 4 * SLICE
-    own_shape, part_shape = ((1, SLICE, wide), jnp.float32), ((2, 4, SLICE, wide), jnp.float32)
-    col_shape = ((count, 2 * WIDTH), jnp.bfloat16)
+def forward(ready, ready_far, line, got, got_sib):
+    rows, wide = 4 * SLICE, 2 * SLICE
+    e_shape, c_shape = ((2, 4, SLICE, wide), jnp.float32), ((2, wide, 2 * WIDTH), jnp.bfloat16)
     return pl.pallas_call(
         forward_kernel,
-        in_specs=[HBM] * 3 + [pl.BlockSpec()] * 4,
-        out_specs=[HBM] * 3 + [pl.BlockSpec()],
-        out_shape=(
-            pltpu.HBM(*own_shape),
-            pltpu.HBM(*part_shape),
-            pltpu.HBM(*col_shape),
-            jax.ShapeDtypeStruct((members, 2, rows), jnp.float32),
-        ),
+        in_specs=[HBM] * 2 + [pl.BlockSpec()] * 3,
+        out_specs=[HBM] * 2 + [pl.BlockSpec()],
+        out_shape=(pltpu.HBM(*e_shape), pltpu.HBM(*c_shape), jax.ShapeDtypeStruct((2, rows), jnp.float32)),
         scratch_shapes=[
             pltpu.VMEM((rows, 3 * WIDTH), jnp.bfloat16),
-            pltpu.VMEM((wide, 2 * WIDTH), jnp.bfloat16),
-            pltpu.VMEM(*col_shape),
-            pltpu.VMEM(*own_shape),
-            pltpu.VMEM(*part_shape),
+            pltpu.VMEM(*c_shape),
+            pltpu.VMEM((2, 3 * WIDTH, wide), jnp.bfloat16),
+            pltpu.VMEM(*e_shape),
             pltpu.VMEM((rows, 128), jnp.float32),
-            pltpu.SemaphoreType.DMA((3,)),
             pltpu.SemaphoreType.DMA((2,)),
-            pltpu.SemaphoreType.DMA,
+            pltpu.SemaphoreType.DMA((2,)),
             pltpu.SemaphoreType.DMA((4,)),
         ],
         cost_estimate=pl.CostEstimate(
-            flops=6 * rows * count * WIDTH, bytes_accessed=4 * rows * count, transcendentals=rows * count
+            flops=12 * rows * wide * WIDTH, bytes_accessed=8 * rows * wide, transcendentals=2 * rows * wide
         ),
         compiler_params=params(VMEM_LARGE),
         name="forward",
-    )(*map(in_hbm, (ready, c_own, ready_far)), line, got, got_sib, pos)
-
-
-def denominator_kernel(member_ref, all_ref, row_ref, own_ref, line_ref, spread_ref):
-    member = member_ref[0]
-    members = all_ref.shape[0]
-
-    def summed(owner, kind):
-        value = 0.0
-        for by, order in ((0, SELF), (2, 0), (members - 2, 1), (4, 3)):
-            held = all_ref[lax.rem(owner + by, members)]
-            value = value + held[kind : kind + 1, order * SLICE : order * SLICE + SLICE]
-        return value
-
-    mate = member + 1 - 2 * lax.rem(member, 2)
-    own = summed(member, 0)
-    line_ref[0:1] = own
-    line_ref[1:2] = summed(member, 1)
-    both = jnp.concatenate([own, summed(mate, 0)], axis=1)
+    )(in_hbm(ready), in_hbm(ready_far), line, got, got_sib)
+
+
+def denominator_kernel(mine, at_left, at_right, at_far, row_ref, line_ref):
+    def part(ref, order):
+        return ref[:, order * SLICE : order * SLICE + SLICE]
+
+    for order, (a, b, c) in enumerate(((2, 3, 1), (3, 2, 0), (1, 0, 3), (0, 1, 2))):
+        value = (part(mine, order) + part(at_left, a)) + (part(at_right, b) + part(at_far, c))
+        row_ref[:, order * SLICE : order * SLICE + SLICE] = value[0:1]
+        if order == SELF:
+            line_ref[...] = value
+
+
+def denominators(*lines):
+    return pl.pallas_call(
+        denominator_kernel,
+        out_shape=(
+            jax.ShapeDtypeStruct((1, 4 * SLICE), jnp.float32),
+            jax.ShapeDtypeStruct((2, SLICE), jnp.float32),
+        ),
+        compiler_params=params(),
+        name="denominators",
+    )(*lines)
+
+
+def spread_kernel(line_ref, sib_ref, own_ref, spread_ref):
+    both = jnp.concatenate([line_ref[0:1], sib_ref[0:1]], axis=1)
     own_ref[...] = both
     spread_ref[...] = jnp.broadcast_to(both.reshape(1, 1, 2 * SLICE), spread_ref.shape)
-    for order, by in enumerate((members - 2, 2, 0, 4)):
-        value = own if by == 0 else summed(lax.rem(member + by, members), 0)
-        row_ref[:, order * SLICE : order * SLICE + SLICE] = value
-
-
-def denominators(member, everything, groups):
-    return pl.pallas_call(
-        denominator_kernel,
-        in_specs=[SMEM, pl.BlockSpec()],
+
+
+def spread(line, sib, groups):
+    return pl.pallas_call(
+        spread_kernel,
         out_shape=(
-            jax.ShapeDtypeStruct((1, 4 * SLICE), jnp.float32),
             jax.ShapeDtypeStruct((1, 2 * SLICE), jnp.float32),
-            jax.ShapeDtypeStruct((2, SLICE), jnp.float32),
             jax.ShapeDtypeStruct((groups, 1, 2 * SLICE), jnp.float32),
         ),
         compiler_params=params(),
-        name="denominators",
-    )(member, everything)
+        name="spread",
+    )(line, sib)
 
 
 def backward_kernel(
@@ -353,19 +341,18 @@
     steps = e_buf.shape[0]
     copies = []
     for k in range(steps):
-        wanted = pl.ds(k * wide, wide)
         group = []
         at = 0
         for which, (order, begin, size) in enumerate(bands):
             rows = pl.ds(begin, size)
             if k == 0:
-                src = e0_in.at[order if e0_in.shape[0] > 1 else 0, rows]
+                src = e0_in.at[order, rows]
             else:
                 src = e1_in.at[k - 1, order, rows]
             group.append(pltpu.make_async_copy(src, e_buf.at[k, pl.ds(at, size)], e_sem.at[k, which]))
             at += size
-        src = c0_in if k == 0 else c1_in.at[pl.ds((k - 1) * wide, wide)]
-        group.append(pltpu.make_async_copy(src, c_buf.at[wanted], c_sem.at[k]))
+        src = c0_in if k == 0 else c1_in.at[k - 1]
+        group.append(pltpu.make_async_copy(src, c_buf.at[k], c_sem.at[k]))
         copies.append(group)
         for copy in group:
             copy.start()
@@ -389,13 +376,9 @@
             hi, lo = split(weight)
             his.append(hi)
             los.append(lo)
-        cols = c_buf[k * wide : k * wide + wide]
-        c_hi, c_lo = cols[:, :WIDTH], cols[:, WIDTH:]
-        part = jnp.dot(
-            jnp.concatenate(his + his + los, axis=1),
-            jnp.concatenate([c_hi, c_lo, c_hi], axis=0),
-            preferred_element_type=jnp.float32,
-        )
+        both = product(jnp.concatenate(his, axis=1), c_buf[k])
+        part = both[:, :WIDTH] + both[:, WIDTH:]
+        part = part + product(jnp.concatenate(los, axis=1), c_buf[k, :, :WIDTH])
         if k == 0:
             run_ref[...] = part
         elif k + 1 < steps:
@@ -416,7 +399,7 @@
         scratch_shapes=[
             pltpu.VMEM((SLICE, WIDTH), jnp.float32),
             pltpu.VMEM((3, SLICE, 2 * SLICE), jnp.float32),
-            pltpu.VMEM((count, 2 * WIDTH), jnp.bfloat16),
+            pltpu.VMEM((3, 2 * SLICE, 2 * WIDTH), jnp.bfloat16),
             pltpu.SemaphoreType.DMA((3, len(bands))),
             pltpu.SemaphoreType.DMA((3,)),
         ],
@@ -494,24 +477,24 @@
     order = jnp.where(turn == 0, SELF, jnp.where(turn == 3, 0, jnp.where(turn == 1, 1, 3)))
     pos = jnp.where(owner % 2 == member % 2, order * rows + both % rows, -1).reshape(1, 2 * rows)
 
-    c_own, e_own, line = own_scores(ready, embeddings, sib, pos)
     ready_far = prepare("prepare_far", *far)
-    got, line, ready_far = lax.optimization_barrier((got, line, ready_far))
-    e_far, e_part, c_part, line = forward(ready, c_own, ready_far, line, got, swap(got), pos, members)
-
-    everything = lax.all_to_all(line, "mem", 0, 0, tiled=True)
-    row_den, own_den, line, spread = denominators(jnp.reshape(member, (1,)), everything, groups)
-    everyone = lax.all_to_all(spread, "grp", 0, 0, tiled=True)
-
-    shared = (pairing[:, group], row_den, own_den, everyone, pos, e_part, c_own, c_part)
-    far_low, far_high = backward(((3, 0, rows),), 2, e_far, *shared)
+    c_own, e_own, line = own_scores(ready, ready_far, embeddings, sib, pos)
+    got, line = lax.optimization_barrier((got, line))
+    e_part, c_part, line = forward(ready, ready_far, line, got, swap(got))
+
+    row_den, line = denominators(line, shift(line, 2), shift(line, -2), shift(line, 4))
+    own_den, spread_den = spread(line, swap(line), groups)
+    everyone = lax.all_to_all(spread_den, "grp", 0, 0, tiled=True)
+
+    shared = (e_own, pairing[:, group], row_den, own_den, everyone, pos, e_part, c_own, c_part)
+    far_low, far_high = backward(((3, 0, rows),), 2, *shared)
     far_low, far_high = shift(far_low, 2), shift(far_high, -2)
-    left_low, right_high = backward(((0, 0, half), (1, half, half)), 2, e_own, *shared)
+    left_low, right_high = backward(((0, 0, half), (1, half, half)), 2, *shared)
     high0, low1 = shift(right_high, 2), shift(left_low, -2)
-    left_high, right_low = backward(((0, half, half), (1, 0, half)), 2, e_own, *shared)
+    left_high, right_low = backward(((0, half, half), (1, 0, half)), 2, *shared)
     right_low, left_high = add_pairs(right_low, far_low, left_high, far_high)
     low0, high1 = shift(right_low, 2), shift(left_high, -2)
-    (run,) = backward(((SELF, 0, rows),), 1, e_own, *shared)
+    (run,) = backward(((SELF, 0, rows),), 1, *shared)
     return finish(embeddings, run, (low0, low1), (high0, high1), line)
 
 

time: 127 us -> 129 us (1.016)
  blocking collectives: 12.4 us -> 0 us
  waiting for transfers between devices: 30.8 us -> 37.9 us
  starting transfers between devices: 40.9 us -> 45.8 us
    all_to_all x1 -> x0, blocking collectives: 12.4 us -> none  [local(): everything = lax.all_to_all(line, 'mem', 0, 0, tiled=True)]
    ppermute x10 -> x13, waiting for transfers between devices: 8.49 us -> 15.5 us  [shift(): lax.ppermute(value, 'mem', [(m, (m + by) % members) for m in range(member...]
    ppermute x10 -> x13, starting transfers between devices: 22.5 us -> 27.3 us  [shift(): lax.ppermute(value, 'mem', [(m, (m + by) % members) for m in range(member...]
    ppermute x3 -> x4, waiting for transfers between devices: 2.29 us -> 3.44 us  [swap(): return lax.ppermute(value, 'mem', [(m, m ^ 1) for m in range(members)])]
    pallas_call x3 -> x4, Pallas kernels: 13.8 us -> 14.2 us  [the longest x1 7.74 us: forward(): pl.pallas_call(forward_kernel, in_specs=[HBM] * 2 + [pl.BlockSpec()] * 3,...]
  transfers between devices with their start and end apart: 16 -> 20, of which waited for: 7 -> 10; matrix products, arithmetic and copies ran while one was open for 1% -> 1% of each run, Pallas kernels for 19% -> 20%
where the time goes in v5:
time: 129 us; the launch traced here: 127 us
  starting transfers between devices  45.8 us (36%)
  Pallas kernels  39.6 us (31%)
  waiting for transfers between devices  37.9 us (29%)
  local copies, waits for them, and re-layouts  2.9 us (2%)
    ppermute x13, starting transfers between devices, shift(): lax.ppermute(value, 'mem', [(m, (m + by) % members) for m in range(member...  27.3 us
    pallas_call x4, Pallas kernels, backward(): pl.pallas_call(functools.partial(backward_kernel, bands), in_specs=[SMEM]...  19.2 us
    ppermute x13, waiting for transfers between devices, shift(): lax.ppermute(value, 'mem', [(m, (m + by) % members) for m in range(member...  15.5 us
    all_to_all x1, starting transfers between devices, local(): lax.all_to_all(as_tiles(embeddings).reshape(groups, per, 128), 'grp', 0,...  7.99 us
    pallas_call x1, Pallas kernels, forward(): pl.pallas_call(forward_kernel, in_specs=[HBM] * 2 + [pl.BlockSpec()] * 3,...  7.74 us
    all_to_all x1, waiting for transfers between devices, local(): everyone = lax.all_to_all(spread_den, 'grp', 0, 0, tiled=True)  7.25 us
    all_to_all x1, waiting for transfers between devices, local(): got = lax.all_to_all(picked, 'grp', 0, 0, tiled=True)  6.49 us
    pallas_call x1, Pallas kernels, own_scores(): pl.pallas_call(own_kernel, in_specs=[HBM] * 2 + [pl.BlockSpec()] * 3, out...  5.82 us
  transfers between devices with their start and end apart: 20, of which 10 were waited for; matrix products, arithmetic and copies ran while one was open for 1% of the time, Pallas kernels for 20%

profile of v5, /device:TPU:8, one launch (start us, length us, event | category | flops | bytes accessed | tf_op | source)
XLA Modules:
  0.0 127.1 jit_solution(15429432243215934951)
XLA Ops:
  0.6 6.4 %collective-permute-start.1 = (f32[384,256]{1,0:T(8,128)}, f32[384,256]{1,0:T(8,128)S(1)}, u32[]{:S(2)}, u32[]{:S(2)}) collective-permute-start(f32[384,256]{1,0:T(8,128)} %emb_ref.3), channel_id=1, source_target_pairs={{0,6},{1,7},{2,0},{3,1},{4,2},{5,3},{6,4},{7,5},{8,14},{9,15},{10,... | collective-permute-start | bytes 1179656 | tf_op jit(solution)/shard_map/ppermute | solution.py:460
  9.3 8.0 %all-to-all-start = ((f32[32,24,128]{2,1,0:T(8,128)}), f32[32,24,128]{2,1,0:T(8,128)S(1)}, u32[]{:S(2)}, u32[]{:S(2)}) async-start(f32[32,24,128]{2,1,0:T(8,128)} %bitcast), calls=%async_computation | async-start | bytes 786432 | tf_op jit(solution)/shard_map/all_to_all | solution.py:468
  18.1 6.1 %collective-permute-done.1.refs_1_ = f32[384,256]{1,0:T(8,128)S(1)} collective-permute-done((f32[384,256]{1,0:T(8,128)}, f32[384,256]{1,0:T(8,128)S(1)}, u32[]{:S(2)}, u32[]{:S(2)}) %collective-permute-start.1) | collective-permute-done | bytes 393248 | tf_op jit(solution)/shard_map/ppermute | solution.py:460
  24.2 4.6 %collective-permute-start.3 = (f32[192,256]{1,0:T(8,128)S(1)}, f32[192,256]{1,0:T(8,128)S(1)}, u32[]{:S(2)}, u32[]{:S(2)}) collective-permute-start(f32[192,256]{1,0:T(8,128)S(1)} %slice.9), channel_id=1, source_target_pairs={{0,6},{1,7},{2,0},{3,1},{4,2},{5,3},{6,4},{7,5},{8,14},{9,15},{10,... | collective-permute-start | bytes 589832 | tf_op jit(solution)/shard_map/ppermute | solution.py:460
  31.6 5.2 %all-to-all-done.pieces_ref = f32[32,24,128]{2,1,0:T(8,128)S(1)} async-done(((f32[32,24,128]{2,1,0:T(8,128)}), f32[32,24,128]{2,1,0:T(8,128)S(1)}, u32[]{:S(2)}, u32[]{:S(2)}) %all-to-all-start) | async-done | bytes 393248 | tf_op jit(solution)/shard_map/all_to_all | solution.py:468
  38.4 4.9 %all-to-all-start.1 = ((f32[32,48,128]{2,1,0:T(8,128)}), f32[32,48,128]{2,1,0:T(8,128)S(1)}, u32[]{:S(2)}, u32[]{:S(2)}) async-start(f32[32,48,128]{2,1,0:T(8,128)} %pick.1), calls=%async_computation.1 | async-start | bytes 1572864 | tf_op jit(solution)/shard_map/all_to_all | solution.py:471
  44.4 5.8 %own_scores.1 = (bf16[768,512]{1,0:T(8,128)(2,1)}, f32[4,384,768]{2,1,0:T(8,128)}, f32[2,1536]{1,0:T(2,128)S(1)}) custom-call(bf16[1152,768]{1,0:T(8,128)(2,1)} %prepare.1.ready, bf16[384,768]{1,0:T(8,128)(2,1)} %prepare_far.1.ready_far, f32[384,256]{1,0:T(8,128)S(1)} %copy-done.2, f32[384,256]{1,0:T(8,128)S(1)} %collective-permute-done.4.sib, ...), custom_call_target="tpu_custom_call" | custom-call | flops 1811939328 | bytes 4718592 | tf_op jit(solution)/shard_map/own_scores/pallas_call | solution.py:168
  50.2 6.5 %all-to-all-done.1.got = f32[32,48,128]{2,1,0:T(8,128)S(1)} async-done(((f32[32,48,128]{2,1,0:T(8,128)}), f32[32,48,128]{2,1,0:T(8,128)S(1)}, u32[]{:S(2)}, u32[]{:S(2)}) %all-to-all-start.1) | async-done | bytes 786464 | tf_op jit(solution)/shard_map/all_to_all | solution.py:471
  56.7 2.3 %collective-permute-done.6.got_sib = f32[32,48,128]{2,1,0:T(8,128)S(1)} collective-permute-done((f32[32,48,128]{2,1,0:T(8,128)S(1)}, f32[32,48,128]{2,1,0:T(8,128)S(1)}, u32[]{:S(2)}, u32[]{:S(2)}) %collective-permute-start.6) | collective-permute-done | bytes 786464 | tf_op jit(solution)/shard_map/ppermute | solution.py:463
  59.0 7.7 %forward.1 = (f32[2,4,384,768]{3,2,1,0:T(8,128)}, bf16[2,768,512]{2,1,0:T(8,128)(2,1)}, f32[2,1536]{1,0:T(2,128)S(1)}) custom-call(bf16[1152,768]{1,0:T(8,128)(2,1)} %prepare.1.ready, bf16[384,768]{1,0:T(8,128)(2,1)} %prepare_far.1.ready_far, f32[2,1536]{1,0:T(2,128)S(1)} %get-tuple-element.27.line_in, f32[32,48,128]{2,1,0:T(8,128)S(1)} %all-to-all-done.1.got, ...), custom_call_target="tpu_custom_call" | custom-call | flops 3623878656 | bytes 9437184 | tf_op jit(solution)/shard_map/forward/pallas_call | solution.py:272
  67.0 2.3 %collective-permute-start.8 = (f32[2,1536]{1,0:T(2,128)S(1)}, f32[2,1536]{1,0:T(2,128)S(1)}, u32[]{:S(2)}, u32[]{:S(2)}) collective-permute-start(f32[2,1536]{1,0:T(2,128)S(1)} %get-tuple-element.29.mine), channel_id=1, source_target_pairs={{0,6},{1,7},{2,0},{3,1},{4,2},{5,3},{6,4},{7,5},{8,14},{9,15},{10,... | collective-permute-start | bytes 36872 | tf_op jit(solution)/shard_map/ppermute | solution.py:460
  69.3 2.2 %collective-permute-start.7 = (f32[2,1536]{1,0:T(2,128)S(1)}, f32[2,1536]{1,0:T(2,128)S(1)}, u32[]{:S(2)}, u32[]{:S(2)}) collective-permute-start(f32[2,1536]{1,0:T(2,128)S(1)} %get-tuple-element.29.mine), channel_id=1, source_target_pairs={{0,2},{1,3},{2,4},{3,5},{4,6},{5,7},{6,0},{7,1},{8,10},{9,11},{10,... | collective-permute-start | bytes 36872 | tf_op jit(solution)/shard_map/ppermute | solution.py:460
  71.5 2.9 %collective-permute-done.9.at_far = f32[2,1536]{1,0:T(2,128)S(1)} collective-permute-done((f32[2,1536]{1,0:T(2,128)S(1)}, f32[2,1536]{1,0:T(2,128)S(1)}, u32[]{:S(2)}, u32[]{:S(2)}) %collective-permute-start.9) | collective-permute-done | bytes 12320 | tf_op jit(solution)/shard_map/ppermute | solution.py:460
  77.0 5.0 %all-to-all-start.2 = ((f32[32,1,768]{2,1,0:T(1,128)}), f32[32,1,768]{2,1,0:T(1,128)S(1)}, u32[]{:S(2)}, u32[]{:S(2)}) async-start(f32[32,1,768]{2,1,0:T(1,128)} %get-tuple-element.33), calls=%async_computation.2 | async-start | bytes 196608 | tf_op jit(solution)/shard_map/all_to_all | solution.py:487
  82.2 7.2 %all-to-all-done.2.everyone_ref = f32[32,1,768]{2,1,0:T(1,128)S(1)} async-done(((f32[32,1,768]{2,1,0:T(1,128)}), f32[32,1,768]{2,1,0:T(1,128)S(1)}, u32[]{:S(2)}, u32[]{:S(2)}) %all-to-all-start.2) | async-done | bytes 98336 | tf_op jit(solution)/shard_map/all_to_all | solution.py:487
  89.4 4.7 %backward_3_0.1 = (f32[192,256]{1,0:T(8,128)S(1)}, f32[192,256]{1,0:T(8,128)S(1)}) custom-call(s32[2]{0:T(128)S(1)} %dynamic-slice_reduce_fusion.partner_ref, f32[1,1536]{1,0:T(1,128)S(1)} %get-tuple-element.30.row_ref, f32[1,768]{1,0:T(1,128)S(1)} %get-tuple-element.32.own_ref, f32[32,1,768]{2,1,0:T(1,128)S(1)} %all-to-all-done.2.everyone_ref, ...), custom_call_target="tpu_custom_call" | custom-call | flops 1358954496 | bytes 3538944 | tf_op jit(solution)/shard_map/backward_3_0/pallas_call | solution.py:395
  94.1 2.4 %collective-permute-start.11 = (f32[192,256]{1,0:T(8,128)S(1)}, f32[192,256]{1,0:T(8,128)S(1)}, u32[]{:S(2)}, u32[]{:S(2)}) collective-permute-start(f32[192,256]{1,0:T(8,128)S(1)} %get-tuple-element.39), channel_id=1, source_target_pairs={{0,2},{1,3},{2,4},{3,5},{4,6},{5,7},{6,0},{7,1},{8,10},{9,11},{10,... | collective-permute-start | bytes 589832 | tf_op jit(solution)/shard_map/ppermute | solution.py:460
  96.6 1.8 %collective-permute-start.12 = (f32[192,256]{1,0:T(8,128)S(1)}, f32[192,256]{1,0:T(8,128)S(1)}, u32[]{:S(2)}, u32[]{:S(2)}) collective-permute-start(f32[192,256]{1,0:T(8,128)S(1)} %get-tuple-element.41), channel_id=1, source_target_pairs={{0,6},{1,7},{2,0},{3,1},{4,2},{5,3},{6,4},{7,5},{8,14},{9,15},{10,... | collective-permute-start | bytes 589832 | tf_op jit(solution)/shard_map/ppermute | solution.py:460
  98.4 4.9 %backward_0_0.1 = (f32[192,256]{1,0:T(8,128)S(1)}, f32[192,256]{1,0:T(8,128)S(1)}) custom-call(s32[2]{0:T(128)S(1)} %dynamic-slice_reduce_fusion.partner_ref, f32[1,1536]{1,0:T(1,128)S(1)} %get-tuple-element.30.row_ref, f32[1,768]{1,0:T(1,128)S(1)} %get-tuple-element.32.own_ref, f32[32,1,768]{2,1,0:T(1,128)S(1)} %all-to-all-done.2.everyone_ref, ...), custom_call_target="tpu_custom_call" | custom-call | flops 1358954496 | bytes 3538944 | tf_op jit(solution)/shard_map/backward_0_0/pallas_call | solution.py:395
  103.3 2.6 %collective-permute-start.14 = (f32[192,256]{1,0:T(8,128)S(1)}, f32[192,256]{1,0:T(8,128)S(1)}, u32[]{:S(2)}, u32[]{:S(2)}) collective-permute-start(f32[192,256]{1,0:T(8,128)S(1)} %get-tuple-element.43), channel_id=1, source_target_pairs={{0,6},{1,7},{2,0},{3,1},{4,2},{5,3},{6,4},{7,5},{8,14},{9,15},{10,... | collective-permute-start | bytes 589832 | tf_op jit(solution)/shard_map/ppermute | solution.py:460
  106.3 4.9 %backward_0_192.1 = (f32[192,256]{1,0:T(8,128)S(1)}, f32[192,256]{1,0:T(8,128)S(1)}) custom-call(s32[2]{0:T(128)S(1)} %dynamic-slice_reduce_fusion.partner_ref, f32[1,1536]{1,0:T(1,128)S(1)} %get-tuple-element.30.row_ref, f32[1,768]{1,0:T(1,128)S(1)} %get-tuple-element.32.own_ref, f32[32,1,768]{2,1,0:T(1,128)S(1)} %all-to-all-done.2.everyone_ref, ...), custom_call_target="tpu_custom_call" | custom-call | flops 1358954496 | bytes 3538944 | tf_op jit(solution)/shard_map/backward_0_192/pallas_call | solution.py:395
  111.3 3.6 %collective-permute-start.13 = (f32[192,256]{1,0:T(8,128)S(1)}, f32[192,256]{1,0:T(8,128)S(1)}, u32[]{:S(2)}, u32[]{:S(2)}) collective-permute-start(f32[192,256]{1,0:T(8,128)S(1)} %get-tuple-element.42), channel_id=1, source_target_pairs={{0,2},{1,3},{2,4},{3,5},{4,6},{5,7},{6,0},{7,1},{8,10},{9,11},{10,... | collective-permute-start | bytes 589832 | tf_op jit(solution)/shard_map/ppermute | solution.py:460
  115.5 4.7 %backward_2_0.1.run_ref = f32[384,256]{1,0:T(8,128)S(1)} custom-call(s32[2]{0:T(128)S(1)} %dynamic-slice_reduce_fusion.partner_ref, f32[1,1536]{1,0:T(1,128)S(1)} %get-tuple-element.30.row_ref, f32[1,768]{1,0:T(1,128)S(1)} %get-tuple-element.32.own_ref, f32[32,1,768]{2,1,0:T(1,128)S(1)} %all-to-all-done.2.everyone_ref, ...), custom_call_target="tpu_custom_call" | custom-call | flops 1358954496 | bytes 3538944 | tf_op jit(solution)/shard_map/backward_2_0/pallas_call | solution.py:395
  120.5 5.5 %collective-permute-done.13.low0 = f32[192,256]{1,0:T(8,128)S(1)} collective-permute-done((f32[192,256]{1,0:T(8,128)S(1)}, f32[192,256]{1,0:T(8,128)S(1)}, u32[]{:S(2)}, u32[]{:S(2)}) %collective-permute-start.13) | collective-permute-done | bytes 196640 | tf_op jit(solution)/shard_map/ppermute | solution.py:460
  (44 shorter events, 13.9 us)
Async XLA Ops:
  0.6 23.5 %collective-permute-start.1 = (f32[384,256]{1,0:T(8,128)}, f32[384,256]{1,0:T(8,128)S(1)}, u32[]{:S(2)}, u32[]{:S(2)}) collective-permute-start(f32[384,256]{1,0:T(8,128)} %emb_ref.3), channel_id=1, source_target_pairs={{0,6},{1,7},{2,0},{3,1},{4,2},{5,3},{6,4},{7,5},{8,14},{9,15},{10,... | collective-permute-start | bytes 1179656 | tf_op jit(solution)/shard_map/ppermute | solution.py:460
  7.0 21.8 %collective-permute-start = (f32[384,256]{1,0:T(8,128)}, f32[384,256]{1,0:T(8,128)S(1)}, u32[]{:S(2)}, u32[]{:S(2)}) collective-permute-start(f32[384,256]{1,0:T(8,128)} %emb_ref.3), channel_id=1, source_target_pairs={{0,2},{1,3},{2,4},{3,5},{4,6},{5,7},{6,0},{7,1},{8,10},{9,11},{10,... | collective-permute-start | bytes 1179656 | tf_op jit(solution)/shard_map/ppermute | solution.py:460
  7.0 37.4 %collective-permute-start.4 = (f32[384,256]{1,0:T(8,128)}, f32[384,256]{1,0:T(8,128)S(1)}, u32[]{:S(2)}, u32[]{:S(2)}) collective-permute-start(f32[384,256]{1,0:T(8,128)} %emb_ref.3), channel_id=1, source_target_pairs={{0,1},{1,0},{2,3},{3,2},{4,5},{5,4},{6,7},{7,6},{8,9},{9,8},{10,11... | collective-permute-start | bytes 1179656 | tf_op jit(solution)/shard_map/ppermute | solution.py:463
  7.0 11.0 %collective-permute-start.5 = (s32[384]{0:T(512)}, s32[384]{0:T(512)S(1)}, u32[]{:S(2)}, u32[]{:S(2)}) collective-permute-start(s32[384]{0:T(512)} %param.4), channel_id=1, source_target_pairs={{0,1},{1,0},{2,3},{3,2},{4,5},{5,4},{6,7},{7,6},{8,9},{9,8},{10,11... | collective-permute-start | bytes 4616 | tf_op jit(solution)/shard_map/ppermute | solution.py:463
  7.5 1.0 copy-start
  9.3 27.6 %all-to-all-start = ((f32[32,24,128]{2,1,0:T(8,128)}), f32[32,24,128]{2,1,0:T(8,128)S(1)}, u32[]{:S(2)}, u32[]{:S(2)}) async-start(f32[32,24,128]{2,1,0:T(8,128)} %bitcast), calls=%async_computation | async-start | bytes 786432 | tf_op jit(solution)/shard_map/all_to_all | solution.py:468
  24.2 19.1 %collective-permute-start.3 = (f32[192,256]{1,0:T(8,128)S(1)}, f32[192,256]{1,0:T(8,128)S(1)}, u32[]{:S(2)}, u32[]{:S(2)}) collective-permute-start(f32[192,256]{1,0:T(8,128)S(1)} %slice.9), channel_id=1, source_target_pairs={{0,6},{1,7},{2,0},{3,1},{4,2},{5,3},{6,4},{7,5},{8,14},{9,15},{10,... | collective-permute-start | bytes 589832 | tf_op jit(solution)/shard_map/ppermute | solution.py:460
  28.8 14.5 %collective-permute-start.2 = (f32[192,256]{1,0:T(8,128)S(1)}, f32[192,256]{1,0:T(8,128)S(1)}, u32[]{:S(2)}, u32[]{:S(2)}) collective-permute-start(f32[192,256]{1,0:T(8,128)S(1)} %slice.8), channel_id=1, source_target_pairs={{0,2},{1,3},{2,4},{3,5},{4,6},{5,7},{6,0},{7,1},{8,10},{9,11},{10,... | collective-permute-start | bytes 589832 | tf_op jit(solution)/shard_map/ppermute | solution.py:460
  28.9 1.0 copy-start.1
  29.9 6.9 %copy-start.3 = (s32[2,32]{1,0:T(2,128)S(1)}, s32[2,32]{1,0:T(2,128)}, u32[]{:S(2)}) copy-start(s32[2,32]{1,0:T(2,128)} %pairing_ref.1) | copy-start | bytes 772
  38.4 18.3 %all-to-all-start.1 = ((f32[32,48,128]{2,1,0:T(8,128)}), f32[32,48,128]{2,1,0:T(8,128)S(1)}, u32[]{:S(2)}, u32[]{:S(2)}) async-start(f32[32,48,128]{2,1,0:T(8,128)} %pick.1), calls=%async_computation.1 | async-start | bytes 1572864 | tf_op jit(solution)/shard_map/all_to_all | solution.py:471
  43.3 1.1 copy-start.2
  56.7 2.3 %collective-permute-start.6 = (f32[32,48,128]{2,1,0:T(8,128)S(1)}, f32[32,48,128]{2,1,0:T(8,128)S(1)}, u32[]{:S(2)}, u32[]{:S(2)}) collective-permute-start(f32[32,48,128]{2,1,0:T(8,128)S(1)} %all-to-all-done.1.got), channel_id=1, source_target_pairs={{0,1},{1,0},{2,3},{3,2},{4,5},{5,4},{6,7},{7,6},{8,9},{9,8},{10,11... | collective-permute-start | bytes 2359304 | tf_op jit(solution)/shard_map/ppermute | solution.py:463
  66.8 7.7 %collective-permute-start.9 = (f32[2,1536]{1,0:T(2,128)S(1)}, f32[2,1536]{1,0:T(2,128)S(1)}, u32[]{:S(2)}, u32[]{:S(2)}) collective-permute-start(f32[2,1536]{1,0:T(2,128)S(1)} %get-tuple-element.29.mine), channel_id=1, source_target_pairs={{0,4},{1,5},{2,6},{3,7},{4,0},{5,1},{6,2},{7,3},{8,12},{9,13},{10,... | collective-permute-start | bytes 36872 | tf_op jit(solution)/shard_map/ppermute | solution.py:460
  67.0 7.5 %collective-permute-start.8 = (f32[2,1536]{1,0:T(2,128)S(1)}, f32[2,1536]{1,0:T(2,128)S(1)}, u32[]{:S(2)}, u32[]{:S(2)}) collective-permute-start(f32[2,1536]{1,0:T(2,128)S(1)} %get-tuple-element.29.mine), channel_id=1, source_target_pairs={{0,6},{1,7},{2,0},{3,1},{4,2},{5,3},{6,4},{7,5},{8,14},{9,15},{10,... | collective-permute-start | bytes 36872 | tf_op jit(solution)/shard_map/ppermute | solution.py:460
  69.3 5.8 %collective-permute-start.7 = (f32[2,1536]{1,0:T(2,128)S(1)}, f32[2,1536]{1,0:T(2,128)S(1)}, u32[]{:S(2)}, u32[]{:S(2)}) collective-permute-start(f32[2,1536]{1,0:T(2,128)S(1)} %get-tuple-element.29.mine), channel_id=1, source_target_pairs={{0,2},{1,3},{2,4},{3,5},{4,6},{5,7},{6,0},{7,1},{8,10},{9,11},{10,... | collective-permute-start | bytes 36872 | tf_op jit(solution)/shard_map/ppermute | solution.py:460
  75.1 1.2 collective-permute-start.10
  77.0 12.4 %all-to-all-start.2 = ((f32[32,1,768]{2,1,0:T(1,128)}), f32[32,1,768]{2,1,0:T(1,128)S(1)}, u32[]{:S(2)}, u32[]{:S(2)}) async-start(f32[32,1,768]{2,1,0:T(1,128)} %get-tuple-element.33), calls=%async_computation.2 | async-start | bytes 196608 | tf_op jit(solution)/shard_map/all_to_all | solution.py:487
  94.1 17.1 %collective-permute-start.11 = (f32[192,256]{1,0:T(8,128)S(1)}, f32[192,256]{1,0:T(8,128)S(1)}, u32[]{:S(2)}, u32[]{:S(2)}) collective-permute-start(f32[192,256]{1,0:T(8,128)S(1)} %get-tuple-element.39), channel_id=1, source_target_pairs={{0,2},{1,3},{2,4},{3,5},{4,6},{5,7},{6,0},{7,1},{8,10},{9,11},{10,... | collective-permute-start | bytes 589832 | tf_op jit(solution)/shard_map/ppermute | solution.py:460
  96.6 14.7 %collective-permute-start.12 = (f32[192,256]{1,0:T(8,128)S(1)}, f32[192,256]{1,0:T(8,128)S(1)}, u32[]{:S(2)}, u32[]{:S(2)}) collective-permute-start(f32[192,256]{1,0:T(8,128)S(1)} %get-tuple-element.41), channel_id=1, source_target_pairs={{0,6},{1,7},{2,0},{3,1},{4,2},{5,3},{6,4},{7,5},{8,14},{9,15},{10,... | collective-permute-start | bytes 589832 | tf_op jit(solution)/shard_map/ppermute | solution.py:460
  103.3 16.9 %collective-permute-start.14 = (f32[192,256]{1,0:T(8,128)S(1)}, f32[192,256]{1,0:T(8,128)S(1)}, u32[]{:S(2)}, u32[]{:S(2)}) collective-permute-start(f32[192,256]{1,0:T(8,128)S(1)} %get-tuple-element.43), channel_id=1, source_target_pairs={{0,6},{1,7},{2,0},{3,1},{4,2},{5,3},{6,4},{7,5},{8,14},{9,15},{10,... | collective-permute-start | bytes 589832 | tf_op jit(solution)/shard_map/ppermute | solution.py:460
  105.9 14.7 %collective-permute-start.15 = (f32[192,256]{1,0:T(8,128)S(1)}, f32[192,256]{1,0:T(8,128)S(1)}, u32[]{:S(2)}, u32[]{:S(2)}) collective-permute-start(f32[192,256]{1,0:T(8,128)S(1)} %get-tuple-element.44), channel_id=1, source_target_pairs={{0,2},{1,3},{2,4},{3,5},{4,6},{5,7},{6,0},{7,1},{8,10},{9,11},{10,... | collective-permute-start | bytes 589832 | tf_op jit(solution)/shard_map/ppermute | solution.py:460
  111.3 14.7 %collective-permute-start.13 = (f32[192,256]{1,0:T(8,128)S(1)}, f32[192,256]{1,0:T(8,128)S(1)}, u32[]{:S(2)}, u32[]{:S(2)}) collective-permute-start(f32[192,256]{1,0:T(8,128)S(1)} %get-tuple-element.42), channel_id=1, source_target_pairs={{0,2},{1,3},{2,4},{3,5},{4,6},{5,7},{6,0},{7,1},{8,10},{9,11},{10,... | collective-permute-start | bytes 589832 | tf_op jit(solution)/shard_map/ppermute | solution.py:460
  114.9 11.2 %collective-permute-start.16 = (f32[192,256]{1,0:T(8,128)S(1)}, f32[192,256]{1,0:T(8,128)S(1)}, u32[]{:S(2)}, u32[]{:S(2)}) collective-permute-start(f32[192,256]{1,0:T(8,128)S(1)} %get-tuple-element.45), channel_id=1, source_target_pairs={{0,6},{1,7},{2,0},{3,1},{4,2},{5,3},{6,4},{7,5},{8,14},{9,15},{10,... | collective-permute-start | bytes 589832 | tf_op jit(solution)/shard_map/ppermute | solution.py:460

commit v6 on v5

--- a/solution.py
+++ b/solution.py
@@ -12,8 +12,11 @@
 SLICE = 384
 WIDTH = 256
 SELF = 2
+PIECE = 256
+STEPS = ((0, 2), (2, 3), (5, 3), (8, 1))
 VMEM = 16 * 1024 * 1024
 VMEM_LARGE = 44 * 1024 * 1024
+VMEM_BACKWARD = 28 * 1024 * 1024
 HBM = pl.BlockSpec(memory_space=pltpu.HBM)
 SMEM = pl.BlockSpec(memory_space=pltpu.SMEM)
 
@@ -89,14 +92,18 @@
 
 
 def unit_parts(values):
-    unit = values * (1.0 / radius_of(values))
-    hi, lo = split(unit)
-    hi_t, lo_t = split(unit.T)
-    return jnp.concatenate([hi, lo], axis=1), jnp.concatenate([hi_t, hi_t, lo_t], axis=0)
-
-
-def product(left, right):
-    return jnp.dot(left, right, preferred_element_type=jnp.float32)
+    hi, lo = split(values * (1.0 / radius_of(values)))
+    return jnp.concatenate([hi, lo], axis=1)
+
+
+def product(left, cols):
+    hi, lo = cols[:, :WIDTH], cols[:, WIDTH:]
+    return lax.dot_general(
+        left,
+        jnp.concatenate([hi, hi, lo], axis=1),
+        (((1,), (1,)), ((), ())),
+        preferred_element_type=jnp.float32,
+    )
 
 
 def exponentials(scores, first_row, pos_ref, store):
@@ -122,8 +129,17 @@
     return jnp.sum(total.T, axis=0, keepdims=True)
 
 
+def put_columns(c_buf, at, parts):
+    done = 0
+    while done < parts.shape[0]:
+        inside = (at + done) % PIECE
+        size = min(PIECE - inside, parts.shape[0] - done)
+        c_buf[(at + done) // PIECE, inside : inside + size] = parts[done : done + size]
+        done += size
+
+
 def own_kernel(
-    ready, ready_far, mine, sib, pos_ref, c_out, e_out, line_ref, left_ref, c_buf, right_ref, e_buf, in_sem, c_sem, e_sem
+    ready, ready_far, mine, sib, pos_ref, c_out, e_out, line_ref, left_ref, c_buf, e_buf, in_sem, c_sem, e_sem
 ):
     at = ready.shape[0]
     ready_copies = [
@@ -133,28 +149,28 @@
     for copy in ready_copies:
         copy.start()
     for which, ref in enumerate((mine, sib)):
-        here = slice(which * SLICE, which * SLICE + SLICE)
-        c_buf[here], right_ref[:, here] = unit_parts(ref[...])
+        put_columns(c_buf, which * SLICE, unit_parts(ref[...]))
+    cols = c_buf[...].reshape(2 * SLICE, 2 * WIDTH)
     copies = [pltpu.make_async_copy(c_buf, c_out, c_sem)]
     copies[0].start()
     for copy in ready_copies:
         copy.wait()
 
-    coming = product(left_ref[:SLICE], right_ref[...])
+    coming = product(left_ref[:SLICE], cols)
     totals, matches = [], []
     for order in range(4):
         scores = coming
         if order < 3:
             at = (order + 1) * SLICE
-            coming = product(left_ref[at : at + SLICE], right_ref[...])
+            coming = product(left_ref[at : at + SLICE], cols)
 
         def store(k, e):
-            e_buf[order, :, k : k + 128] = e
+            e_buf[k // PIECE, order, :, k % PIECE : k % PIECE + 128] = e
 
         total, match = exponentials(scores, order * SLICE, pos_ref, store)
         totals.append(as_line(total))
         matches.append(as_line(match))
-        copies.append(pltpu.make_async_copy(e_buf.at[order], e_out.at[order], e_sem.at[order]))
+        copies.append(pltpu.make_async_copy(e_buf.at[:, order], e_out.at[:, order], e_sem.at[order]))
         copies[-1].start()
     line_ref[0:1] = jnp.concatenate(totals, axis=1)
     line_ref[1:2] = jnp.concatenate(matches, axis=1)
@@ -164,7 +180,7 @@
 
 def own_scores(ready, ready_far, mine, sib, pos):
     rows, wide = 4 * SLICE, 2 * SLICE
-    shapes = [((wide, 2 * WIDTH), jnp.bfloat16), ((4, SLICE, wide), jnp.float32)]
+    shapes = [((3, PIECE, 2 * WIDTH), jnp.bfloat16), ((3, 4, SLICE, PIECE), jnp.float32)]
     return pl.pallas_call(
         own_kernel,
         in_specs=[HBM] * 2 + [pl.BlockSpec()] * 3,
@@ -173,7 +189,6 @@
         scratch_shapes=[
             pltpu.VMEM((rows, 3 * WIDTH), jnp.bfloat16),
             pltpu.VMEM(*shapes[0]),
-            pltpu.VMEM((3 * WIDTH, wide), jnp.bfloat16),
             pltpu.VMEM(*shapes[1]),
             pltpu.SemaphoreType.DMA((2,)),
             pltpu.SemaphoreType.DMA,
@@ -211,9 +226,11 @@
 
 def forward_kernel(
     ready, ready_far, line_in, got, got_sib, e_out, c_out, line_ref,
-    left_ref, c_buf, right_ref, e_buf, tot_ref, in_sem, c_sem, e_sem,
+    left_ref, c_buf, e_buf, tot_ref, in_sem, c_sem, e_sem,
 ):
-    chunks, orders, _, wide = e_buf.shape
+    orders, wide = e_buf.shape[1], 2 * SLICE
+    many = wide // PIECE
+    chunks = e_buf.shape[0] // many
     at = ready.shape[0]
     ready_copies = [
         pltpu.make_async_copy(ready, left_ref.at[pl.ds(0, at)], in_sem.at[0]),
@@ -228,13 +245,14 @@
     def columns(chunk):
         for which, ref in enumerate((got, got_sib)):
             piece = rows_of(ref[:, chunk * half : chunk * half + half].reshape(tiles, 8, 128))
-            here = slice(which * SLICE, which * SLICE + SLICE)
-            c_buf[chunk, here], right_ref[chunk, :, here] = unit_parts(piece)
-        copies.append(pltpu.make_async_copy(c_buf.at[chunk], c_out.at[chunk], c_sem.at[chunk]))
+            put_columns(c_buf, chunk * wide + which * SLICE, unit_parts(piece))
+        view = (pl.ds(chunk * many, many),)
+        copies.append(pltpu.make_async_copy(c_buf.at[view], c_out.at[view], c_sem.at[chunk]))
         copies[-1].start()
 
     def scores_of(chunk, band):
-        return product(left_ref[band * wide : band * wide + wide], right_ref[chunk])
+        cols = c_buf[chunk * many : chunk * many + many].reshape(wide, 2 * WIDTH)
+        return product(left_ref[band * wide : band * wide + wide], cols)
 
     columns(0)
     for copy in ready_copies:
@@ -249,35 +267,42 @@
             coming = scores_of(*items[turn + 1])
 
         def store(k, e):
-            e_buf[chunk, 2 * band : 2 * band + 2, :, k : k + 128] = e.reshape(2, SLICE, 128)
+            lane = k % PIECE
+            e = e.reshape(2, SLICE, 128)
+            e_buf[chunk * many + k // PIECE, 2 * band : 2 * band + 2, :, lane : lane + 128] = e
 
         total, _ = exponentials(scores, None, None, store)
         if chunk == 0:
             tot_ref[band * wide : band * wide + wide] = total
         else:
             tot_ref[band * wide : band * wide + wide] += total
-        view = (chunk, pl.ds(2 * band, 2))
+        view = (pl.ds(chunk * many, many), pl.ds(2 * band, 2))
         copies.append(pltpu.make_async_copy(e_buf.at[view], e_out.at[view], e_sem.at[turn]))
         copies[-1].start()
 
-    line_ref[0:1] = as_line(tot_ref[...]) + line_in[0:1]
-    line_ref[1:2] = line_in[1:2]
+    total = as_line(tot_ref[...]) + line_in[0:1]
+    for member in range(line_ref.shape[0]):
+        line_ref[member, 0:1] = total
+        line_ref[member, 1:2] = line_in[1:2]
     for copy in copies:
         copy.wait()
 
 
-def forward(ready, ready_far, line, got, got_sib):
+def forward(ready, ready_far, line, got, got_sib, members):
     rows, wide = 4 * SLICE, 2 * SLICE
-    e_shape, c_shape = ((2, 4, SLICE, wide), jnp.float32), ((2, wide, 2 * WIDTH), jnp.bfloat16)
+    e_shape, c_shape = ((6, 4, SLICE, PIECE), jnp.float32), ((6, PIECE, 2 * WIDTH), jnp.bfloat16)
     return pl.pallas_call(
         forward_kernel,
         in_specs=[HBM] * 2 + [pl.BlockSpec()] * 3,
         out_specs=[HBM] * 2 + [pl.BlockSpec()],
-        out_shape=(pltpu.HBM(*e_shape), pltpu.HBM(*c_shape), jax.ShapeDtypeStruct((2, rows), jnp.float32)),
+        out_shape=(
+            pltpu.HBM(*e_shape),
+            pltpu.HBM(*c_shape),
+            jax.ShapeDtypeStruct((members, 2, rows), jnp.float32),
+        ),
         scratch_shapes=[
             pltpu.VMEM((rows, 3 * WIDTH), jnp.bfloat16),
             pltpu.VMEM(*c_shape),
-            pltpu.VMEM((2, 3 * WIDTH, wide), jnp.bfloat16),
             pltpu.VMEM(*e_shape),
             pltpu.VMEM((rows, 128), jnp.float32),
             pltpu.SemaphoreType.DMA((2,)),
@@ -292,96 +317,111 @@
     )(in_hbm(ready), in_hbm(ready_far), line, got, got_sib)
 
 
-def denominator_kernel(mine, at_left, at_right, at_far, row_ref, line_ref):
-    def part(ref, order):
-        return ref[:, order * SLICE : order * SLICE + SLICE]
-
-    for order, (a, b, c) in enumerate(((2, 3, 1), (3, 2, 0), (1, 0, 3), (0, 1, 2))):
-        value = (part(mine, order) + part(at_left, a)) + (part(at_right, b) + part(at_far, c))
-        row_ref[:, order * SLICE : order * SLICE + SLICE] = value[0:1]
-        if order == SELF:
-            line_ref[...] = value
-
-
-def denominators(*lines):
+def denominator_kernel(member_ref, all_ref, row_ref, own_ref, line_ref, spread_ref):
+    member = member_ref[0]
+    members = all_ref.shape[0]
+
+    def summed(owner, kind):
+        value = 0.0
+        for by, order in ((0, SELF), (2, 0), (members - 2, 1), (4, 3)):
+            held = all_ref[lax.rem(owner + by, members)]
+            value = value + held[kind : kind + 1, order * SLICE : order * SLICE + SLICE]
+        return value
+
+    mate = member + 1 - 2 * lax.rem(member, 2)
+    own = summed(member, 0)
+    line_ref[0:1] = own
+    line_ref[1:2] = summed(member, 1)
+    both = jnp.concatenate([own, summed(mate, 0)], axis=1)
+    own_ref[...] = both
+    spread_ref[...] = jnp.broadcast_to(both.reshape(1, 1, 2 * SLICE), spread_ref.shape)
+    for order, by in enumerate((members - 2, 2, 0, 4)):
+        value = own if by == 0 else summed(lax.rem(member + by, members), 0)
+        row_ref[:, order * SLICE : order * SLICE + SLICE] = value
+
+
+def denominators(member, everything, groups):
     return pl.pallas_call(
         denominator_kernel,
+        in_specs=[SMEM, pl.BlockSpec()],
         out_shape=(
             jax.ShapeDtypeStruct((1, 4 * SLICE), jnp.float32),
+            jax.ShapeDtypeStruct((1, 2 * SLICE), jnp.float32),
             jax.ShapeDtypeStruct((2, SLICE), jnp.float32),
+            jax.ShapeDtypeStruct((groups, 1, 2 * SLICE), jnp.float32),
         ),
         compiler_params=params(),
         name="denominators",
-    )(*lines)
-
-
-def spread_kernel(line_ref, sib_ref, own_ref, spread_ref):
-    both = jnp.concatenate([line_ref[0:1], sib_ref[0:1]], axis=1)
-    own_ref[...] = both
-    spread_ref[...] = jnp.broadcast_to(both.reshape(1, 1, 2 * SLICE), spread_ref.shape)
-
-
-def spread(line, sib, groups):
-    return pl.pallas_call(
-        spread_kernel,
-        out_shape=(
-            jax.ShapeDtypeStruct((1, 2 * SLICE), jnp.float32),
-            jax.ShapeDtypeStruct((groups, 1, 2 * SLICE), jnp.float32),
-        ),
-        compiler_params=params(),
-        name="spread",
-    )(line, sib)
+    )(member, everything)
 
 
 def backward_kernel(
-    bands, partner_ref, row_ref, own_ref, everyone_ref, pos_ref, e0_in, e1_in, c0_in, c1_in, *refs
+    bands, first, partner_ref, row_ref, own_ref, everyone_ref, pos_ref, e0_in, e1_in, *refs
 ):
-    out_refs, (run_ref, e_buf, c_buf, e_sem, c_sem) = refs[:-5], refs[-5:]
-    wide = 2 * SLICE
-    steps = e_buf.shape[0]
+    if first:
+        c0_in, c1_in, c_ref, refs = refs[0], refs[1], refs[2], refs[3:]
+    else:
+        c_ref, refs = refs[0], refs[1:]
+    out_refs, (run_ref, e_buf, e_sem, c_sem) = refs[:-4], refs[-4:]
+    own_pieces = e0_in.shape[0]
     copies = []
-    for k in range(steps):
+    for step, (start, many) in enumerate(STEPS):
         group = []
-        at = 0
-        for which, (order, begin, size) in enumerate(bands):
-            rows = pl.ds(begin, size)
-            if k == 0:
-                src = e0_in.at[order, rows]
-            else:
-                src = e1_in.at[k - 1, order, rows]
-            group.append(pltpu.make_async_copy(src, e_buf.at[k, pl.ds(at, size)], e_sem.at[k, which]))
-            at += size
-        src = c0_in if k == 0 else c1_in.at[k - 1]
-        group.append(pltpu.make_async_copy(src, c_buf.at[k], c_sem.at[k]))
+        for k, (source, low, high) in enumerate(
+            ((0, 0, own_pieces), (1, own_pieces, own_pieces + e1_in.shape[0]))
+        ):
+            begin, end = max(start, low), min(start + many, high)
+            if begin >= end:
+                continue
+            here, there = pl.ds(begin, end - begin), pl.ds(begin - low, end - begin)
+            at = 0
+            for which, (order, row, size) in enumerate(bands):
+                group.append(
+                    pltpu.make_async_copy(
+                        (e0_in, e1_in)[source].at[there, order, pl.ds(row, size)],
+                        e_buf.at[here, pl.ds(at, size)],
+                        e_sem.at[step, k, which],
+                    )
+                )
+                at += size
+            if first:
+                src = (c0_in, c1_in)[source].at[there]
+                group.append(pltpu.make_async_copy(src, c_ref.at[here], c_sem.at[step, k]))
         copies.append(group)
         for copy in group:
             copy.start()
 
     columns, places = [], []
-    for order, begin, size in bands:
+    for order, row, size in bands:
         column = as_column(row_ref[:, order * SLICE : order * SLICE + SLICE])
-        columns.append(column[begin : begin + size])
-        places.append(lax.broadcasted_iota(jnp.int32, (size, 128), 0) + (order * SLICE + begin))
+        columns.append(column[row : row + size])
+        places.append(lax.broadcasted_iota(jnp.int32, (size, 128), 0) + (order * SLICE + row))
     row_inv = 1.0 / jnp.concatenate(columns, axis=0)
     row_ids = jnp.concatenate(places, axis=0)
-    for k in range(steps):
-        col_inv = 1.0 / (own_ref[...] if k == 0 else everyone_ref[partner_ref[k - 1]])
-        for copy in copies[k]:
+    wide = 2 * SLICE
+    col_inv = [1.0 / own_ref[...]] + [1.0 / everyone_ref[partner_ref[k]] for k in range(2)]
+    for step, (start, many) in enumerate(STEPS):
+        for copy in copies[step]:
             copy.wait()
         his, los = [], []
-        for at in range(0, wide, 128):
-            weight = e_buf[k, :, at : at + 128] * (row_inv + col_inv[:, at : at + 128])
-            if k == 0:
+        for at in range(start * PIECE, (start + many) * PIECE, 128):
+            inv = col_inv[at // wide][:, at % wide : at % wide + 128]
+            weight = e_buf[at // PIECE, :, at % PIECE : at % PIECE + 128] * (row_inv + inv)
+            if at < wide:
                 weight = weight - jnp.where(row_ids == pos_ref[:, at : at + 128], 2.0, 0.0)
             hi, lo = split(weight)
             his.append(hi)
             los.append(lo)
-        both = product(jnp.concatenate(his, axis=1), c_buf[k])
-        part = both[:, :WIDTH] + both[:, WIDTH:]
-        part = part + product(jnp.concatenate(los, axis=1), c_buf[k, :, :WIDTH])
-        if k == 0:
+        cols = c_ref[start : start + many].reshape(many * PIECE, 2 * WIDTH)
+        c_hi, c_lo = cols[:, :WIDTH], cols[:, WIDTH:]
+        part = jnp.dot(
+            jnp.concatenate(his + his + los, axis=1),
+            jnp.concatenate([c_hi, c_lo, c_hi], axis=0),
+            preferred_element_type=jnp.float32,
+        )
+        if step == 0:
             run_ref[...] = part
-        elif k + 1 < steps:
+        elif step + 1 < len(STEPS):
             run_ref[...] += part
         else:
             part = run_ref[...] + part
@@ -390,25 +430,26 @@
                 ref[...] = part[which * size : which * size + size]
 
 
-def backward(bands, pieces, e0, partners, row_den, own_den, everyone, pos, e1, c0, c1):
-    count = 6 * SLICE
-    return pl.pallas_call(
-        functools.partial(backward_kernel, bands),
-        in_specs=[SMEM] + [pl.BlockSpec()] * 4 + [HBM] * 4,
-        out_shape=[jax.ShapeDtypeStruct((SLICE // pieces, WIDTH), jnp.float32)] * pieces,
+def backward(bands, pieces, partners, row_den, own_den, everyone, pos, e0, e1, *cols):
+    first = len(cols) == 2
+    count = 9 * PIECE
+    col_shape = [jax.ShapeDtypeStruct((9, PIECE, 2 * WIDTH), jnp.bfloat16)]
+    return pl.pallas_call(
+        functools.partial(backward_kernel, bands, first),
+        in_specs=[SMEM] + [pl.BlockSpec()] * 4 + [HBM] * 2 + ([HBM] * 2 if first else [pl.BlockSpec()]),
+        out_shape=col_shape * first + [jax.ShapeDtypeStruct((SLICE // pieces, WIDTH), jnp.float32)] * pieces,
         scratch_shapes=[
             pltpu.VMEM((SLICE, WIDTH), jnp.float32),
-            pltpu.VMEM((3, SLICE, 2 * SLICE), jnp.float32),
-            pltpu.VMEM((3, 2 * SLICE, 2 * WIDTH), jnp.bfloat16),
-            pltpu.SemaphoreType.DMA((3, len(bands))),
-            pltpu.SemaphoreType.DMA((3,)),
+            pltpu.VMEM((9, SLICE, PIECE), jnp.float32),
+            pltpu.SemaphoreType.DMA((len(STEPS), 2, len(bands))),
+            pltpu.SemaphoreType.DMA((len(STEPS), 2)),
         ],
         cost_estimate=pl.CostEstimate(
             flops=6 * SLICE * count * WIDTH, bytes_accessed=4 * SLICE * count, transcendentals=0
         ),
-        compiler_params=params(VMEM_LARGE),
+        compiler_params=params(VMEM_BACKWARD),
         name="backward_%d_%d" % bands[0][:2],
-    )(partners, row_den, own_den, everyone, pos, *map(in_hbm, (e0, e1, c0, c1)))
+    )(partners, row_den, own_den, everyone, pos, in_hbm(e0), in_hbm(e1), *(map(in_hbm, cols) if first else cols))
 
 
 def add_kernel(a_ref, b_ref, c_ref, d_ref, ab_ref, cd_ref):
@@ -480,14 +521,15 @@
     ready_far = prepare("prepare_far", *far)
     c_own, e_own, line = own_scores(ready, ready_far, embeddings, sib, pos)
     got, line = lax.optimization_barrier((got, line))
-    e_part, c_part, line = forward(ready, ready_far, line, got, swap(got))
-
-    row_den, line = denominators(line, shift(line, 2), shift(line, -2), shift(line, 4))
-    own_den, spread_den = spread(line, swap(line), groups)
-    everyone = lax.all_to_all(spread_den, "grp", 0, 0, tiled=True)
-
-    shared = (e_own, pairing[:, group], row_den, own_den, everyone, pos, e_part, c_own, c_part)
-    far_low, far_high = backward(((3, 0, rows),), 2, *shared)
+    e_part, c_part, line = forward(ready, ready_far, line, got, swap(got), members)
+
+    everything = lax.all_to_all(line, "mem", 0, 0, tiled=True)
+    row_den, own_den, line, spread = denominators(jnp.reshape(member, (1,)), everything, groups)
+    everyone = lax.all_to_all(spread, "grp", 0, 0, tiled=True)
+
+    shared = (pairing[:, group], row_den, own_den, everyone, pos, e_own, e_part)
+    cols, far_low, far_high = backward(((3, 0, rows),), 2, *shared, c_own, c_part)
+    shared += (cols,)
     far_low, far_high = shift(far_low, 2), shift(far_high, -2)
     left_low, right_high = backward(((0, 0, half), (1, half, half)), 2, *shared)
     high0, low1 = shift(right_high, 2), shift(left_low, -2)

time: 129 us -> 126 us (0.977)
  blocking collectives: 0 us -> 12.4 us
  waiting for transfers between devices: 37.9 us -> 29.8 us
  starting transfers between devices: 45.8 us -> 40.9 us
    all_to_all x0 -> x1, blocking collectives: none -> 12.4 us  [local(): everything = lax.all_to_all(line, 'mem', 0, 0, tiled=True)]
    ppermute x13 -> x10, waiting for transfers between devices: 15.5 us -> 8.35 us  [shift(): lax.ppermute(value, 'mem', [(m, (m + by) % members) for m in range(member...]
    ppermute x13 -> x10, starting transfers between devices: 27.3 us -> 22.5 us  [shift(): lax.ppermute(value, 'mem', [(m, (m + by) % members) for m in range(member...]
    ppermute x4 -> x3, waiting for transfers between devices: 3.44 us -> 2.29 us  [swap(): return lax.ppermute(value, 'mem', [(m, m ^ 1) for m in range(members)])]
    pallas_call x6 -> x5, Pallas kernels: 19.9 us -> 20.3 us  [the longest x4 19.6 us: backward(): pl.pallas_call(functools.partial(backward_kernel, bands, first), in_specs...]
  transfers between devices with their start and end apart: 20 -> 16, of which waited for: 10 -> 7; matrix products, arithmetic and copies ran while one was open for 1% -> 1% of each run, Pallas kernels for 20% -> 20%
where the time goes in v6:
time: 126 us; the launch traced here: 125 us
  starting transfers between devices  40.9 us (32%)
  Pallas kernels  39.2 us (31%)
  waiting for transfers between devices  29.8 us (24%)
  blocking collectives  12.4 us (10%)
  local copies, waits for them, and re-layouts  1.91 us (2%)
    ppermute x10, starting transfers between devices, shift(): lax.ppermute(value, 'mem', [(m, (m + by) % members) for m in range(member...  22.5 us
    pallas_call x4, Pallas kernels, backward(): pl.pallas_call(functools.partial(backward_kernel, bands, first), in_specs...  19.6 us
    all_to_all x1, blocking collectives, local(): everything = lax.all_to_all(line, 'mem', 0, 0, tiled=True)  12.4 us
    ppermute x10, waiting for transfers between devices, shift(): lax.ppermute(value, 'mem', [(m, (m + by) % members) for m in range(member...  8.35 us
    all_to_all x1, starting transfers between devices, local(): lax.all_to_all(as_tiles(embeddings).reshape(groups, per, 128), 'grp', 0,...  7.99 us
    pallas_call x1, Pallas kernels, forward(): pl.pallas_call(forward_kernel, in_specs=[HBM] * 2 + [pl.BlockSpec()] * 3,...  7.44 us
    all_to_all x1, waiting for transfers between devices, local(): everyone = lax.all_to_all(spread, 'grp', 0, 0, tiled=True)  7.25 us
    all_to_all x1, waiting for transfers between devices, local(): lax.all_to_all(as_tiles(embeddings).reshape(groups, per, 128), 'grp', 0,...  6.21 us
  transfers between devices with their start and end apart: 16, of which 7 were waited for; matrix products, arithmetic and copies ran while one was open for 1% of the time, Pallas kernels for 20%

profile of v6, /device:TPU:8, one launch (start us, length us, event | category | flops | bytes accessed | tf_op | source)
XLA Modules:
  0.0 125.1 jit_solution(11237651993622613745)
XLA Ops:
  0.6 6.4 %collective-permute-start.1 = (f32[384,256]{1,0:T(8,128)}, f32[384,256]{1,0:T(8,128)S(1)}, u32[]{:S(2)}, u32[]{:S(2)}) collective-permute-start(f32[384,256]{1,0:T(8,128)} %emb_ref.3), channel_id=1, source_target_pairs={{0,6},{1,7},{2,0},{3,1},{4,2},{5,3},{6,4},{7,5},{8,14},{9,15},{10,... | collective-permute-start | bytes 1179656 | tf_op jit(solution)/shard_map/ppermute | solution.py:501
  9.3 8.0 %all-to-all-start = ((f32[32,24,128]{2,1,0:T(8,128)}), f32[32,24,128]{2,1,0:T(8,128)S(1)}, u32[]{:S(2)}, u32[]{:S(2)}) async-start(f32[32,24,128]{2,1,0:T(8,128)} %bitcast.1), calls=%async_computation | async-start | bytes 786432 | tf_op jit(solution)/shard_map/all_to_all | solution.py:509
  18.1 6.1 %collective-permute-done.1.refs_1_ = f32[384,256]{1,0:T(8,128)S(1)} collective-permute-done((f32[384,256]{1,0:T(8,128)}, f32[384,256]{1,0:T(8,128)S(1)}, u32[]{:S(2)}, u32[]{:S(2)}) %collective-permute-start.1) | collective-permute-done | bytes 393248 | tf_op jit(solution)/shard_map/ppermute | solution.py:501
  24.2 4.6 %collective-permute-start.3 = (f32[192,256]{1,0:T(8,128)S(1)}, f32[192,256]{1,0:T(8,128)S(1)}, u32[]{:S(2)}, u32[]{:S(2)}) collective-permute-start(f32[192,256]{1,0:T(8,128)S(1)} %slice.9), channel_id=1, source_target_pairs={{0,6},{1,7},{2,0},{3,1},{4,2},{5,3},{6,4},{7,5},{8,14},{9,15},{10,... | collective-permute-start | bytes 589832 | tf_op jit(solution)/shard_map/ppermute | solution.py:501
  28.9 1.7 %prepare.1.ready = bf16[1152,768]{1,0:T(8,128)(2,1)} custom-call(f32[384,256]{1,0:T(8,128)S(1)} %collective-permute-done.refs_0_, f32[384,256]{1,0:T(8,128)S(1)} %collective-permute-done.1.refs_1_, f32[384,256]{1,0:T(8,128)S(1)} %copy-done.1), custom_call_target="tpu_custom_call" | custom-call | flops 20000000000 | bytes 2359296 | tf_op jit(solution)/shard_map/prepare/pallas_call | solution.py:216
  30.7 6.2 %all-to-all-done.pieces_ref = f32[32,24,128]{2,1,0:T(8,128)S(1)} async-done(((f32[32,24,128]{2,1,0:T(8,128)}), f32[32,24,128]{2,1,0:T(8,128)S(1)}, u32[]{:S(2)}, u32[]{:S(2)}) %all-to-all-start) | async-done | bytes 393248 | tf_op jit(solution)/shard_map/all_to_all | solution.py:509
  36.9 1.5 %pick.1 = f32[32,48,128]{2,1,0:T(8,128)} custom-call(s32[2,32]{1,0:T(2,128)S(1)} %copy-done.2, f32[32,24,128]{2,1,0:T(8,128)S(1)} %all-to-all-done.pieces_ref), custom_call_target="tpu_custom_call" | custom-call | tf_op jit(solution)/shard_map/pick/pallas_call | solution.py:77
  38.4 4.9 %all-to-all-start.1 = ((f32[32,48,128]{2,1,0:T(8,128)}), f32[32,48,128]{2,1,0:T(8,128)S(1)}, u32[]{:S(2)}, u32[]{:S(2)}) async-start(f32[32,48,128]{2,1,0:T(8,128)} %pick.1), calls=%async_computation.1 | async-start | bytes 1572864 | tf_op jit(solution)/shard_map/all_to_all | solution.py:512
  44.3 5.4 %own_scores.1 = (bf16[3,256,512]{2,1,0:T(8,128)(2,1)}, f32[3,4,384,256]{3,2,1,0:T(8,128)}, f32[2,1536]{1,0:T(2,128)S(1)}) custom-call(bf16[1152,768]{1,0:T(8,128)(2,1)} %prepare.1.ready, bf16[384,768]{1,0:T(8,128)(2,1)} %prepare_far.1.ready_far, f32[384,256]{1,0:T(8,128)S(1)} %copy-done.1, f32[384,256]{1,0:T(8,128)S(1)} %collective-permute-done.4.sib, ...), custom_call_target="tpu_custom_call" | custom-call | flops 1811939328 | bytes 4718592 | tf_op jit(solution)/shard_map/own_scores/pallas_call | solution.py:184
  49.7 5.7 %all-to-all-done.1.got = f32[32,48,128]{2,1,0:T(8,128)S(1)} async-done(((f32[32,48,128]{2,1,0:T(8,128)}), f32[32,48,128]{2,1,0:T(8,128)S(1)}, u32[]{:S(2)}, u32[]{:S(2)}) %all-to-all-start.1) | async-done | bytes 786464 | tf_op jit(solution)/shard_map/all_to_all | solution.py:512
  55.4 2.3 %collective-permute-done.6.got_sib = f32[32,48,128]{2,1,0:T(8,128)S(1)} collective-permute-done((f32[32,48,128]{2,1,0:T(8,128)S(1)}, f32[32,48,128]{2,1,0:T(8,128)S(1)}, u32[]{:S(2)}, u32[]{:S(2)}) %collective-permute-start.6) | collective-permute-done | bytes 786464 | tf_op jit(solution)/shard_map/ppermute | solution.py:504
  57.7 7.4 %forward.1 = (f32[6,4,384,256]{3,2,1,0:T(8,128)}, bf16[6,256,512]{2,1,0:T(8,128)(2,1)}, f32[8,2,1536]{2,1,0:T(2,128)S(1)}) custom-call(bf16[1152,768]{1,0:T(8,128)(2,1)} %prepare.1.ready, bf16[384,768]{1,0:T(8,128)(2,1)} %prepare_far.1.ready_far, f32[2,1536]{1,0:T(2,128)S(1)} %get-tuple-element.28.line_in, f32[32,48,128]{2,1,0:T(8,128)S(1)} %all-to-all-done.1.got, ...), custom_call_target="tpu_custom_call" | custom-call | flops 3623878656 | bytes 9437184 | tf_op jit(solution)/shard_map/forward/pallas_call | solution.py:294
  65.2 12.4 %all_to_all.20.all_ref = f32[8,2,1536]{2,1,0:T(2,128)S(1)} all-to-all(f32[8,2,1536]{2,1,0:T(2,128)S(1)} %get-tuple-element.30), channel_id=1, replica_groups=mesh['grp'=32,'mem'=8] {'mem'}, dimensions={0} | all-to-all | bytes 196608 | tf_op jit(solution)/shard_map/all_to_all | solution.py:526
  78.2 5.0 %all-to-all-start.3 = ((f32[32,1,768]{2,1,0:T(1,128)}), f32[32,1,768]{2,1,0:T(1,128)S(1)}, u32[]{:S(2)}, u32[]{:S(2)}) async-start(f32[32,1,768]{2,1,0:T(1,128)} %get-tuple-element.33), calls=%async_computation.3 | async-start | bytes 196608 | tf_op jit(solution)/shard_map/all_to_all | solution.py:528
  83.4 7.2 %all-to-all-done.3.everyone_ref = f32[32,1,768]{2,1,0:T(1,128)S(1)} async-done(((f32[32,1,768]{2,1,0:T(1,128)}), f32[32,1,768]{2,1,0:T(1,128)S(1)}, u32[]{:S(2)}, u32[]{:S(2)}) %all-to-all-start.3) | async-done | bytes 98336 | tf_op jit(solution)/shard_map/all_to_all | solution.py:528
  90.6 5.0 %backward_3_0.1 = (bf16[9,256,512]{2,1,0:T(8,128)(2,1)S(1)}, f32[192,256]{1,0:T(8,128)S(1)}, f32[192,256]{1,0:T(8,128)S(1)}) custom-call(s32[2]{0:T(128)S(1)} %dynamic-slice_reduce_fusion.partner_ref, f32[1,1536]{1,0:T(1,128)S(1)} %get-tuple-element.31.row_ref, f32[1,768]{1,0:T(1,128)S(1)} %get-tuple-element.32.own_ref, ...), custom_call_target="tpu_custom_call" | custom-call | flops 1358954496 | bytes 3538944 | tf_op jit(solution)/shard_map/backward_3_0/pallas_call | solution.py:437
  96.6 3.2 %collective-permute-start.8 = (f32[192,256]{1,0:T(8,128)S(1)}, f32[192,256]{1,0:T(8,128)S(1)}, u32[]{:S(2)}, u32[]{:S(2)}) collective-permute-start(f32[192,256]{1,0:T(8,128)S(1)} %get-tuple-element.42), channel_id=1, source_target_pairs={{0,6},{1,7},{2,0},{3,1},{4,2},{5,3},{6,4},{7,5},{8,14},{9,15},{10,... | collective-permute-start | bytes 589832 | tf_op jit(solution)/shard_map/ppermute | solution.py:501
  99.8 4.9 %backward_0_0.1 = (f32[192,256]{1,0:T(8,128)S(1)}, f32[192,256]{1,0:T(8,128)S(1)}) custom-call(s32[2]{0:T(128)S(1)} %dynamic-slice_reduce_fusion.partner_ref, f32[1,1536]{1,0:T(1,128)S(1)} %get-tuple-element.31.row_ref, f32[1,768]{1,0:T(1,128)S(1)} %get-tuple-element.32.own_ref, f32[32,1,768]{2,1,0:T(1,128)S(1)} %all-to-all-done.3.everyone_ref, ...), custom_call_target="tpu_custom_call" | custom-call | flops 1358954496 | bytes 3538944 | tf_op jit(solution)/shard_map/backward_0_0/pallas_call | solution.py:437
  104.8 2.9 %collective-permute-start.11 = (f32[192,256]{1,0:T(8,128)S(1)}, f32[192,256]{1,0:T(8,128)S(1)}, u32[]{:S(2)}, u32[]{:S(2)}) collective-permute-start(f32[192,256]{1,0:T(8,128)S(1)} %get-tuple-element.45), channel_id=1, source_target_pairs={{0,2},{1,3},{2,4},{3,5},{4,6},{5,7},{6,0},{7,1},{8,10},{9,11},{10,... | collective-permute-start | bytes 589832 | tf_op jit(solution)/shard_map/ppermute | solution.py:501
  107.7 4.9 %backward_0_192.1 = (f32[192,256]{1,0:T(8,128)S(1)}, f32[192,256]{1,0:T(8,128)S(1)}) custom-call(s32[2]{0:T(128)S(1)} %dynamic-slice_reduce_fusion.partner_ref, f32[1,1536]{1,0:T(1,128)S(1)} %get-tuple-element.31.row_ref, f32[1,768]{1,0:T(1,128)S(1)} %get-tuple-element.32.own_ref, f32[32,1,768]{2,1,0:T(1,128)S(1)} %all-to-all-done.3.everyone_ref, ...), custom_call_target="tpu_custom_call" | custom-call | flops 1358954496 | bytes 3538944 | tf_op jit(solution)/shard_map/backward_0_192/pallas_call | solution.py:437
  113.7 3.2 %collective-permute-start.12 = (f32[192,256]{1,0:T(8,128)S(1)}, f32[192,256]{1,0:T(8,128)S(1)}, u32[]{:S(2)}, u32[]{:S(2)}) collective-permute-start(f32[192,256]{1,0:T(8,128)S(1)} %get-tuple-element.46), channel_id=1, source_target_pairs={{0,6},{1,7},{2,0},{3,1},{4,2},{5,3},{6,4},{7,5},{8,14},{9,15},{10,... | collective-permute-start | bytes 589832 | tf_op jit(solution)/shard_map/ppermute | solution.py:501
  116.9 4.8 %backward_2_0.1.run_ref = f32[384,256]{1,0:T(8,128)S(1)} custom-call(s32[2]{0:T(128)S(1)} %dynamic-slice_reduce_fusion.partner_ref, f32[1,1536]{1,0:T(1,128)S(1)} %get-tuple-element.31.row_ref, f32[1,768]{1,0:T(1,128)S(1)} %get-tuple-element.32.own_ref, f32[32,1,768]{2,1,0:T(1,128)S(1)} %all-to-all-done.3.everyone_ref, ...), custom_call_target="tpu_custom_call" | custom-call | flops 1358954496 | bytes 3538944 | tf_op jit(solution)/shard_map/backward_2_0/pallas_call | solution.py:437
  121.8 1.8 %collective-permute-done.9.low0 = f32[192,256]{1,0:T(8,128)S(1)} collective-permute-done((f32[192,256]{1,0:T(8,128)S(1)}, f32[192,256]{1,0:T(8,128)S(1)}, u32[]{:S(2)}, u32[]{:S(2)}) %collective-permute-start.9) | collective-permute-done | bytes 196640 | tf_op jit(solution)/shard_map/ppermute | solution.py:501
  124.0 1.1 finish.1
  (34 shorter events, 7.7 us)
Async XLA Ops:
  0.6 23.5 %collective-permute-start.1 = (f32[384,256]{1,0:T(8,128)}, f32[384,256]{1,0:T(8,128)S(1)}, u32[]{:S(2)}, u32[]{:S(2)}) collective-permute-start(f32[384,256]{1,0:T(8,128)} %emb_ref.3), channel_id=1, source_target_pairs={{0,6},{1,7},{2,0},{3,1},{4,2},{5,3},{6,4},{7,5},{8,14},{9,15},{10,... | collective-permute-start | bytes 1179656 | tf_op jit(solution)/shard_map/ppermute | solution.py:501
  7.0 21.8 %collective-permute-start = (f32[384,256]{1,0:T(8,128)}, f32[384,256]{1,0:T(8,128)S(1)}, u32[]{:S(2)}, u32[]{:S(2)}) collective-permute-start(f32[384,256]{1,0:T(8,128)} %emb_ref.3), channel_id=1, source_target_pairs={{0,2},{1,3},{2,4},{3,5},{4,6},{5,7},{6,0},{7,1},{8,10},{9,11},{10,... | collective-permute-start | bytes 1179656 | tf_op jit(solution)/shard_map/ppermute | solution.py:501
  7.0 37.3 %collective-permute-start.4 = (f32[384,256]{1,0:T(8,128)}, f32[384,256]{1,0:T(8,128)S(1)}, u32[]{:S(2)}, u32[]{:S(2)}) collective-permute-start(f32[384,256]{1,0:T(8,128)} %emb_ref.3), channel_id=1, source_target_pairs={{0,1},{1,0},{2,3},{3,2},{4,5},{5,4},{6,7},{7,6},{8,9},{9,8},{10,11... | collective-permute-start | bytes 1179656 | tf_op jit(solution)/shard_map/ppermute | solution.py:504
  7.0 11.0 %collective-permute-start.5 = (s32[384]{0:T(512)}, s32[384]{0:T(512)S(1)}, u32[]{:S(2)}, u32[]{:S(2)}) collective-permute-start(s32[384]{0:T(512)} %param.4), channel_id=1, source_target_pairs={{0,1},{1,0},{2,3},{3,2},{4,5},{5,4},{6,7},{7,6},{8,9},{9,8},{10,11... | collective-permute-start | bytes 4616 | tf_op jit(solution)/shard_map/ppermute | solution.py:504
  7.5 1.0 copy-start
  8.5 20.4 %copy-start.1 = (f32[384,256]{1,0:T(8,128)S(1)}, f32[384,256]{1,0:T(8,128)}, u32[]{:S(2)}) copy-start(f32[384,256]{1,0:T(8,128)} %emb_ref.3) | copy-start | bytes 1179652
  9.3 27.6 %all-to-all-start = ((f32[32,24,128]{2,1,0:T(8,128)}), f32[32,24,128]{2,1,0:T(8,128)S(1)}, u32[]{:S(2)}, u32[]{:S(2)}) async-start(f32[32,24,128]{2,1,0:T(8,128)} %bitcast.1), calls=%async_computation | async-start | bytes 786432 | tf_op jit(solution)/shard_map/all_to_all | solution.py:509
  24.2 19.1 %collective-permute-start.3 = (f32[192,256]{1,0:T(8,128)S(1)}, f32[192,256]{1,0:T(8,128)S(1)}, u32[]{:S(2)}, u32[]{:S(2)}) collective-permute-start(f32[192,256]{1,0:T(8,128)S(1)} %slice.9), channel_id=1, source_target_pairs={{0,6},{1,7},{2,0},{3,1},{4,2},{5,3},{6,4},{7,5},{8,14},{9,15},{10,... | collective-permute-start | bytes 589832 | tf_op jit(solution)/shard_map/ppermute | solution.py:501
  28.8 8.0 %copy-start.2 = (s32[2,32]{1,0:T(2,128)S(1)}, s32[2,32]{1,0:T(2,128)}, u32[]{:S(2)}) copy-start(s32[2,32]{1,0:T(2,128)} %pairing_ref.1) | copy-start | bytes 772
  28.8 14.5 %collective-permute-start.2 = (f32[192,256]{1,0:T(8,128)S(1)}, f32[192,256]{1,0:T(8,128)S(1)}, u32[]{:S(2)}, u32[]{:S(2)}) collective-permute-start(f32[192,256]{1,0:T(8,128)S(1)} %slice.8), channel_id=1, source_target_pairs={{0,2},{1,3},{2,4},{3,5},{4,6},{5,7},{6,0},{7,1},{8,10},{9,11},{10,... | collective-permute-start | bytes 589832 | tf_op jit(solution)/shard_map/ppermute | solution.py:501
  38.4 17.1 %all-to-all-start.1 = ((f32[32,48,128]{2,1,0:T(8,128)}), f32[32,48,128]{2,1,0:T(8,128)S(1)}, u32[]{:S(2)}, u32[]{:S(2)}) async-start(f32[32,48,128]{2,1,0:T(8,128)} %pick.1), calls=%async_computation.1 | async-start | bytes 1572864 | tf_op jit(solution)/shard_map/all_to_all | solution.py:512
  55.4 2.3 %collective-permute-start.6 = (f32[32,48,128]{2,1,0:T(8,128)S(1)}, f32[32,48,128]{2,1,0:T(8,128)S(1)}, u32[]{:S(2)}, u32[]{:S(2)}) collective-permute-start(f32[32,48,128]{2,1,0:T(8,128)S(1)} %all-to-all-done.1.got), channel_id=1, source_target_pairs={{0,1},{1,0},{2,3},{3,2},{4,5},{5,4},{6,7},{7,6},{8,9},{9,8},{10,11... | collective-permute-start | bytes 2359304 | tf_op jit(solution)/shard_map/ppermute | solution.py:504
  78.2 12.4 %all-to-all-start.3 = ((f32[32,1,768]{2,1,0:T(1,128)}), f32[32,1,768]{2,1,0:T(1,128)S(1)}, u32[]{:S(2)}, u32[]{:S(2)}) async-start(f32[32,1,768]{2,1,0:T(1,128)} %get-tuple-element.33), calls=%async_computation.3 | async-start | bytes 196608 | tf_op jit(solution)/shard_map/all_to_all | solution.py:528
  95.6 17.0 %collective-permute-start.7 = (f32[192,256]{1,0:T(8,128)S(1)}, f32[192,256]{1,0:T(8,128)S(1)}, u32[]{:S(2)}, u32[]{:S(2)}) collective-permute-start(f32[192,256]{1,0:T(8,128)S(1)} %get-tuple-element.40), channel_id=1, source_target_pairs={{0,2},{1,3},{2,4},{3,5},{4,6},{5,7},{6,0},{7,1},{8,10},{9,11},{10,... | collective-permute-start | bytes 589832 | tf_op jit(solution)/shard_map/ppermute | solution.py:501
  96.6 16.0 %collective-permute-start.8 = (f32[192,256]{1,0:T(8,128)S(1)}, f32[192,256]{1,0:T(8,128)S(1)}, u32[]{:S(2)}, u32[]{:S(2)}) collective-permute-start(f32[192,256]{1,0:T(8,128)S(1)} %get-tuple-element.42), channel_id=1, source_target_pairs={{0,6},{1,7},{2,0},{3,1},{4,2},{5,3},{6,4},{7,5},{8,14},{9,15},{10,... | collective-permute-start | bytes 589832 | tf_op jit(solution)/shard_map/ppermute | solution.py:501
  104.7 17.0 %collective-permute-start.10 = (f32[192,256]{1,0:T(8,128)S(1)}, f32[192,256]{1,0:T(8,128)S(1)}, u32[]{:S(2)}, u32[]{:S(2)}) collective-permute-start(f32[192,256]{1,0:T(8,128)S(1)} %get-tuple-element.44), channel_id=1, source_target_pairs={{0,6},{1,7},{2,0},{3,1},{4,2},{5,3},{6,4},{7,5},{8,14},{9,15},{10,... | collective-permute-start | bytes 589832 | tf_op jit(solution)/shard_map/ppermute | solution.py:501
  104.8 17.0 %collective-permute-start.11 = (f32[192,256]{1,0:T(8,128)S(1)}, f32[192,256]{1,0:T(8,128)S(1)}, u32[]{:S(2)}, u32[]{:S(2)}) collective-permute-start(f32[192,256]{1,0:T(8,128)S(1)} %get-tuple-element.45), channel_id=1, source_target_pairs={{0,2},{1,3},{2,4},{3,5},{4,6},{5,7},{6,0},{7,1},{8,10},{9,11},{10,... | collective-permute-start | bytes 589832 | tf_op jit(solution)/shard_map/ppermute | solution.py:501
  112.7 10.9 %collective-permute-start.9 = (f32[192,256]{1,0:T(8,128)S(1)}, f32[192,256]{1,0:T(8,128)S(1)}, u32[]{:S(2)}, u32[]{:S(2)}) collective-permute-start(f32[192,256]{1,0:T(8,128)S(1)} %get-tuple-element.43), channel_id=1, source_target_pairs={{0,2},{1,3},{2,4},{3,5},{4,6},{5,7},{6,0},{7,1},{8,10},{9,11},{10,... | collective-permute-start | bytes 589832 | tf_op jit(solution)/shard_map/ppermute | solution.py:501
  113.7 10.3 %collective-permute-start.12 = (f32[192,256]{1,0:T(8,128)S(1)}, f32[192,256]{1,0:T(8,128)S(1)}, u32[]{:S(2)}, u32[]{:S(2)}) collective-permute-start(f32[192,256]{1,0:T(8,128)S(1)} %get-tuple-element.46), channel_id=1, source_target_pairs={{0,6},{1,7},{2,0},{3,1},{4,2},{5,3},{6,4},{7,5},{8,14},{9,15},{10,... | collective-permute-start | bytes 589832 | tf_op jit(solution)/shard_map/ppermute | solution.py:501

commit v7 on v6

--- a/solution.py
+++ b/solution.py
@@ -16,7 +16,6 @@
 STEPS = ((0, 2), (2, 3), (5, 3), (8, 1))
 VMEM = 16 * 1024 * 1024
 VMEM_LARGE = 44 * 1024 * 1024
-VMEM_BACKWARD = 28 * 1024 * 1024
 HBM = pl.BlockSpec(memory_space=pltpu.HBM)
 SMEM = pl.BlockSpec(memory_space=pltpu.SMEM)
 
@@ -106,23 +105,26 @@
     )
 
 
-def exponentials(scores, first_row, pos_ref, store):
-    height = scores.shape[0]
-    total = jnp.zeros((height, 128), jnp.float32)
-    match = jnp.zeros((height, 128), jnp.float32)
-    if first_row is not None:
-        row_ids = lax.broadcasted_iota(jnp.int32, (height, 128), 0) + first_row
-        lane_ids = lax.broadcasted_iota(jnp.int32, (height, 128), 1)
-    for k in range(0, scores.shape[1], 128):
-        score = scores[:, k : k + 128]
-        e = jnp.exp(score)
-        if first_row is not None:
-            match = match + jnp.where(row_ids == pos_ref[:, k : k + 128], score, 0.0)
-            if first_row <= SELF * SLICE < first_row + height and k < SLICE:
-                e = jnp.where(row_ids - SELF * SLICE == lane_ids + k, 0.0, e)
-        total = total + e
-        store(k, e)
-    return total, match
+def exponentials(scores, own, pos_ref, store):
+    totals, matches = [], []
+    lane_ids = lax.broadcasted_iota(jnp.int32, (128, 128), 1)
+    place_ids = lax.broadcasted_iota(jnp.int32, (128, 128), 0)
+    for top in range(0, scores.shape[0], 128):
+        total = jnp.zeros((128, 128), jnp.float32)
+        match = jnp.zeros((128, 128), jnp.float32)
+        for k in range(0, scores.shape[1], 128):
+            score = scores[top : top + 128, k : k + 128]
+            e = jnp.exp(score)
+            if own is not None:
+                here = place_ids + top == pos_ref[:, own + k : own + k + 128]
+                match = match + jnp.where(here, score, 0.0)
+                if top // SLICE == SELF and top - SELF * SLICE == own + k:
+                    e = jnp.where(place_ids == lane_ids, 0.0, e)
+            total = total + e
+            store(top // SLICE, slice(top % SLICE, top % SLICE + 128), slice(k, k + 128), e)
+        totals.append(total)
+        matches.append(match)
+    return jnp.concatenate(totals, axis=0), jnp.concatenate(matches, axis=0)
 
 
 def as_line(total):
@@ -139,7 +141,7 @@
 
 
 def own_kernel(
-    ready, ready_far, mine, sib, pos_ref, c_out, e_out, line_ref, left_ref, c_buf, e_buf, in_sem, c_sem, e_sem
+    ready, ready_far, mine, sib, pos_ref, c_out, e_out, line_ref, left_ref, c_buf, e_buf, tot_ref, in_sem, c_sem, e_sem
 ):
     at = ready.shape[0]
     ready_copies = [
@@ -150,30 +152,28 @@
         copy.start()
     for which, ref in enumerate((mine, sib)):
         put_columns(c_buf, which * SLICE, unit_parts(ref[...]))
-    cols = c_buf[...].reshape(2 * SLICE, 2 * WIDTH)
     copies = [pltpu.make_async_copy(c_buf, c_out, c_sem)]
     copies[0].start()
     for copy in ready_copies:
         copy.wait()
 
-    coming = product(left_ref[:SLICE], cols)
-    totals, matches = [], []
-    for order in range(4):
+    pieces = e_buf.shape[0]
+    coming = product(left_ref[...], c_buf[0])
+    for piece in range(pieces):
         scores = coming
-        if order < 3:
-            at = (order + 1) * SLICE
-            coming = product(left_ref[at : at + SLICE], cols)
-
-        def store(k, e):
-            e_buf[k // PIECE, order, :, k % PIECE : k % PIECE + 128] = e
-
-        total, match = exponentials(scores, order * SLICE, pos_ref, store)
-        totals.append(as_line(total))
-        matches.append(as_line(match))
-        copies.append(pltpu.make_async_copy(e_buf.at[:, order], e_out.at[:, order], e_sem.at[order]))
+        if piece + 1 < pieces:
+            coming = product(left_ref[...], c_buf[piece + 1])
+
+        def store(order, rows, lanes, e):
+            e_buf[piece, order, rows, lanes] = e
+
+        total, match = exponentials(scores, piece * PIECE, pos_ref, store)
+        for which, value in enumerate((total, match)):
+            tot_ref[which] = value if piece == 0 else tot_ref[which] + value
+        copies.append(pltpu.make_async_copy(e_buf.at[piece], e_out.at[piece], e_sem.at[piece]))
         copies[-1].start()
-    line_ref[0:1] = jnp.concatenate(totals, axis=1)
-    line_ref[1:2] = jnp.concatenate(matches, axis=1)
+    for which in range(2):
+        line_ref[which : which + 1] = as_line(tot_ref[which])
     for copy in copies:
         copy.wait()
 
@@ -190,9 +190,10 @@
             pltpu.VMEM((rows, 3 * WIDTH), jnp.bfloat16),
             pltpu.VMEM(*shapes[0]),
             pltpu.VMEM(*shapes[1]),
+            pltpu.VMEM((2, rows, 128), jnp.float32),
             pltpu.SemaphoreType.DMA((2,)),
             pltpu.SemaphoreType.DMA,
-            pltpu.SemaphoreType.DMA((4,)),
+            pltpu.SemaphoreType.DMA((3,)),
         ],
         cost_estimate=pl.CostEstimate(
             flops=6 * rows * wide * WIDTH, bytes_accessed=4 * rows * wide, transcendentals=rows * wide
@@ -228,9 +229,8 @@
     ready, ready_far, line_in, got, got_sib, e_out, c_out, line_ref,
     left_ref, c_buf, e_buf, tot_ref, in_sem, c_sem, e_sem,
 ):
-    orders, wide = e_buf.shape[1], 2 * SLICE
+    wide, pieces = 2 * SLICE, e_buf.shape[0]
     many = wide // PIECE
-    chunks = e_buf.shape[0] // many
     at = ready.shape[0]
     ready_copies = [
         pltpu.make_async_copy(ready, left_ref.at[pl.ds(0, at)], in_sem.at[0]),
@@ -250,34 +250,23 @@
         copies.append(pltpu.make_async_copy(c_buf.at[view], c_out.at[view], c_sem.at[chunk]))
         copies[-1].start()
 
-    def scores_of(chunk, band):
-        cols = c_buf[chunk * many : chunk * many + many].reshape(wide, 2 * WIDTH)
-        return product(left_ref[band * wide : band * wide + wide], cols)
-
     columns(0)
     for copy in ready_copies:
         copy.wait()
-    items = [(chunk, band) for chunk in range(chunks) for band in range(orders // 2)]
-    coming = scores_of(*items[0])
-    for turn, (chunk, band) in enumerate(items):
+    coming = product(left_ref[...], c_buf[0])
+    for piece in range(pieces):
         scores = coming
-        if turn + 1 < len(items):
-            if items[turn + 1][0] != chunk:
-                columns(items[turn + 1][0])
-            coming = scores_of(*items[turn + 1])
-
-        def store(k, e):
-            lane = k % PIECE
-            e = e.reshape(2, SLICE, 128)
-            e_buf[chunk * many + k // PIECE, 2 * band : 2 * band + 2, :, lane : lane + 128] = e
+        if piece + 1 < pieces:
+            if (piece + 1) % many == 0:
+                columns((piece + 1) // many)
+            coming = product(left_ref[...], c_buf[piece + 1])
+
+        def store(order, rows, lanes, e):
+            e_buf[piece, order, rows, lanes] = e
 
         total, _ = exponentials(scores, None, None, store)
-        if chunk == 0:
-            tot_ref[band * wide : band * wide + wide] = total
-        else:
-            tot_ref[band * wide : band * wide + wide] += total
-        view = (pl.ds(chunk * many, many), pl.ds(2 * band, 2))
-        copies.append(pltpu.make_async_copy(e_buf.at[view], e_out.at[view], e_sem.at[turn]))
+        tot_ref[...] = total if piece == 0 else tot_ref[...] + total
+        copies.append(pltpu.make_async_copy(e_buf.at[piece], e_out.at[piece], e_sem.at[piece]))
         copies[-1].start()
 
     total = as_line(tot_ref[...]) + line_in[0:1]
@@ -307,7 +296,7 @@
             pltpu.VMEM((rows, 128), jnp.float32),
             pltpu.SemaphoreType.DMA((2,)),
             pltpu.SemaphoreType.DMA((2,)),
-            pltpu.SemaphoreType.DMA((4,)),
+            pltpu.SemaphoreType.DMA((6,)),
         ],
         cost_estimate=pl.CostEstimate(
             flops=12 * rows * wide * WIDTH, bytes_accessed=8 * rows * wide, transcendentals=2 * rows * wide
@@ -433,21 +422,22 @@
 def backward(bands, pieces, partners, row_den, own_den, everyone, pos, e0, e1, *cols):
     first = len(cols) == 2
     count = 9 * PIECE
+    height = sum(size for _, _, size in bands)
     col_shape = [jax.ShapeDtypeStruct((9, PIECE, 2 * WIDTH), jnp.bfloat16)]
     return pl.pallas_call(
         functools.partial(backward_kernel, bands, first),
         in_specs=[SMEM] + [pl.BlockSpec()] * 4 + [HBM] * 2 + ([HBM] * 2 if first else [pl.BlockSpec()]),
-        out_shape=col_shape * first + [jax.ShapeDtypeStruct((SLICE // pieces, WIDTH), jnp.float32)] * pieces,
+        out_shape=col_shape * first + [jax.ShapeDtypeStruct((height // pieces, WIDTH), jnp.float32)] * pieces,
         scratch_shapes=[
-            pltpu.VMEM((SLICE, WIDTH), jnp.float32),
-            pltpu.VMEM((9, SLICE, PIECE), jnp.float32),
+            pltpu.VMEM((height, WIDTH), jnp.float32),
+            pltpu.VMEM((9, height, PIECE), jnp.float32),
             pltpu.SemaphoreType.DMA((len(STEPS), 2, len(bands))),
             pltpu.SemaphoreType.DMA((len(STEPS), 2)),
         ],
         cost_estimate=pl.CostEstimate(
-            flops=6 * SLICE * count * WIDTH, bytes_accessed=4 * SLICE * count, transcendentals=0
+            flops=6 * height * count * WIDTH, bytes_accessed=4 * height * count, transcendentals=0
         ),
-        compiler_params=params(VMEM_BACKWARD),
+        compiler_params=params(VMEM_LARGE),
         name="backward_%d_%d" % bands[0][:2],
     )(partners, row_den, own_den, everyone, pos, in_hbm(e0), in_hbm(e1), *(map(in_hbm, cols) if first else cols))
 
@@ -528,10 +518,10 @@
     everyone = lax.all_to_all(spread, "grp", 0, 0, tiled=True)
 
     shared = (pairing[:, group], row_den, own_den, everyone, pos, e_own, e_part)
-    cols, far_low, far_high = backward(((3, 0, rows),), 2, *shared, c_own, c_part)
+    bands = ((3, 0, rows), (0, 0, half), (1, half, half))
+    cols, far_low, far_high, left_low, right_high = backward(bands, 4, *shared, c_own, c_part)
     shared += (cols,)
     far_low, far_high = shift(far_low, 2), shift(far_high, -2)
-    left_low, right_high = backward(((0, 0, half), (1, half, half)), 2, *shared)
     high0, low1 = shift(right_high, 2), shift(left_low, -2)
     left_high, right_low = backward(((0, half, half), (1, 0, half)), 2, *shared)
     right_low, left_high = add_pairs(right_low, far_low, left_high, far_high)

time: 126 us -> 131 us (1.040)
  waiting for transfers between devices: 29.8 us -> 33.3 us
    ppermute x10, waiting for transfers between devices: 8.35 us -> 12.7 us  [shift(): lax.ppermute(value, 'mem', [(m, (m + by) % members) for m in range(member...]
    pallas_call x4 -> x3, Pallas kernels: 19.6 us -> 18.7 us  [backward(): pl.pallas_call(functools.partial(backward_kernel, bands, first), in_specs...]
  transfers between devices with their start and end apart: 16 -> 16, of which waited for: 7 -> 8; matrix products, arithmetic and copies ran while one was open for 1% -> 1% of each run, Pallas kernels for 20% -> 16%
where the time goes in v7:
time: 131 us; the launch traced here: 129 us
  starting transfers between devices  41.2 us (31%)
  Pallas kernels  39.6 us (30%)
  waiting for transfers between devices  33.3 us (25%)
  blocking collectives  12.4 us (9%)
  local copies, waits for them, and re-layouts  1.91 us (1%)
    ppermute x10, starting transfers between devices, shift(): lax.ppermute(value, 'mem', [(m, (m + by) % members) for m in range(member...  22.4 us
    pallas_call x3, Pallas kernels, backward(): pl.pallas_call(functools.partial(backward_kernel, bands, first), in_specs...  18.7 us
    ppermute x10, waiting for transfers between devices, shift(): lax.ppermute(value, 'mem', [(m, (m + by) % members) for m in range(member...  12.7 us
    all_to_all x1, blocking collectives, local(): everything = lax.all_to_all(line, 'mem', 0, 0, tiled=True)  12.4 us
    all_to_all x1, starting transfers between devices, local(): lax.all_to_all(as_tiles(embeddings).reshape(groups, per, 128), 'grp', 0,...  7.99 us
    pallas_call x1, Pallas kernels, forward(): pl.pallas_call(forward_kernel, in_specs=[HBM] * 2 + [pl.BlockSpec()] * 3,...  7.97 us
    all_to_all x1, waiting for transfers between devices, local(): everyone = lax.all_to_all(spread, 'grp', 0, 0, tiled=True)  7.14 us
    all_to_all x1, waiting for transfers between devices, local(): lax.all_to_all(as_tiles(embeddings).reshape(groups, per, 128), 'grp', 0,...  6.21 us
  transfers between devices with their start and end apart: 16, of which 8 were waited for; matrix products, arithmetic and copies ran while one was open for 1% of the time, Pallas kernels for 16%

profile of v7, /device:TPU:8, one launch (start us, length us, event | category | flops | bytes accessed | tf_op | source)
XLA Modules:
  0.0 129.3 jit_solution(13526695868056971433)
XLA Ops:
  0.6 6.4 %collective-permute-start.1 = (f32[384,256]{1,0:T(8,128)}, f32[384,256]{1,0:T(8,128)S(1)}, u32[]{:S(2)}, u32[]{:S(2)}) collective-permute-start(f32[384,256]{1,0:T(8,128)} %emb_ref.3), channel_id=1, source_target_pairs={{0,6},{1,7},{2,0},{3,1},{4,2},{5,3},{6,4},{7,5},{8,14},{9,15},{10,... | collective-permute-start | bytes 1179656 | tf_op jit(solution)/shard_map/ppermute | solution.py:491
  9.3 8.0 %all-to-all-start = ((f32[32,24,128]{2,1,0:T(8,128)}), f32[32,24,128]{2,1,0:T(8,128)S(1)}, u32[]{:S(2)}, u32[]{:S(2)}) async-start(f32[32,24,128]{2,1,0:T(8,128)} %bitcast.1), calls=%async_computation | async-start | bytes 786432 | tf_op jit(solution)/shard_map/all_to_all | solution.py:499
  18.1 6.1 %collective-permute-done.1.refs_1_ = f32[384,256]{1,0:T(8,128)S(1)} collective-permute-done((f32[384,256]{1,0:T(8,128)}, f32[384,256]{1,0:T(8,128)S(1)}, u32[]{:S(2)}, u32[]{:S(2)}) %collective-permute-start.1) | collective-permute-done | bytes 393248 | tf_op jit(solution)/shard_map/ppermute | solution.py:491
  24.2 4.6 %collective-permute-start.3 = (f32[192,256]{1,0:T(8,128)S(1)}, f32[192,256]{1,0:T(8,128)S(1)}, u32[]{:S(2)}, u32[]{:S(2)}) collective-permute-start(f32[192,256]{1,0:T(8,128)S(1)} %slice.9), channel_id=1, source_target_pairs={{0,6},{1,7},{2,0},{3,1},{4,2},{5,3},{6,4},{7,5},{8,14},{9,15},{10,... | collective-permute-start | bytes 589832 | tf_op jit(solution)/shard_map/ppermute | solution.py:491
  28.9 1.7 %prepare.1.ready = bf16[1152,768]{1,0:T(8,128)(2,1)} custom-call(f32[384,256]{1,0:T(8,128)S(1)} %collective-permute-done.refs_0_, f32[384,256]{1,0:T(8,128)S(1)} %collective-permute-done.1.refs_1_, f32[384,256]{1,0:T(8,128)S(1)} %copy-done.1), custom_call_target="tpu_custom_call" | custom-call | flops 20000000000 | bytes 2359296 | tf_op jit(solution)/shard_map/prepare/pallas_call | solution.py:217
  30.7 6.2 %all-to-all-done.pieces_ref = f32[32,24,128]{2,1,0:T(8,128)S(1)} async-done(((f32[32,24,128]{2,1,0:T(8,128)}), f32[32,24,128]{2,1,0:T(8,128)S(1)}, u32[]{:S(2)}, u32[]{:S(2)}) %all-to-all-start) | async-done | bytes 393248 | tf_op jit(solution)/shard_map/all_to_all | solution.py:499
  36.9 1.5 %pick.1 = f32[32,48,128]{2,1,0:T(8,128)} custom-call(s32[2,32]{1,0:T(2,128)S(1)} %copy-done.2, f32[32,24,128]{2,1,0:T(8,128)S(1)} %all-to-all-done.pieces_ref), custom_call_target="tpu_custom_call" | custom-call | tf_op jit(solution)/shard_map/pick/pallas_call | solution.py:76
  38.4 4.9 %all-to-all-start.1 = ((f32[32,48,128]{2,1,0:T(8,128)}), f32[32,48,128]{2,1,0:T(8,128)S(1)}, u32[]{:S(2)}, u32[]{:S(2)}) async-start(f32[32,48,128]{2,1,0:T(8,128)} %pick.1), calls=%async_computation.1 | async-start | bytes 1572864 | tf_op jit(solution)/shard_map/all_to_all | solution.py:502
  44.3 6.1 %own_scores.1 = (bf16[3,256,512]{2,1,0:T(8,128)(2,1)}, f32[3,4,384,256]{3,2,1,0:T(8,128)}, f32[2,1536]{1,0:T(2,128)S(1)}) custom-call(bf16[1152,768]{1,0:T(8,128)(2,1)} %prepare.1.ready, bf16[384,768]{1,0:T(8,128)(2,1)} %prepare_far.1.ready_far, f32[384,256]{1,0:T(8,128)S(1)} %copy-done.1, f32[384,256]{1,0:T(8,128)S(1)} %collective-permute-done.4.sib, ...), custom_call_target="tpu_custom_call" | custom-call | flops 1811939328 | bytes 4718592 | tf_op jit(solution)/shard_map/own_scores/pallas_call | solution.py:184
  50.5 4.9 %all-to-all-done.1.got = f32[32,48,128]{2,1,0:T(8,128)S(1)} async-done(((f32[32,48,128]{2,1,0:T(8,128)}), f32[32,48,128]{2,1,0:T(8,128)S(1)}, u32[]{:S(2)}, u32[]{:S(2)}) %all-to-all-start.1) | async-done | bytes 786464 | tf_op jit(solution)/shard_map/all_to_all | solution.py:502
  55.4 2.3 %collective-permute-done.6.got_sib = f32[32,48,128]{2,1,0:T(8,128)S(1)} collective-permute-done((f32[32,48,128]{2,1,0:T(8,128)S(1)}, f32[32,48,128]{2,1,0:T(8,128)S(1)}, u32[]{:S(2)}, u32[]{:S(2)}) %collective-permute-start.6) | collective-permute-done | bytes 786464 | tf_op jit(solution)/shard_map/ppermute | solution.py:494
  57.7 8.0 %forward.1 = (f32[6,4,384,256]{3,2,1,0:T(8,128)}, bf16[6,256,512]{2,1,0:T(8,128)(2,1)}, f32[8,2,1536]{2,1,0:T(2,128)S(1)}) custom-call(bf16[1152,768]{1,0:T(8,128)(2,1)} %prepare.1.ready, bf16[384,768]{1,0:T(8,128)(2,1)} %prepare_far.1.ready_far, f32[2,1536]{1,0:T(2,128)S(1)} %get-tuple-element.28.line_in, f32[32,48,128]{2,1,0:T(8,128)S(1)} %all-to-all-done.1.got, ...), custom_call_target="tpu_custom_call" | custom-call | flops 3623878656 | bytes 9437184 | tf_op jit(solution)/shard_map/forward/pallas_call | solution.py:283
  65.7 12.4 %all_to_all.20.all_ref = f32[8,2,1536]{2,1,0:T(2,128)S(1)} all-to-all(f32[8,2,1536]{2,1,0:T(2,128)S(1)} %get-tuple-element.30), channel_id=1, replica_groups=mesh['grp'=32,'mem'=8] {'mem'}, dimensions={0} | all-to-all | bytes 196608 | tf_op jit(solution)/shard_map/all_to_all | solution.py:516
  78.7 5.3 %all-to-all-start.3 = ((f32[32,1,768]{2,1,0:T(1,128)}), f32[32,1,768]{2,1,0:T(1,128)S(1)}, u32[]{:S(2)}, u32[]{:S(2)}) async-start(f32[32,1,768]{2,1,0:T(1,128)} %get-tuple-element.33), calls=%async_computation.3 | async-start | bytes 196608 | tf_op jit(solution)/shard_map/all_to_all | solution.py:518
  84.2 7.1 %all-to-all-done.3.everyone_ref = f32[32,1,768]{2,1,0:T(1,128)S(1)} async-done(((f32[32,1,768]{2,1,0:T(1,128)}), f32[32,1,768]{2,1,0:T(1,128)S(1)}, u32[]{:S(2)}, u32[]{:S(2)}) %all-to-all-start.3) | async-done | bytes 98336 | tf_op jit(solution)/shard_map/all_to_all | solution.py:518
  91.4 9.0 %backward_3_0.1 = (bf16[9,256,512]{2,1,0:T(8,128)(2,1)S(1)}, f32[192,256]{1,0:T(8,128)S(1)}, f32[192,256]{1,0:T(8,128)S(1)}, f32[192,256]{1,0:T(8,128)S(1)}, f32[192,256]{1,0:T(8,128)S(1)}) custom-call(s32[2]{0:T(128)S(1)} %dynamic-slice_reduce_fusion.partner_ref, f32[1,1536]{1,0:T(1,128)S(1)} %get-tuple-element.31.row_ref, ...), custom_call_target="tpu_custom_call" | custom-call | flops 2717908992 | bytes 7077888 | tf_op jit(solution)/shard_map/backward_3_0/pallas_call | solution.py:427
  101.2 3.4 %collective-permute-start.8 = (f32[192,256]{1,0:T(8,128)S(1)}, f32[192,256]{1,0:T(8,128)S(1)}, u32[]{:S(2)}, u32[]{:S(2)}) collective-permute-start(f32[192,256]{1,0:T(8,128)S(1)} %get-tuple-element.42), channel_id=1, source_target_pairs={{0,6},{1,7},{2,0},{3,1},{4,2},{5,3},{6,4},{7,5},{8,14},{9,15},{10,... | collective-permute-start | bytes 589832 | tf_op jit(solution)/shard_map/ppermute | solution.py:491
  104.7 2.9 %collective-permute-start.11 = (f32[192,256]{1,0:T(8,128)S(1)}, f32[192,256]{1,0:T(8,128)S(1)}, u32[]{:S(2)}, u32[]{:S(2)}) collective-permute-start(f32[192,256]{1,0:T(8,128)S(1)} %get-tuple-element.45), channel_id=1, source_target_pairs={{0,2},{1,3},{2,4},{3,5},{4,6},{5,7},{6,0},{7,1},{8,10},{9,11},{10,... | collective-permute-start | bytes 589832 | tf_op jit(solution)/shard_map/ppermute | solution.py:491
  107.6 4.9 %backward_0_192.1 = (f32[192,256]{1,0:T(8,128)S(1)}, f32[192,256]{1,0:T(8,128)S(1)}) custom-call(s32[2]{0:T(128)S(1)} %dynamic-slice_reduce_fusion.partner_ref, f32[1,1536]{1,0:T(1,128)S(1)} %get-tuple-element.31.row_ref, f32[1,768]{1,0:T(1,128)S(1)} %get-tuple-element.32.own_ref, f32[32,1,768]{2,1,0:T(1,128)S(1)} %all-to-all-done.3.everyone_ref, ...), custom_call_target="tpu_custom_call" | custom-call | flops 1358954496 | bytes 3538944 | tf_op jit(solution)/shard_map/backward_0_192/pallas_call | solution.py:427
  112.5 2.6 %collective-permute-done.7.b_ref = f32[192,256]{1,0:T(8,128)S(1)} collective-permute-done((f32[192,256]{1,0:T(8,128)S(1)}, f32[192,256]{1,0:T(8,128)S(1)}, u32[]{:S(2)}, u32[]{:S(2)}) %collective-permute-start.7) | collective-permute-done | bytes 196640 | tf_op jit(solution)/shard_map/ppermute | solution.py:491
  115.0 3.4 %collective-permute-done.8.d_ref = f32[192,256]{1,0:T(8,128)S(1)} collective-permute-done((f32[192,256]{1,0:T(8,128)S(1)}, f32[192,256]{1,0:T(8,128)S(1)}, u32[]{:S(2)}, u32[]{:S(2)}) %collective-permute-start.8) | collective-permute-done | bytes 196640 | tf_op jit(solution)/shard_map/ppermute | solution.py:491
  118.5 1.2 collective-permute-start.9
  119.8 3.0 %collective-permute-start.12 = (f32[192,256]{1,0:T(8,128)S(1)}, f32[192,256]{1,0:T(8,128)S(1)}, u32[]{:S(2)}, u32[]{:S(2)}) collective-permute-start(f32[192,256]{1,0:T(8,128)S(1)} %get-tuple-element.46), channel_id=1, source_target_pairs={{0,6},{1,7},{2,0},{3,1},{4,2},{5,3},{6,4},{7,5},{8,14},{9,15},{10,... | collective-permute-start | bytes 589832 | tf_op jit(solution)/shard_map/ppermute | solution.py:491
  122.7 4.8 %backward_2_0.1.run_ref = f32[384,256]{1,0:T(8,128)S(1)} custom-call(s32[2]{0:T(128)S(1)} %dynamic-slice_reduce_fusion.partner_ref, f32[1,1536]{1,0:T(1,128)S(1)} %get-tuple-element.31.row_ref, f32[1,768]{1,0:T(1,128)S(1)} %get-tuple-element.32.own_ref, f32[32,1,768]{2,1,0:T(1,128)S(1)} %all-to-all-done.3.everyone_ref, ...), custom_call_target="tpu_custom_call" | custom-call | flops 1358954496 | bytes 3538944 | tf_op jit(solution)/shard_map/backward_2_0/pallas_call | solution.py:427
  (33 shorter events, 7.6 us)
Async XLA Ops:
  0.6 23.5 %collective-permute-start.1 = (f32[384,256]{1,0:T(8,128)}, f32[384,256]{1,0:T(8,128)S(1)}, u32[]{:S(2)}, u32[]{:S(2)}) collective-permute-start(f32[384,256]{1,0:T(8,128)} %emb_ref.3), channel_id=1, source_target_pairs={{0,6},{1,7},{2,0},{3,1},{4,2},{5,3},{6,4},{7,5},{8,14},{9,15},{10,... | collective-permute-start | bytes 1179656 | tf_op jit(solution)/shard_map/ppermute | solution.py:491
  7.0 21.8 %collective-permute-start = (f32[384,256]{1,0:T(8,128)}, f32[384,256]{1,0:T(8,128)S(1)}, u32[]{:S(2)}, u32[]{:S(2)}) collective-permute-start(f32[384,256]{1,0:T(8,128)} %emb_ref.3), channel_id=1, source_target_pairs={{0,2},{1,3},{2,4},{3,5},{4,6},{5,7},{6,0},{7,1},{8,10},{9,11},{10,... | collective-permute-start | bytes 1179656 | tf_op jit(solution)/shard_map/ppermute | solution.py:491
  7.0 37.3 %collective-permute-start.4 = (f32[384,256]{1,0:T(8,128)}, f32[384,256]{1,0:T(8,128)S(1)}, u32[]{:S(2)}, u32[]{:S(2)}) collective-permute-start(f32[384,256]{1,0:T(8,128)} %emb_ref.3), channel_id=1, source_target_pairs={{0,1},{1,0},{2,3},{3,2},{4,5},{5,4},{6,7},{7,6},{8,9},{9,8},{10,11... | collective-permute-start | bytes 1179656 | tf_op jit(solution)/shard_map/ppermute | solution.py:494
  7.0 11.0 %collective-permute-start.5 = (s32[384]{0:T(512)}, s32[384]{0:T(512)S(1)}, u32[]{:S(2)}, u32[]{:S(2)}) collective-permute-start(s32[384]{0:T(512)} %param.4), channel_id=1, source_target_pairs={{0,1},{1,0},{2,3},{3,2},{4,5},{5,4},{6,7},{7,6},{8,9},{9,8},{10,11... | collective-permute-start | bytes 4616 | tf_op jit(solution)/shard_map/ppermute | solution.py:494
  7.5 1.0 copy-start
  8.5 20.4 %copy-start.1 = (f32[384,256]{1,0:T(8,128)S(1)}, f32[384,256]{1,0:T(8,128)}, u32[]{:S(2)}) copy-start(f32[384,256]{1,0:T(8,128)} %emb_ref.3) | copy-start | bytes 1179652
  9.3 27.6 %all-to-all-start = ((f32[32,24,128]{2,1,0:T(8,128)}), f32[32,24,128]{2,1,0:T(8,128)S(1)}, u32[]{:S(2)}, u32[]{:S(2)}) async-start(f32[32,24,128]{2,1,0:T(8,128)} %bitcast.1), calls=%async_computation | async-start | bytes 786432 | tf_op jit(solution)/shard_map/all_to_all | solution.py:499
  24.2 19.1 %collective-permute-start.3 = (f32[192,256]{1,0:T(8,128)S(1)}, f32[192,256]{1,0:T(8,128)S(1)}, u32[]{:S(2)}, u32[]{:S(2)}) collective-permute-start(f32[192,256]{1,0:T(8,128)S(1)} %slice.9), channel_id=1, source_target_pairs={{0,6},{1,7},{2,0},{3,1},{4,2},{5,3},{6,4},{7,5},{8,14},{9,15},{10,... | collective-permute-start | bytes 589832 | tf_op jit(solution)/shard_map/ppermute | solution.py:491
  28.8 8.0 %copy-start.2 = (s32[2,32]{1,0:T(2,128)S(1)}, s32[2,32]{1,0:T(2,128)}, u32[]{:S(2)}) copy-start(s32[2,32]{1,0:T(2,128)} %pairing_ref.1) | copy-start | bytes 772
  28.8 14.5 %collective-permute-start.2 = (f32[192,256]{1,0:T(8,128)S(1)}, f32[192,256]{1,0:T(8,128)S(1)}, u32[]{:S(2)}, u32[]{:S(2)}) collective-permute-start(f32[192,256]{1,0:T(8,128)S(1)} %slice.8), channel_id=1, source_target_pairs={{0,2},{1,3},{2,4},{3,5},{4,6},{5,7},{6,0},{7,1},{8,10},{9,11},{10,... | collective-permute-start | bytes 589832 | tf_op jit(solution)/shard_map/ppermute | solution.py:491
  38.4 17.1 %all-to-all-start.1 = ((f32[32,48,128]{2,1,0:T(8,128)}), f32[32,48,128]{2,1,0:T(8,128)S(1)}, u32[]{:S(2)}, u32[]{:S(2)}) async-start(f32[32,48,128]{2,1,0:T(8,128)} %pick.1), calls=%async_computation.1 | async-start | bytes 1572864 | tf_op jit(solution)/shard_map/all_to_all | solution.py:502
  55.4 2.3 %collective-permute-start.6 = (f32[32,48,128]{2,1,0:T(8,128)S(1)}, f32[32,48,128]{2,1,0:T(8,128)S(1)}, u32[]{:S(2)}, u32[]{:S(2)}) collective-permute-start(f32[32,48,128]{2,1,0:T(8,128)S(1)} %all-to-all-done.1.got), channel_id=1, source_target_pairs={{0,1},{1,0},{2,3},{3,2},{4,5},{5,4},{6,7},{7,6},{8,9},{9,8},{10,11... | collective-permute-start | bytes 2359304 | tf_op jit(solution)/shard_map/ppermute | solution.py:494
  78.7 12.6 %all-to-all-start.3 = ((f32[32,1,768]{2,1,0:T(1,128)}), f32[32,1,768]{2,1,0:T(1,128)S(1)}, u32[]{:S(2)}, u32[]{:S(2)}) async-start(f32[32,1,768]{2,1,0:T(1,128)} %get-tuple-element.33), calls=%async_computation.3 | async-start | bytes 196608 | tf_op jit(solution)/shard_map/all_to_all | solution.py:518
  100.4 14.6 %collective-permute-start.7 = (f32[192,256]{1,0:T(8,128)S(1)}, f32[192,256]{1,0:T(8,128)S(1)}, u32[]{:S(2)}, u32[]{:S(2)}) collective-permute-start(f32[192,256]{1,0:T(8,128)S(1)} %get-tuple-element.40), channel_id=1, source_target_pairs={{0,2},{1,3},{2,4},{3,5},{4,6},{5,7},{6,0},{7,1},{8,10},{9,11},{10,... | collective-permute-start | bytes 589832 | tf_op jit(solution)/shard_map/ppermute | solution.py:491
  101.2 17.3 %collective-permute-start.8 = (f32[192,256]{1,0:T(8,128)S(1)}, f32[192,256]{1,0:T(8,128)S(1)}, u32[]{:S(2)}, u32[]{:S(2)}) collective-permute-start(f32[192,256]{1,0:T(8,128)S(1)} %get-tuple-element.42), channel_id=1, source_target_pairs={{0,6},{1,7},{2,0},{3,1},{4,2},{5,3},{6,4},{7,5},{8,14},{9,15},{10,... | collective-permute-start | bytes 589832 | tf_op jit(solution)/shard_map/ppermute | solution.py:491
  104.6 23.0 %collective-permute-start.10 = (f32[192,256]{1,0:T(8,128)S(1)}, f32[192,256]{1,0:T(8,128)S(1)}, u32[]{:S(2)}, u32[]{:S(2)}) collective-permute-start(f32[192,256]{1,0:T(8,128)S(1)} %get-tuple-element.44), channel_id=1, source_target_pairs={{0,6},{1,7},{2,0},{3,1},{4,2},{5,3},{6,4},{7,5},{8,14},{9,15},{10,... | collective-permute-start | bytes 589832 | tf_op jit(solution)/shard_map/ppermute | solution.py:491
  104.7 22.9 %collective-permute-start.11 = (f32[192,256]{1,0:T(8,128)S(1)}, f32[192,256]{1,0:T(8,128)S(1)}, u32[]{:S(2)}, u32[]{:S(2)}) collective-permute-start(f32[192,256]{1,0:T(8,128)S(1)} %get-tuple-element.45), channel_id=1, source_target_pairs={{0,2},{1,3},{2,4},{3,5},{4,6},{5,7},{6,0},{7,1},{8,10},{9,11},{10,... | collective-permute-start | bytes 589832 | tf_op jit(solution)/shard_map/ppermute | solution.py:491
  118.5 9.1 %collective-permute-start.9 = (f32[192,256]{1,0:T(8,128)S(1)}, f32[192,256]{1,0:T(8,128)S(1)}, u32[]{:S(2)}, u32[]{:S(2)}) collective-permute-start(f32[192,256]{1,0:T(8,128)S(1)} %get-tuple-element.43), channel_id=1, source_target_pairs={{0,2},{1,3},{2,4},{3,5},{4,6},{5,7},{6,0},{7,1},{8,10},{9,11},{10,... | collective-permute-start | bytes 589832 | tf_op jit(solution)/shard_map/ppermute | solution.py:491
  119.8 8.4 %collective-permute-start.12 = (f32[192,256]{1,0:T(8,128)S(1)}, f32[192,256]{1,0:T(8,128)S(1)}, u32[]{:S(2)}, u32[]{:S(2)}) collective-permute-start(f32[192,256]{1,0:T(8,128)S(1)} %get-tuple-element.46), channel_id=1, source_target_pairs={{0,6},{1,7},{2,0},{3,1},{4,2},{5,3},{6,4},{7,5},{8,14},{9,15},{10,... | collective-permute-start | bytes 589832 | tf_op jit(solution)/shard_map/ppermute | solution.py:491

commit v8 on v6

--- a/solution.py
+++ b/solution.py
@@ -13,7 +13,7 @@
 WIDTH = 256
 SELF = 2
 PIECE = 256
-STEPS = ((0, 2), (2, 3), (5, 3), (8, 1))
+STEPS = ((0, 3), (3, 3), (6, 3))
 VMEM = 16 * 1024 * 1024
 VMEM_LARGE = 44 * 1024 * 1024
 VMEM_BACKWARD = 28 * 1024 * 1024
@@ -47,22 +47,6 @@
 
 def params(limit=VMEM):
     return pltpu.CompilerParams(vmem_limit_bytes=limit)
-
-
-def tile_kernel(emb_ref, tile_ref):
-    rows = emb_ref.shape[0]
-    for half in range(2):
-        tile_ref[:, half] = emb_ref[:, half * 128 : half * 128 + 128].reshape(rows // 8, 8, 128)
-
-
-def as_tiles(embeddings):
-    rows, _ = embeddings.shape
-    return pl.pallas_call(
-        tile_kernel,
-        out_shape=jax.ShapeDtypeStruct((rows // 8, 2, 8, 128), jnp.float32),
-        compiler_params=params(),
-        name="as_tiles",
-    )(embeddings)
 
 
 def pick_kernel(pairing_ref, pieces_ref, out_ref):
@@ -506,11 +490,12 @@
     left, right = shift(embeddings, 2), shift(embeddings, -2)
     far = (shift(left[:half], 2), shift(right[half:], -2))
     per = rows * width // (groups * 128)
-    pieces = lax.all_to_all(as_tiles(embeddings).reshape(groups, per, 128), "grp", 0, 0, tiled=True)
+    tiles = embeddings.reshape(rows // 8, 8, width // 128, 128).transpose(0, 2, 1, 3)
+    pieces = lax.all_to_all(tiles.reshape(groups, per, 128), "grp", 0, 0, tiled=True)
     ready = prepare("prepare", left, right, embeddings)
-    picked, ready = lax.optimization_barrier((pick(pairing, pieces), ready))
+    picked, ready, mine, same = lax.optimization_barrier((pick(pairing, pieces), ready, embeddings, positive))
     got = lax.all_to_all(picked, "grp", 0, 0, tiled=True)
-    sib, pos_sib = swap(embeddings), swap(positive)
+    sib, pos_sib = swap(mine), swap(same)
 
     both = jnp.concatenate([positive, pos_sib]) - group * block
     owner = both // rows

time: 126 us -> 127 us (level)
  blocking collectives: 12.4 us -> 15.1 us
  Pallas kernels: 39.2 us -> 37.2 us
    ppermute x10, waiting for transfers between devices: 8.35 us -> 11.6 us  [shift(): lax.ppermute(value, 'mem', [(m, (m + by) % members) for m in range(member...]
    all_to_all x1, blocking collectives: 12.4 us -> 15.1 us  [local(): everything = lax.all_to_all(line, 'mem', 0, 0, tiled=True)]
    all_to_all x1, waiting for transfers between devices: 6.21 us -> 4.03 us  [local(): lax.all_to_all(tiles.reshape(groups, per, 128), 'grp', 0, 0, tiled=True)]
    all_to_all x1, waiting for transfers between devices: 5.69 us -> 4.3 us  [local(): got = lax.all_to_all(picked, 'grp', 0, 0, tiled=True)]
  transfers between devices with their start and end apart: 16 -> 16, of which waited for: 7 -> 9; matrix products, arithmetic and copies ran while one was open for 1% -> 1% of each run, Pallas kernels for 20% -> 19%
where the time goes in v8:
time: 127 us; the launch traced here: 126 us
  starting transfers between devices  41.2 us (32%)
  Pallas kernels  37.2 us (29%)
  waiting for transfers between devices  29.6 us (23%)
  blocking collectives  15.1 us (12%)
  local copies, waits for them, and re-layouts  1.91 us (2%)
    ppermute x10, starting transfers between devices, shift(): lax.ppermute(value, 'mem', [(m, (m + by) % members) for m in range(member...  22.5 us
    pallas_call x4, Pallas kernels, backward(): pl.pallas_call(functools.partial(backward_kernel, bands, first), in_specs...  18.4 us
    all_to_all x1, blocking collectives, local(): everything = lax.all_to_all(line, 'mem', 0, 0, tiled=True)  15.1 us
    ppermute x10, waiting for transfers between devices, shift(): lax.ppermute(value, 'mem', [(m, (m + by) % members) for m in range(member...  11.6 us
    all_to_all x1, starting transfers between devices, local(): lax.all_to_all(tiles.reshape(groups, per, 128), 'grp', 0, 0, tiled=True)  7.99 us
    pallas_call x1, Pallas kernels, forward(): pl.pallas_call(forward_kernel, in_specs=[HBM] * 2 + [pl.BlockSpec()] * 3,...  7.42 us
    all_to_all x1, waiting for transfers between devices, local(): everyone = lax.all_to_all(spread, 'grp', 0, 0, tiled=True)  7.14 us
    pallas_call x1, Pallas kernels, own_scores(): pl.pallas_call(own_kernel, in_specs=[HBM] * 2 + [pl.BlockSpec()] * 3, out...  5.4 us
  transfers between devices with their start and end apart: 16, of which 9 were waited for; matrix products, arithmetic and copies ran while one was open for 1% of the time, Pallas kernels for 19%

profile of v8, /device:TPU:8, one launch (start us, length us, event | category | flops | bytes accessed | tf_op | source)
XLA Modules:
  0.0 126.0 jit_solution(18117319961705584569)
XLA Ops:
  0.6 6.4 %collective-permute-start.1 = (f32[384,256]{1,0:T(8,128)}, f32[384,256]{1,0:T(8,128)S(1)}, u32[]{:S(2)}, u32[]{:S(2)}) collective-permute-start(f32[384,256]{1,0:T(8,128)} %emb_ref.1), channel_id=1, source_target_pairs={{0,6},{1,7},{2,0},{3,1},{4,2},{5,3},{6,4},{7,5},{8,14},{9,15},{10,... | collective-permute-start | bytes 1179656 | tf_op jit(solution)/shard_map/ppermute | solution.py:485
  7.0 8.0 %all-to-all-start = ((f32[32,24,128]{2,1,0:T(8,128)}), f32[32,24,128]{2,1,0:T(8,128)S(1)}, u32[]{:S(2)}, u32[]{:S(2)}) async-start(f32[32,24,128]{2,1,0:T(8,128)} %bitcast.6), calls=%async_computation | async-start | bytes 786432 | tf_op jit(solution)/shard_map/all_to_all | solution.py:494
  15.7 8.4 %collective-permute-done.1.refs_1_ = f32[384,256]{1,0:T(8,128)S(1)} collective-permute-done((f32[384,256]{1,0:T(8,128)}, f32[384,256]{1,0:T(8,128)S(1)}, u32[]{:S(2)}, u32[]{:S(2)}) %collective-permute-start.1) | collective-permute-done | bytes 393248 | tf_op jit(solution)/shard_map/ppermute | solution.py:485
  24.2 4.6 %collective-permute-start.3 = (f32[192,256]{1,0:T(8,128)S(1)}, f32[192,256]{1,0:T(8,128)S(1)}, u32[]{:S(2)}, u32[]{:S(2)}) collective-permute-start(f32[192,256]{1,0:T(8,128)S(1)} %slice.9), channel_id=1, source_target_pairs={{0,6},{1,7},{2,0},{3,1},{4,2},{5,3},{6,4},{7,5},{8,14},{9,15},{10,... | collective-permute-start | bytes 589832 | tf_op jit(solution)/shard_map/ppermute | solution.py:485
  30.0 1.7 %prepare.1.ready = bf16[1152,768]{1,0:T(8,128)(2,1)} custom-call(f32[384,256]{1,0:T(8,128)S(1)} %collective-permute-done.refs_0_, f32[384,256]{1,0:T(8,128)S(1)} %collective-permute-done.1.refs_1_, f32[384,256]{1,0:T(8,128)S(1)} %copy-done), custom_call_target="tpu_custom_call" | custom-call | flops 20000000000 | bytes 2359296 | tf_op jit(solution)/shard_map/prepare/pallas_call | solution.py:200
  31.7 4.0 %all-to-all-done.pieces_ref = f32[32,24,128]{2,1,0:T(8,128)S(1)} async-done(((f32[32,24,128]{2,1,0:T(8,128)}), f32[32,24,128]{2,1,0:T(8,128)S(1)}, u32[]{:S(2)}, u32[]{:S(2)}) %all-to-all-start) | async-done | bytes 393248 | tf_op jit(solution)/shard_map/all_to_all | solution.py:494
  35.8 1.5 %pick.1 = f32[32,48,128]{2,1,0:T(8,128)} custom-call(s32[2,32]{1,0:T(2,128)S(1)} %copy-done.2, f32[32,24,128]{2,1,0:T(8,128)S(1)} %all-to-all-done.pieces_ref), custom_call_target="tpu_custom_call" | custom-call | tf_op jit(solution)/shard_map/pick/pallas_call | solution.py:61
  37.2 4.8 %all-to-all-start.1 = ((f32[32,48,128]{2,1,0:T(8,128)}), f32[32,48,128]{2,1,0:T(8,128)S(1)}, u32[]{:S(2)}, u32[]{:S(2)}) async-start(f32[32,48,128]{2,1,0:T(8,128)} %pick.1), calls=%async_computation.1 | async-start | bytes 1572864 | tf_op jit(solution)/shard_map/all_to_all | solution.py:497
  44.0 5.4 %own_scores.1 = (bf16[3,256,512]{2,1,0:T(8,128)(2,1)}, f32[3,4,384,256]{3,2,1,0:T(8,128)}, f32[2,1536]{1,0:T(2,128)S(1)}) custom-call(bf16[1152,768]{1,0:T(8,128)(2,1)} %prepare.1.ready, bf16[384,768]{1,0:T(8,128)(2,1)} %prepare_far.1.ready_far, f32[384,256]{1,0:T(8,128)S(1)} %copy-done.1, f32[384,256]{1,0:T(8,128)S(1)} %collective-permute-done.4.sib, ...), custom_call_target="tpu_custom_call" | custom-call | flops 1811939328 | bytes 4718592 | tf_op jit(solution)/shard_map/own_scores/pallas_call | solution.py:168
  49.4 4.3 %all-to-all-done.1.got = f32[32,48,128]{2,1,0:T(8,128)S(1)} async-done(((f32[32,48,128]{2,1,0:T(8,128)}), f32[32,48,128]{2,1,0:T(8,128)S(1)}, u32[]{:S(2)}, u32[]{:S(2)}) %all-to-all-start.1) | async-done | bytes 786464 | tf_op jit(solution)/shard_map/all_to_all | solution.py:497
  53.7 2.3 %collective-permute-done.6.got_sib = f32[32,48,128]{2,1,0:T(8,128)S(1)} collective-permute-done((f32[32,48,128]{2,1,0:T(8,128)S(1)}, f32[32,48,128]{2,1,0:T(8,128)S(1)}, u32[]{:S(2)}, u32[]{:S(2)}) %collective-permute-start.6) | collective-permute-done | bytes 786464 | tf_op jit(solution)/shard_map/ppermute | solution.py:488
  56.0 7.4 %forward.1 = (f32[6,4,384,256]{3,2,1,0:T(8,128)}, bf16[6,256,512]{2,1,0:T(8,128)(2,1)}, f32[8,2,1536]{2,1,0:T(2,128)S(1)}) custom-call(bf16[1152,768]{1,0:T(8,128)(2,1)} %prepare.1.ready, bf16[384,768]{1,0:T(8,128)(2,1)} %prepare_far.1.ready_far, f32[2,1536]{1,0:T(2,128)S(1)} %get-tuple-element.32.line_in, f32[32,48,128]{2,1,0:T(8,128)S(1)} %all-to-all-done.1.got, ...), custom_call_target="tpu_custom_call" | custom-call | flops 3623878656 | bytes 9437184 | tf_op jit(solution)/shard_map/forward/pallas_call | solution.py:278
  63.5 15.1 %all_to_all.20.all_ref = f32[8,2,1536]{2,1,0:T(2,128)S(1)} all-to-all(f32[8,2,1536]{2,1,0:T(2,128)S(1)} %get-tuple-element.34), channel_id=1, replica_groups=mesh['grp'=32,'mem'=8] {'mem'}, dimensions={0} | all-to-all | bytes 196608 | tf_op jit(solution)/shard_map/all_to_all | solution.py:511
  79.2 5.3 %all-to-all-start.3 = ((f32[32,1,768]{2,1,0:T(1,128)}), f32[32,1,768]{2,1,0:T(1,128)S(1)}, u32[]{:S(2)}, u32[]{:S(2)}) async-start(f32[32,1,768]{2,1,0:T(1,128)} %get-tuple-element.37), calls=%async_computation.3 | async-start | bytes 196608 | tf_op jit(solution)/shard_map/all_to_all | solution.py:513
  84.8 7.1 %all-to-all-done.3.everyone_ref = f32[32,1,768]{2,1,0:T(1,128)S(1)} async-done(((f32[32,1,768]{2,1,0:T(1,128)}), f32[32,1,768]{2,1,0:T(1,128)S(1)}, u32[]{:S(2)}, u32[]{:S(2)}) %all-to-all-start.3) | async-done | bytes 98336 | tf_op jit(solution)/shard_map/all_to_all | solution.py:513
  91.9 4.8 %backward_3_0.1 = (bf16[9,256,512]{2,1,0:T(8,128)(2,1)S(1)}, f32[192,256]{1,0:T(8,128)S(1)}, f32[192,256]{1,0:T(8,128)S(1)}) custom-call(s32[2]{0:T(128)S(1)} %dynamic-slice_reduce_fusion.partner_ref, f32[1,1536]{1,0:T(1,128)S(1)} %get-tuple-element.35.row_ref, f32[1,768]{1,0:T(1,128)S(1)} %get-tuple-element.36.own_ref, ...), custom_call_target="tpu_custom_call" | custom-call | flops 1358954496 | bytes 3538944 | tf_op jit(solution)/shard_map/backward_3_0/pallas_call | solution.py:421
  97.4 3.4 %collective-permute-start.8 = (f32[192,256]{1,0:T(8,128)S(1)}, f32[192,256]{1,0:T(8,128)S(1)}, u32[]{:S(2)}, u32[]{:S(2)}) collective-permute-start(f32[192,256]{1,0:T(8,128)S(1)} %get-tuple-element.46), channel_id=1, source_target_pairs={{0,6},{1,7},{2,0},{3,1},{4,2},{5,3},{6,4},{7,5},{8,14},{9,15},{10,... | collective-permute-start | bytes 589832 | tf_op jit(solution)/shard_map/ppermute | solution.py:485
  100.9 4.6 %backward_0_0.1 = (f32[192,256]{1,0:T(8,128)S(1)}, f32[192,256]{1,0:T(8,128)S(1)}) custom-call(s32[2]{0:T(128)S(1)} %dynamic-slice_reduce_fusion.partner_ref, f32[1,1536]{1,0:T(1,128)S(1)} %get-tuple-element.35.row_ref, f32[1,768]{1,0:T(1,128)S(1)} %get-tuple-element.36.own_ref, f32[32,1,768]{2,1,0:T(1,128)S(1)} %all-to-all-done.3.everyone_ref, ...), custom_call_target="tpu_custom_call" | custom-call | flops 1358954496 | bytes 3538944 | tf_op jit(solution)/shard_map/backward_0_0/pallas_call | solution.py:421
  105.5 2.9 %collective-permute-start.11 = (f32[192,256]{1,0:T(8,128)S(1)}, f32[192,256]{1,0:T(8,128)S(1)}, u32[]{:S(2)}, u32[]{:S(2)}) collective-permute-start(f32[192,256]{1,0:T(8,128)S(1)} %get-tuple-element.49), channel_id=1, source_target_pairs={{0,2},{1,3},{2,4},{3,5},{4,6},{5,7},{6,0},{7,1},{8,10},{9,11},{10,... | collective-permute-start | bytes 589832 | tf_op jit(solution)/shard_map/ppermute | solution.py:485
  108.5 4.6 %backward_0_192.1 = (f32[192,256]{1,0:T(8,128)S(1)}, f32[192,256]{1,0:T(8,128)S(1)}) custom-call(s32[2]{0:T(128)S(1)} %dynamic-slice_reduce_fusion.partner_ref, f32[1,1536]{1,0:T(1,128)S(1)} %get-tuple-element.35.row_ref, f32[1,768]{1,0:T(1,128)S(1)} %get-tuple-element.36.own_ref, f32[32,1,768]{2,1,0:T(1,128)S(1)} %all-to-all-done.3.everyone_ref, ...), custom_call_target="tpu_custom_call" | custom-call | flops 1358954496 | bytes 3538944 | tf_op jit(solution)/shard_map/backward_0_192/pallas_call | solution.py:421
  113.9 3.4 %collective-permute-start.12 = (f32[192,256]{1,0:T(8,128)S(1)}, f32[192,256]{1,0:T(8,128)S(1)}, u32[]{:S(2)}, u32[]{:S(2)}) collective-permute-start(f32[192,256]{1,0:T(8,128)S(1)} %get-tuple-element.50), channel_id=1, source_target_pairs={{0,6},{1,7},{2,0},{3,1},{4,2},{5,3},{6,4},{7,5},{8,14},{9,15},{10,... | collective-permute-start | bytes 589832 | tf_op jit(solution)/shard_map/ppermute | solution.py:485
  117.3 4.5 %backward_2_0.1.run_ref = f32[384,256]{1,0:T(8,128)S(1)} custom-call(s32[2]{0:T(128)S(1)} %dynamic-slice_reduce_fusion.partner_ref, f32[1,1536]{1,0:T(1,128)S(1)} %get-tuple-element.35.row_ref, f32[1,768]{1,0:T(1,128)S(1)} %get-tuple-element.36.own_ref, f32[32,1,768]{2,1,0:T(1,128)S(1)} %all-to-all-done.3.everyone_ref, ...), custom_call_target="tpu_custom_call" | custom-call | flops 1358954496 | bytes 3538944 | tf_op jit(solution)/shard_map/backward_2_0/pallas_call | solution.py:421
  121.9 1.4 %collective-permute-done.9.low0 = f32[192,256]{1,0:T(8,128)S(1)} collective-permute-done((f32[192,256]{1,0:T(8,128)S(1)}, f32[192,256]{1,0:T(8,128)S(1)}, u32[]{:S(2)}, u32[]{:S(2)}) %collective-permute-start.9) | collective-permute-done | bytes 196640 | tf_op jit(solution)/shard_map/ppermute | solution.py:485
  123.3 1.7 %collective-permute-done.12.high1 = f32[192,256]{1,0:T(8,128)S(1)} collective-permute-done((f32[192,256]{1,0:T(8,128)S(1)}, f32[192,256]{1,0:T(8,128)S(1)}, u32[]{:S(2)}, u32[]{:S(2)}) %collective-permute-start.12) | collective-permute-done | bytes 196640 | tf_op jit(solution)/shard_map/ppermute | solution.py:485
  (35 shorter events, 7.4 us)
Async XLA Ops:
  0.6 23.5 %collective-permute-start.1 = (f32[384,256]{1,0:T(8,128)}, f32[384,256]{1,0:T(8,128)S(1)}, u32[]{:S(2)}, u32[]{:S(2)}) collective-permute-start(f32[384,256]{1,0:T(8,128)} %emb_ref.1), channel_id=1, source_target_pairs={{0,6},{1,7},{2,0},{3,1},{4,2},{5,3},{6,4},{7,5},{8,14},{9,15},{10,... | collective-permute-start | bytes 1179656 | tf_op jit(solution)/shard_map/ppermute | solution.py:485
  7.0 21.9 %collective-permute-start = (f32[384,256]{1,0:T(8,128)}, f32[384,256]{1,0:T(8,128)S(1)}, u32[]{:S(2)}, u32[]{:S(2)}) collective-permute-start(f32[384,256]{1,0:T(8,128)} %emb_ref.1), channel_id=1, source_target_pairs={{0,2},{1,3},{2,4},{3,5},{4,6},{5,7},{6,0},{7,1},{8,10},{9,11},{10,... | collective-permute-start | bytes 1179656 | tf_op jit(solution)/shard_map/ppermute | solution.py:485
  7.0 28.7 %all-to-all-start = ((f32[32,24,128]{2,1,0:T(8,128)}), f32[32,24,128]{2,1,0:T(8,128)S(1)}, u32[]{:S(2)}, u32[]{:S(2)}) async-start(f32[32,24,128]{2,1,0:T(8,128)} %bitcast.6), calls=%async_computation | async-start | bytes 786432 | tf_op jit(solution)/shard_map/all_to_all | solution.py:494
  24.2 18.5 %collective-permute-start.3 = (f32[192,256]{1,0:T(8,128)S(1)}, f32[192,256]{1,0:T(8,128)S(1)}, u32[]{:S(2)}, u32[]{:S(2)}) collective-permute-start(f32[192,256]{1,0:T(8,128)S(1)} %slice.9), channel_id=1, source_target_pairs={{0,6},{1,7},{2,0},{3,1},{4,2},{5,3},{6,4},{7,5},{8,14},{9,15},{10,... | collective-permute-start | bytes 589832 | tf_op jit(solution)/shard_map/ppermute | solution.py:485
  28.9 13.8 %collective-permute-start.2 = (f32[192,256]{1,0:T(8,128)S(1)}, f32[192,256]{1,0:T(8,128)S(1)}, u32[]{:S(2)}, u32[]{:S(2)}) collective-permute-start(f32[192,256]{1,0:T(8,128)S(1)} %slice.8), channel_id=1, source_target_pairs={{0,2},{1,3},{2,4},{3,5},{4,6},{5,7},{6,0},{7,1},{8,10},{9,11},{10,... | collective-permute-start | bytes 589832 | tf_op jit(solution)/shard_map/ppermute | solution.py:485
  29.0 1.0 copy-start
  30.0 5.8 %copy-start.2 = (s32[2,32]{1,0:T(2,128)S(1)}, s32[2,32]{1,0:T(2,128)}, u32[]{:S(2)}) copy-start(s32[2,32]{1,0:T(2,128)} %pairing_ref.1) | copy-start | bytes 772
  31.7 10.4 %copy-start.3 = (s32[384]{0:T(512)S(1)}, s32[384]{0:T(512)}, u32[]{:S(2)}) copy-start(s32[384]{0:T(512)} %param.4) | copy-start | bytes 4612
  31.7 10.5 %copy-start.1 = (f32[384,256]{1,0:T(8,128)S(1)}, f32[384,256]{1,0:T(8,128)}, u32[]{:S(2)}) copy-start(f32[384,256]{1,0:T(8,128)} %emb_ref.1) | copy-start | bytes 1179652
  37.2 16.5 %all-to-all-start.1 = ((f32[32,48,128]{2,1,0:T(8,128)}), f32[32,48,128]{2,1,0:T(8,128)S(1)}, u32[]{:S(2)}, u32[]{:S(2)}) async-start(f32[32,48,128]{2,1,0:T(8,128)} %pick.1), calls=%async_computation.1 | async-start | bytes 1572864 | tf_op jit(solution)/shard_map/all_to_all | solution.py:497
  42.1 1.6 %collective-permute-start.5 = (s32[384]{0:T(512)S(1)}, s32[384]{0:T(512)S(1)}, u32[]{:S(2)}, u32[]{:S(2)}) collective-permute-start(s32[384]{0:T(512)S(1)} %copy-done.3), channel_id=1, source_target_pairs={{0,1},{1,0},{2,3},{3,2},{4,5},{5,4},{6,7},{7,6},{8,9},{9,8},{10,11... | collective-permute-start | bytes 4616 | tf_op jit(solution)/shard_map/ppermute | solution.py:488
  42.2 1.8 %collective-permute-start.4 = (f32[384,256]{1,0:T(8,128)S(1)}, f32[384,256]{1,0:T(8,128)S(1)}, u32[]{:S(2)}, u32[]{:S(2)}) collective-permute-start(f32[384,256]{1,0:T(8,128)S(1)} %copy-done.1), channel_id=1, source_target_pairs={{0,1},{1,0},{2,3},{3,2},{4,5},{5,4},{6,7},{7,6},{8,9},{9,8},{10,11... | collective-permute-start | bytes 1179656 | tf_op jit(solution)/shard_map/ppermute | solution.py:488
  53.7 2.3 %collective-permute-start.6 = (f32[32,48,128]{2,1,0:T(8,128)S(1)}, f32[32,48,128]{2,1,0:T(8,128)S(1)}, u32[]{:S(2)}, u32[]{:S(2)}) collective-permute-start(f32[32,48,128]{2,1,0:T(8,128)S(1)} %all-to-all-done.1.got), channel_id=1, source_target_pairs={{0,1},{1,0},{2,3},{3,2},{4,5},{5,4},{6,7},{7,6},{8,9},{9,8},{10,11... | collective-permute-start | bytes 2359304 | tf_op jit(solution)/shard_map/ppermute | solution.py:488
  79.2 12.7 %all-to-all-start.3 = ((f32[32,1,768]{2,1,0:T(1,128)}), f32[32,1,768]{2,1,0:T(1,128)S(1)}, u32[]{:S(2)}, u32[]{:S(2)}) async-start(f32[32,1,768]{2,1,0:T(1,128)} %get-tuple-element.37), calls=%async_computation.3 | async-start | bytes 196608 | tf_op jit(solution)/shard_map/all_to_all | solution.py:513
  96.7 16.4 %collective-permute-start.7 = (f32[192,256]{1,0:T(8,128)S(1)}, f32[192,256]{1,0:T(8,128)S(1)}, u32[]{:S(2)}, u32[]{:S(2)}) collective-permute-start(f32[192,256]{1,0:T(8,128)S(1)} %get-tuple-element.44), channel_id=1, source_target_pairs={{0,2},{1,3},{2,4},{3,5},{4,6},{5,7},{6,0},{7,1},{8,10},{9,11},{10,... | collective-permute-start | bytes 589832 | tf_op jit(solution)/shard_map/ppermute | solution.py:485
  97.4 15.6 %collective-permute-start.8 = (f32[192,256]{1,0:T(8,128)S(1)}, f32[192,256]{1,0:T(8,128)S(1)}, u32[]{:S(2)}, u32[]{:S(2)}) collective-permute-start(f32[192,256]{1,0:T(8,128)S(1)} %get-tuple-element.46), channel_id=1, source_target_pairs={{0,6},{1,7},{2,0},{3,1},{4,2},{5,3},{6,4},{7,5},{8,14},{9,15},{10,... | collective-permute-start | bytes 589832 | tf_op jit(solution)/shard_map/ppermute | solution.py:485
  105.5 16.4 %collective-permute-start.10 = (f32[192,256]{1,0:T(8,128)S(1)}, f32[192,256]{1,0:T(8,128)S(1)}, u32[]{:S(2)}, u32[]{:S(2)}) collective-permute-start(f32[192,256]{1,0:T(8,128)S(1)} %get-tuple-element.48), channel_id=1, source_target_pairs={{0,6},{1,7},{2,0},{3,1},{4,2},{5,3},{6,4},{7,5},{8,14},{9,15},{10,... | collective-permute-start | bytes 589832 | tf_op jit(solution)/shard_map/ppermute | solution.py:485
  105.5 16.3 %collective-permute-start.11 = (f32[192,256]{1,0:T(8,128)S(1)}, f32[192,256]{1,0:T(8,128)S(1)}, u32[]{:S(2)}, u32[]{:S(2)}) collective-permute-start(f32[192,256]{1,0:T(8,128)S(1)} %get-tuple-element.49), channel_id=1, source_target_pairs={{0,2},{1,3},{2,4},{3,5},{4,6},{5,7},{6,0},{7,1},{8,10},{9,11},{10,... | collective-permute-start | bytes 589832 | tf_op jit(solution)/shard_map/ppermute | solution.py:485
  113.1 10.2 %collective-permute-start.9 = (f32[192,256]{1,0:T(8,128)S(1)}, f32[192,256]{1,0:T(8,128)S(1)}, u32[]{:S(2)}, u32[]{:S(2)}) collective-permute-start(f32[192,256]{1,0:T(8,128)S(1)} %get-tuple-element.47), channel_id=1, source_target_pairs={{0,2},{1,3},{2,4},{3,5},{4,6},{5,7},{6,0},{7,1},{8,10},{9,11},{10,... | collective-permute-start | bytes 589832 | tf_op jit(solution)/shard_map/ppermute | solution.py:485
  113.9 11.1 %collective-permute-start.12 = (f32[192,256]{1,0:T(8,128)S(1)}, f32[192,256]{1,0:T(8,128)S(1)}, u32[]{:S(2)}, u32[]{:S(2)}) collective-permute-start(f32[192,256]{1,0:T(8,128)S(1)} %get-tuple-element.50), channel_id=1, source_target_pairs={{0,6},{1,7},{2,0},{3,1},{4,2},{5,3},{6,4},{7,5},{8,14},{9,15},{10,... | collective-permute-start | bytes 589832 | tf_op jit(solution)/shard_map/ppermute | solution.py:485

commit v9 on v8

--- a/solution.py
+++ b/solution.py
@@ -128,7 +128,7 @@
     at = ready.shape[0]
     ready_copies = [
         pltpu.make_async_copy(ready, left_ref.at[pl.ds(0, at)], in_sem.at[0]),
-        pltpu.make_async_copy(ready_far, left_ref.at[pl.ds(at, SLICE)], in_sem.at[1]),
+        pltpu.make_async_copy(ready_far, left_ref.at[pl.ds(at, ready_far.shape[0])], in_sem.at[1]),
     ]
     for copy in ready_copies:
         copy.start()
@@ -218,7 +218,7 @@
     at = ready.shape[0]
     ready_copies = [
         pltpu.make_async_copy(ready, left_ref.at[pl.ds(0, at)], in_sem.at[0]),
-        pltpu.make_async_copy(ready_far, left_ref.at[pl.ds(at, SLICE)], in_sem.at[1]),
+        pltpu.make_async_copy(ready_far, left_ref.at[pl.ds(at, ready_far.shape[0])], in_sem.at[1]),
     ]
     for copy in ready_copies:
         copy.start()
@@ -492,10 +492,10 @@
     per = rows * width // (groups * 128)
     tiles = embeddings.reshape(rows // 8, 8, width // 128, 128).transpose(0, 2, 1, 3)
     pieces = lax.all_to_all(tiles.reshape(groups, per, 128), "grp", 0, 0, tiled=True)
-    ready = prepare("prepare", left, right, embeddings)
-    picked, ready, mine, same = lax.optimization_barrier((pick(pairing, pieces), ready, embeddings, positive))
+    ready = prepare("prepare", left, right)
+    picked, ready = lax.optimization_barrier((pick(pairing, pieces), ready))
     got = lax.all_to_all(picked, "grp", 0, 0, tiled=True)
-    sib, pos_sib = swap(mine), swap(same)
+    sib, pos_sib = swap(embeddings), swap(positive)
 
     both = jnp.concatenate([positive, pos_sib]) - group * block
     owner = both // rows
@@ -503,7 +503,7 @@
     order = jnp.where(turn == 0, SELF, jnp.where(turn == 3, 0, jnp.where(turn == 1, 1, 3)))
     pos = jnp.where(owner % 2 == member % 2, order * rows + both % rows, -1).reshape(1, 2 * rows)
 
-    ready_far = prepare("prepare_far", *far)
+    ready_far = prepare("prepare_far", embeddings, *far)
     c_own, e_own, line = own_scores(ready, ready_far, embeddings, sib, pos)
     got, line = lax.optimization_barrier((got, line))
     e_part, c_part, line = forward(ready, ready_far, line, got, swap(got), members)

time: 127 us -> 127 us (level)
  waiting for transfers between devices: 29.6 us -> 31.1 us
    all_to_all x1, waiting for transfers between devices: 4.3 us -> 6.03 us  [local(): got = lax.all_to_all(picked, 'grp', 0, 0, tiled=True)]
where the time goes in v9:
time: 127 us; the launch traced here: 126 us
  starting transfers between devices  40.5 us (32%)
  Pallas kernels  37.4 us (29%)
  waiting for transfers between devices  31.1 us (24%)
  blocking collectives  15 us (12%)
    ppermute x10, starting transfers between devices, shift(): lax.ppermute(value, 'mem', [(m, (m + by) % members) for m in range(member...  22.5 us
    pallas_call x4, Pallas kernels, backward(): pl.pallas_call(functools.partial(backward_kernel, bands, first), in_specs...  18.4 us
    all_to_all x1, blocking collectives, local(): everything = lax.all_to_all(line, 'mem', 0, 0, tiled=True)  15 us
    ppermute x10, waiting for transfers between devices, shift(): lax.ppermute(value, 'mem', [(m, (m + by) % members) for m in range(member...  10.8 us
    all_to_all x1, starting transfers between devices, local(): lax.all_to_all(tiles.reshape(groups, per, 128), 'grp', 0, 0, tiled=True)  7.99 us
    pallas_call x1, Pallas kernels, forward(): pl.pallas_call(forward_kernel, in_specs=[HBM] * 2 + [pl.BlockSpec()] * 3,...  7.54 us
    all_to_all x1, waiting for transfers between devices, local(): everyone = lax.all_to_all(spread, 'grp', 0, 0, tiled=True)  7.25 us
    all_to_all x1, waiting for transfers between devices, local(): got = lax.all_to_all(picked, 'grp', 0, 0, tiled=True)  6.03 us
  transfers between devices with their start and end apart: 16, of which 9 were waited for; matrix products, arithmetic and copies ran while one was open for 1% of the time, Pallas kernels for 19%

profile of v9, /device:TPU:8, one launch (start us, length us, event | category | flops | bytes accessed | tf_op | source)
XLA Modules:
  0.0 125.8 jit_solution(8931734649482159296)
XLA Ops:
  0.6 6.4 %collective-permute-start.1 = (f32[384,256]{1,0:T(8,128)}, f32[384,256]{1,0:T(8,128)S(1)}, u32[]{:S(2)}, u32[]{:S(2)}) collective-permute-start(f32[384,256]{1,0:T(8,128)} %emb_ref.1), channel_id=1, source_target_pairs={{0,6},{1,7},{2,0},{3,1},{4,2},{5,3},{6,4},{7,5},{8,14},{9,15},{10,... | collective-permute-start | bytes 1179656 | tf_op jit(solution)/shard_map/ppermute | solution.py:485
  7.0 8.0 %all-to-all-start = ((f32[32,24,128]{2,1,0:T(8,128)}), f32[32,24,128]{2,1,0:T(8,128)S(1)}, u32[]{:S(2)}, u32[]{:S(2)}) async-start(f32[32,24,128]{2,1,0:T(8,128)} %bitcast.6), calls=%async_computation | async-start | bytes 786432 | tf_op jit(solution)/shard_map/all_to_all | solution.py:494
  16.5 7.6 %collective-permute-done.1.refs_1_ = f32[384,256]{1,0:T(8,128)S(1)} collective-permute-done((f32[384,256]{1,0:T(8,128)}, f32[384,256]{1,0:T(8,128)S(1)}, u32[]{:S(2)}, u32[]{:S(2)}) %collective-permute-start.1) | collective-permute-done | bytes 393248 | tf_op jit(solution)/shard_map/ppermute | solution.py:485
  24.2 4.6 %collective-permute-start.3 = (f32[192,256]{1,0:T(8,128)S(1)}, f32[192,256]{1,0:T(8,128)S(1)}, u32[]{:S(2)}, u32[]{:S(2)}) collective-permute-start(f32[192,256]{1,0:T(8,128)S(1)} %slice.9), channel_id=1, source_target_pairs={{0,6},{1,7},{2,0},{3,1},{4,2},{5,3},{6,4},{7,5},{8,14},{9,15},{10,... | collective-permute-start | bytes 589832 | tf_op jit(solution)/shard_map/ppermute | solution.py:485
  29.0 1.4 %prepare.1.ready = bf16[768,768]{1,0:T(8,128)(2,1)} custom-call(f32[384,256]{1,0:T(8,128)S(1)} %collective-permute-done.refs_0_, f32[384,256]{1,0:T(8,128)S(1)} %collective-permute-done.1.refs_1_), custom_call_target="tpu_custom_call" | custom-call | flops 20000000000 | bytes 1572864 | tf_op jit(solution)/shard_map/prepare/pallas_call | solution.py:200
  30.4 4.1 %all-to-all-done.pieces_ref = f32[32,24,128]{2,1,0:T(8,128)S(1)} async-done(((f32[32,24,128]{2,1,0:T(8,128)}), f32[32,24,128]{2,1,0:T(8,128)S(1)}, u32[]{:S(2)}, u32[]{:S(2)}) %all-to-all-start) | async-done | bytes 393248 | tf_op jit(solution)/shard_map/all_to_all | solution.py:494
  34.5 1.5 %pick.1 = f32[32,48,128]{2,1,0:T(8,128)} custom-call(s32[2,32]{1,0:T(2,128)S(1)} %copy-done.1, f32[32,24,128]{2,1,0:T(8,128)S(1)} %all-to-all-done.pieces_ref), custom_call_target="tpu_custom_call" | custom-call | tf_op jit(solution)/shard_map/pick/pallas_call | solution.py:61
  36.1 4.9 %all-to-all-start.1 = ((f32[32,48,128]{2,1,0:T(8,128)}), f32[32,48,128]{2,1,0:T(8,128)S(1)}, u32[]{:S(2)}, u32[]{:S(2)}) async-start(f32[32,48,128]{2,1,0:T(8,128)} %pick.1), calls=%async_computation.1 | async-start | bytes 1572864 | tf_op jit(solution)/shard_map/all_to_all | solution.py:497
  41.0 1.4 %prepare_far.1.ready_far = bf16[768,768]{1,0:T(8,128)(2,1)} custom-call(f32[384,256]{1,0:T(8,128)S(1)} %copy-done, f32[192,256]{1,0:T(8,128)S(1)} %collective-permute-done.2.refs_1_, f32[192,256]{1,0:T(8,128)S(1)} %collective-permute-done.3.refs_2_), custom_call_target="tpu_custom_call" | custom-call | flops 20000000000 | bytes 1572864 | tf_op jit(solution)/shard_map/prepare_far/pallas_call | solution.py:200
  42.4 5.4 %own_scores.1 = (bf16[3,256,512]{2,1,0:T(8,128)(2,1)}, f32[3,4,384,256]{3,2,1,0:T(8,128)}, f32[2,1536]{1,0:T(2,128)S(1)}) custom-call(bf16[768,768]{1,0:T(8,128)(2,1)} %prepare.1.ready, bf16[768,768]{1,0:T(8,128)(2,1)} %prepare_far.1.ready_far, f32[384,256]{1,0:T(8,128)S(1)} %copy-done, f32[384,256]{1,0:T(8,128)S(1)} %collective-permute-done.4.sib, ...), custom_call_target="tpu_custom_call" | custom-call | flops 1811939328 | bytes 4718592 | tf_op jit(solution)/shard_map/own_scores/pallas_call | solution.py:168
  47.8 6.0 %all-to-all-done.1.got = f32[32,48,128]{2,1,0:T(8,128)S(1)} async-done(((f32[32,48,128]{2,1,0:T(8,128)}), f32[32,48,128]{2,1,0:T(8,128)S(1)}, u32[]{:S(2)}, u32[]{:S(2)}) %all-to-all-start.1) | async-done | bytes 786464 | tf_op jit(solution)/shard_map/all_to_all | solution.py:497
  53.8 2.3 %collective-permute-done.6.got_sib = f32[32,48,128]{2,1,0:T(8,128)S(1)} collective-permute-done((f32[32,48,128]{2,1,0:T(8,128)S(1)}, f32[32,48,128]{2,1,0:T(8,128)S(1)}, u32[]{:S(2)}, u32[]{:S(2)}) %collective-permute-start.6) | collective-permute-done | bytes 786464 | tf_op jit(solution)/shard_map/ppermute | solution.py:488
  56.1 7.5 %forward.1 = (f32[6,4,384,256]{3,2,1,0:T(8,128)}, bf16[6,256,512]{2,1,0:T(8,128)(2,1)}, f32[8,2,1536]{2,1,0:T(2,128)S(1)}) custom-call(bf16[768,768]{1,0:T(8,128)(2,1)} %prepare.1.ready, bf16[768,768]{1,0:T(8,128)(2,1)} %prepare_far.1.ready_far, f32[2,1536]{1,0:T(2,128)S(1)} %get-tuple-element.28.line_in, f32[32,48,128]{2,1,0:T(8,128)S(1)} %all-to-all-done.1.got, ...), custom_call_target="tpu_custom_call" | custom-call | flops 3623878656 | bytes 9437184 | tf_op jit(solution)/shard_map/forward/pallas_call | solution.py:278
  63.7 15.0 %all_to_all.20.all_ref = f32[8,2,1536]{2,1,0:T(2,128)S(1)} all-to-all(f32[8,2,1536]{2,1,0:T(2,128)S(1)} %get-tuple-element.30), channel_id=1, replica_groups=mesh['grp'=32,'mem'=8] {'mem'}, dimensions={0} | all-to-all | bytes 196608 | tf_op jit(solution)/shard_map/all_to_all | solution.py:511
  79.3 5.0 %all-to-all-start.3 = ((f32[32,1,768]{2,1,0:T(1,128)}), f32[32,1,768]{2,1,0:T(1,128)S(1)}, u32[]{:S(2)}, u32[]{:S(2)}) async-start(f32[32,1,768]{2,1,0:T(1,128)} %get-tuple-element.33), calls=%async_computation.3 | async-start | bytes 196608 | tf_op jit(solution)/shard_map/all_to_all | solution.py:513
  84.5 7.2 %all-to-all-done.3.everyone_ref = f32[32,1,768]{2,1,0:T(1,128)S(1)} async-done(((f32[32,1,768]{2,1,0:T(1,128)}), f32[32,1,768]{2,1,0:T(1,128)S(1)}, u32[]{:S(2)}, u32[]{:S(2)}) %all-to-all-start.3) | async-done | bytes 98336 | tf_op jit(solution)/shard_map/all_to_all | solution.py:513
  91.7 4.8 %backward_3_0.1 = (bf16[9,256,512]{2,1,0:T(8,128)(2,1)S(1)}, f32[192,256]{1,0:T(8,128)S(1)}, f32[192,256]{1,0:T(8,128)S(1)}) custom-call(s32[2]{0:T(128)S(1)} %dynamic-slice_reduce_fusion.partner_ref, f32[1,1536]{1,0:T(1,128)S(1)} %get-tuple-element.31.row_ref, f32[1,768]{1,0:T(1,128)S(1)} %get-tuple-element.32.own_ref, ...), custom_call_target="tpu_custom_call" | custom-call | flops 1358954496 | bytes 3538944 | tf_op jit(solution)/shard_map/backward_3_0/pallas_call | solution.py:421
  97.5 3.2 %collective-permute-start.8 = (f32[192,256]{1,0:T(8,128)S(1)}, f32[192,256]{1,0:T(8,128)S(1)}, u32[]{:S(2)}, u32[]{:S(2)}) collective-permute-start(f32[192,256]{1,0:T(8,128)S(1)} %get-tuple-element.42), channel_id=1, source_target_pairs={{0,6},{1,7},{2,0},{3,1},{4,2},{5,3},{6,4},{7,5},{8,14},{9,15},{10,... | collective-permute-start | bytes 589832 | tf_op jit(solution)/shard_map/ppermute | solution.py:485
  100.7 4.6 %backward_0_0.1 = (f32[192,256]{1,0:T(8,128)S(1)}, f32[192,256]{1,0:T(8,128)S(1)}) custom-call(s32[2]{0:T(128)S(1)} %dynamic-slice_reduce_fusion.partner_ref, f32[1,1536]{1,0:T(1,128)S(1)} %get-tuple-element.31.row_ref, f32[1,768]{1,0:T(1,128)S(1)} %get-tuple-element.32.own_ref, f32[32,1,768]{2,1,0:T(1,128)S(1)} %all-to-all-done.3.everyone_ref, ...), custom_call_target="tpu_custom_call" | custom-call | flops 1358954496 | bytes 3538944 | tf_op jit(solution)/shard_map/backward_0_0/pallas_call | solution.py:421
  105.4 2.9 %collective-permute-start.11 = (f32[192,256]{1,0:T(8,128)S(1)}, f32[192,256]{1,0:T(8,128)S(1)}, u32[]{:S(2)}, u32[]{:S(2)}) collective-permute-start(f32[192,256]{1,0:T(8,128)S(1)} %get-tuple-element.45), channel_id=1, source_target_pairs={{0,2},{1,3},{2,4},{3,5},{4,6},{5,7},{6,0},{7,1},{8,10},{9,11},{10,... | collective-permute-start | bytes 589832 | tf_op jit(solution)/shard_map/ppermute | solution.py:485
  108.3 4.6 %backward_0_192.1 = (f32[192,256]{1,0:T(8,128)S(1)}, f32[192,256]{1,0:T(8,128)S(1)}) custom-call(s32[2]{0:T(128)S(1)} %dynamic-slice_reduce_fusion.partner_ref, f32[1,1536]{1,0:T(1,128)S(1)} %get-tuple-element.31.row_ref, f32[1,768]{1,0:T(1,128)S(1)} %get-tuple-element.32.own_ref, f32[32,1,768]{2,1,0:T(1,128)S(1)} %all-to-all-done.3.everyone_ref, ...), custom_call_target="tpu_custom_call" | custom-call | flops 1358954496 | bytes 3538944 | tf_op jit(solution)/shard_map/backward_0_192/pallas_call | solution.py:421
  114.0 3.2 %collective-permute-start.12 = (f32[192,256]{1,0:T(8,128)S(1)}, f32[192,256]{1,0:T(8,128)S(1)}, u32[]{:S(2)}, u32[]{:S(2)}) collective-permute-start(f32[192,256]{1,0:T(8,128)S(1)} %get-tuple-element.46), channel_id=1, source_target_pairs={{0,6},{1,7},{2,0},{3,1},{4,2},{5,3},{6,4},{7,5},{8,14},{9,15},{10,... | collective-permute-start | bytes 589832 | tf_op jit(solution)/shard_map/ppermute | solution.py:485
  117.2 4.5 %backward_2_0.1.run_ref = f32[384,256]{1,0:T(8,128)S(1)} custom-call(s32[2]{0:T(128)S(1)} %dynamic-slice_reduce_fusion.partner_ref, f32[1,1536]{1,0:T(1,128)S(1)} %get-tuple-element.31.row_ref, f32[1,768]{1,0:T(1,128)S(1)} %get-tuple-element.32.own_ref, f32[32,1,768]{2,1,0:T(1,128)S(1)} %all-to-all-done.3.everyone_ref, ...), custom_call_target="tpu_custom_call" | custom-call | flops 1358954496 | bytes 3538944 | tf_op jit(solution)/shard_map/backward_2_0/pallas_call | solution.py:421
  121.7 2.8 %collective-permute-done.9.low0 = f32[192,256]{1,0:T(8,128)S(1)} collective-permute-done((f32[192,256]{1,0:T(8,128)S(1)}, f32[192,256]{1,0:T(8,128)S(1)}, u32[]{:S(2)}, u32[]{:S(2)}) %collective-permute-start.9) | collective-permute-done | bytes 196640 | tf_op jit(solution)/shard_map/ppermute | solution.py:485
  (31 shorter events, 6.1 us)
Async XLA Ops:
  0.6 23.5 %collective-permute-start.1 = (f32[384,256]{1,0:T(8,128)}, f32[384,256]{1,0:T(8,128)S(1)}, u32[]{:S(2)}, u32[]{:S(2)}) collective-permute-start(f32[384,256]{1,0:T(8,128)} %emb_ref.1), channel_id=1, source_target_pairs={{0,6},{1,7},{2,0},{3,1},{4,2},{5,3},{6,4},{7,5},{8,14},{9,15},{10,... | collective-permute-start | bytes 1179656 | tf_op jit(solution)/shard_map/ppermute | solution.py:485
  7.0 21.9 %collective-permute-start = (f32[384,256]{1,0:T(8,128)}, f32[384,256]{1,0:T(8,128)S(1)}, u32[]{:S(2)}, u32[]{:S(2)}) collective-permute-start(f32[384,256]{1,0:T(8,128)} %emb_ref.1), channel_id=1, source_target_pairs={{0,2},{1,3},{2,4},{3,5},{4,6},{5,7},{6,0},{7,1},{8,10},{9,11},{10,... | collective-permute-start | bytes 1179656 | tf_op jit(solution)/shard_map/ppermute | solution.py:485
  7.0 35.4 %collective-permute-start.4 = (f32[384,256]{1,0:T(8,128)}, f32[384,256]{1,0:T(8,128)S(1)}, u32[]{:S(2)}, u32[]{:S(2)}) collective-permute-start(f32[384,256]{1,0:T(8,128)} %emb_ref.1), channel_id=1, source_target_pairs={{0,1},{1,0},{2,3},{3,2},{4,5},{5,4},{6,7},{7,6},{8,9},{9,8},{10,11... | collective-permute-start | bytes 1179656 | tf_op jit(solution)/shard_map/ppermute | solution.py:488
  7.0 27.5 %all-to-all-start = ((f32[32,24,128]{2,1,0:T(8,128)}), f32[32,24,128]{2,1,0:T(8,128)S(1)}, u32[]{:S(2)}, u32[]{:S(2)}) async-start(f32[32,24,128]{2,1,0:T(8,128)} %bitcast.6), calls=%async_computation | async-start | bytes 786432 | tf_op jit(solution)/shard_map/all_to_all | solution.py:494
  15.0 1.5 %collective-permute-start.5 = (s32[384]{0:T(512)}, s32[384]{0:T(512)S(1)}, u32[]{:S(2)}, u32[]{:S(2)}) collective-permute-start(s32[384]{0:T(512)} %param.4), channel_id=1, source_target_pairs={{0,1},{1,0},{2,3},{3,2},{4,5},{5,4},{6,7},{7,6},{8,9},{9,8},{10,11... | collective-permute-start | bytes 4616 | tf_op jit(solution)/shard_map/ppermute | solution.py:488
  24.2 16.8 %collective-permute-start.3 = (f32[192,256]{1,0:T(8,128)S(1)}, f32[192,256]{1,0:T(8,128)S(1)}, u32[]{:S(2)}, u32[]{:S(2)}) collective-permute-start(f32[192,256]{1,0:T(8,128)S(1)} %slice.9), channel_id=1, source_target_pairs={{0,6},{1,7},{2,0},{3,1},{4,2},{5,3},{6,4},{7,5},{8,14},{9,15},{10,... | collective-permute-start | bytes 589832 | tf_op jit(solution)/shard_map/ppermute | solution.py:485
  28.9 5.6 %copy-start.1 = (s32[2,32]{1,0:T(2,128)S(1)}, s32[2,32]{1,0:T(2,128)}, u32[]{:S(2)}) copy-start(s32[2,32]{1,0:T(2,128)} %pairing_ref.1) | copy-start | bytes 772
  28.9 12.1 %collective-permute-start.2 = (f32[192,256]{1,0:T(8,128)S(1)}, f32[192,256]{1,0:T(8,128)S(1)}, u32[]{:S(2)}, u32[]{:S(2)}) collective-permute-start(f32[192,256]{1,0:T(8,128)S(1)} %slice.8), channel_id=1, source_target_pairs={{0,2},{1,3},{2,4},{3,5},{4,6},{5,7},{6,0},{7,1},{8,10},{9,11},{10,... | collective-permute-start | bytes 589832 | tf_op jit(solution)/shard_map/ppermute | solution.py:485
  30.4 10.6 %copy-start = (f32[384,256]{1,0:T(8,128)S(1)}, f32[384,256]{1,0:T(8,128)}, u32[]{:S(2)}) copy-start(f32[384,256]{1,0:T(8,128)} %emb_ref.1) | copy-start | bytes 1179652
  36.1 17.8 %all-to-all-start.1 = ((f32[32,48,128]{2,1,0:T(8,128)}), f32[32,48,128]{2,1,0:T(8,128)S(1)}, u32[]{:S(2)}, u32[]{:S(2)}) async-start(f32[32,48,128]{2,1,0:T(8,128)} %pick.1), calls=%async_computation.1 | async-start | bytes 1572864 | tf_op jit(solution)/shard_map/all_to_all | solution.py:497
  53.8 2.3 %collective-permute-start.6 = (f32[32,48,128]{2,1,0:T(8,128)S(1)}, f32[32,48,128]{2,1,0:T(8,128)S(1)}, u32[]{:S(2)}, u32[]{:S(2)}) collective-permute-start(f32[32,48,128]{2,1,0:T(8,128)S(1)} %all-to-all-done.1.got), channel_id=1, source_target_pairs={{0,1},{1,0},{2,3},{3,2},{4,5},{5,4},{6,7},{7,6},{8,9},{9,8},{10,11... | collective-permute-start | bytes 2359304 | tf_op jit(solution)/shard_map/ppermute | solution.py:488
  79.3 12.4 %all-to-all-start.3 = ((f32[32,1,768]{2,1,0:T(1,128)}), f32[32,1,768]{2,1,0:T(1,128)S(1)}, u32[]{:S(2)}, u32[]{:S(2)}) async-start(f32[32,1,768]{2,1,0:T(1,128)} %get-tuple-element.33), calls=%async_computation.3 | async-start | bytes 196608 | tf_op jit(solution)/shard_map/all_to_all | solution.py:513
  96.5 16.4 %collective-permute-start.7 = (f32[192,256]{1,0:T(8,128)S(1)}, f32[192,256]{1,0:T(8,128)S(1)}, u32[]{:S(2)}, u32[]{:S(2)}) collective-permute-start(f32[192,256]{1,0:T(8,128)S(1)} %get-tuple-element.40), channel_id=1, source_target_pairs={{0,2},{1,3},{2,4},{3,5},{4,6},{5,7},{6,0},{7,1},{8,10},{9,11},{10,... | collective-permute-start | bytes 589832 | tf_op jit(solution)/shard_map/ppermute | solution.py:485
  97.5 15.3 %collective-permute-start.8 = (f32[192,256]{1,0:T(8,128)S(1)}, f32[192,256]{1,0:T(8,128)S(1)}, u32[]{:S(2)}, u32[]{:S(2)}) collective-permute-start(f32[192,256]{1,0:T(8,128)S(1)} %get-tuple-element.42), channel_id=1, source_target_pairs={{0,6},{1,7},{2,0},{3,1},{4,2},{5,3},{6,4},{7,5},{8,14},{9,15},{10,... | collective-permute-start | bytes 589832 | tf_op jit(solution)/shard_map/ppermute | solution.py:485
  105.3 16.4 %collective-permute-start.10 = (f32[192,256]{1,0:T(8,128)S(1)}, f32[192,256]{1,0:T(8,128)S(1)}, u32[]{:S(2)}, u32[]{:S(2)}) collective-permute-start(f32[192,256]{1,0:T(8,128)S(1)} %get-tuple-element.44), channel_id=1, source_target_pairs={{0,6},{1,7},{2,0},{3,1},{4,2},{5,3},{6,4},{7,5},{8,14},{9,15},{10,... | collective-permute-start | bytes 589832 | tf_op jit(solution)/shard_map/ppermute | solution.py:485
  105.4 16.3 %collective-permute-start.11 = (f32[192,256]{1,0:T(8,128)S(1)}, f32[192,256]{1,0:T(8,128)S(1)}, u32[]{:S(2)}, u32[]{:S(2)}) collective-permute-start(f32[192,256]{1,0:T(8,128)S(1)} %get-tuple-element.45), channel_id=1, source_target_pairs={{0,2},{1,3},{2,4},{3,5},{4,6},{5,7},{6,0},{7,1},{8,10},{9,11},{10,... | collective-permute-start | bytes 589832 | tf_op jit(solution)/shard_map/ppermute | solution.py:485
  112.9 11.5 %collective-permute-start.9 = (f32[192,256]{1,0:T(8,128)S(1)}, f32[192,256]{1,0:T(8,128)S(1)}, u32[]{:S(2)}, u32[]{:S(2)}) collective-permute-start(f32[192,256]{1,0:T(8,128)S(1)} %get-tuple-element.43), channel_id=1, source_target_pairs={{0,2},{1,3},{2,4},{3,5},{4,6},{5,7},{6,0},{7,1},{8,10},{9,11},{10,... | collective-permute-start | bytes 589832 | tf_op jit(solution)/shard_map/ppermute | solution.py:485
  114.0 10.8 %collective-permute-start.12 = (f32[192,256]{1,0:T(8,128)S(1)}, f32[192,256]{1,0:T(8,128)S(1)}, u32[]{:S(2)}, u32[]{:S(2)}) collective-permute-start(f32[192,256]{1,0:T(8,128)S(1)} %get-tuple-element.46), channel_id=1, source_target_pairs={{0,6},{1,7},{2,0},{3,1},{4,2},{5,3},{6,4},{7,5},{8,14},{9,15},{10,... | collective-permute-start | bytes 589832 | tf_op jit(solution)/shard_map/ppermute | solution.py:485

commit v10 on v9

--- a/solution.py
+++ b/solution.py
@@ -49,22 +49,26 @@
     return pltpu.CompilerParams(vmem_limit_bytes=limit)
 
 
-def pick_kernel(pairing_ref, pieces_ref, out_ref):
-    size = pieces_ref.shape[1]
+def pick_kernel(place_ref, same_ref, other_ref, out_ref):
+    size = same_ref.shape[1]
     for which in range(out_ref.shape[1] // size):
-        for group in range(out_ref.shape[0]):
-            out_ref[group, which * size : which * size + size] = pieces_ref[pairing_ref[which, group]]
-
-
-def pick(pairing, pieces):
-    rounds, groups = pairing.shape
+        for column in range(out_ref.shape[0]):
+            place = place_ref[which, column]
+            near = jnp.full((size, 128), place_ref[which + 2, column]) == 1
+            piece = jnp.where(near, same_ref[place], other_ref[place])
+            out_ref[column, which * size : which * size + size] = piece
+
+
+def pick(places, same, other):
+    columns, size, _ = same.shape
+    rounds = places.shape[0] // 2
     return pl.pallas_call(
         pick_kernel,
-        in_specs=[SMEM, pl.BlockSpec()],
-        out_shape=jax.ShapeDtypeStruct((groups, rounds * pieces.shape[1], 128), jnp.float32),
+        in_specs=[SMEM] + [pl.BlockSpec()] * 2,
+        out_shape=jax.ShapeDtypeStruct((columns, rounds * size, 128), jnp.float32),
         compiler_params=params(),
         name="pick",
-    )(pairing, pieces)
+    )(places, same, other)
 
 
 def scaled_rows(refs, out_ref, at=0):
@@ -340,7 +344,7 @@
 
 
 def backward_kernel(
-    bands, first, partner_ref, row_ref, own_ref, everyone_ref, pos_ref, e0_in, e1_in, *refs
+    bands, first, partner_ref, row_ref, own_ref, same_ref, other_ref, pos_ref, e0_in, e1_in, *refs
 ):
     if first:
         c0_in, c1_in, c_ref, refs = refs[0], refs[1], refs[2], refs[3:]
@@ -383,7 +387,11 @@
     row_inv = 1.0 / jnp.concatenate(columns, axis=0)
     row_ids = jnp.concatenate(places, axis=0)
     wide = 2 * SLICE
-    col_inv = [1.0 / own_ref[...]] + [1.0 / everyone_ref[partner_ref[k]] for k in range(2)]
+    col_inv = [1.0 / own_ref[...]]
+    for k in range(2):
+        place = partner_ref[k]
+        near = jnp.full((1, wide), partner_ref[k + 2]) == 1
+        col_inv.append(1.0 / jnp.where(near, same_ref[place], other_ref[place]))
     for step, (start, many) in enumerate(STEPS):
         for copy in copies[step]:
             copy.wait()
@@ -414,13 +422,13 @@
                 ref[...] = part[which * size : which * size + size]
 
 
-def backward(bands, pieces, partners, row_den, own_den, everyone, pos, e0, e1, *cols):
+def backward(bands, pieces, partners, row_den, own_den, same, other, pos, e0, e1, *cols):
     first = len(cols) == 2
     count = 9 * PIECE
     col_shape = [jax.ShapeDtypeStruct((9, PIECE, 2 * WIDTH), jnp.bfloat16)]
     return pl.pallas_call(
         functools.partial(backward_kernel, bands, first),
-        in_specs=[SMEM] + [pl.BlockSpec()] * 4 + [HBM] * 2 + ([HBM] * 2 if first else [pl.BlockSpec()]),
+        in_specs=[SMEM] + [pl.BlockSpec()] * 5 + [HBM] * 2 + ([HBM] * 2 if first else [pl.BlockSpec()]),
         out_shape=col_shape * first + [jax.ShapeDtypeStruct((SLICE // pieces, WIDTH), jnp.float32)] * pieces,
         scratch_shapes=[
             pltpu.VMEM((SLICE, WIDTH), jnp.float32),
@@ -433,7 +441,7 @@
         ),
         compiler_params=params(VMEM_BACKWARD),
         name="backward_%d_%d" % bands[0][:2],
-    )(partners, row_den, own_den, everyone, pos, in_hbm(e0), in_hbm(e1), *(map(in_hbm, cols) if first else cols))
+    )(partners, row_den, own_den, same, other, pos, in_hbm(e0), in_hbm(e1), *(map(in_hbm, cols) if first else cols))
 
 
 def add_kernel(a_ref, b_ref, c_ref, d_ref, ab_ref, cd_ref):
@@ -487,14 +495,28 @@
     def swap(value):
         return lax.ppermute(value, "mem", [(m, m ^ 1) for m in range(members)])
 
+    layers = [list(range(layer, groups, 2)) for layer in range(2)]
+    columns = groups // 2
+
+    def across(value):
+        return lax.all_to_all(value, "grp", 0, 0, tiled=True, axis_index_groups=layers)
+
+    def flip(value):
+        return lax.ppermute(value, "grp", [(g, g ^ 1) for g in range(groups)])
+
+    layer = group % 2
+    mates = jnp.where(layer == 0, pairing[:, 0::2], pairing[:, 1::2])
+    places = jnp.concatenate([mates // 2, (mates % 2 == layer).astype(jnp.int32)])
+    partners = lax.dynamic_index_in_dim(places, group // 2, 1, keepdims=False)
+
     left, right = shift(embeddings, 2), shift(embeddings, -2)
     far = (shift(left[:half], 2), shift(right[half:], -2))
-    per = rows * width // (groups * 128)
+    per = rows * width // (columns * 128)
     tiles = embeddings.reshape(rows // 8, 8, width // 128, 128).transpose(0, 2, 1, 3)
-    pieces = lax.all_to_all(tiles.reshape(groups, per, 128), "grp", 0, 0, tiled=True)
+    pieces = across(tiles.reshape(columns, per, 128))
     ready = prepare("prepare", left, right)
-    picked, ready = lax.optimization_barrier((pick(pairing, pieces), ready))
-    got = lax.all_to_all(picked, "grp", 0, 0, tiled=True)
+    picked, ready = lax.optimization_barrier((pick(places, pieces, flip(pieces)), ready))
+    got = across(picked)
     sib, pos_sib = swap(embeddings), swap(positive)
 
     both = jnp.concatenate([positive, pos_sib]) - group * block
@@ -509,10 +531,10 @@
     e_part, c_part, line = forward(ready, ready_far, line, got, swap(got), members)
 
     everything = lax.all_to_all(line, "mem", 0, 0, tiled=True)
-    row_den, own_den, line, spread = denominators(jnp.reshape(member, (1,)), everything, groups)
-    everyone = lax.all_to_all(spread, "grp", 0, 0, tiled=True)
-
-    shared = (pairing[:, group], row_den, own_den, everyone, pos, e_own, e_part)
+    row_den, own_den, line, spread = denominators(jnp.reshape(member, (1,)), everything, columns)
+    same = across(spread)
+
+    shared = (partners, row_den, own_den, same, flip(same), pos, e_own, e_part)
     cols, far_low, far_high = backward(((3, 0, rows),), 2, *shared, c_own, c_part)
     shared += (cols,)
     far_low, far_high = shift(far_low, 2), shift(far_high, -2)

time: 127 us -> 134 us (1.055)
  blocking collectives: 15 us -> 23.3 us
  waiting for transfers between devices: 31.1 us -> 28.2 us
  local copies, waits for them, and re-layouts: 0.91 us -> 2.46 us
    ppermute x0 -> x2, waiting for transfers between devices: none -> 10.9 us  [flip(): return lax.ppermute(value, 'grp', [(g, g ^ 1) for g in range(groups)])]
    all_to_all x0 -> x1, blocking collectives: none -> 10.8 us  [across(): lax.all_to_all(value, 'grp', 0, 0, tiled=True, axis_index_groups=layers)]
    ppermute x10, waiting for transfers between devices: 10.8 us -> 3.55 us  [shift(): lax.ppermute(value, 'mem', [(m, (m + by) % members) for m in range(member...]
    all_to_all x3 -> x2, waiting for transfers between devices: 17.4 us -> 11.4 us  [across(): lax.all_to_all(value, 'grp', 0, 0, tiled=True, axis_index_groups=layers)]
    ppermute x0 -> x2, starting transfers between devices: none -> 3.5 us  [flip(): return lax.ppermute(value, 'grp', [(g, g ^ 1) for g in range(groups)])]
    all_to_all x3 -> x2, starting transfers between devices: 17.9 us -> 14.8 us  [across(): lax.all_to_all(value, 'grp', 0, 0, tiled=True, axis_index_groups=layers)]
    all_to_all x1, blocking collectives: 15 us -> 12.4 us  [local(): everything = lax.all_to_all(line, 'mem', 0, 0, tiled=True)]
    slice x0 -> x2, local copies, waits for them, and re-layouts: none -> 1.55 us  [local(): mates = jnp.where(layer == 0, pairing[:, 0::2], pairing[:, 1::2])]
  transfers between devices with their start and end apart: 16 -> 17, of which waited for: 9 -> 8; matrix products, arithmetic and copies ran while one was open for 1% -> 2% of each run, Pallas kernels for 19% -> 18%
where the time goes in v10:
time: 134 us; the launch traced here: 133 us
  starting transfers between devices  40.9 us (31%)
  Pallas kernels  36.8 us (27%)
  waiting for transfers between devices  28.2 us (21%)
  blocking collectives  23.3 us (17%)
  local copies, waits for them, and re-layouts  2.46 us (2%)
    ppermute x10, starting transfers between devices, shift(): lax.ppermute(value, 'mem', [(m, (m + by) % members) for m in range(member...  22.5 us
    pallas_call x4, Pallas kernels, backward(): pl.pallas_call(functools.partial(backward_kernel, bands, first), in_specs...  18.4 us
    all_to_all x2, starting transfers between devices, across(): lax.all_to_all(value, 'grp', 0, 0, tiled=True, axis_index_groups=layers)  14.8 us
    all_to_all x1, blocking collectives, local(): everything = lax.all_to_all(line, 'mem', 0, 0, tiled=True)  12.4 us
    all_to_all x2, waiting for transfers between devices, across(): lax.all_to_all(value, 'grp', 0, 0, tiled=True, axis_index_groups=layers)  11.4 us
    ppermute x2, waiting for transfers between devices, flip(): return lax.ppermute(value, 'grp', [(g, g ^ 1) for g in range(groups)])  10.9 us
    all_to_all x1, blocking collectives, across(): lax.all_to_all(value, 'grp', 0, 0, tiled=True, axis_index_groups=layers)  10.8 us
    pallas_call x1, Pallas kernels, forward(): pl.pallas_call(forward_kernel, in_specs=[HBM] * 2 + [pl.BlockSpec()] * 3,...  7.54 us
  transfers between devices with their start and end apart: 17, of which 8 were waited for; matrix products, arithmetic and copies ran while one was open for 2% of the time, Pallas kernels for 18%

profile of v10, /device:TPU:8, one launch (start us, length us, event | category | flops | bytes accessed | tf_op | source)
XLA Modules:
  0.0 132.6 jit_solution(17194797242867692280)
XLA Ops:
  0.7 6.4 %collective-permute-start.2 = (f32[384,256]{1,0:T(8,128)}, f32[384,256]{1,0:T(8,128)S(1)}, u32[]{:S(2)}, u32[]{:S(2)}) collective-permute-start(f32[384,256]{1,0:T(8,128)} %emb_ref.1), channel_id=1, source_target_pairs={{0,6},{1,7},{2,0},{3,1},{4,2},{5,3},{6,4},{7,5},{8,14},{9,15},{10,... | collective-permute-start | bytes 1179656 | tf_op jit(solution)/shard_map/ppermute | solution.py:493
  7.1 7.4 %all-to-all-start = ((f32[16,48,128]{2,1,0:T(8,128)}), f32[16,48,128]{2,1,0:T(8,128)S(1)}, u32[]{:S(2)}, u32[]{:S(2)}) async-start(f32[16,48,128]{2,1,0:T(8,128)} %bitcast.6), calls=%async_computation | async-start | bytes 786432 | tf_op jit(solution)/shard_map/all_to_all | solution.py:502
  16.9 6.1 %all-to-all-done.same_ref = f32[16,48,128]{2,1,0:T(8,128)S(1)} async-done(((f32[16,48,128]{2,1,0:T(8,128)}), f32[16,48,128]{2,1,0:T(8,128)S(1)}, u32[]{:S(2)}, u32[]{:S(2)}) %all-to-all-start) | async-done | bytes 393248 | tf_op jit(solution)/shard_map/all_to_all | solution.py:502
  24.9 4.6 %collective-permute-start.4 = (f32[192,256]{1,0:T(8,128)S(1)}, f32[192,256]{1,0:T(8,128)S(1)}, u32[]{:S(2)}, u32[]{:S(2)}) collective-permute-start(f32[192,256]{1,0:T(8,128)S(1)} %slice.17), channel_id=1, source_target_pairs={{0,6},{1,7},{2,0},{3,1},{4,2},{5,3},{6,4},{7,5},{8,14},{9,15},{10,... | collective-permute-start | bytes 589832 | tf_op jit(solution)/shard_map/ppermute | solution.py:493
  29.6 1.4 %prepare.1.ready = bf16[768,768]{1,0:T(8,128)(2,1)} custom-call(f32[384,256]{1,0:T(8,128)S(1)} %collective-permute-done.1.refs_0_, f32[384,256]{1,0:T(8,128)S(1)} %collective-permute-done.2.refs_1_), custom_call_target="tpu_custom_call" | custom-call | flops 20000000000 | bytes 1572864 | tf_op jit(solution)/shard_map/prepare/pallas_call | solution.py:204
  31.0 9.1 %collective-permute-done.other_ref = f32[16,48,128]{2,1,0:T(8,128)S(1)} collective-permute-done((f32[16,48,128]{2,1,0:T(8,128)S(1)}, f32[16,48,128]{2,1,0:T(8,128)S(1)}, u32[]{:S(2)}, u32[]{:S(2)}) %collective-permute-start) | collective-permute-done | bytes 393248 | tf_op jit(solution)/shard_map/ppermute | solution.py:505
  40.1 1.6 %pick.1 = f32[16,96,128]{2,1,0:T(8,128)} custom-call(s32[4,16]{1,0:T(4,128)S(1)} %pad_add_fusion.place_ref, f32[16,48,128]{2,1,0:T(8,128)S(1)} %all-to-all-done.same_ref, f32[16,48,128]{2,1,0:T(8,128)S(1)} %collective-permute-done.other_ref), custom_call_target="tpu_custom_call" | custom-call | tf_op jit(solution)/shard_map/pick/pallas_call | solution.py:65
  41.6 7.4 %all-to-all-start.1 = ((f32[16,96,128]{2,1,0:T(8,128)}), f32[16,96,128]{2,1,0:T(8,128)S(1)}, u32[]{:S(2)}, u32[]{:S(2)}) async-start(f32[16,96,128]{2,1,0:T(8,128)} %pick.1), calls=%async_computation.1 | async-start | bytes 1572864 | tf_op jit(solution)/shard_map/all_to_all | solution.py:502
  50.5 5.4 %own_scores.1 = (bf16[3,256,512]{2,1,0:T(8,128)(2,1)}, f32[3,4,384,256]{3,2,1,0:T(8,128)}, f32[2,1536]{1,0:T(2,128)S(1)}) custom-call(bf16[768,768]{1,0:T(8,128)(2,1)} %prepare.1.ready, bf16[768,768]{1,0:T(8,128)(2,1)} %prepare_far.1.ready_far, f32[384,256]{1,0:T(8,128)S(1)} %copy-done, f32[384,256]{1,0:T(8,128)S(1)} %collective-permute-done.5.sib, ...), custom_call_target="tpu_custom_call" | custom-call | flops 1811939328 | bytes 4718592 | tf_op jit(solution)/shard_map/own_scores/pallas_call | solution.py:172
  55.9 5.3 %all-to-all-done.1.got = f32[16,96,128]{2,1,0:T(8,128)S(1)} async-done(((f32[16,96,128]{2,1,0:T(8,128)}), f32[16,96,128]{2,1,0:T(8,128)S(1)}, u32[]{:S(2)}, u32[]{:S(2)}) %all-to-all-start.1) | async-done | bytes 786464 | tf_op jit(solution)/shard_map/all_to_all | solution.py:502
  61.2 2.3 %collective-permute-done.7.got_sib = f32[16,96,128]{2,1,0:T(8,128)S(1)} collective-permute-done((f32[16,96,128]{2,1,0:T(8,128)S(1)}, f32[16,96,128]{2,1,0:T(8,128)S(1)}, u32[]{:S(2)}, u32[]{:S(2)}) %collective-permute-start.7) | collective-permute-done | bytes 786464 | tf_op jit(solution)/shard_map/ppermute | solution.py:496
  63.5 7.5 %forward.1 = (f32[6,4,384,256]{3,2,1,0:T(8,128)}, bf16[6,256,512]{2,1,0:T(8,128)(2,1)}, f32[8,2,1536]{2,1,0:T(2,128)S(1)}) custom-call(bf16[768,768]{1,0:T(8,128)(2,1)} %prepare.1.ready, bf16[768,768]{1,0:T(8,128)(2,1)} %prepare_far.1.ready_far, f32[2,1536]{1,0:T(2,128)S(1)} %get-tuple-element.28.line_in, f32[16,96,128]{2,1,0:T(8,128)S(1)} %all-to-all-done.1.got, ...), custom_call_target="tpu_custom_call" | custom-call | flops 3623878656 | bytes 9437184 | tf_op jit(solution)/shard_map/forward/pallas_call | solution.py:282
  71.0 12.4 %all_to_all.20.all_ref = f32[8,2,1536]{2,1,0:T(2,128)S(1)} all-to-all(f32[8,2,1536]{2,1,0:T(2,128)S(1)} %get-tuple-element.30), channel_id=1, replica_groups=mesh['grp'=32,'mem'=8] {'mem'}, dimensions={0} | all-to-all | bytes 196608 | tf_op jit(solution)/shard_map/all_to_all | solution.py:533
  83.5 10.8 %all_to_all.21.same_ref = f32[16,1,768]{2,1,0:T(1,128)S(1)} all-to-all(f32[16,1,768]{2,1,0:T(1,128)S(1)} %get-tuple-element.33), channel_id=1, replica_groups={{0,16,32,48,64,80,96,112,128,144,160,176,192,208,224,240},{8,24,40,56,7..., dimensions={0} | all-to-all | bytes 98304 | tf_op jit(solution)/shard_map/all_to_all | solution.py:502
  94.3 2.5 %collective-permute-start.8 = (f32[16,1,768]{2,1,0:T(1,128)S(1)}, f32[16,1,768]{2,1,0:T(1,128)S(1)}, u32[]{:S(2)}, u32[]{:S(2)}) collective-permute-start(f32[16,1,768]{2,1,0:T(1,128)S(1)} %all_to_all.21.same_ref), channel_id=1, source_target_pairs={{0,8},{8,0},{16,24},{24,16},{32,40},{40,32},{48,56},{56,48},{64,72... | collective-permute-start | bytes 147464 | tf_op jit(solution)/shard_map/ppermute | solution.py:505
  97.0 1.9 %collective-permute-done.8.other_ref = f32[16,1,768]{2,1,0:T(1,128)S(1)} collective-permute-done((f32[16,1,768]{2,1,0:T(1,128)S(1)}, f32[16,1,768]{2,1,0:T(1,128)S(1)}, u32[]{:S(2)}, u32[]{:S(2)}) %collective-permute-start.8) | collective-permute-done | bytes 49184 | tf_op jit(solution)/shard_map/ppermute | solution.py:505
  98.9 4.8 %backward_3_0.1 = (bf16[9,256,512]{2,1,0:T(8,128)(2,1)S(1)}, f32[192,256]{1,0:T(8,128)S(1)}, f32[192,256]{1,0:T(8,128)S(1)}) custom-call(s32[4]{0:T(128)S(1)} %dynamic-slice_reduce_fusion.partner_ref, f32[1,1536]{1,0:T(1,128)S(1)} %get-tuple-element.31.row_ref, f32[1,768]{1,0:T(1,128)S(1)} %get-tuple-element.32.own_ref, ...), custom_call_target="tpu_custom_call" | custom-call | flops 1358954496 | bytes 3538944 | tf_op jit(solution)/shard_map/backward_3_0/pallas_call | solution.py:429
  104.0 3.8 %collective-permute-start.10 = (f32[192,256]{1,0:T(8,128)S(1)}, f32[192,256]{1,0:T(8,128)S(1)}, u32[]{:S(2)}, u32[]{:S(2)}) collective-permute-start(f32[192,256]{1,0:T(8,128)S(1)} %get-tuple-element.42), channel_id=1, source_target_pairs={{0,6},{1,7},{2,0},{3,1},{4,2},{5,3},{6,4},{7,5},{8,14},{9,15},{10,... | collective-permute-start | bytes 589832 | tf_op jit(solution)/shard_map/ppermute | solution.py:493
  107.9 4.6 %backward_0_0.1 = (f32[192,256]{1,0:T(8,128)S(1)}, f32[192,256]{1,0:T(8,128)S(1)}) custom-call(s32[4]{0:T(128)S(1)} %dynamic-slice_reduce_fusion.partner_ref, f32[1,1536]{1,0:T(1,128)S(1)} %get-tuple-element.31.row_ref, f32[1,768]{1,0:T(1,128)S(1)} %get-tuple-element.32.own_ref, f32[16,1,768]{2,1,0:T(1,128)S(1)} %all_to_all.21.same_ref, ...), custom_call_target="tpu_custom_call" | custom-call | flops 1358954496 | bytes 3538944 | tf_op jit(solution)/shard_map/backward_0_0/pallas_call | solution.py:429
  112.5 2.9 %collective-permute-start.13 = (f32[192,256]{1,0:T(8,128)S(1)}, f32[192,256]{1,0:T(8,128)S(1)}, u32[]{:S(2)}, u32[]{:S(2)}) collective-permute-start(f32[192,256]{1,0:T(8,128)S(1)} %get-tuple-element.45), channel_id=1, source_target_pairs={{0,2},{1,3},{2,4},{3,5},{4,6},{5,7},{6,0},{7,1},{8,10},{9,11},{10,... | collective-permute-start | bytes 589832 | tf_op jit(solution)/shard_map/ppermute | solution.py:493
  115.4 4.6 %backward_0_192.1 = (f32[192,256]{1,0:T(8,128)S(1)}, f32[192,256]{1,0:T(8,128)S(1)}) custom-call(s32[4]{0:T(128)S(1)} %dynamic-slice_reduce_fusion.partner_ref, f32[1,1536]{1,0:T(1,128)S(1)} %get-tuple-element.31.row_ref, f32[1,768]{1,0:T(1,128)S(1)} %get-tuple-element.32.own_ref, f32[16,1,768]{2,1,0:T(1,128)S(1)} %all_to_all.21.same_ref, ...), custom_call_target="tpu_custom_call" | custom-call | flops 1358954496 | bytes 3538944 | tf_op jit(solution)/shard_map/backward_0_192/pallas_call | solution.py:429
  120.5 3.8 %collective-permute-start.14 = (f32[192,256]{1,0:T(8,128)S(1)}, f32[192,256]{1,0:T(8,128)S(1)}, u32[]{:S(2)}, u32[]{:S(2)}) collective-permute-start(f32[192,256]{1,0:T(8,128)S(1)} %get-tuple-element.46), channel_id=1, source_target_pairs={{0,6},{1,7},{2,0},{3,1},{4,2},{5,3},{6,4},{7,5},{8,14},{9,15},{10,... | collective-permute-start | bytes 589832 | tf_op jit(solution)/shard_map/ppermute | solution.py:493
  124.3 4.5 %backward_2_0.1.run_ref = f32[384,256]{1,0:T(8,128)S(1)} custom-call(s32[4]{0:T(128)S(1)} %dynamic-slice_reduce_fusion.partner_ref, f32[1,1536]{1,0:T(1,128)S(1)} %get-tuple-element.31.row_ref, f32[1,768]{1,0:T(1,128)S(1)} %get-tuple-element.32.own_ref, f32[16,1,768]{2,1,0:T(1,128)S(1)} %all_to_all.21.same_ref, ...), custom_call_target="tpu_custom_call" | custom-call | flops 1358954496 | bytes 3538944 | tf_op jit(solution)/shard_map/backward_2_0/pallas_call | solution.py:429
  128.9 2.5 %collective-permute-done.11.low0 = f32[192,256]{1,0:T(8,128)S(1)} collective-permute-done((f32[192,256]{1,0:T(8,128)S(1)}, f32[192,256]{1,0:T(8,128)S(1)}, u32[]{:S(2)}, u32[]{:S(2)}) %collective-permute-start.11) | collective-permute-done | bytes 196640 | tf_op jit(solution)/shard_map/ppermute | solution.py:493
  (37 shorter events, 8.2 us)
Async XLA Ops:
  0.6 49.8 %collective-permute-start.5 = (f32[384,256]{1,0:T(8,128)}, f32[384,256]{1,0:T(8,128)S(1)}, u32[]{:S(2)}, u32[]{:S(2)}) collective-permute-start(f32[384,256]{1,0:T(8,128)} %emb_ref.1), channel_id=1, source_target_pairs={{0,1},{1,0},{2,3},{3,2},{4,5},{5,4},{6,7},{7,6},{8,9},{9,8},{10,11... | collective-permute-start | bytes 1179656 | tf_op jit(solution)/shard_map/ppermute | solution.py:496
  0.7 24.1 %collective-permute-start.2 = (f32[384,256]{1,0:T(8,128)}, f32[384,256]{1,0:T(8,128)S(1)}, u32[]{:S(2)}, u32[]{:S(2)}) collective-permute-start(f32[384,256]{1,0:T(8,128)} %emb_ref.1), channel_id=1, source_target_pairs={{0,6},{1,7},{2,0},{3,1},{4,2},{5,3},{6,4},{7,5},{8,14},{9,15},{10,... | collective-permute-start | bytes 1179656 | tf_op jit(solution)/shard_map/ppermute | solution.py:493
  7.1 22.4 %collective-permute-start.1 = (f32[384,256]{1,0:T(8,128)}, f32[384,256]{1,0:T(8,128)S(1)}, u32[]{:S(2)}, u32[]{:S(2)}) collective-permute-start(f32[384,256]{1,0:T(8,128)} %emb_ref.1), channel_id=1, source_target_pairs={{0,2},{1,3},{2,4},{3,5},{4,6},{5,7},{6,0},{7,1},{8,10},{9,11},{10,... | collective-permute-start | bytes 1179656 | tf_op jit(solution)/shard_map/ppermute | solution.py:493
  7.1 15.9 %all-to-all-start = ((f32[16,48,128]{2,1,0:T(8,128)}), f32[16,48,128]{2,1,0:T(8,128)S(1)}, u32[]{:S(2)}, u32[]{:S(2)}) async-start(f32[16,48,128]{2,1,0:T(8,128)} %bitcast.6), calls=%async_computation | async-start | bytes 786432 | tf_op jit(solution)/shard_map/all_to_all | solution.py:502
  14.5 2.3 %collective-permute-start.6 = (s32[384]{0:T(512)}, s32[384]{0:T(512)S(1)}, u32[]{:S(2)}, u32[]{:S(2)}) collective-permute-start(s32[384]{0:T(512)} %param.4), channel_id=1, source_target_pairs={{0,1},{1,0},{2,3},{3,2},{4,5},{5,4},{6,7},{7,6},{8,9},{9,8},{10,11... | collective-permute-start | bytes 4616 | tf_op jit(solution)/shard_map/ppermute | solution.py:496
  23.0 17.1 %collective-permute-start = (f32[16,48,128]{2,1,0:T(8,128)S(1)}, f32[16,48,128]{2,1,0:T(8,128)S(1)}, u32[]{:S(2)}, u32[]{:S(2)}) collective-permute-start(f32[16,48,128]{2,1,0:T(8,128)S(1)} %all-to-all-done.same_ref), channel_id=1, source_target_pairs={{0,8},{8,0},{16,24},{24,16},{32,40},{40,32},{48,56},{56,48},{64,72... | collective-permute-start | bytes 1179656 | tf_op jit(solution)/shard_map/ppermute | solution.py:505
  24.9 24.2 %collective-permute-start.4 = (f32[192,256]{1,0:T(8,128)S(1)}, f32[192,256]{1,0:T(8,128)S(1)}, u32[]{:S(2)}, u32[]{:S(2)}) collective-permute-start(f32[192,256]{1,0:T(8,128)S(1)} %slice.17), channel_id=1, source_target_pairs={{0,6},{1,7},{2,0},{3,1},{4,2},{5,3},{6,4},{7,5},{8,14},{9,15},{10,... | collective-permute-start | bytes 589832 | tf_op jit(solution)/shard_map/ppermute | solution.py:493
  29.5 19.5 %collective-permute-start.3 = (f32[192,256]{1,0:T(8,128)S(1)}, f32[192,256]{1,0:T(8,128)S(1)}, u32[]{:S(2)}, u32[]{:S(2)}) collective-permute-start(f32[192,256]{1,0:T(8,128)S(1)} %slice.16), channel_id=1, source_target_pairs={{0,2},{1,3},{2,4},{3,5},{4,6},{5,7},{6,0},{7,1},{8,10},{9,11},{10,... | collective-permute-start | bytes 589832 | tf_op jit(solution)/shard_map/ppermute | solution.py:493
  31.0 18.1 %copy-start = (f32[384,256]{1,0:T(8,128)S(1)}, f32[384,256]{1,0:T(8,128)}, u32[]{:S(2)}) copy-start(f32[384,256]{1,0:T(8,128)} %emb_ref.1) | copy-start | bytes 1179652
  41.6 19.6 %all-to-all-start.1 = ((f32[16,96,128]{2,1,0:T(8,128)}), f32[16,96,128]{2,1,0:T(8,128)S(1)}, u32[]{:S(2)}, u32[]{:S(2)}) async-start(f32[16,96,128]{2,1,0:T(8,128)} %pick.1), calls=%async_computation.1 | async-start | bytes 1572864 | tf_op jit(solution)/shard_map/all_to_all | solution.py:502
  61.2 2.3 %collective-permute-start.7 = (f32[16,96,128]{2,1,0:T(8,128)S(1)}, f32[16,96,128]{2,1,0:T(8,128)S(1)}, u32[]{:S(2)}, u32[]{:S(2)}) collective-permute-start(f32[16,96,128]{2,1,0:T(8,128)S(1)} %all-to-all-done.1.got), channel_id=1, source_target_pairs={{0,1},{1,0},{2,3},{3,2},{4,5},{5,4},{6,7},{7,6},{8,9},{9,8},{10,11... | collective-permute-start | bytes 2359304 | tf_op jit(solution)/shard_map/ppermute | solution.py:496
  94.3 4.5 %collective-permute-start.8 = (f32[16,1,768]{2,1,0:T(1,128)S(1)}, f32[16,1,768]{2,1,0:T(1,128)S(1)}, u32[]{:S(2)}, u32[]{:S(2)}) collective-permute-start(f32[16,1,768]{2,1,0:T(1,128)S(1)} %all_to_all.21.same_ref), channel_id=1, source_target_pairs={{0,8},{8,0},{16,24},{24,16},{32,40},{40,32},{48,56},{56,48},{64,72... | collective-permute-start | bytes 147464 | tf_op jit(solution)/shard_map/ppermute | solution.py:505
  103.7 16.4 %collective-permute-start.9 = (f32[192,256]{1,0:T(8,128)S(1)}, f32[192,256]{1,0:T(8,128)S(1)}, u32[]{:S(2)}, u32[]{:S(2)}) collective-permute-start(f32[192,256]{1,0:T(8,128)S(1)} %get-tuple-element.40), channel_id=1, source_target_pairs={{0,2},{1,3},{2,4},{3,5},{4,6},{5,7},{6,0},{7,1},{8,10},{9,11},{10,... | collective-permute-start | bytes 589832 | tf_op jit(solution)/shard_map/ppermute | solution.py:493
  104.0 16.0 %collective-permute-start.10 = (f32[192,256]{1,0:T(8,128)S(1)}, f32[192,256]{1,0:T(8,128)S(1)}, u32[]{:S(2)}, u32[]{:S(2)}) collective-permute-start(f32[192,256]{1,0:T(8,128)S(1)} %get-tuple-element.42), channel_id=1, source_target_pairs={{0,6},{1,7},{2,0},{3,1},{4,2},{5,3},{6,4},{7,5},{8,14},{9,15},{10,... | collective-permute-start | bytes 589832 | tf_op jit(solution)/shard_map/ppermute | solution.py:493
  112.4 16.4 %collective-permute-start.12 = (f32[192,256]{1,0:T(8,128)S(1)}, f32[192,256]{1,0:T(8,128)S(1)}, u32[]{:S(2)}, u32[]{:S(2)}) collective-permute-start(f32[192,256]{1,0:T(8,128)S(1)} %get-tuple-element.44), channel_id=1, source_target_pairs={{0,6},{1,7},{2,0},{3,1},{4,2},{5,3},{6,4},{7,5},{8,14},{9,15},{10,... | collective-permute-start | bytes 589832 | tf_op jit(solution)/shard_map/ppermute | solution.py:493
  112.5 16.3 %collective-permute-start.13 = (f32[192,256]{1,0:T(8,128)S(1)}, f32[192,256]{1,0:T(8,128)S(1)}, u32[]{:S(2)}, u32[]{:S(2)}) collective-permute-start(f32[192,256]{1,0:T(8,128)S(1)} %get-tuple-element.45), channel_id=1, source_target_pairs={{0,2},{1,3},{2,4},{3,5},{4,6},{5,7},{6,0},{7,1},{8,10},{9,11},{10,... | collective-permute-start | bytes 589832 | tf_op jit(solution)/shard_map/ppermute | solution.py:493
  120.1 11.3 %collective-permute-start.11 = (f32[192,256]{1,0:T(8,128)S(1)}, f32[192,256]{1,0:T(8,128)S(1)}, u32[]{:S(2)}, u32[]{:S(2)}) collective-permute-start(f32[192,256]{1,0:T(8,128)S(1)} %get-tuple-element.43), channel_id=1, source_target_pairs={{0,2},{1,3},{2,4},{3,5},{4,6},{5,7},{6,0},{7,1},{8,10},{9,11},{10,... | collective-permute-start | bytes 589832 | tf_op jit(solution)/shard_map/ppermute | solution.py:493
  120.5 11.1 %collective-permute-start.14 = (f32[192,256]{1,0:T(8,128)S(1)}, f32[192,256]{1,0:T(8,128)S(1)}, u32[]{:S(2)}, u32[]{:S(2)}) collective-permute-start(f32[192,256]{1,0:T(8,128)S(1)} %get-tuple-element.46), channel_id=1, source_target_pairs={{0,6},{1,7},{2,0},{3,1},{4,2},{5,3},{6,4},{7,5},{8,14},{9,15},{10,... | collective-permute-start | bytes 589832 | tf_op jit(solution)/shard_map/ppermute | solution.py:493

commit v11 on v9

--- a/solution.py
+++ b/solution.py
@@ -239,10 +239,10 @@
         return product(left_ref[band * wide : band * wide + wide], cols)
 
     columns(0)
-    for copy in ready_copies:
-        copy.wait()
+    ready_copies[0].wait()
     items = [(chunk, band) for chunk in range(chunks) for band in range(orders // 2)]
     coming = scores_of(*items[0])
+    ready_copies[1].wait()
     for turn, (chunk, band) in enumerate(items):
         scores = coming
         if turn + 1 < len(items):
@@ -505,14 +505,14 @@
 
     ready_far = prepare("prepare_far", embeddings, *far)
     c_own, e_own, line = own_scores(ready, ready_far, embeddings, sib, pos)
-    got, line = lax.optimization_barrier((got, line))
+    got, line, partners = lax.optimization_barrier((got, line, pairing[:, group]))
     e_part, c_part, line = forward(ready, ready_far, line, got, swap(got), members)
 
     everything = lax.all_to_all(line, "mem", 0, 0, tiled=True)
     row_den, own_den, line, spread = denominators(jnp.reshape(member, (1,)), everything, groups)
     everyone = lax.all_to_all(spread, "grp", 0, 0, tiled=True)
 
-    shared = (pairing[:, group], row_den, own_den, everyone, pos, e_own, e_part)
+    shared = (partners, row_den, own_den, everyone, pos, e_own, e_part)
     cols, far_low, far_high = backward(((3, 0, rows),), 2, *shared, c_own, c_part)
     shared += (cols,)
     far_low, far_high = shift(far_low, 2), shift(far_high, -2)

time: 127 us -> 126 us (level)
  blocking collectives: 15 us -> 27 us
  waiting for transfers between devices: 31.1 us -> 23.1 us
  starting transfers between devices: 40.5 us -> 35.5 us
    all_to_all x0 -> x1, blocking collectives: none -> 12 us  [local(): everyone = lax.all_to_all(spread, 'grp', 0, 0, tiled=True)]
    all_to_all x1 -> x0, waiting for transfers between devices: 7.25 us -> none  [local(): everyone = lax.all_to_all(spread, 'grp', 0, 0, tiled=True)]
    all_to_all x1 -> x0, starting transfers between devices: 4.97 us -> none  [local(): everyone = lax.all_to_all(spread, 'grp', 0, 0, tiled=True)]
  transfers between devices with their start and end apart: 16 -> 15, of which waited for: 9 -> 7; matrix products, arithmetic and copies ran while one was open for 1% -> 1% of each run, Pallas kernels for 19% -> 19%
where the time goes in v11:
time: 126 us; the launch traced here: 125 us
  Pallas kernels  37.1 us (29%)
  starting transfers between devices  35.5 us (28%)
  blocking collectives  27 us (21%)
  waiting for transfers between devices  23.1 us (18%)
  local copies, waits for them, and re-layouts  1.59 us (1%)
    ppermute x10, starting transfers between devices, shift(): lax.ppermute(value, 'mem', [(m, (m + by) % members) for m in range(member...  22.5 us
    pallas_call x4, Pallas kernels, backward(): pl.pallas_call(functools.partial(backward_kernel, bands, first), in_specs...  18.4 us
    all_to_all x1, blocking collectives, local(): everything = lax.all_to_all(line, 'mem', 0, 0, tiled=True)  15 us
    all_to_all x1, blocking collectives, local(): everyone = lax.all_to_all(spread, 'grp', 0, 0, tiled=True)  12 us
    ppermute x10, waiting for transfers between devices, shift(): lax.ppermute(value, 'mem', [(m, (m + by) % members) for m in range(member...  10.6 us
    all_to_all x1, starting transfers between devices, local(): lax.all_to_all(tiles.reshape(groups, per, 128), 'grp', 0, 0, tiled=True)  7.99 us
    pallas_call x1, Pallas kernels, forward(): pl.pallas_call(forward_kernel, in_specs=[HBM] * 2 + [pl.BlockSpec()] * 3,...  7.92 us
    all_to_all x1, waiting for transfers between devices, local(): got = lax.all_to_all(picked, 'grp', 0, 0, tiled=True)  6.07 us
  transfers between devices with their start and end apart: 15, of which 7 were waited for; matrix products, arithmetic and copies ran while one was open for 1% of the time, Pallas kernels for 19%

profile of v11, /device:TPU:8, one launch (start us, length us, event | category | flops | bytes accessed | tf_op | source)
XLA Modules:
  0.0 125.2 jit_solution(9208923386977688177)
XLA Ops:
  0.6 6.4 %collective-permute-start.1 = (f32[384,256]{1,0:T(8,128)}, f32[384,256]{1,0:T(8,128)S(1)}, u32[]{:S(2)}, u32[]{:S(2)}) collective-permute-start(f32[384,256]{1,0:T(8,128)} %emb_ref.1), channel_id=1, source_target_pairs={{0,6},{1,7},{2,0},{3,1},{4,2},{5,3},{6,4},{7,5},{8,14},{9,15},{10,... | collective-permute-start | bytes 1179656 | tf_op jit(solution)/shard_map/ppermute | solution.py:485
  7.0 8.0 %all-to-all-start = ((f32[32,24,128]{2,1,0:T(8,128)}), f32[32,24,128]{2,1,0:T(8,128)S(1)}, u32[]{:S(2)}, u32[]{:S(2)}) async-start(f32[32,24,128]{2,1,0:T(8,128)} %bitcast.6), calls=%async_computation | async-start | bytes 786432 | tf_op jit(solution)/shard_map/all_to_all | solution.py:494
  16.8 7.4 %collective-permute-done.1.refs_1_ = f32[384,256]{1,0:T(8,128)S(1)} collective-permute-done((f32[384,256]{1,0:T(8,128)}, f32[384,256]{1,0:T(8,128)S(1)}, u32[]{:S(2)}, u32[]{:S(2)}) %collective-permute-start.1) | collective-permute-done | bytes 393248 | tf_op jit(solution)/shard_map/ppermute | solution.py:485
  24.2 4.6 %collective-permute-start.3 = (f32[192,256]{1,0:T(8,128)S(1)}, f32[192,256]{1,0:T(8,128)S(1)}, u32[]{:S(2)}, u32[]{:S(2)}) collective-permute-start(f32[192,256]{1,0:T(8,128)S(1)} %slice.9), channel_id=1, source_target_pairs={{0,6},{1,7},{2,0},{3,1},{4,2},{5,3},{6,4},{7,5},{8,14},{9,15},{10,... | collective-permute-start | bytes 589832 | tf_op jit(solution)/shard_map/ppermute | solution.py:485
  29.0 1.4 %prepare.1.ready = bf16[768,768]{1,0:T(8,128)(2,1)} custom-call(f32[384,256]{1,0:T(8,128)S(1)} %collective-permute-done.refs_0_, f32[384,256]{1,0:T(8,128)S(1)} %collective-permute-done.1.refs_1_), custom_call_target="tpu_custom_call" | custom-call | flops 20000000000 | bytes 1572864 | tf_op jit(solution)/shard_map/prepare/pallas_call | solution.py:200
  30.4 4.1 %all-to-all-done.pieces_ref = f32[32,24,128]{2,1,0:T(8,128)S(1)} async-done(((f32[32,24,128]{2,1,0:T(8,128)}), f32[32,24,128]{2,1,0:T(8,128)S(1)}, u32[]{:S(2)}, u32[]{:S(2)}) %all-to-all-start) | async-done | bytes 393248 | tf_op jit(solution)/shard_map/all_to_all | solution.py:494
  34.5 1.5 %pick.1 = f32[32,48,128]{2,1,0:T(8,128)} custom-call(s32[2,32]{1,0:T(2,128)S(1)} %copy-done.1, f32[32,24,128]{2,1,0:T(8,128)S(1)} %all-to-all-done.pieces_ref), custom_call_target="tpu_custom_call" | custom-call | tf_op jit(solution)/shard_map/pick/pallas_call | solution.py:61
  36.0 4.9 %all-to-all-start.1 = ((f32[32,48,128]{2,1,0:T(8,128)}), f32[32,48,128]{2,1,0:T(8,128)S(1)}, u32[]{:S(2)}, u32[]{:S(2)}) async-start(f32[32,48,128]{2,1,0:T(8,128)} %pick.1), calls=%async_computation.1 | async-start | bytes 1572864 | tf_op jit(solution)/shard_map/all_to_all | solution.py:497
  41.0 1.4 %prepare_far.1.ready_far = bf16[768,768]{1,0:T(8,128)(2,1)} custom-call(f32[384,256]{1,0:T(8,128)S(1)} %copy-done, f32[192,256]{1,0:T(8,128)S(1)} %collective-permute-done.2.refs_1_, f32[192,256]{1,0:T(8,128)S(1)} %collective-permute-done.3.refs_2_), custom_call_target="tpu_custom_call" | custom-call | flops 20000000000 | bytes 1572864 | tf_op jit(solution)/shard_map/prepare_far/pallas_call | solution.py:200
  42.4 5.4 %own_scores.1 = (bf16[3,256,512]{2,1,0:T(8,128)(2,1)}, f32[3,4,384,256]{3,2,1,0:T(8,128)}, f32[2,1536]{1,0:T(2,128)S(1)}) custom-call(bf16[768,768]{1,0:T(8,128)(2,1)} %prepare.1.ready, bf16[768,768]{1,0:T(8,128)(2,1)} %prepare_far.1.ready_far, f32[384,256]{1,0:T(8,128)S(1)} %copy-done, f32[384,256]{1,0:T(8,128)S(1)} %collective-permute-done.4.sib, ...), custom_call_target="tpu_custom_call" | custom-call | flops 1811939328 | bytes 4718592 | tf_op jit(solution)/shard_map/own_scores/pallas_call | solution.py:168
  47.8 6.1 %all-to-all-done.1.got = f32[32,48,128]{2,1,0:T(8,128)S(1)} async-done(((f32[32,48,128]{2,1,0:T(8,128)}), f32[32,48,128]{2,1,0:T(8,128)S(1)}, u32[]{:S(2)}, u32[]{:S(2)}) %all-to-all-start.1) | async-done | bytes 786464 | tf_op jit(solution)/shard_map/all_to_all | solution.py:497
  53.8 2.3 %collective-permute-done.6.got_sib = f32[32,48,128]{2,1,0:T(8,128)S(1)} collective-permute-done((f32[32,48,128]{2,1,0:T(8,128)S(1)}, f32[32,48,128]{2,1,0:T(8,128)S(1)}, u32[]{:S(2)}, u32[]{:S(2)}) %collective-permute-start.6) | collective-permute-done | bytes 786464 | tf_op jit(solution)/shard_map/ppermute | solution.py:488
  56.1 7.9 %forward.1 = (f32[6,4,384,256]{3,2,1,0:T(8,128)}, bf16[6,256,512]{2,1,0:T(8,128)(2,1)}, f32[8,2,1536]{2,1,0:T(2,128)S(1)}) custom-call(bf16[768,768]{1,0:T(8,128)(2,1)} %prepare.1.ready, bf16[768,768]{1,0:T(8,128)(2,1)} %prepare_far.1.ready_far, f32[2,1536]{1,0:T(2,128)S(1)} %get-tuple-element.30.line_in, f32[32,48,128]{2,1,0:T(8,128)S(1)} %all-to-all-done.1.got, ...), custom_call_target="tpu_custom_call" | custom-call | flops 3623878656 | bytes 9437184 | tf_op jit(solution)/shard_map/forward/pallas_call | solution.py:278
  64.1 15.0 %all_to_all.20.all_ref = f32[8,2,1536]{2,1,0:T(2,128)S(1)} all-to-all(f32[8,2,1536]{2,1,0:T(2,128)S(1)} %get-tuple-element.32), channel_id=1, replica_groups=mesh['grp'=32,'mem'=8] {'mem'}, dimensions={0} | all-to-all | bytes 196608 | tf_op jit(solution)/shard_map/all_to_all | solution.py:511
  79.1 12.0 %all_to_all.21.everyone_ref = f32[32,1,768]{2,1,0:T(1,128)S(1)} all-to-all(f32[32,1,768]{2,1,0:T(1,128)S(1)} %get-tuple-element.35), channel_id=1, replica_groups=mesh['grp'=32,'mem'=8] {'grp'}, dimensions={0} | all-to-all | bytes 196608 | tf_op jit(solution)/shard_map/all_to_all | solution.py:513
  91.1 4.8 %backward_3_0.1 = (bf16[9,256,512]{2,1,0:T(8,128)(2,1)S(1)}, f32[192,256]{1,0:T(8,128)S(1)}, f32[192,256]{1,0:T(8,128)S(1)}) custom-call(s32[2]{0:T(128)S(1)} %dynamic-slice_reduce_fusion.partner_ref, f32[1,1536]{1,0:T(1,128)S(1)} %get-tuple-element.33.row_ref, f32[1,768]{1,0:T(1,128)S(1)} %get-tuple-element.34.own_ref, ...), custom_call_target="tpu_custom_call" | custom-call | flops 1358954496 | bytes 3538944 | tf_op jit(solution)/shard_map/backward_3_0/pallas_call | solution.py:421
  96.4 3.7 %collective-permute-start.8 = (f32[192,256]{1,0:T(8,128)S(1)}, f32[192,256]{1,0:T(8,128)S(1)}, u32[]{:S(2)}, u32[]{:S(2)}) collective-permute-start(f32[192,256]{1,0:T(8,128)S(1)} %get-tuple-element.44), channel_id=1, source_target_pairs={{0,6},{1,7},{2,0},{3,1},{4,2},{5,3},{6,4},{7,5},{8,14},{9,15},{10,... | collective-permute-start | bytes 589832 | tf_op jit(solution)/shard_map/ppermute | solution.py:485
  100.1 4.6 %backward_0_0.1 = (f32[192,256]{1,0:T(8,128)S(1)}, f32[192,256]{1,0:T(8,128)S(1)}) custom-call(s32[2]{0:T(128)S(1)} %dynamic-slice_reduce_fusion.partner_ref, f32[1,1536]{1,0:T(1,128)S(1)} %get-tuple-element.33.row_ref, f32[1,768]{1,0:T(1,128)S(1)} %get-tuple-element.34.own_ref, f32[32,1,768]{2,1,0:T(1,128)S(1)} %all_to_all.21.everyone_ref, ...), custom_call_target="tpu_custom_call" | custom-call | flops 1358954496 | bytes 3538944 | tf_op jit(solution)/shard_map/backward_0_0/pallas_call | solution.py:421
  104.7 2.9 %collective-permute-start.11 = (f32[192,256]{1,0:T(8,128)S(1)}, f32[192,256]{1,0:T(8,128)S(1)}, u32[]{:S(2)}, u32[]{:S(2)}) collective-permute-start(f32[192,256]{1,0:T(8,128)S(1)} %get-tuple-element.47), channel_id=1, source_target_pairs={{0,2},{1,3},{2,4},{3,5},{4,6},{5,7},{6,0},{7,1},{8,10},{9,11},{10,... | collective-permute-start | bytes 589832 | tf_op jit(solution)/shard_map/ppermute | solution.py:485
  107.7 4.6 %backward_0_192.1 = (f32[192,256]{1,0:T(8,128)S(1)}, f32[192,256]{1,0:T(8,128)S(1)}) custom-call(s32[2]{0:T(128)S(1)} %dynamic-slice_reduce_fusion.partner_ref, f32[1,1536]{1,0:T(1,128)S(1)} %get-tuple-element.33.row_ref, f32[1,768]{1,0:T(1,128)S(1)} %get-tuple-element.34.own_ref, f32[32,1,768]{2,1,0:T(1,128)S(1)} %all_to_all.21.everyone_ref, ...), custom_call_target="tpu_custom_call" | custom-call | flops 1358954496 | bytes 3538944 | tf_op jit(solution)/shard_map/backward_0_192/pallas_call | solution.py:421
  112.8 3.7 %collective-permute-start.12 = (f32[192,256]{1,0:T(8,128)S(1)}, f32[192,256]{1,0:T(8,128)S(1)}, u32[]{:S(2)}, u32[]{:S(2)}) collective-permute-start(f32[192,256]{1,0:T(8,128)S(1)} %get-tuple-element.48), channel_id=1, source_target_pairs={{0,6},{1,7},{2,0},{3,1},{4,2},{5,3},{6,4},{7,5},{8,14},{9,15},{10,... | collective-permute-start | bytes 589832 | tf_op jit(solution)/shard_map/ppermute | solution.py:485
  116.5 4.5 %backward_2_0.1.run_ref = f32[384,256]{1,0:T(8,128)S(1)} custom-call(s32[2]{0:T(128)S(1)} %dynamic-slice_reduce_fusion.partner_ref, f32[1,1536]{1,0:T(1,128)S(1)} %get-tuple-element.33.row_ref, f32[1,768]{1,0:T(1,128)S(1)} %get-tuple-element.34.own_ref, f32[32,1,768]{2,1,0:T(1,128)S(1)} %all_to_all.21.everyone_ref, ...), custom_call_target="tpu_custom_call" | custom-call | flops 1358954496 | bytes 3538944 | tf_op jit(solution)/shard_map/backward_2_0/pallas_call | solution.py:421
  121.1 2.1 %collective-permute-done.9.low0 = f32[192,256]{1,0:T(8,128)S(1)} collective-permute-done((f32[192,256]{1,0:T(8,128)S(1)}, f32[192,256]{1,0:T(8,128)S(1)}, u32[]{:S(2)}, u32[]{:S(2)}) %collective-permute-start.9) | collective-permute-done | bytes 196640 | tf_op jit(solution)/shard_map/ppermute | solution.py:485
  124.2 1.1 finish.1
  (30 shorter events, 4.1 us)
Async XLA Ops:
  0.6 23.5 %collective-permute-start.1 = (f32[384,256]{1,0:T(8,128)}, f32[384,256]{1,0:T(8,128)S(1)}, u32[]{:S(2)}, u32[]{:S(2)}) collective-permute-start(f32[384,256]{1,0:T(8,128)} %emb_ref.1), channel_id=1, source_target_pairs={{0,6},{1,7},{2,0},{3,1},{4,2},{5,3},{6,4},{7,5},{8,14},{9,15},{10,... | collective-permute-start | bytes 1179656 | tf_op jit(solution)/shard_map/ppermute | solution.py:485
  7.0 21.9 %collective-permute-start = (f32[384,256]{1,0:T(8,128)}, f32[384,256]{1,0:T(8,128)S(1)}, u32[]{:S(2)}, u32[]{:S(2)}) collective-permute-start(f32[384,256]{1,0:T(8,128)} %emb_ref.1), channel_id=1, source_target_pairs={{0,2},{1,3},{2,4},{3,5},{4,6},{5,7},{6,0},{7,1},{8,10},{9,11},{10,... | collective-permute-start | bytes 1179656 | tf_op jit(solution)/shard_map/ppermute | solution.py:485
  7.0 35.4 %collective-permute-start.4 = (f32[384,256]{1,0:T(8,128)}, f32[384,256]{1,0:T(8,128)S(1)}, u32[]{:S(2)}, u32[]{:S(2)}) collective-permute-start(f32[384,256]{1,0:T(8,128)} %emb_ref.1), channel_id=1, source_target_pairs={{0,1},{1,0},{2,3},{3,2},{4,5},{5,4},{6,7},{7,6},{8,9},{9,8},{10,11... | collective-permute-start | bytes 1179656 | tf_op jit(solution)/shard_map/ppermute | solution.py:488
  7.0 27.5 %all-to-all-start = ((f32[32,24,128]{2,1,0:T(8,128)}), f32[32,24,128]{2,1,0:T(8,128)S(1)}, u32[]{:S(2)}, u32[]{:S(2)}) async-start(f32[32,24,128]{2,1,0:T(8,128)} %bitcast.6), calls=%async_computation | async-start | bytes 786432 | tf_op jit(solution)/shard_map/all_to_all | solution.py:494
  15.0 1.7 %collective-permute-start.5 = (s32[384]{0:T(512)}, s32[384]{0:T(512)S(1)}, u32[]{:S(2)}, u32[]{:S(2)}) collective-permute-start(s32[384]{0:T(512)} %param.4), channel_id=1, source_target_pairs={{0,1},{1,0},{2,3},{3,2},{4,5},{5,4},{6,7},{7,6},{8,9},{9,8},{10,11... | collective-permute-start | bytes 4616 | tf_op jit(solution)/shard_map/ppermute | solution.py:488
  24.2 16.8 %collective-permute-start.3 = (f32[192,256]{1,0:T(8,128)S(1)}, f32[192,256]{1,0:T(8,128)S(1)}, u32[]{:S(2)}, u32[]{:S(2)}) collective-permute-start(f32[192,256]{1,0:T(8,128)S(1)} %slice.9), channel_id=1, source_target_pairs={{0,6},{1,7},{2,0},{3,1},{4,2},{5,3},{6,4},{7,5},{8,14},{9,15},{10,... | collective-permute-start | bytes 589832 | tf_op jit(solution)/shard_map/ppermute | solution.py:485
  28.9 5.6 %copy-start.1 = (s32[2,32]{1,0:T(2,128)S(1)}, s32[2,32]{1,0:T(2,128)}, u32[]{:S(2)}) copy-start(s32[2,32]{1,0:T(2,128)} %pairing_ref.1) | copy-start | bytes 772
  28.9 12.1 %collective-permute-start.2 = (f32[192,256]{1,0:T(8,128)S(1)}, f32[192,256]{1,0:T(8,128)S(1)}, u32[]{:S(2)}, u32[]{:S(2)}) collective-permute-start(f32[192,256]{1,0:T(8,128)S(1)} %slice.8), channel_id=1, source_target_pairs={{0,2},{1,3},{2,4},{3,5},{4,6},{5,7},{6,0},{7,1},{8,10},{9,11},{10,... | collective-permute-start | bytes 589832 | tf_op jit(solution)/shard_map/ppermute | solution.py:485
  30.4 10.6 %copy-start = (f32[384,256]{1,0:T(8,128)S(1)}, f32[384,256]{1,0:T(8,128)}, u32[]{:S(2)}) copy-start(f32[384,256]{1,0:T(8,128)} %emb_ref.1) | copy-start | bytes 1179652
  36.0 17.8 %all-to-all-start.1 = ((f32[32,48,128]{2,1,0:T(8,128)}), f32[32,48,128]{2,1,0:T(8,128)S(1)}, u32[]{:S(2)}, u32[]{:S(2)}) async-start(f32[32,48,128]{2,1,0:T(8,128)} %pick.1), calls=%async_computation.1 | async-start | bytes 1572864 | tf_op jit(solution)/shard_map/all_to_all | solution.py:497
  53.8 2.3 %collective-permute-start.6 = (f32[32,48,128]{2,1,0:T(8,128)S(1)}, f32[32,48,128]{2,1,0:T(8,128)S(1)}, u32[]{:S(2)}, u32[]{:S(2)}) collective-permute-start(f32[32,48,128]{2,1,0:T(8,128)S(1)} %all-to-all-done.1.got), channel_id=1, source_target_pairs={{0,1},{1,0},{2,3},{3,2},{4,5},{5,4},{6,7},{7,6},{8,9},{9,8},{10,11... | collective-permute-start | bytes 2359304 | tf_op jit(solution)/shard_map/ppermute | solution.py:488
  95.9 16.4 %collective-permute-start.7 = (f32[192,256]{1,0:T(8,128)S(1)}, f32[192,256]{1,0:T(8,128)S(1)}, u32[]{:S(2)}, u32[]{:S(2)}) collective-permute-start(f32[192,256]{1,0:T(8,128)S(1)} %get-tuple-element.42), channel_id=1, source_target_pairs={{0,2},{1,3},{2,4},{3,5},{4,6},{5,7},{6,0},{7,1},{8,10},{9,11},{10,... | collective-permute-start | bytes 589832 | tf_op jit(solution)/shard_map/ppermute | solution.py:485
  96.4 15.8 %collective-permute-start.8 = (f32[192,256]{1,0:T(8,128)S(1)}, f32[192,256]{1,0:T(8,128)S(1)}, u32[]{:S(2)}, u32[]{:S(2)}) collective-permute-start(f32[192,256]{1,0:T(8,128)S(1)} %get-tuple-element.44), channel_id=1, source_target_pairs={{0,6},{1,7},{2,0},{3,1},{4,2},{5,3},{6,4},{7,5},{8,14},{9,15},{10,... | collective-permute-start | bytes 589832 | tf_op jit(solution)/shard_map/ppermute | solution.py:485
  104.6 16.4 %collective-permute-start.10 = (f32[192,256]{1,0:T(8,128)S(1)}, f32[192,256]{1,0:T(8,128)S(1)}, u32[]{:S(2)}, u32[]{:S(2)}) collective-permute-start(f32[192,256]{1,0:T(8,128)S(1)} %get-tuple-element.46), channel_id=1, source_target_pairs={{0,6},{1,7},{2,0},{3,1},{4,2},{5,3},{6,4},{7,5},{8,14},{9,15},{10,... | collective-permute-start | bytes 589832 | tf_op jit(solution)/shard_map/ppermute | solution.py:485
  104.7 16.3 %collective-permute-start.11 = (f32[192,256]{1,0:T(8,128)S(1)}, f32[192,256]{1,0:T(8,128)S(1)}, u32[]{:S(2)}, u32[]{:S(2)}) collective-permute-start(f32[192,256]{1,0:T(8,128)S(1)} %get-tuple-element.47), channel_id=1, source_target_pairs={{0,2},{1,3},{2,4},{3,5},{4,6},{5,7},{6,0},{7,1},{8,10},{9,11},{10,... | collective-permute-start | bytes 589832 | tf_op jit(solution)/shard_map/ppermute | solution.py:485
  112.3 10.9 %collective-permute-start.9 = (f32[192,256]{1,0:T(8,128)S(1)}, f32[192,256]{1,0:T(8,128)S(1)}, u32[]{:S(2)}, u32[]{:S(2)}) collective-permute-start(f32[192,256]{1,0:T(8,128)S(1)} %get-tuple-element.45), channel_id=1, source_target_pairs={{0,2},{1,3},{2,4},{3,5},{4,6},{5,7},{6,0},{7,1},{8,10},{9,11},{10,... | collective-permute-start | bytes 589832 | tf_op jit(solution)/shard_map/ppermute | solution.py:485
  112.8 11.3 %collective-permute-start.12 = (f32[192,256]{1,0:T(8,128)S(1)}, f32[192,256]{1,0:T(8,128)S(1)}, u32[]{:S(2)}, u32[]{:S(2)}) collective-permute-start(f32[192,256]{1,0:T(8,128)S(1)} %get-tuple-element.48), channel_id=1, source_target_pairs={{0,6},{1,7},{2,0},{3,1},{4,2},{5,3},{6,4},{7,5},{8,14},{9,15},{10,... | collective-permute-start | bytes 589832 | tf_op jit(solution)/shard_map/ppermute | solution.py:485

commit v12 on v11

--- a/solution.py
+++ b/solution.py
@@ -140,21 +140,18 @@
     for copy in ready_copies:
         copy.wait()
 
-    coming = product(left_ref[:SLICE], cols)
     totals, matches = [], []
-    for order in range(4):
-        scores = coming
-        if order < 3:
-            at = (order + 1) * SLICE
-            coming = product(left_ref[at : at + SLICE], cols)
+    for band in range(2):
+        scores = product(left_ref[band * 2 * SLICE : (band + 1) * 2 * SLICE], cols)
 
         def store(k, e):
-            e_buf[k // PIECE, order, :, k % PIECE : k % PIECE + 128] = e
-
-        total, match = exponentials(scores, order * SLICE, pos_ref, store)
+            e_buf[k // PIECE, 2 * band : 2 * band + 2, :, k % PIECE : k % PIECE + 128] = e.reshape(2, SLICE, 128)
+
+        total, match = exponentials(scores, band * 2 * SLICE, pos_ref, store)
         totals.append(as_line(total))
         matches.append(as_line(match))
-        copies.append(pltpu.make_async_copy(e_buf.at[:, order], e_out.at[:, order], e_sem.at[order]))
+        view = (slice(None), pl.ds(2 * band, 2))
+        copies.append(pltpu.make_async_copy(e_buf.at[view], e_out.at[view], e_sem.at[band]))
         copies[-1].start()
     line_ref[0:1] = jnp.concatenate(totals, axis=1)
     line_ref[1:2] = jnp.concatenate(matches, axis=1)
@@ -176,7 +173,7 @@
             pltpu.VMEM(*shapes[1]),
             pltpu.SemaphoreType.DMA((2,)),
             pltpu.SemaphoreType.DMA,
-            pltpu.SemaphoreType.DMA((4,)),
+            pltpu.SemaphoreType.DMA((2,)),
         ],
         cost_estimate=pl.CostEstimate(
             flops=6 * rows * wide * WIDTH, bytes_accessed=4 * rows * wide, transcendentals=rows * wide
@@ -239,16 +236,13 @@
         return product(left_ref[band * wide : band * wide + wide], cols)
 
     columns(0)
-    ready_copies[0].wait()
+    for copy in ready_copies:
+        copy.wait()
     items = [(chunk, band) for chunk in range(chunks) for band in range(orders // 2)]
-    coming = scores_of(*items[0])
-    ready_copies[1].wait()
     for turn, (chunk, band) in enumerate(items):
-        scores = coming
-        if turn + 1 < len(items):
-            if items[turn + 1][0] != chunk:
-                columns(items[turn + 1][0])
-            coming = scores_of(*items[turn + 1])
+        if turn > 0 and band == 0:
+            columns(chunk)
+        scores = scores_of(chunk, band)
 
         def store(k, e):
             lane = k % PIECE

time: 126 us -> 125 us (level)
  no operation moved by 1% of the time
where the time goes in v12:
time: 125 us
  Pallas kernels  37.1 us (30%)
  starting transfers between devices  35.5 us (28%)
  blocking collectives  27.3 us (22%)
  waiting for transfers between devices  22.5 us (18%)
  local copies, waits for them, and re-layouts  1.59 us (1%)
    ppermute x10, starting transfers between devices, shift(): lax.ppermute(value, 'mem', [(m, (m + by) % members) for m in range(member...  22.5 us
    pallas_call x4, Pallas kernels, backward(): pl.pallas_call(functools.partial(backward_kernel, bands, first), in_specs...  18.4 us
    all_to_all x1, blocking collectives, local(): everything = lax.all_to_all(line, 'mem', 0, 0, tiled=True)  15 us
    all_to_all x1, blocking collectives, local(): everyone = lax.all_to_all(spread, 'grp', 0, 0, tiled=True)  12.4 us
    ppermute x10, waiting for transfers between devices, shift(): lax.ppermute(value, 'mem', [(m, (m + by) % members) for m in range(member...  10.3 us
    all_to_all x1, starting transfers between devices, local(): lax.all_to_all(tiles.reshape(groups, per, 128), 'grp', 0, 0, tiled=True)  7.99 us
    pallas_call x1, Pallas kernels, forward(): pl.pallas_call(forward_kernel, in_specs=[HBM] * 2 + [pl.BlockSpec()] * 3,...  7.52 us
    pallas_call x1, Pallas kernels, own_scores(): pl.pallas_call(own_kernel, in_specs=[HBM] * 2 + [pl.BlockSpec()] * 3, out...  5.74 us
  transfers between devices with their start and end apart: 15, of which 7 were waited for; matrix products, arithmetic and copies ran while one was open for 1% of the time, Pallas kernels for 19%

profile of v12, /device:TPU:8, one launch (start us, length us, event | category | flops | bytes accessed | tf_op | source)
XLA Modules:
  0.0 124.9 jit_solution(8855094206521773337)
XLA Ops:
  0.6 6.4 %collective-permute-start.1 = (f32[384,256]{1,0:T(8,128)}, f32[384,256]{1,0:T(8,128)S(1)}, u32[]{:S(2)}, u32[]{:S(2)}) collective-permute-start(f32[384,256]{1,0:T(8,128)} %emb_ref.1), channel_id=1, source_target_pairs={{0,6},{1,7},{2,0},{3,1},{4,2},{5,3},{6,4},{7,5},{8,14},{9,15},{10,... | collective-permute-start | bytes 1179656 | tf_op jit(solution)/shard_map/ppermute | solution.py:479
  7.0 8.0 %all-to-all-start = ((f32[32,24,128]{2,1,0:T(8,128)}), f32[32,24,128]{2,1,0:T(8,128)S(1)}, u32[]{:S(2)}, u32[]{:S(2)}) async-start(f32[32,24,128]{2,1,0:T(8,128)} %bitcast.6), calls=%async_computation | async-start | bytes 786432 | tf_op jit(solution)/shard_map/all_to_all | solution.py:488
  16.8 7.4 %collective-permute-done.1.refs_1_ = f32[384,256]{1,0:T(8,128)S(1)} collective-permute-done((f32[384,256]{1,0:T(8,128)}, f32[384,256]{1,0:T(8,128)S(1)}, u32[]{:S(2)}, u32[]{:S(2)}) %collective-permute-start.1) | collective-permute-done | bytes 393248 | tf_op jit(solution)/shard_map/ppermute | solution.py:479
  24.2 4.6 %collective-permute-start.3 = (f32[192,256]{1,0:T(8,128)S(1)}, f32[192,256]{1,0:T(8,128)S(1)}, u32[]{:S(2)}, u32[]{:S(2)}) collective-permute-start(f32[192,256]{1,0:T(8,128)S(1)} %slice.9), channel_id=1, source_target_pairs={{0,6},{1,7},{2,0},{3,1},{4,2},{5,3},{6,4},{7,5},{8,14},{9,15},{10,... | collective-permute-start | bytes 589832 | tf_op jit(solution)/shard_map/ppermute | solution.py:479
  29.0 1.4 %prepare.1.ready = bf16[768,768]{1,0:T(8,128)(2,1)} custom-call(f32[384,256]{1,0:T(8,128)S(1)} %collective-permute-done.refs_0_, f32[384,256]{1,0:T(8,128)S(1)} %collective-permute-done.1.refs_1_), custom_call_target="tpu_custom_call" | custom-call | flops 20000000000 | bytes 1572864 | tf_op jit(solution)/shard_map/prepare/pallas_call | solution.py:197
  30.4 4.1 %all-to-all-done.pieces_ref = f32[32,24,128]{2,1,0:T(8,128)S(1)} async-done(((f32[32,24,128]{2,1,0:T(8,128)}), f32[32,24,128]{2,1,0:T(8,128)S(1)}, u32[]{:S(2)}, u32[]{:S(2)}) %all-to-all-start) | async-done | bytes 393248 | tf_op jit(solution)/shard_map/all_to_all | solution.py:488
  34.5 1.5 %pick.1 = f32[32,48,128]{2,1,0:T(8,128)} custom-call(s32[2,32]{1,0:T(2,128)S(1)} %copy-done.1, f32[32,24,128]{2,1,0:T(8,128)S(1)} %all-to-all-done.pieces_ref), custom_call_target="tpu_custom_call" | custom-call | tf_op jit(solution)/shard_map/pick/pallas_call | solution.py:61
  36.0 4.9 %all-to-all-start.1 = ((f32[32,48,128]{2,1,0:T(8,128)}), f32[32,48,128]{2,1,0:T(8,128)S(1)}, u32[]{:S(2)}, u32[]{:S(2)}) async-start(f32[32,48,128]{2,1,0:T(8,128)} %pick.1), calls=%async_computation.1 | async-start | bytes 1572864 | tf_op jit(solution)/shard_map/all_to_all | solution.py:491
  41.0 1.4 %prepare_far.1.ready_far = bf16[768,768]{1,0:T(8,128)(2,1)} custom-call(f32[384,256]{1,0:T(8,128)S(1)} %copy-done, f32[192,256]{1,0:T(8,128)S(1)} %collective-permute-done.2.refs_1_, f32[192,256]{1,0:T(8,128)S(1)} %collective-permute-done.3.refs_2_), custom_call_target="tpu_custom_call" | custom-call | flops 20000000000 | bytes 1572864 | tf_op jit(solution)/shard_map/prepare_far/pallas_call | solution.py:197
  42.4 5.7 %own_scores.1 = (bf16[3,256,512]{2,1,0:T(8,128)(2,1)}, f32[3,4,384,256]{3,2,1,0:T(8,128)}, f32[2,1536]{1,0:T(2,128)S(1)}) custom-call(bf16[768,768]{1,0:T(8,128)(2,1)} %prepare.1.ready, bf16[768,768]{1,0:T(8,128)(2,1)} %prepare_far.1.ready_far, f32[384,256]{1,0:T(8,128)S(1)} %copy-done, f32[384,256]{1,0:T(8,128)S(1)} %collective-permute-done.4.sib, ...), custom_call_target="tpu_custom_call" | custom-call | flops 1811939328 | bytes 4718592 | tf_op jit(solution)/shard_map/own_scores/pallas_call | solution.py:165
  48.1 5.7 %all-to-all-done.1.got = f32[32,48,128]{2,1,0:T(8,128)S(1)} async-done(((f32[32,48,128]{2,1,0:T(8,128)}), f32[32,48,128]{2,1,0:T(8,128)S(1)}, u32[]{:S(2)}, u32[]{:S(2)}) %all-to-all-start.1) | async-done | bytes 786464 | tf_op jit(solution)/shard_map/all_to_all | solution.py:491
  53.8 2.3 %collective-permute-done.6.got_sib = f32[32,48,128]{2,1,0:T(8,128)S(1)} collective-permute-done((f32[32,48,128]{2,1,0:T(8,128)S(1)}, f32[32,48,128]{2,1,0:T(8,128)S(1)}, u32[]{:S(2)}, u32[]{:S(2)}) %collective-permute-start.6) | collective-permute-done | bytes 786464 | tf_op jit(solution)/shard_map/ppermute | solution.py:482
  56.1 7.5 %forward.1 = (f32[6,4,384,256]{3,2,1,0:T(8,128)}, bf16[6,256,512]{2,1,0:T(8,128)(2,1)}, f32[8,2,1536]{2,1,0:T(2,128)S(1)}) custom-call(bf16[768,768]{1,0:T(8,128)(2,1)} %prepare.1.ready, bf16[768,768]{1,0:T(8,128)(2,1)} %prepare_far.1.ready_far, f32[2,1536]{1,0:T(2,128)S(1)} %get-tuple-element.30.line_in, f32[32,48,128]{2,1,0:T(8,128)S(1)} %all-to-all-done.1.got, ...), custom_call_target="tpu_custom_call" | custom-call | flops 3623878656 | bytes 9437184 | tf_op jit(solution)/shard_map/forward/pallas_call | solution.py:272
  63.7 15.0 %all_to_all.20.all_ref = f32[8,2,1536]{2,1,0:T(2,128)S(1)} all-to-all(f32[8,2,1536]{2,1,0:T(2,128)S(1)} %get-tuple-element.32), channel_id=1, replica_groups=mesh['grp'=32,'mem'=8] {'mem'}, dimensions={0} | all-to-all | bytes 196608 | tf_op jit(solution)/shard_map/all_to_all | solution.py:505
  78.7 12.4 %all_to_all.21.everyone_ref = f32[32,1,768]{2,1,0:T(1,128)S(1)} all-to-all(f32[32,1,768]{2,1,0:T(1,128)S(1)} %get-tuple-element.35), channel_id=1, replica_groups=mesh['grp'=32,'mem'=8] {'grp'}, dimensions={0} | all-to-all | bytes 196608 | tf_op jit(solution)/shard_map/all_to_all | solution.py:507
  91.0 4.8 %backward_3_0.1 = (bf16[9,256,512]{2,1,0:T(8,128)(2,1)S(1)}, f32[192,256]{1,0:T(8,128)S(1)}, f32[192,256]{1,0:T(8,128)S(1)}) custom-call(s32[2]{0:T(128)S(1)} %dynamic-slice_reduce_fusion.partner_ref, f32[1,1536]{1,0:T(1,128)S(1)} %get-tuple-element.33.row_ref, f32[1,768]{1,0:T(1,128)S(1)} %get-tuple-element.34.own_ref, ...), custom_call_target="tpu_custom_call" | custom-call | flops 1358954496 | bytes 3538944 | tf_op jit(solution)/shard_map/backward_3_0/pallas_call | solution.py:415
  96.3 3.7 %collective-permute-start.8 = (f32[192,256]{1,0:T(8,128)S(1)}, f32[192,256]{1,0:T(8,128)S(1)}, u32[]{:S(2)}, u32[]{:S(2)}) collective-permute-start(f32[192,256]{1,0:T(8,128)S(1)} %get-tuple-element.44), channel_id=1, source_target_pairs={{0,6},{1,7},{2,0},{3,1},{4,2},{5,3},{6,4},{7,5},{8,14},{9,15},{10,... | collective-permute-start | bytes 589832 | tf_op jit(solution)/shard_map/ppermute | solution.py:479
  100.0 4.6 %backward_0_0.1 = (f32[192,256]{1,0:T(8,128)S(1)}, f32[192,256]{1,0:T(8,128)S(1)}) custom-call(s32[2]{0:T(128)S(1)} %dynamic-slice_reduce_fusion.partner_ref, f32[1,1536]{1,0:T(1,128)S(1)} %get-tuple-element.33.row_ref, f32[1,768]{1,0:T(1,128)S(1)} %get-tuple-element.34.own_ref, f32[32,1,768]{2,1,0:T(1,128)S(1)} %all_to_all.21.everyone_ref, ...), custom_call_target="tpu_custom_call" | custom-call | flops 1358954496 | bytes 3538944 | tf_op jit(solution)/shard_map/backward_0_0/pallas_call | solution.py:415
  104.7 2.9 %collective-permute-start.11 = (f32[192,256]{1,0:T(8,128)S(1)}, f32[192,256]{1,0:T(8,128)S(1)}, u32[]{:S(2)}, u32[]{:S(2)}) collective-permute-start(f32[192,256]{1,0:T(8,128)S(1)} %get-tuple-element.47), channel_id=1, source_target_pairs={{0,2},{1,3},{2,4},{3,5},{4,6},{5,7},{6,0},{7,1},{8,10},{9,11},{10,... | collective-permute-start | bytes 589832 | tf_op jit(solution)/shard_map/ppermute | solution.py:479
  107.6 4.6 %backward_0_192.1 = (f32[192,256]{1,0:T(8,128)S(1)}, f32[192,256]{1,0:T(8,128)S(1)}) custom-call(s32[2]{0:T(128)S(1)} %dynamic-slice_reduce_fusion.partner_ref, f32[1,1536]{1,0:T(1,128)S(1)} %get-tuple-element.33.row_ref, f32[1,768]{1,0:T(1,128)S(1)} %get-tuple-element.34.own_ref, f32[32,1,768]{2,1,0:T(1,128)S(1)} %all_to_all.21.everyone_ref, ...), custom_call_target="tpu_custom_call" | custom-call | flops 1358954496 | bytes 3538944 | tf_op jit(solution)/shard_map/backward_0_192/pallas_call | solution.py:415
  112.8 3.7 %collective-permute-start.12 = (f32[192,256]{1,0:T(8,128)S(1)}, f32[192,256]{1,0:T(8,128)S(1)}, u32[]{:S(2)}, u32[]{:S(2)}) collective-permute-start(f32[192,256]{1,0:T(8,128)S(1)} %get-tuple-element.48), channel_id=1, source_target_pairs={{0,6},{1,7},{2,0},{3,1},{4,2},{5,3},{6,4},{7,5},{8,14},{9,15},{10,... | collective-permute-start | bytes 589832 | tf_op jit(solution)/shard_map/ppermute | solution.py:479
  116.4 4.5 %backward_2_0.1.run_ref = f32[384,256]{1,0:T(8,128)S(1)} custom-call(s32[2]{0:T(128)S(1)} %dynamic-slice_reduce_fusion.partner_ref, f32[1,1536]{1,0:T(1,128)S(1)} %get-tuple-element.33.row_ref, f32[1,768]{1,0:T(1,128)S(1)} %get-tuple-element.34.own_ref, f32[32,1,768]{2,1,0:T(1,128)S(1)} %all_to_all.21.everyone_ref, ...), custom_call_target="tpu_custom_call" | custom-call | flops 1358954496 | bytes 3538944 | tf_op jit(solution)/shard_map/backward_2_0/pallas_call | solution.py:415
  121.0 1.6 %collective-permute-done.9.low0 = f32[192,256]{1,0:T(8,128)S(1)} collective-permute-done((f32[192,256]{1,0:T(8,128)S(1)}, f32[192,256]{1,0:T(8,128)S(1)}, u32[]{:S(2)}, u32[]{:S(2)}) %collective-permute-start.9) | collective-permute-done | bytes 196640 | tf_op jit(solution)/shard_map/ppermute | solution.py:479
  122.6 1.3 %collective-permute-done.12.high1 = f32[192,256]{1,0:T(8,128)S(1)} collective-permute-done((f32[192,256]{1,0:T(8,128)S(1)}, f32[192,256]{1,0:T(8,128)S(1)}, u32[]{:S(2)}, u32[]{:S(2)}) %collective-permute-start.12) | collective-permute-done | bytes 196640 | tf_op jit(solution)/shard_map/ppermute | solution.py:479
  (30 shorter events, 4.3 us)
Async XLA Ops:
  0.6 23.5 %collective-permute-start.1 = (f32[384,256]{1,0:T(8,128)}, f32[384,256]{1,0:T(8,128)S(1)}, u32[]{:S(2)}, u32[]{:S(2)}) collective-permute-start(f32[384,256]{1,0:T(8,128)} %emb_ref.1), channel_id=1, source_target_pairs={{0,6},{1,7},{2,0},{3,1},{4,2},{5,3},{6,4},{7,5},{8,14},{9,15},{10,... | collective-permute-start | bytes 1179656 | tf_op jit(solution)/shard_map/ppermute | solution.py:479
  7.0 21.9 %collective-permute-start = (f32[384,256]{1,0:T(8,128)}, f32[384,256]{1,0:T(8,128)S(1)}, u32[]{:S(2)}, u32[]{:S(2)}) collective-permute-start(f32[384,256]{1,0:T(8,128)} %emb_ref.1), channel_id=1, source_target_pairs={{0,2},{1,3},{2,4},{3,5},{4,6},{5,7},{6,0},{7,1},{8,10},{9,11},{10,... | collective-permute-start | bytes 1179656 | tf_op jit(solution)/shard_map/ppermute | solution.py:479
  7.0 35.4 %collective-permute-start.4 = (f32[384,256]{1,0:T(8,128)}, f32[384,256]{1,0:T(8,128)S(1)}, u32[]{:S(2)}, u32[]{:S(2)}) collective-permute-start(f32[384,256]{1,0:T(8,128)} %emb_ref.1), channel_id=1, source_target_pairs={{0,1},{1,0},{2,3},{3,2},{4,5},{5,4},{6,7},{7,6},{8,9},{9,8},{10,11... | collective-permute-start | bytes 1179656 | tf_op jit(solution)/shard_map/ppermute | solution.py:482
  7.0 27.5 %all-to-all-start = ((f32[32,24,128]{2,1,0:T(8,128)}), f32[32,24,128]{2,1,0:T(8,128)S(1)}, u32[]{:S(2)}, u32[]{:S(2)}) async-start(f32[32,24,128]{2,1,0:T(8,128)} %bitcast.6), calls=%async_computation | async-start | bytes 786432 | tf_op jit(solution)/shard_map/all_to_all | solution.py:488
  15.0 1.7 %collective-permute-start.5 = (s32[384]{0:T(512)}, s32[384]{0:T(512)S(1)}, u32[]{:S(2)}, u32[]{:S(2)}) collective-permute-start(s32[384]{0:T(512)} %param.4), channel_id=1, source_target_pairs={{0,1},{1,0},{2,3},{3,2},{4,5},{5,4},{6,7},{7,6},{8,9},{9,8},{10,11... | collective-permute-start | bytes 4616 | tf_op jit(solution)/shard_map/ppermute | solution.py:482
  24.2 16.8 %collective-permute-start.3 = (f32[192,256]{1,0:T(8,128)S(1)}, f32[192,256]{1,0:T(8,128)S(1)}, u32[]{:S(2)}, u32[]{:S(2)}) collective-permute-start(f32[192,256]{1,0:T(8,128)S(1)} %slice.9), channel_id=1, source_target_pairs={{0,6},{1,7},{2,0},{3,1},{4,2},{5,3},{6,4},{7,5},{8,14},{9,15},{10,... | collective-permute-start | bytes 589832 | tf_op jit(solution)/shard_map/ppermute | solution.py:479
  28.9 5.6 %copy-start.1 = (s32[2,32]{1,0:T(2,128)S(1)}, s32[2,32]{1,0:T(2,128)}, u32[]{:S(2)}) copy-start(s32[2,32]{1,0:T(2,128)} %pairing_ref.1) | copy-start | bytes 772
  28.9 12.1 %collective-permute-start.2 = (f32[192,256]{1,0:T(8,128)S(1)}, f32[192,256]{1,0:T(8,128)S(1)}, u32[]{:S(2)}, u32[]{:S(2)}) collective-permute-start(f32[192,256]{1,0:T(8,128)S(1)} %slice.8), channel_id=1, source_target_pairs={{0,2},{1,3},{2,4},{3,5},{4,6},{5,7},{6,0},{7,1},{8,10},{9,11},{10,... | collective-permute-start | bytes 589832 | tf_op jit(solution)/shard_map/ppermute | solution.py:479
  30.4 10.6 %copy-start = (f32[384,256]{1,0:T(8,128)S(1)}, f32[384,256]{1,0:T(8,128)}, u32[]{:S(2)}) copy-start(f32[384,256]{1,0:T(8,128)} %emb_ref.1) | copy-start | bytes 1179652
  36.0 17.8 %all-to-all-start.1 = ((f32[32,48,128]{2,1,0:T(8,128)}), f32[32,48,128]{2,1,0:T(8,128)S(1)}, u32[]{:S(2)}, u32[]{:S(2)}) async-start(f32[32,48,128]{2,1,0:T(8,128)} %pick.1), calls=%async_computation.1 | async-start | bytes 1572864 | tf_op jit(solution)/shard_map/all_to_all | solution.py:491
  53.8 2.3 %collective-permute-start.6 = (f32[32,48,128]{2,1,0:T(8,128)S(1)}, f32[32,48,128]{2,1,0:T(8,128)S(1)}, u32[]{:S(2)}, u32[]{:S(2)}) collective-permute-start(f32[32,48,128]{2,1,0:T(8,128)S(1)} %all-to-all-done.1.got), channel_id=1, source_target_pairs={{0,1},{1,0},{2,3},{3,2},{4,5},{5,4},{6,7},{7,6},{8,9},{9,8},{10,11... | collective-permute-start | bytes 2359304 | tf_op jit(solution)/shard_map/ppermute | solution.py:482
  95.8 16.4 %collective-permute-start.7 = (f32[192,256]{1,0:T(8,128)S(1)}, f32[192,256]{1,0:T(8,128)S(1)}, u32[]{:S(2)}, u32[]{:S(2)}) collective-permute-start(f32[192,256]{1,0:T(8,128)S(1)} %get-tuple-element.42), channel_id=1, source_target_pairs={{0,2},{1,3},{2,4},{3,5},{4,6},{5,7},{6,0},{7,1},{8,10},{9,11},{10,... | collective-permute-start | bytes 589832 | tf_op jit(solution)/shard_map/ppermute | solution.py:479
  96.3 15.8 %collective-permute-start.8 = (f32[192,256]{1,0:T(8,128)S(1)}, f32[192,256]{1,0:T(8,128)S(1)}, u32[]{:S(2)}, u32[]{:S(2)}) collective-permute-start(f32[192,256]{1,0:T(8,128)S(1)} %get-tuple-element.44), channel_id=1, source_target_pairs={{0,6},{1,7},{2,0},{3,1},{4,2},{5,3},{6,4},{7,5},{8,14},{9,15},{10,... | collective-permute-start | bytes 589832 | tf_op jit(solution)/shard_map/ppermute | solution.py:479
  104.6 16.4 %collective-permute-start.10 = (f32[192,256]{1,0:T(8,128)S(1)}, f32[192,256]{1,0:T(8,128)S(1)}, u32[]{:S(2)}, u32[]{:S(2)}) collective-permute-start(f32[192,256]{1,0:T(8,128)S(1)} %get-tuple-element.46), channel_id=1, source_target_pairs={{0,6},{1,7},{2,0},{3,1},{4,2},{5,3},{6,4},{7,5},{8,14},{9,15},{10,... | collective-permute-start | bytes 589832 | tf_op jit(solution)/shard_map/ppermute | solution.py:479
  104.7 16.3 %collective-permute-start.11 = (f32[192,256]{1,0:T(8,128)S(1)}, f32[192,256]{1,0:T(8,128)S(1)}, u32[]{:S(2)}, u32[]{:S(2)}) collective-permute-start(f32[192,256]{1,0:T(8,128)S(1)} %get-tuple-element.47), channel_id=1, source_target_pairs={{0,2},{1,3},{2,4},{3,5},{4,6},{5,7},{6,0},{7,1},{8,10},{9,11},{10,... | collective-permute-start | bytes 589832 | tf_op jit(solution)/shard_map/ppermute | solution.py:479
  112.2 10.3 %collective-permute-start.9 = (f32[192,256]{1,0:T(8,128)S(1)}, f32[192,256]{1,0:T(8,128)S(1)}, u32[]{:S(2)}, u32[]{:S(2)}) collective-permute-start(f32[192,256]{1,0:T(8,128)S(1)} %get-tuple-element.45), channel_id=1, source_target_pairs={{0,2},{1,3},{2,4},{3,5},{4,6},{5,7},{6,0},{7,1},{8,10},{9,11},{10,... | collective-permute-start | bytes 589832 | tf_op jit(solution)/shard_map/ppermute | solution.py:479
  112.8 11.1 %collective-permute-start.12 = (f32[192,256]{1,0:T(8,128)S(1)}, f32[192,256]{1,0:T(8,128)S(1)}, u32[]{:S(2)}, u32[]{:S(2)}) collective-permute-start(f32[192,256]{1,0:T(8,128)S(1)} %get-tuple-element.48), channel_id=1, source_target_pairs={{0,6},{1,7},{2,0},{3,1},{4,2},{5,3},{6,4},{7,5},{8,14},{9,15},{10,... | collective-permute-start | bytes 589832 | tf_op jit(solution)/shard_map/ppermute | solution.py:479

commit v13 on v12

--- a/solution.py
+++ b/solution.py
@@ -49,19 +49,30 @@
     return pltpu.CompilerParams(vmem_limit_bytes=limit)
 
 
-def pick_kernel(pairing_ref, pieces_ref, out_ref):
+def pick_kernel(pairing_ref, pieces_ref, out_ref, buf, sems):
     size = pieces_ref.shape[1]
-    for which in range(out_ref.shape[1] // size):
-        for group in range(out_ref.shape[0]):
-            out_ref[group, which * size : which * size + size] = pieces_ref[pairing_ref[which, group]]
+    part = buf.shape[0] // sems.shape[0]
+    copies = []
+    for begin in range(0, buf.shape[0], part):
+        for group in range(begin, begin + part):
+            for which in range(buf.shape[1] // size):
+                buf[group, which * size : which * size + size] = pieces_ref[pairing_ref[which, group]]
+        view = (pl.ds(begin, part),)
+        copies.append(pltpu.make_async_copy(buf.at[view], out_ref.at[view], sems.at[begin // part]))
+        copies[-1].start()
+    for copy in copies:
+        copy.wait()
 
 
 def pick(pairing, pieces):
     rounds, groups = pairing.shape
+    shape = ((groups, rounds * pieces.shape[1], 128), jnp.float32)
     return pl.pallas_call(
         pick_kernel,
         in_specs=[SMEM, pl.BlockSpec()],
-        out_shape=jax.ShapeDtypeStruct((groups, rounds * pieces.shape[1], 128), jnp.float32),
+        out_specs=HBM,
+        out_shape=pltpu.HBM(*shape),
+        scratch_shapes=[pltpu.VMEM(*shape), pltpu.SemaphoreType.DMA((4,))],
         compiler_params=params(),
         name="pick",
     )(pairing, pieces)
@@ -254,9 +265,10 @@
             tot_ref[band * wide : band * wide + wide] = total
         else:
             tot_ref[band * wide : band * wide + wide] += total
-        view = (pl.ds(chunk * many, many), pl.ds(2 * band, 2))
-        copies.append(pltpu.make_async_copy(e_buf.at[view], e_out.at[view], e_sem.at[turn]))
-        copies[-1].start()
+        for k in range(many):
+            view = (chunk * many + k, pl.ds(2 * band, 2))
+            copies.append(pltpu.make_async_copy(e_buf.at[view], e_out.at[view], e_sem.at[turn, k]))
+            copies[-1].start()
 
     total = as_line(tot_ref[...]) + line_in[0:1]
     for member in range(line_ref.shape[0]):
@@ -285,7 +297,7 @@
             pltpu.VMEM((rows, 128), jnp.float32),
             pltpu.SemaphoreType.DMA((2,)),
             pltpu.SemaphoreType.DMA((2,)),
-            pltpu.SemaphoreType.DMA((4,)),
+            pltpu.SemaphoreType.DMA((4, 3)),
         ],
         cost_estimate=pl.CostEstimate(
             flops=12 * rows * wide * WIDTH, bytes_accessed=8 * rows * wide, transcendentals=2 * rows * wide
@@ -345,26 +357,25 @@
     copies = []
     for step, (start, many) in enumerate(STEPS):
         group = []
-        for k, (source, low, high) in enumerate(
-            ((0, 0, own_pieces), (1, own_pieces, own_pieces + e1_in.shape[0]))
-        ):
-            begin, end = max(start, low), min(start + many, high)
-            if begin >= end:
-                continue
-            here, there = pl.ds(begin, end - begin), pl.ds(begin - low, end - begin)
+        for k in range(many):
+            piece = start + k
+            if piece < own_pieces:
+                e_src, place = e0_in, piece
+            else:
+                e_src, place = e1_in, piece - own_pieces
             at = 0
             for which, (order, row, size) in enumerate(bands):
                 group.append(
                     pltpu.make_async_copy(
-                        (e0_in, e1_in)[source].at[there, order, pl.ds(row, size)],
-                        e_buf.at[here, pl.ds(at, size)],
+                        e_src.at[place, order, pl.ds(row, size)],
+                        e_buf.at[piece, pl.ds(at, size)],
                         e_sem.at[step, k, which],
                     )
                 )
                 at += size
             if first:
-                src = (c0_in, c1_in)[source].at[there]
-                group.append(pltpu.make_async_copy(src, c_ref.at[here], c_sem.at[step, k]))
+                c_src = c0_in if piece < own_pieces else c1_in
+                group.append(pltpu.make_async_copy(c_src.at[place], c_ref.at[piece], c_sem.at[step, k]))
         copies.append(group)
         for copy in group:
             copy.start()
@@ -419,8 +430,8 @@
         scratch_shapes=[
             pltpu.VMEM((SLICE, WIDTH), jnp.float32),
             pltpu.VMEM((9, SLICE, PIECE), jnp.float32),
-            pltpu.SemaphoreType.DMA((len(STEPS), 2, len(bands))),
-            pltpu.SemaphoreType.DMA((len(STEPS), 2)),
+            pltpu.SemaphoreType.DMA((len(STEPS), 3, len(bands))),
+            pltpu.SemaphoreType.DMA((len(STEPS), 3)),
         ],
         cost_estimate=pl.CostEstimate(
             flops=6 * SLICE * count * WIDTH, bytes_accessed=4 * SLICE * count, transcendentals=0

time: 125 us -> 126 us (level)
  no operation moved by 1% of the time
where the time goes in v13:
time: 126 us
  Pallas kernels  38.1 us (30%)
  starting transfers between devices  35.5 us (28%)
  blocking collectives  27.3 us (22%)
  waiting for transfers between devices  22.1 us (18%)
  local copies, waits for them, and re-layouts  1.59 us (1%)
    ppermute x10, starting transfers between devices, shift(): lax.ppermute(value, 'mem', [(m, (m + by) % members) for m in range(member...  22.5 us
    pallas_call x4, Pallas kernels, backward(): pl.pallas_call(functools.partial(backward_kernel, bands, first), in_specs...  19.2 us
    all_to_all x1, blocking collectives, local(): everything = lax.all_to_all(line, 'mem', 0, 0, tiled=True)  15 us
    all_to_all x1, blocking collectives, local(): everyone = lax.all_to_all(spread, 'grp', 0, 0, tiled=True)  12.4 us
    ppermute x10, waiting for transfers between devices, shift(): lax.ppermute(value, 'mem', [(m, (m + by) % members) for m in range(member...  9.91 us
    all_to_all x1, starting transfers between devices, local(): lax.all_to_all(tiles.reshape(groups, per, 128), 'grp', 0, 0, tiled=True)  7.99 us
    pallas_call x1, Pallas kernels, forward(): pl.pallas_call(forward_kernel, in_specs=[HBM] * 2 + [pl.BlockSpec()] * 3,...  7.83 us
    all_to_all x1, waiting for transfers between devices, local(): got = lax.all_to_all(picked, 'grp', 0, 0, tiled=True)  5.73 us
  transfers between devices with their start and end apart: 15, of which 7 were waited for; matrix products, arithmetic and copies ran while one was open for 1% of the time, Pallas kernels for 19%

profile of v13, /device:TPU:8, one launch (start us, length us, event | category | flops | bytes accessed | tf_op | source)
XLA Modules:
  0.0 125.6 jit_solution(15995159104809875514)
XLA Ops:
  0.6 6.4 %collective-permute-start.1 = (f32[384,256]{1,0:T(8,128)}, f32[384,256]{1,0:T(8,128)S(1)}, u32[]{:S(2)}, u32[]{:S(2)}) collective-permute-start(f32[384,256]{1,0:T(8,128)} %emb_ref.1), channel_id=1, source_target_pairs={{0,6},{1,7},{2,0},{3,1},{4,2},{5,3},{6,4},{7,5},{8,14},{9,15},{10,... | collective-permute-start | bytes 1179656 | tf_op jit(solution)/shard_map/ppermute | solution.py:490
  7.0 8.0 %all-to-all-start = ((f32[32,24,128]{2,1,0:T(8,128)}), f32[32,24,128]{2,1,0:T(8,128)S(1)}, u32[]{:S(2)}, u32[]{:S(2)}) async-start(f32[32,24,128]{2,1,0:T(8,128)} %bitcast.6), calls=%async_computation | async-start | bytes 786432 | tf_op jit(solution)/shard_map/all_to_all | solution.py:499
  16.8 7.4 %collective-permute-done.1.refs_1_ = f32[384,256]{1,0:T(8,128)S(1)} collective-permute-done((f32[384,256]{1,0:T(8,128)}, f32[384,256]{1,0:T(8,128)S(1)}, u32[]{:S(2)}, u32[]{:S(2)}) %collective-permute-start.1) | collective-permute-done | bytes 393248 | tf_op jit(solution)/shard_map/ppermute | solution.py:490
  24.2 4.6 %collective-permute-start.3 = (f32[192,256]{1,0:T(8,128)S(1)}, f32[192,256]{1,0:T(8,128)S(1)}, u32[]{:S(2)}, u32[]{:S(2)}) collective-permute-start(f32[192,256]{1,0:T(8,128)S(1)} %slice.9), channel_id=1, source_target_pairs={{0,6},{1,7},{2,0},{3,1},{4,2},{5,3},{6,4},{7,5},{8,14},{9,15},{10,... | collective-permute-start | bytes 589832 | tf_op jit(solution)/shard_map/ppermute | solution.py:490
  29.0 1.4 %prepare.1.ready = bf16[768,768]{1,0:T(8,128)(2,1)} custom-call(f32[384,256]{1,0:T(8,128)S(1)} %collective-permute-done.refs_0_, f32[384,256]{1,0:T(8,128)S(1)} %collective-permute-done.1.refs_1_), custom_call_target="tpu_custom_call" | custom-call | flops 20000000000 | bytes 1572864 | tf_op jit(solution)/shard_map/prepare/pallas_call | solution.py:208
  30.4 4.1 %all-to-all-done.pieces_ref = f32[32,24,128]{2,1,0:T(8,128)S(1)} async-done(((f32[32,24,128]{2,1,0:T(8,128)}), f32[32,24,128]{2,1,0:T(8,128)S(1)}, u32[]{:S(2)}, u32[]{:S(2)}) %all-to-all-start) | async-done | bytes 393248 | tf_op jit(solution)/shard_map/all_to_all | solution.py:499
  34.5 1.5 %pick.1 = f32[32,48,128]{2,1,0:T(8,128)} custom-call(s32[2,32]{1,0:T(2,128)S(1)} %copy-done.1, f32[32,24,128]{2,1,0:T(8,128)S(1)} %all-to-all-done.pieces_ref), custom_call_target="tpu_custom_call" | custom-call | tf_op jit(solution)/shard_map/pick/pallas_call | solution.py:70
  36.0 4.9 %all-to-all-start.1 = ((f32[32,48,128]{2,1,0:T(8,128)}), f32[32,48,128]{2,1,0:T(8,128)S(1)}, u32[]{:S(2)}, u32[]{:S(2)}) async-start(f32[32,48,128]{2,1,0:T(8,128)} %pick.1), calls=%async_computation.1 | async-start | bytes 1572864 | tf_op jit(solution)/shard_map/all_to_all | solution.py:502
  41.0 1.4 %prepare_far.1.ready_far = bf16[768,768]{1,0:T(8,128)(2,1)} custom-call(f32[384,256]{1,0:T(8,128)S(1)} %copy-done, f32[192,256]{1,0:T(8,128)S(1)} %collective-permute-done.2.refs_1_, f32[192,256]{1,0:T(8,128)S(1)} %collective-permute-done.3.refs_2_), custom_call_target="tpu_custom_call" | custom-call | flops 20000000000 | bytes 1572864 | tf_op jit(solution)/shard_map/prepare_far/pallas_call | solution.py:208
  42.4 5.7 %own_scores.1 = (bf16[3,256,512]{2,1,0:T(8,128)(2,1)}, f32[3,4,384,256]{3,2,1,0:T(8,128)}, f32[2,1536]{1,0:T(2,128)S(1)}) custom-call(bf16[768,768]{1,0:T(8,128)(2,1)} %prepare.1.ready, bf16[768,768]{1,0:T(8,128)(2,1)} %prepare_far.1.ready_far, f32[384,256]{1,0:T(8,128)S(1)} %copy-done, f32[384,256]{1,0:T(8,128)S(1)} %collective-permute-done.4.sib, ...), custom_call_target="tpu_custom_call" | custom-call | flops 1811939328 | bytes 4718592 | tf_op jit(solution)/shard_map/own_scores/pallas_call | solution.py:176
  48.1 5.7 %all-to-all-done.1.got = f32[32,48,128]{2,1,0:T(8,128)S(1)} async-done(((f32[32,48,128]{2,1,0:T(8,128)}), f32[32,48,128]{2,1,0:T(8,128)S(1)}, u32[]{:S(2)}, u32[]{:S(2)}) %all-to-all-start.1) | async-done | bytes 786464 | tf_op jit(solution)/shard_map/all_to_all | solution.py:502
  53.9 2.3 %collective-permute-done.6.got_sib = f32[32,48,128]{2,1,0:T(8,128)S(1)} collective-permute-done((f32[32,48,128]{2,1,0:T(8,128)S(1)}, f32[32,48,128]{2,1,0:T(8,128)S(1)}, u32[]{:S(2)}, u32[]{:S(2)}) %collective-permute-start.6) | collective-permute-done | bytes 786464 | tf_op jit(solution)/shard_map/ppermute | solution.py:493
  56.1 7.8 %forward.1 = (f32[6,4,384,256]{3,2,1,0:T(8,128)}, bf16[6,256,512]{2,1,0:T(8,128)(2,1)}, f32[8,2,1536]{2,1,0:T(2,128)S(1)}) custom-call(bf16[768,768]{1,0:T(8,128)(2,1)} %prepare.1.ready, bf16[768,768]{1,0:T(8,128)(2,1)} %prepare_far.1.ready_far, f32[2,1536]{1,0:T(2,128)S(1)} %get-tuple-element.30.line_in, f32[32,48,128]{2,1,0:T(8,128)S(1)} %all-to-all-done.1.got, ...), custom_call_target="tpu_custom_call" | custom-call | flops 3623878656 | bytes 9437184 | tf_op jit(solution)/shard_map/forward/pallas_call | solution.py:284
  64.0 15.0 %all_to_all.20.all_ref = f32[8,2,1536]{2,1,0:T(2,128)S(1)} all-to-all(f32[8,2,1536]{2,1,0:T(2,128)S(1)} %get-tuple-element.32), channel_id=1, replica_groups=mesh['grp'=32,'mem'=8] {'mem'}, dimensions={0} | all-to-all | bytes 196608 | tf_op jit(solution)/shard_map/all_to_all | solution.py:516
  79.0 12.4 %all_to_all.21.everyone_ref = f32[32,1,768]{2,1,0:T(1,128)S(1)} all-to-all(f32[32,1,768]{2,1,0:T(1,128)S(1)} %get-tuple-element.35), channel_id=1, replica_groups=mesh['grp'=32,'mem'=8] {'grp'}, dimensions={0} | all-to-all | bytes 196608 | tf_op jit(solution)/shard_map/all_to_all | solution.py:518
  91.4 4.9 %backward_3_0.1 = (bf16[9,256,512]{2,1,0:T(8,128)(2,1)S(1)}, f32[192,256]{1,0:T(8,128)S(1)}, f32[192,256]{1,0:T(8,128)S(1)}) custom-call(s32[2]{0:T(128)S(1)} %dynamic-slice_reduce_fusion.partner_ref, f32[1,1536]{1,0:T(1,128)S(1)} %get-tuple-element.33.row_ref, f32[1,768]{1,0:T(1,128)S(1)} %get-tuple-element.34.own_ref, ...), custom_call_target="tpu_custom_call" | custom-call | flops 1358954496 | bytes 3538944 | tf_op jit(solution)/shard_map/backward_3_0/pallas_call | solution.py:426
  96.8 3.7 %collective-permute-start.8 = (f32[192,256]{1,0:T(8,128)S(1)}, f32[192,256]{1,0:T(8,128)S(1)}, u32[]{:S(2)}, u32[]{:S(2)}) collective-permute-start(f32[192,256]{1,0:T(8,128)S(1)} %get-tuple-element.44), channel_id=1, source_target_pairs={{0,6},{1,7},{2,0},{3,1},{4,2},{5,3},{6,4},{7,5},{8,14},{9,15},{10,... | collective-permute-start | bytes 589832 | tf_op jit(solution)/shard_map/ppermute | solution.py:490
  100.4 4.8 %backward_0_0.1 = (f32[192,256]{1,0:T(8,128)S(1)}, f32[192,256]{1,0:T(8,128)S(1)}) custom-call(s32[2]{0:T(128)S(1)} %dynamic-slice_reduce_fusion.partner_ref, f32[1,1536]{1,0:T(1,128)S(1)} %get-tuple-element.33.row_ref, f32[1,768]{1,0:T(1,128)S(1)} %get-tuple-element.34.own_ref, f32[32,1,768]{2,1,0:T(1,128)S(1)} %all_to_all.21.everyone_ref, ...), custom_call_target="tpu_custom_call" | custom-call | flops 1358954496 | bytes 3538944 | tf_op jit(solution)/shard_map/backward_0_0/pallas_call | solution.py:426
  105.4 2.9 %collective-permute-start.11 = (f32[192,256]{1,0:T(8,128)S(1)}, f32[192,256]{1,0:T(8,128)S(1)}, u32[]{:S(2)}, u32[]{:S(2)}) collective-permute-start(f32[192,256]{1,0:T(8,128)S(1)} %get-tuple-element.47), channel_id=1, source_target_pairs={{0,2},{1,3},{2,4},{3,5},{4,6},{5,7},{6,0},{7,1},{8,10},{9,11},{10,... | collective-permute-start | bytes 589832 | tf_op jit(solution)/shard_map/ppermute | solution.py:490
  108.3 4.8 %backward_0_192.1 = (f32[192,256]{1,0:T(8,128)S(1)}, f32[192,256]{1,0:T(8,128)S(1)}) custom-call(s32[2]{0:T(128)S(1)} %dynamic-slice_reduce_fusion.partner_ref, f32[1,1536]{1,0:T(1,128)S(1)} %get-tuple-element.33.row_ref, f32[1,768]{1,0:T(1,128)S(1)} %get-tuple-element.34.own_ref, f32[32,1,768]{2,1,0:T(1,128)S(1)} %all_to_all.21.everyone_ref, ...), custom_call_target="tpu_custom_call" | custom-call | flops 1358954496 | bytes 3538944 | tf_op jit(solution)/shard_map/backward_0_192/pallas_call | solution.py:426
  113.7 3.7 %collective-permute-start.12 = (f32[192,256]{1,0:T(8,128)S(1)}, f32[192,256]{1,0:T(8,128)S(1)}, u32[]{:S(2)}, u32[]{:S(2)}) collective-permute-start(f32[192,256]{1,0:T(8,128)S(1)} %get-tuple-element.48), channel_id=1, source_target_pairs={{0,6},{1,7},{2,0},{3,1},{4,2},{5,3},{6,4},{7,5},{8,14},{9,15},{10,... | collective-permute-start | bytes 589832 | tf_op jit(solution)/shard_map/ppermute | solution.py:490
  117.4 4.6 %backward_2_0.1.run_ref = f32[384,256]{1,0:T(8,128)S(1)} custom-call(s32[2]{0:T(128)S(1)} %dynamic-slice_reduce_fusion.partner_ref, f32[1,1536]{1,0:T(1,128)S(1)} %get-tuple-element.33.row_ref, f32[1,768]{1,0:T(1,128)S(1)} %get-tuple-element.34.own_ref, f32[32,1,768]{2,1,0:T(1,128)S(1)} %all_to_all.21.everyone_ref, ...), custom_call_target="tpu_custom_call" | custom-call | flops 1358954496 | bytes 3538944 | tf_op jit(solution)/shard_map/backward_2_0/pallas_call | solution.py:426
  122.1 1.1 collective-permute-done.9.low0
  123.2 1.4 %collective-permute-done.12.high1 = f32[192,256]{1,0:T(8,128)S(1)} collective-permute-done((f32[192,256]{1,0:T(8,128)S(1)}, f32[192,256]{1,0:T(8,128)S(1)}, u32[]{:S(2)}, u32[]{:S(2)}) %collective-permute-start.12) | collective-permute-done | bytes 196640 | tf_op jit(solution)/shard_map/ppermute | solution.py:490
  (30 shorter events, 4.3 us)
Async XLA Ops:
  0.6 23.5 %collective-permute-start.1 = (f32[384,256]{1,0:T(8,128)}, f32[384,256]{1,0:T(8,128)S(1)}, u32[]{:S(2)}, u32[]{:S(2)}) collective-permute-start(f32[384,256]{1,0:T(8,128)} %emb_ref.1), channel_id=1, source_target_pairs={{0,6},{1,7},{2,0},{3,1},{4,2},{5,3},{6,4},{7,5},{8,14},{9,15},{10,... | collective-permute-start | bytes 1179656 | tf_op jit(solution)/shard_map/ppermute | solution.py:490
  7.0 21.9 %collective-permute-start = (f32[384,256]{1,0:T(8,128)}, f32[384,256]{1,0:T(8,128)S(1)}, u32[]{:S(2)}, u32[]{:S(2)}) collective-permute-start(f32[384,256]{1,0:T(8,128)} %emb_ref.1), channel_id=1, source_target_pairs={{0,2},{1,3},{2,4},{3,5},{4,6},{5,7},{6,0},{7,1},{8,10},{9,11},{10,... | collective-permute-start | bytes 1179656 | tf_op jit(solution)/shard_map/ppermute | solution.py:490
  7.0 35.4 %collective-permute-start.4 = (f32[384,256]{1,0:T(8,128)}, f32[384,256]{1,0:T(8,128)S(1)}, u32[]{:S(2)}, u32[]{:S(2)}) collective-permute-start(f32[384,256]{1,0:T(8,128)} %emb_ref.1), channel_id=1, source_target_pairs={{0,1},{1,0},{2,3},{3,2},{4,5},{5,4},{6,7},{7,6},{8,9},{9,8},{10,11... | collective-permute-start | bytes 1179656 | tf_op jit(solution)/shard_map/ppermute | solution.py:493
  7.0 27.5 %all-to-all-start = ((f32[32,24,128]{2,1,0:T(8,128)}), f32[32,24,128]{2,1,0:T(8,128)S(1)}, u32[]{:S(2)}, u32[]{:S(2)}) async-start(f32[32,24,128]{2,1,0:T(8,128)} %bitcast.6), calls=%async_computation | async-start | bytes 786432 | tf_op jit(solution)/shard_map/all_to_all | solution.py:499
  15.0 1.7 %collective-permute-start.5 = (s32[384]{0:T(512)}, s32[384]{0:T(512)S(1)}, u32[]{:S(2)}, u32[]{:S(2)}) collective-permute-start(s32[384]{0:T(512)} %param.4), channel_id=1, source_target_pairs={{0,1},{1,0},{2,3},{3,2},{4,5},{5,4},{6,7},{7,6},{8,9},{9,8},{10,11... | collective-permute-start | bytes 4616 | tf_op jit(solution)/shard_map/ppermute | solution.py:493
  24.2 16.8 %collective-permute-start.3 = (f32[192,256]{1,0:T(8,128)S(1)}, f32[192,256]{1,0:T(8,128)S(1)}, u32[]{:S(2)}, u32[]{:S(2)}) collective-permute-start(f32[192,256]{1,0:T(8,128)S(1)} %slice.9), channel_id=1, source_target_pairs={{0,6},{1,7},{2,0},{3,1},{4,2},{5,3},{6,4},{7,5},{8,14},{9,15},{10,... | collective-permute-start | bytes 589832 | tf_op jit(solution)/shard_map/ppermute | solution.py:490
  28.9 5.6 %copy-start.1 = (s32[2,32]{1,0:T(2,128)S(1)}, s32[2,32]{1,0:T(2,128)}, u32[]{:S(2)}) copy-start(s32[2,32]{1,0:T(2,128)} %pairing_ref.1) | copy-start | bytes 772
  28.9 12.1 %collective-permute-start.2 = (f32[192,256]{1,0:T(8,128)S(1)}, f32[192,256]{1,0:T(8,128)S(1)}, u32[]{:S(2)}, u32[]{:S(2)}) collective-permute-start(f32[192,256]{1,0:T(8,128)S(1)} %slice.8), channel_id=1, source_target_pairs={{0,2},{1,3},{2,4},{3,5},{4,6},{5,7},{6,0},{7,1},{8,10},{9,11},{10,... | collective-permute-start | bytes 589832 | tf_op jit(solution)/shard_map/ppermute | solution.py:490
  30.4 10.6 %copy-start = (f32[384,256]{1,0:T(8,128)S(1)}, f32[384,256]{1,0:T(8,128)}, u32[]{:S(2)}) copy-start(f32[384,256]{1,0:T(8,128)} %emb_ref.1) | copy-start | bytes 1179652
  36.0 17.8 %all-to-all-start.1 = ((f32[32,48,128]{2,1,0:T(8,128)}), f32[32,48,128]{2,1,0:T(8,128)S(1)}, u32[]{:S(2)}, u32[]{:S(2)}) async-start(f32[32,48,128]{2,1,0:T(8,128)} %pick.1), calls=%async_computation.1 | async-start | bytes 1572864 | tf_op jit(solution)/shard_map/all_to_all | solution.py:502
  53.9 2.3 %collective-permute-start.6 = (f32[32,48,128]{2,1,0:T(8,128)S(1)}, f32[32,48,128]{2,1,0:T(8,128)S(1)}, u32[]{:S(2)}, u32[]{:S(2)}) collective-permute-start(f32[32,48,128]{2,1,0:T(8,128)S(1)} %all-to-all-done.1.got), channel_id=1, source_target_pairs={{0,1},{1,0},{2,3},{3,2},{4,5},{5,4},{6,7},{7,6},{8,9},{9,8},{10,11... | collective-permute-start | bytes 2359304 | tf_op jit(solution)/shard_map/ppermute | solution.py:493
  96.2 16.9 %collective-permute-start.7 = (f32[192,256]{1,0:T(8,128)S(1)}, f32[192,256]{1,0:T(8,128)S(1)}, u32[]{:S(2)}, u32[]{:S(2)}) collective-permute-start(f32[192,256]{1,0:T(8,128)S(1)} %get-tuple-element.42), channel_id=1, source_target_pairs={{0,2},{1,3},{2,4},{3,5},{4,6},{5,7},{6,0},{7,1},{8,10},{9,11},{10,... | collective-permute-start | bytes 589832 | tf_op jit(solution)/shard_map/ppermute | solution.py:490
  96.8 16.4 %collective-permute-start.8 = (f32[192,256]{1,0:T(8,128)S(1)}, f32[192,256]{1,0:T(8,128)S(1)}, u32[]{:S(2)}, u32[]{:S(2)}) collective-permute-start(f32[192,256]{1,0:T(8,128)S(1)} %get-tuple-element.44), channel_id=1, source_target_pairs={{0,6},{1,7},{2,0},{3,1},{4,2},{5,3},{6,4},{7,5},{8,14},{9,15},{10,... | collective-permute-start | bytes 589832 | tf_op jit(solution)/shard_map/ppermute | solution.py:490
  105.3 16.8 %collective-permute-start.10 = (f32[192,256]{1,0:T(8,128)S(1)}, f32[192,256]{1,0:T(8,128)S(1)}, u32[]{:S(2)}, u32[]{:S(2)}) collective-permute-start(f32[192,256]{1,0:T(8,128)S(1)} %get-tuple-element.46), channel_id=1, source_target_pairs={{0,6},{1,7},{2,0},{3,1},{4,2},{5,3},{6,4},{7,5},{8,14},{9,15},{10,... | collective-permute-start | bytes 589832 | tf_op jit(solution)/shard_map/ppermute | solution.py:490
  105.4 16.7 %collective-permute-start.11 = (f32[192,256]{1,0:T(8,128)S(1)}, f32[192,256]{1,0:T(8,128)S(1)}, u32[]{:S(2)}, u32[]{:S(2)}) collective-permute-start(f32[192,256]{1,0:T(8,128)S(1)} %get-tuple-element.47), channel_id=1, source_target_pairs={{0,2},{1,3},{2,4},{3,5},{4,6},{5,7},{6,0},{7,1},{8,10},{9,11},{10,... | collective-permute-start | bytes 589832 | tf_op jit(solution)/shard_map/ppermute | solution.py:490
  113.2 9.9 %collective-permute-start.9 = (f32[192,256]{1,0:T(8,128)S(1)}, f32[192,256]{1,0:T(8,128)S(1)}, u32[]{:S(2)}, u32[]{:S(2)}) collective-permute-start(f32[192,256]{1,0:T(8,128)S(1)} %get-tuple-element.45), channel_id=1, source_target_pairs={{0,2},{1,3},{2,4},{3,5},{4,6},{5,7},{6,0},{7,1},{8,10},{9,11},{10,... | collective-permute-start | bytes 589832 | tf_op jit(solution)/shard_map/ppermute | solution.py:490
  113.7 10.8 %collective-permute-start.12 = (f32[192,256]{1,0:T(8,128)S(1)}, f32[192,256]{1,0:T(8,128)S(1)}, u32[]{:S(2)}, u32[]{:S(2)}) collective-permute-start(f32[192,256]{1,0:T(8,128)S(1)} %get-tuple-element.48), channel_id=1, source_target_pairs={{0,6},{1,7},{2,0},{3,1},{4,2},{5,3},{6,4},{7,5},{8,14},{9,15},{10,... | collective-permute-start | bytes 589832 | tf_op jit(solution)/shard_map/ppermute | solution.py:490

commit v14 on v12

--- a/solution.py
+++ b/solution.py
@@ -13,7 +13,7 @@
 WIDTH = 256
 SELF = 2
 PIECE = 256
-STEPS = ((0, 3), (3, 3), (6, 3))
+STEPS = ((0, 4), (4, 5))
 VMEM = 16 * 1024 * 1024
 VMEM_LARGE = 44 * 1024 * 1024
 VMEM_BACKWARD = 28 * 1024 * 1024

time: 125 us -> 126 us (level)
  no operation moved by 1% of the time
where the time goes in v14:
time: 126 us; the launch traced here: 125 us
  Pallas kernels  37.9 us (30%)
  starting transfers between devices  35.5 us (28%)
  blocking collectives  27.3 us (22%)
  waiting for transfers between devices  22.1 us (18%)
  local copies, waits for them, and re-layouts  1.59 us (1%)
    ppermute x10, starting transfers between devices, shift(): lax.ppermute(value, 'mem', [(m, (m + by) % members) for m in range(member...  22.5 us
    pallas_call x4, Pallas kernels, backward(): pl.pallas_call(functools.partial(backward_kernel, bands, first), in_specs...  19.3 us
    all_to_all x1, blocking collectives, local(): everything = lax.all_to_all(line, 'mem', 0, 0, tiled=True)  15 us
    all_to_all x1, blocking collectives, local(): everyone = lax.all_to_all(spread, 'grp', 0, 0, tiled=True)  12.4 us
    ppermute x10, waiting for transfers between devices, shift(): lax.ppermute(value, 'mem', [(m, (m + by) % members) for m in range(member...  9.93 us
    all_to_all x1, starting transfers between devices, local(): lax.all_to_all(tiles.reshape(groups, per, 128), 'grp', 0, 0, tiled=True)  7.99 us
    pallas_call x1, Pallas kernels, forward(): pl.pallas_call(forward_kernel, in_specs=[HBM] * 2 + [pl.BlockSpec()] * 3,...  7.52 us
    pallas_call x1, Pallas kernels, own_scores(): pl.pallas_call(own_kernel, in_specs=[HBM] * 2 + [pl.BlockSpec()] * 3, out...  5.74 us
  transfers between devices with their start and end apart: 15, of which 7 were waited for; matrix products, arithmetic and copies ran while one was open for 1% of the time, Pallas kernels for 19%

profile of v14, /device:TPU:8, one launch (start us, length us, event | category | flops | bytes accessed | tf_op | source)
XLA Modules:
  0.0 125.4 jit_solution(16948916755591566568)
XLA Ops:
  0.6 6.4 %collective-permute-start.1 = (f32[384,256]{1,0:T(8,128)}, f32[384,256]{1,0:T(8,128)S(1)}, u32[]{:S(2)}, u32[]{:S(2)}) collective-permute-start(f32[384,256]{1,0:T(8,128)} %emb_ref.1), channel_id=1, source_target_pairs={{0,6},{1,7},{2,0},{3,1},{4,2},{5,3},{6,4},{7,5},{8,14},{9,15},{10,... | collective-permute-start | bytes 1179656 | tf_op jit(solution)/shard_map/ppermute | solution.py:479
  7.0 8.0 %all-to-all-start = ((f32[32,24,128]{2,1,0:T(8,128)}), f32[32,24,128]{2,1,0:T(8,128)S(1)}, u32[]{:S(2)}, u32[]{:S(2)}) async-start(f32[32,24,128]{2,1,0:T(8,128)} %bitcast.6), calls=%async_computation | async-start | bytes 786432 | tf_op jit(solution)/shard_map/all_to_all | solution.py:488
  16.8 7.4 %collective-permute-done.1.refs_1_ = f32[384,256]{1,0:T(8,128)S(1)} collective-permute-done((f32[384,256]{1,0:T(8,128)}, f32[384,256]{1,0:T(8,128)S(1)}, u32[]{:S(2)}, u32[]{:S(2)}) %collective-permute-start.1) | collective-permute-done | bytes 393248 | tf_op jit(solution)/shard_map/ppermute | solution.py:479
  24.2 4.6 %collective-permute-start.3 = (f32[192,256]{1,0:T(8,128)S(1)}, f32[192,256]{1,0:T(8,128)S(1)}, u32[]{:S(2)}, u32[]{:S(2)}) collective-permute-start(f32[192,256]{1,0:T(8,128)S(1)} %slice.9), channel_id=1, source_target_pairs={{0,6},{1,7},{2,0},{3,1},{4,2},{5,3},{6,4},{7,5},{8,14},{9,15},{10,... | collective-permute-start | bytes 589832 | tf_op jit(solution)/shard_map/ppermute | solution.py:479
  29.0 1.4 %prepare.1.ready = bf16[768,768]{1,0:T(8,128)(2,1)} custom-call(f32[384,256]{1,0:T(8,128)S(1)} %collective-permute-done.refs_0_, f32[384,256]{1,0:T(8,128)S(1)} %collective-permute-done.1.refs_1_), custom_call_target="tpu_custom_call" | custom-call | flops 20000000000 | bytes 1572864 | tf_op jit(solution)/shard_map/prepare/pallas_call | solution.py:197
  30.4 4.1 %all-to-all-done.pieces_ref = f32[32,24,128]{2,1,0:T(8,128)S(1)} async-done(((f32[32,24,128]{2,1,0:T(8,128)}), f32[32,24,128]{2,1,0:T(8,128)S(1)}, u32[]{:S(2)}, u32[]{:S(2)}) %all-to-all-start) | async-done | bytes 393248 | tf_op jit(solution)/shard_map/all_to_all | solution.py:488
  34.5 1.5 %pick.1 = f32[32,48,128]{2,1,0:T(8,128)} custom-call(s32[2,32]{1,0:T(2,128)S(1)} %copy-done.1, f32[32,24,128]{2,1,0:T(8,128)S(1)} %all-to-all-done.pieces_ref), custom_call_target="tpu_custom_call" | custom-call | tf_op jit(solution)/shard_map/pick/pallas_call | solution.py:61
  36.0 4.9 %all-to-all-start.1 = ((f32[32,48,128]{2,1,0:T(8,128)}), f32[32,48,128]{2,1,0:T(8,128)S(1)}, u32[]{:S(2)}, u32[]{:S(2)}) async-start(f32[32,48,128]{2,1,0:T(8,128)} %pick.1), calls=%async_computation.1 | async-start | bytes 1572864 | tf_op jit(solution)/shard_map/all_to_all | solution.py:491
  41.0 1.4 %prepare_far.1.ready_far = bf16[768,768]{1,0:T(8,128)(2,1)} custom-call(f32[384,256]{1,0:T(8,128)S(1)} %copy-done, f32[192,256]{1,0:T(8,128)S(1)} %collective-permute-done.2.refs_1_, f32[192,256]{1,0:T(8,128)S(1)} %collective-permute-done.3.refs_2_), custom_call_target="tpu_custom_call" | custom-call | flops 20000000000 | bytes 1572864 | tf_op jit(solution)/shard_map/prepare_far/pallas_call | solution.py:197
  42.4 5.7 %own_scores.1 = (bf16[3,256,512]{2,1,0:T(8,128)(2,1)}, f32[3,4,384,256]{3,2,1,0:T(8,128)}, f32[2,1536]{1,0:T(2,128)S(1)}) custom-call(bf16[768,768]{1,0:T(8,128)(2,1)} %prepare.1.ready, bf16[768,768]{1,0:T(8,128)(2,1)} %prepare_far.1.ready_far, f32[384,256]{1,0:T(8,128)S(1)} %copy-done, f32[384,256]{1,0:T(8,128)S(1)} %collective-permute-done.4.sib, ...), custom_call_target="tpu_custom_call" | custom-call | flops 1811939328 | bytes 4718592 | tf_op jit(solution)/shard_map/own_scores/pallas_call | solution.py:165
  48.1 5.7 %all-to-all-done.1.got = f32[32,48,128]{2,1,0:T(8,128)S(1)} async-done(((f32[32,48,128]{2,1,0:T(8,128)}), f32[32,48,128]{2,1,0:T(8,128)S(1)}, u32[]{:S(2)}, u32[]{:S(2)}) %all-to-all-start.1) | async-done | bytes 786464 | tf_op jit(solution)/shard_map/all_to_all | solution.py:491
  53.8 2.3 %collective-permute-done.6.got_sib = f32[32,48,128]{2,1,0:T(8,128)S(1)} collective-permute-done((f32[32,48,128]{2,1,0:T(8,128)S(1)}, f32[32,48,128]{2,1,0:T(8,128)S(1)}, u32[]{:S(2)}, u32[]{:S(2)}) %collective-permute-start.6) | collective-permute-done | bytes 786464 | tf_op jit(solution)/shard_map/ppermute | solution.py:482
  56.1 7.5 %forward.1 = (f32[6,4,384,256]{3,2,1,0:T(8,128)}, bf16[6,256,512]{2,1,0:T(8,128)(2,1)}, f32[8,2,1536]{2,1,0:T(2,128)S(1)}) custom-call(bf16[768,768]{1,0:T(8,128)(2,1)} %prepare.1.ready, bf16[768,768]{1,0:T(8,128)(2,1)} %prepare_far.1.ready_far, f32[2,1536]{1,0:T(2,128)S(1)} %get-tuple-element.30.line_in, f32[32,48,128]{2,1,0:T(8,128)S(1)} %all-to-all-done.1.got, ...), custom_call_target="tpu_custom_call" | custom-call | flops 3623878656 | bytes 9437184 | tf_op jit(solution)/shard_map/forward/pallas_call | solution.py:272
  63.7 15.0 %all_to_all.20.all_ref = f32[8,2,1536]{2,1,0:T(2,128)S(1)} all-to-all(f32[8,2,1536]{2,1,0:T(2,128)S(1)} %get-tuple-element.32), channel_id=1, replica_groups=mesh['grp'=32,'mem'=8] {'mem'}, dimensions={0} | all-to-all | bytes 196608 | tf_op jit(solution)/shard_map/all_to_all | solution.py:505
  78.7 12.4 %all_to_all.21.everyone_ref = f32[32,1,768]{2,1,0:T(1,128)S(1)} all-to-all(f32[32,1,768]{2,1,0:T(1,128)S(1)} %get-tuple-element.35), channel_id=1, replica_groups=mesh['grp'=32,'mem'=8] {'grp'}, dimensions={0} | all-to-all | bytes 196608 | tf_op jit(solution)/shard_map/all_to_all | solution.py:507
  91.0 5.0 %backward_3_0.1 = (bf16[9,256,512]{2,1,0:T(8,128)(2,1)S(1)}, f32[192,256]{1,0:T(8,128)S(1)}, f32[192,256]{1,0:T(8,128)S(1)}) custom-call(s32[2]{0:T(128)S(1)} %dynamic-slice_reduce_fusion.partner_ref, f32[1,1536]{1,0:T(1,128)S(1)} %get-tuple-element.33.row_ref, f32[1,768]{1,0:T(1,128)S(1)} %get-tuple-element.34.own_ref, ...), custom_call_target="tpu_custom_call" | custom-call | flops 1358954496 | bytes 3538944 | tf_op jit(solution)/shard_map/backward_3_0/pallas_call | solution.py:415
  96.6 3.7 %collective-permute-start.8 = (f32[192,256]{1,0:T(8,128)S(1)}, f32[192,256]{1,0:T(8,128)S(1)}, u32[]{:S(2)}, u32[]{:S(2)}) collective-permute-start(f32[192,256]{1,0:T(8,128)S(1)} %get-tuple-element.44), channel_id=1, source_target_pairs={{0,6},{1,7},{2,0},{3,1},{4,2},{5,3},{6,4},{7,5},{8,14},{9,15},{10,... | collective-permute-start | bytes 589832 | tf_op jit(solution)/shard_map/ppermute | solution.py:479
  100.3 4.8 %backward_0_0.1 = (f32[192,256]{1,0:T(8,128)S(1)}, f32[192,256]{1,0:T(8,128)S(1)}) custom-call(s32[2]{0:T(128)S(1)} %dynamic-slice_reduce_fusion.partner_ref, f32[1,1536]{1,0:T(1,128)S(1)} %get-tuple-element.33.row_ref, f32[1,768]{1,0:T(1,128)S(1)} %get-tuple-element.34.own_ref, f32[32,1,768]{2,1,0:T(1,128)S(1)} %all_to_all.21.everyone_ref, ...), custom_call_target="tpu_custom_call" | custom-call | flops 1358954496 | bytes 3538944 | tf_op jit(solution)/shard_map/backward_0_0/pallas_call | solution.py:415
  105.2 2.9 %collective-permute-start.11 = (f32[192,256]{1,0:T(8,128)S(1)}, f32[192,256]{1,0:T(8,128)S(1)}, u32[]{:S(2)}, u32[]{:S(2)}) collective-permute-start(f32[192,256]{1,0:T(8,128)S(1)} %get-tuple-element.47), channel_id=1, source_target_pairs={{0,2},{1,3},{2,4},{3,5},{4,6},{5,7},{6,0},{7,1},{8,10},{9,11},{10,... | collective-permute-start | bytes 589832 | tf_op jit(solution)/shard_map/ppermute | solution.py:479
  108.1 4.8 %backward_0_192.1 = (f32[192,256]{1,0:T(8,128)S(1)}, f32[192,256]{1,0:T(8,128)S(1)}) custom-call(s32[2]{0:T(128)S(1)} %dynamic-slice_reduce_fusion.partner_ref, f32[1,1536]{1,0:T(1,128)S(1)} %get-tuple-element.33.row_ref, f32[1,768]{1,0:T(1,128)S(1)} %get-tuple-element.34.own_ref, f32[32,1,768]{2,1,0:T(1,128)S(1)} %all_to_all.21.everyone_ref, ...), custom_call_target="tpu_custom_call" | custom-call | flops 1358954496 | bytes 3538944 | tf_op jit(solution)/shard_map/backward_0_192/pallas_call | solution.py:415
  113.4 3.7 %collective-permute-start.12 = (f32[192,256]{1,0:T(8,128)S(1)}, f32[192,256]{1,0:T(8,128)S(1)}, u32[]{:S(2)}, u32[]{:S(2)}) collective-permute-start(f32[192,256]{1,0:T(8,128)S(1)} %get-tuple-element.48), channel_id=1, source_target_pairs={{0,6},{1,7},{2,0},{3,1},{4,2},{5,3},{6,4},{7,5},{8,14},{9,15},{10,... | collective-permute-start | bytes 589832 | tf_op jit(solution)/shard_map/ppermute | solution.py:479
  117.1 4.7 %backward_2_0.1.run_ref = f32[384,256]{1,0:T(8,128)S(1)} custom-call(s32[2]{0:T(128)S(1)} %dynamic-slice_reduce_fusion.partner_ref, f32[1,1536]{1,0:T(1,128)S(1)} %get-tuple-element.33.row_ref, f32[1,768]{1,0:T(1,128)S(1)} %get-tuple-element.34.own_ref, f32[32,1,768]{2,1,0:T(1,128)S(1)} %all_to_all.21.everyone_ref, ...), custom_call_target="tpu_custom_call" | custom-call | flops 1358954496 | bytes 3538944 | tf_op jit(solution)/shard_map/backward_2_0/pallas_call | solution.py:415
  121.9 1.1 collective-permute-done.9.low0
  123.0 1.4 %collective-permute-done.12.high1 = f32[192,256]{1,0:T(8,128)S(1)} collective-permute-done((f32[192,256]{1,0:T(8,128)S(1)}, f32[192,256]{1,0:T(8,128)S(1)}, u32[]{:S(2)}, u32[]{:S(2)}) %collective-permute-start.12) | collective-permute-done | bytes 196640 | tf_op jit(solution)/shard_map/ppermute | solution.py:479
  (30 shorter events, 4.3 us)
Async XLA Ops:
  0.6 23.5 %collective-permute-start.1 = (f32[384,256]{1,0:T(8,128)}, f32[384,256]{1,0:T(8,128)S(1)}, u32[]{:S(2)}, u32[]{:S(2)}) collective-permute-start(f32[384,256]{1,0:T(8,128)} %emb_ref.1), channel_id=1, source_target_pairs={{0,6},{1,7},{2,0},{3,1},{4,2},{5,3},{6,4},{7,5},{8,14},{9,15},{10,... | collective-permute-start | bytes 1179656 | tf_op jit(solution)/shard_map/ppermute | solution.py:479
  7.0 21.9 %collective-permute-start = (f32[384,256]{1,0:T(8,128)}, f32[384,256]{1,0:T(8,128)S(1)}, u32[]{:S(2)}, u32[]{:S(2)}) collective-permute-start(f32[384,256]{1,0:T(8,128)} %emb_ref.1), channel_id=1, source_target_pairs={{0,2},{1,3},{2,4},{3,5},{4,6},{5,7},{6,0},{7,1},{8,10},{9,11},{10,... | collective-permute-start | bytes 1179656 | tf_op jit(solution)/shard_map/ppermute | solution.py:479
  7.0 35.4 %collective-permute-start.4 = (f32[384,256]{1,0:T(8,128)}, f32[384,256]{1,0:T(8,128)S(1)}, u32[]{:S(2)}, u32[]{:S(2)}) collective-permute-start(f32[384,256]{1,0:T(8,128)} %emb_ref.1), channel_id=1, source_target_pairs={{0,1},{1,0},{2,3},{3,2},{4,5},{5,4},{6,7},{7,6},{8,9},{9,8},{10,11... | collective-permute-start | bytes 1179656 | tf_op jit(solution)/shard_map/ppermute | solution.py:482
  7.0 27.5 %all-to-all-start = ((f32[32,24,128]{2,1,0:T(8,128)}), f32[32,24,128]{2,1,0:T(8,128)S(1)}, u32[]{:S(2)}, u32[]{:S(2)}) async-start(f32[32,24,128]{2,1,0:T(8,128)} %bitcast.6), calls=%async_computation | async-start | bytes 786432 | tf_op jit(solution)/shard_map/all_to_all | solution.py:488
  15.0 1.7 %collective-permute-start.5 = (s32[384]{0:T(512)}, s32[384]{0:T(512)S(1)}, u32[]{:S(2)}, u32[]{:S(2)}) collective-permute-start(s32[384]{0:T(512)} %param.4), channel_id=1, source_target_pairs={{0,1},{1,0},{2,3},{3,2},{4,5},{5,4},{6,7},{7,6},{8,9},{9,8},{10,11... | collective-permute-start | bytes 4616 | tf_op jit(solution)/shard_map/ppermute | solution.py:482
  24.2 16.8 %collective-permute-start.3 = (f32[192,256]{1,0:T(8,128)S(1)}, f32[192,256]{1,0:T(8,128)S(1)}, u32[]{:S(2)}, u32[]{:S(2)}) collective-permute-start(f32[192,256]{1,0:T(8,128)S(1)} %slice.9), channel_id=1, source_target_pairs={{0,6},{1,7},{2,0},{3,1},{4,2},{5,3},{6,4},{7,5},{8,14},{9,15},{10,... | collective-permute-start | bytes 589832 | tf_op jit(solution)/shard_map/ppermute | solution.py:479
  28.9 5.6 %copy-start.1 = (s32[2,32]{1,0:T(2,128)S(1)}, s32[2,32]{1,0:T(2,128)}, u32[]{:S(2)}) copy-start(s32[2,32]{1,0:T(2,128)} %pairing_ref.1) | copy-start | bytes 772
  28.9 12.1 %collective-permute-start.2 = (f32[192,256]{1,0:T(8,128)S(1)}, f32[192,256]{1,0:T(8,128)S(1)}, u32[]{:S(2)}, u32[]{:S(2)}) collective-permute-start(f32[192,256]{1,0:T(8,128)S(1)} %slice.8), channel_id=1, source_target_pairs={{0,2},{1,3},{2,4},{3,5},{4,6},{5,7},{6,0},{7,1},{8,10},{9,11},{10,... | collective-permute-start | bytes 589832 | tf_op jit(solution)/shard_map/ppermute | solution.py:479
  30.4 10.6 %copy-start = (f32[384,256]{1,0:T(8,128)S(1)}, f32[384,256]{1,0:T(8,128)}, u32[]{:S(2)}) copy-start(f32[384,256]{1,0:T(8,128)} %emb_ref.1) | copy-start | bytes 1179652
  36.0 17.8 %all-to-all-start.1 = ((f32[32,48,128]{2,1,0:T(8,128)}), f32[32,48,128]{2,1,0:T(8,128)S(1)}, u32[]{:S(2)}, u32[]{:S(2)}) async-start(f32[32,48,128]{2,1,0:T(8,128)} %pick.1), calls=%async_computation.1 | async-start | bytes 1572864 | tf_op jit(solution)/shard_map/all_to_all | solution.py:491
  53.8 2.3 %collective-permute-start.6 = (f32[32,48,128]{2,1,0:T(8,128)S(1)}, f32[32,48,128]{2,1,0:T(8,128)S(1)}, u32[]{:S(2)}, u32[]{:S(2)}) collective-permute-start(f32[32,48,128]{2,1,0:T(8,128)S(1)} %all-to-all-done.1.got), channel_id=1, source_target_pairs={{0,1},{1,0},{2,3},{3,2},{4,5},{5,4},{6,7},{7,6},{8,9},{9,8},{10,11... | collective-permute-start | bytes 2359304 | tf_op jit(solution)/shard_map/ppermute | solution.py:482
  96.1 16.7 %collective-permute-start.7 = (f32[192,256]{1,0:T(8,128)S(1)}, f32[192,256]{1,0:T(8,128)S(1)}, u32[]{:S(2)}, u32[]{:S(2)}) collective-permute-start(f32[192,256]{1,0:T(8,128)S(1)} %get-tuple-element.42), channel_id=1, source_target_pairs={{0,2},{1,3},{2,4},{3,5},{4,6},{5,7},{6,0},{7,1},{8,10},{9,11},{10,... | collective-permute-start | bytes 589832 | tf_op jit(solution)/shard_map/ppermute | solution.py:479
  96.6 16.2 %collective-permute-start.8 = (f32[192,256]{1,0:T(8,128)S(1)}, f32[192,256]{1,0:T(8,128)S(1)}, u32[]{:S(2)}, u32[]{:S(2)}) collective-permute-start(f32[192,256]{1,0:T(8,128)S(1)} %get-tuple-element.44), channel_id=1, source_target_pairs={{0,6},{1,7},{2,0},{3,1},{4,2},{5,3},{6,4},{7,5},{8,14},{9,15},{10,... | collective-permute-start | bytes 589832 | tf_op jit(solution)/shard_map/ppermute | solution.py:479
  105.1 16.8 %collective-permute-start.10 = (f32[192,256]{1,0:T(8,128)S(1)}, f32[192,256]{1,0:T(8,128)S(1)}, u32[]{:S(2)}, u32[]{:S(2)}) collective-permute-start(f32[192,256]{1,0:T(8,128)S(1)} %get-tuple-element.46), channel_id=1, source_target_pairs={{0,6},{1,7},{2,0},{3,1},{4,2},{5,3},{6,4},{7,5},{8,14},{9,15},{10,... | collective-permute-start | bytes 589832 | tf_op jit(solution)/shard_map/ppermute | solution.py:479
  105.2 16.7 %collective-permute-start.11 = (f32[192,256]{1,0:T(8,128)S(1)}, f32[192,256]{1,0:T(8,128)S(1)}, u32[]{:S(2)}, u32[]{:S(2)}) collective-permute-start(f32[192,256]{1,0:T(8,128)S(1)} %get-tuple-element.47), channel_id=1, source_target_pairs={{0,2},{1,3},{2,4},{3,5},{4,6},{5,7},{6,0},{7,1},{8,10},{9,11},{10,... | collective-permute-start | bytes 589832 | tf_op jit(solution)/shard_map/ppermute | solution.py:479
  112.9 10.0 %collective-permute-start.9 = (f32[192,256]{1,0:T(8,128)S(1)}, f32[192,256]{1,0:T(8,128)S(1)}, u32[]{:S(2)}, u32[]{:S(2)}) collective-permute-start(f32[192,256]{1,0:T(8,128)S(1)} %get-tuple-element.45), channel_id=1, source_target_pairs={{0,2},{1,3},{2,4},{3,5},{4,6},{5,7},{6,0},{7,1},{8,10},{9,11},{10,... | collective-permute-start | bytes 589832 | tf_op jit(solution)/shard_map/ppermute | solution.py:479
  113.4 10.9 %collective-permute-start.12 = (f32[192,256]{1,0:T(8,128)S(1)}, f32[192,256]{1,0:T(8,128)S(1)}, u32[]{:S(2)}, u32[]{:S(2)}) collective-permute-start(f32[192,256]{1,0:T(8,128)S(1)} %get-tuple-element.48), channel_id=1, source_target_pairs={{0,6},{1,7},{2,0},{3,1},{4,2},{5,3},{6,4},{7,5},{8,14},{9,15},{10,... | collective-permute-start | bytes 589832 | tf_op jit(solution)/shard_map/ppermute | solution.py:479

commit v15 on v12

--- a/solution.py
+++ b/solution.py
@@ -411,19 +411,20 @@
 def backward(bands, pieces, partners, row_den, own_den, everyone, pos, e0, e1, *cols):
     first = len(cols) == 2
     count = 9 * PIECE
+    height = sum(size for _, _, size in bands)
     col_shape = [jax.ShapeDtypeStruct((9, PIECE, 2 * WIDTH), jnp.bfloat16)]
     return pl.pallas_call(
         functools.partial(backward_kernel, bands, first),
         in_specs=[SMEM] + [pl.BlockSpec()] * 4 + [HBM] * 2 + ([HBM] * 2 if first else [pl.BlockSpec()]),
-        out_shape=col_shape * first + [jax.ShapeDtypeStruct((SLICE // pieces, WIDTH), jnp.float32)] * pieces,
+        out_shape=col_shape * first + [jax.ShapeDtypeStruct((height // pieces, WIDTH), jnp.float32)] * pieces,
         scratch_shapes=[
-            pltpu.VMEM((SLICE, WIDTH), jnp.float32),
-            pltpu.VMEM((9, SLICE, PIECE), jnp.float32),
+            pltpu.VMEM((height, WIDTH), jnp.float32),
+            pltpu.VMEM((9, height, PIECE), jnp.float32),
             pltpu.SemaphoreType.DMA((len(STEPS), 2, len(bands))),
             pltpu.SemaphoreType.DMA((len(STEPS), 2)),
         ],
         cost_estimate=pl.CostEstimate(
-            flops=6 * SLICE * count * WIDTH, bytes_accessed=4 * SLICE * count, transcendentals=0
+            flops=6 * height * count * WIDTH, bytes_accessed=4 * height * count, transcendentals=0
         ),
         compiler_params=params(VMEM_BACKWARD),
         name="backward_%d_%d" % bands[0][:2],
@@ -510,9 +511,9 @@
     cols, far_low, far_high = backward(((3, 0, rows),), 2, *shared, c_own, c_part)
     shared += (cols,)
     far_low, far_high = shift(far_low, 2), shift(far_high, -2)
-    left_low, right_high = backward(((0, 0, half), (1, half, half)), 2, *shared)
+    bands = ((0, 0, rows), (1, 0, rows))
+    left_low, left_high, right_low, right_high = backward(bands, 4, *shared)
     high0, low1 = shift(right_high, 2), shift(left_low, -2)
-    left_high, right_low = backward(((0, half, half), (1, 0, half)), 2, *shared)
     right_low, left_high = add_pairs(right_low, far_low, left_high, far_high)
     low0, high1 = shift(right_low, 2), shift(left_high, -2)
     (run,) = backward(((SELF, 0, rows),), 1, *shared)

time: 125 us -> 128 us (1.024)
  waiting for transfers between devices: 22.5 us -> 25.9 us
  Pallas kernels: 37.1 us -> 35.2 us
    ppermute x10, waiting for transfers between devices: 10.3 us -> 13.7 us  [shift(): lax.ppermute(value, 'mem', [(m, (m + by) % members) for m in range(member...]
    pallas_call x4 -> x3, Pallas kernels: 18.4 us -> 16.5 us  [backward(): pl.pallas_call(functools.partial(backward_kernel, bands, first), in_specs...]
  transfers between devices with their start and end apart: 15 -> 15, of which waited for: 7 -> 7; matrix products, arithmetic and copies ran while one was open for 1% -> 1% of each run, Pallas kernels for 19% -> 17%
where the time goes in v15:
time: 128 us; the launch traced here: 127 us
  starting transfers between devices  35.7 us (28%)
  Pallas kernels  35.2 us (28%)
  blocking collectives  27.3 us (21%)
  waiting for transfers between devices  25.9 us (20%)
  local copies, waits for them, and re-layouts  1.59 us (1%)
    ppermute x10, starting transfers between devices, shift(): lax.ppermute(value, 'mem', [(m, (m + by) % members) for m in range(member...  22.7 us
    pallas_call x3, Pallas kernels, backward(): pl.pallas_call(functools.partial(backward_kernel, bands, first), in_specs...  16.5 us
    all_to_all x1, blocking collectives, local(): everything = lax.all_to_all(line, 'mem', 0, 0, tiled=True)  15 us
    ppermute x10, waiting for transfers between devices, shift(): lax.ppermute(value, 'mem', [(m, (m + by) % members) for m in range(member...  13.7 us
    all_to_all x1, blocking collectives, local(): everyone = lax.all_to_all(spread, 'grp', 0, 0, tiled=True)  12.4 us
    all_to_all x1, starting transfers between devices, local(): lax.all_to_all(tiles.reshape(groups, per, 128), 'grp', 0, 0, tiled=True)  7.99 us
    pallas_call x1, Pallas kernels, forward(): pl.pallas_call(forward_kernel, in_specs=[HBM] * 2 + [pl.BlockSpec()] * 3,...  7.52 us
    pallas_call x1, Pallas kernels, own_scores(): pl.pallas_call(own_kernel, in_specs=[HBM] * 2 + [pl.BlockSpec()] * 3, out...  5.75 us
  transfers between devices with their start and end apart: 15, of which 7 were waited for; matrix products, arithmetic and copies ran while one was open for 1% of the time, Pallas kernels for 17%

profile of v15, /device:TPU:8, one launch (start us, length us, event | category | flops | bytes accessed | tf_op | source)
XLA Modules:
  0.0 126.6 jit_solution(16422331008381625447)
XLA Ops:
  0.6 6.4 %collective-permute-start.1 = (f32[384,256]{1,0:T(8,128)}, f32[384,256]{1,0:T(8,128)S(1)}, u32[]{:S(2)}, u32[]{:S(2)}) collective-permute-start(f32[384,256]{1,0:T(8,128)} %emb_ref.1), channel_id=1, source_target_pairs={{0,6},{1,7},{2,0},{3,1},{4,2},{5,3},{6,4},{7,5},{8,14},{9,15},{10,... | collective-permute-start | bytes 1179656 | tf_op jit(solution)/shard_map/ppermute | solution.py:480
  7.0 8.0 %all-to-all-start = ((f32[32,24,128]{2,1,0:T(8,128)}), f32[32,24,128]{2,1,0:T(8,128)S(1)}, u32[]{:S(2)}, u32[]{:S(2)}) async-start(f32[32,24,128]{2,1,0:T(8,128)} %bitcast.6), calls=%async_computation | async-start | bytes 786432 | tf_op jit(solution)/shard_map/all_to_all | solution.py:489
  16.8 7.4 %collective-permute-done.1.refs_1_ = f32[384,256]{1,0:T(8,128)S(1)} collective-permute-done((f32[384,256]{1,0:T(8,128)}, f32[384,256]{1,0:T(8,128)S(1)}, u32[]{:S(2)}, u32[]{:S(2)}) %collective-permute-start.1) | collective-permute-done | bytes 393248 | tf_op jit(solution)/shard_map/ppermute | solution.py:480
  24.2 4.6 %collective-permute-start.3 = (f32[192,256]{1,0:T(8,128)S(1)}, f32[192,256]{1,0:T(8,128)S(1)}, u32[]{:S(2)}, u32[]{:S(2)}) collective-permute-start(f32[192,256]{1,0:T(8,128)S(1)} %slice.9), channel_id=1, source_target_pairs={{0,6},{1,7},{2,0},{3,1},{4,2},{5,3},{6,4},{7,5},{8,14},{9,15},{10,... | collective-permute-start | bytes 589832 | tf_op jit(solution)/shard_map/ppermute | solution.py:480
  29.0 1.4 %prepare.1.ready = bf16[768,768]{1,0:T(8,128)(2,1)} custom-call(f32[384,256]{1,0:T(8,128)S(1)} %collective-permute-done.refs_0_, f32[384,256]{1,0:T(8,128)S(1)} %collective-permute-done.1.refs_1_), custom_call_target="tpu_custom_call" | custom-call | flops 20000000000 | bytes 1572864 | tf_op jit(solution)/shard_map/prepare/pallas_call | solution.py:197
  30.4 4.1 %all-to-all-done.pieces_ref = f32[32,24,128]{2,1,0:T(8,128)S(1)} async-done(((f32[32,24,128]{2,1,0:T(8,128)}), f32[32,24,128]{2,1,0:T(8,128)S(1)}, u32[]{:S(2)}, u32[]{:S(2)}) %all-to-all-start) | async-done | bytes 393248 | tf_op jit(solution)/shard_map/all_to_all | solution.py:489
  34.5 1.5 %pick.1 = f32[32,48,128]{2,1,0:T(8,128)} custom-call(s32[2,32]{1,0:T(2,128)S(1)} %copy-done.1, f32[32,24,128]{2,1,0:T(8,128)S(1)} %all-to-all-done.pieces_ref), custom_call_target="tpu_custom_call" | custom-call | tf_op jit(solution)/shard_map/pick/pallas_call | solution.py:61
  36.1 4.9 %all-to-all-start.1 = ((f32[32,48,128]{2,1,0:T(8,128)}), f32[32,48,128]{2,1,0:T(8,128)S(1)}, u32[]{:S(2)}, u32[]{:S(2)}) async-start(f32[32,48,128]{2,1,0:T(8,128)} %pick.1), calls=%async_computation.1 | async-start | bytes 1572864 | tf_op jit(solution)/shard_map/all_to_all | solution.py:492
  41.0 1.4 %prepare_far.1.ready_far = bf16[768,768]{1,0:T(8,128)(2,1)} custom-call(f32[384,256]{1,0:T(8,128)S(1)} %copy-done, f32[192,256]{1,0:T(8,128)S(1)} %collective-permute-done.2.refs_1_, f32[192,256]{1,0:T(8,128)S(1)} %collective-permute-done.3.refs_2_), custom_call_target="tpu_custom_call" | custom-call | flops 20000000000 | bytes 1572864 | tf_op jit(solution)/shard_map/prepare_far/pallas_call | solution.py:197
  42.4 5.7 %own_scores.1 = (bf16[3,256,512]{2,1,0:T(8,128)(2,1)}, f32[3,4,384,256]{3,2,1,0:T(8,128)}, f32[2,1536]{1,0:T(2,128)S(1)}) custom-call(bf16[768,768]{1,0:T(8,128)(2,1)} %prepare.1.ready, bf16[768,768]{1,0:T(8,128)(2,1)} %prepare_far.1.ready_far, f32[384,256]{1,0:T(8,128)S(1)} %copy-done, f32[384,256]{1,0:T(8,128)S(1)} %collective-permute-done.4.sib, ...), custom_call_target="tpu_custom_call" | custom-call | flops 1811939328 | bytes 4718592 | tf_op jit(solution)/shard_map/own_scores/pallas_call | solution.py:165
  48.1 5.7 %all-to-all-done.1.got = f32[32,48,128]{2,1,0:T(8,128)S(1)} async-done(((f32[32,48,128]{2,1,0:T(8,128)}), f32[32,48,128]{2,1,0:T(8,128)S(1)}, u32[]{:S(2)}, u32[]{:S(2)}) %all-to-all-start.1) | async-done | bytes 786464 | tf_op jit(solution)/shard_map/all_to_all | solution.py:492
  53.9 2.3 %collective-permute-done.6.got_sib = f32[32,48,128]{2,1,0:T(8,128)S(1)} collective-permute-done((f32[32,48,128]{2,1,0:T(8,128)S(1)}, f32[32,48,128]{2,1,0:T(8,128)S(1)}, u32[]{:S(2)}, u32[]{:S(2)}) %collective-permute-start.6) | collective-permute-done | bytes 786464 | tf_op jit(solution)/shard_map/ppermute | solution.py:483
  56.1 7.5 %forward.1 = (f32[6,4,384,256]{3,2,1,0:T(8,128)}, bf16[6,256,512]{2,1,0:T(8,128)(2,1)}, f32[8,2,1536]{2,1,0:T(2,128)S(1)}) custom-call(bf16[768,768]{1,0:T(8,128)(2,1)} %prepare.1.ready, bf16[768,768]{1,0:T(8,128)(2,1)} %prepare_far.1.ready_far, f32[2,1536]{1,0:T(2,128)S(1)} %get-tuple-element.30.line_in, f32[32,48,128]{2,1,0:T(8,128)S(1)} %all-to-all-done.1.got, ...), custom_call_target="tpu_custom_call" | custom-call | flops 3623878656 | bytes 9437184 | tf_op jit(solution)/shard_map/forward/pallas_call | solution.py:272
  63.7 15.0 %all_to_all.20.all_ref = f32[8,2,1536]{2,1,0:T(2,128)S(1)} all-to-all(f32[8,2,1536]{2,1,0:T(2,128)S(1)} %get-tuple-element.32), channel_id=1, replica_groups=mesh['grp'=32,'mem'=8] {'mem'}, dimensions={0} | all-to-all | bytes 196608 | tf_op jit(solution)/shard_map/all_to_all | solution.py:506
  78.7 12.4 %all_to_all.21.everyone_ref = f32[32,1,768]{2,1,0:T(1,128)S(1)} all-to-all(f32[32,1,768]{2,1,0:T(1,128)S(1)} %get-tuple-element.35), channel_id=1, replica_groups=mesh['grp'=32,'mem'=8] {'grp'}, dimensions={0} | all-to-all | bytes 196608 | tf_op jit(solution)/shard_map/all_to_all | solution.py:508
  91.1 4.8 %backward_3_0.1 = (bf16[9,256,512]{2,1,0:T(8,128)(2,1)S(1)}, f32[192,256]{1,0:T(8,128)S(1)}, f32[192,256]{1,0:T(8,128)S(1)}) custom-call(s32[2]{0:T(128)S(1)} %dynamic-slice_reduce_fusion.partner_ref, f32[1,1536]{1,0:T(1,128)S(1)} %get-tuple-element.33.row_ref, f32[1,768]{1,0:T(1,128)S(1)} %get-tuple-element.34.own_ref, ...), custom_call_target="tpu_custom_call" | custom-call | flops 1358954496 | bytes 3538944 | tf_op jit(solution)/shard_map/backward_3_0/pallas_call | solution.py:416
  96.4 3.7 %collective-permute-start.8 = (f32[192,256]{1,0:T(8,128)S(1)}, f32[192,256]{1,0:T(8,128)S(1)}, u32[]{:S(2)}, u32[]{:S(2)}) collective-permute-start(f32[192,256]{1,0:T(8,128)S(1)} %get-tuple-element.44), channel_id=1, source_target_pairs={{0,6},{1,7},{2,0},{3,1},{4,2},{5,3},{6,4},{7,5},{8,14},{9,15},{10,... | collective-permute-start | bytes 589832 | tf_op jit(solution)/shard_map/ppermute | solution.py:480
  100.0 7.2 %backward_0_0.1 = (f32[192,256]{1,0:T(8,128)S(1)}, f32[192,256]{1,0:T(8,128)S(1)}, f32[192,256]{1,0:T(8,128)S(1)}, f32[192,256]{1,0:T(8,128)S(1)}) custom-call(s32[2]{0:T(128)S(1)} %dynamic-slice_reduce_fusion.partner_ref, f32[1,1536]{1,0:T(1,128)S(1)} %get-tuple-element.33.row_ref, f32[1,768]{1,0:T(1,128)S(1)} %get-tuple-element.34.own_ref, ...), custom_call_target="tpu_custom_call" | custom-call | flops 2717908992 | bytes 7077888 | tf_op jit(solution)/shard_map/backward_0_0/pallas_call | solution.py:416
  107.6 2.9 %collective-permute-start.11 = (f32[192,256]{1,0:T(8,128)S(1)}, f32[192,256]{1,0:T(8,128)S(1)}, u32[]{:S(2)}, u32[]{:S(2)}) collective-permute-start(f32[192,256]{1,0:T(8,128)S(1)} %get-tuple-element.47), channel_id=1, source_target_pairs={{0,2},{1,3},{2,4},{3,5},{4,6},{5,7},{6,0},{7,1},{8,10},{9,11},{10,... | collective-permute-start | bytes 589832 | tf_op jit(solution)/shard_map/ppermute | solution.py:480
  111.1 3.7 %collective-permute-start.12 = (f32[192,256]{1,0:T(8,128)S(1)}, f32[192,256]{1,0:T(8,128)S(1)}, u32[]{:S(2)}, u32[]{:S(2)}) collective-permute-start(f32[192,256]{1,0:T(8,128)S(1)} %get-tuple-element.48), channel_id=1, source_target_pairs={{0,6},{1,7},{2,0},{3,1},{4,2},{5,3},{6,4},{7,5},{8,14},{9,15},{10,... | collective-permute-start | bytes 589832 | tf_op jit(solution)/shard_map/ppermute | solution.py:480
  114.8 4.5 %backward_2_0.1.run_ref = f32[384,256]{1,0:T(8,128)S(1)} custom-call(s32[2]{0:T(128)S(1)} %dynamic-slice_reduce_fusion.partner_ref, f32[1,1536]{1,0:T(1,128)S(1)} %get-tuple-element.33.row_ref, f32[1,768]{1,0:T(1,128)S(1)} %get-tuple-element.34.own_ref, f32[32,1,768]{2,1,0:T(1,128)S(1)} %all_to_all.21.everyone_ref, ...), custom_call_target="tpu_custom_call" | custom-call | flops 1358954496 | bytes 3538944 | tf_op jit(solution)/shard_map/backward_2_0/pallas_call | solution.py:416
  119.3 3.7 %collective-permute-done.10.low1 = f32[192,256]{1,0:T(8,128)S(1)} collective-permute-done((f32[192,256]{1,0:T(8,128)S(1)}, f32[192,256]{1,0:T(8,128)S(1)}, u32[]{:S(2)}, u32[]{:S(2)}) %collective-permute-start.10) | collective-permute-done | bytes 196640 | tf_op jit(solution)/shard_map/ppermute | solution.py:480
  123.0 2.5 %collective-permute-done.9.low0 = f32[192,256]{1,0:T(8,128)S(1)} collective-permute-done((f32[192,256]{1,0:T(8,128)S(1)}, f32[192,256]{1,0:T(8,128)S(1)}, u32[]{:S(2)}, u32[]{:S(2)}) %collective-permute-start.9) | collective-permute-done | bytes 196640 | tf_op jit(solution)/shard_map/ppermute | solution.py:480
  125.6 1.1 finish.1
  (29 shorter events, 3.4 us)
Async XLA Ops:
  0.6 23.5 %collective-permute-start.1 = (f32[384,256]{1,0:T(8,128)}, f32[384,256]{1,0:T(8,128)S(1)}, u32[]{:S(2)}, u32[]{:S(2)}) collective-permute-start(f32[384,256]{1,0:T(8,128)} %emb_ref.1), channel_id=1, source_target_pairs={{0,6},{1,7},{2,0},{3,1},{4,2},{5,3},{6,4},{7,5},{8,14},{9,15},{10,... | collective-permute-start | bytes 1179656 | tf_op jit(solution)/shard_map/ppermute | solution.py:480
  7.0 21.9 %collective-permute-start = (f32[384,256]{1,0:T(8,128)}, f32[384,256]{1,0:T(8,128)S(1)}, u32[]{:S(2)}, u32[]{:S(2)}) collective-permute-start(f32[384,256]{1,0:T(8,128)} %emb_ref.1), channel_id=1, source_target_pairs={{0,2},{1,3},{2,4},{3,5},{4,6},{5,7},{6,0},{7,1},{8,10},{9,11},{10,... | collective-permute-start | bytes 1179656 | tf_op jit(solution)/shard_map/ppermute | solution.py:480
  7.0 35.4 %collective-permute-start.4 = (f32[384,256]{1,0:T(8,128)}, f32[384,256]{1,0:T(8,128)S(1)}, u32[]{:S(2)}, u32[]{:S(2)}) collective-permute-start(f32[384,256]{1,0:T(8,128)} %emb_ref.1), channel_id=1, source_target_pairs={{0,1},{1,0},{2,3},{3,2},{4,5},{5,4},{6,7},{7,6},{8,9},{9,8},{10,11... | collective-permute-start | bytes 1179656 | tf_op jit(solution)/shard_map/ppermute | solution.py:483
  7.0 27.5 %all-to-all-start = ((f32[32,24,128]{2,1,0:T(8,128)}), f32[32,24,128]{2,1,0:T(8,128)S(1)}, u32[]{:S(2)}, u32[]{:S(2)}) async-start(f32[32,24,128]{2,1,0:T(8,128)} %bitcast.6), calls=%async_computation | async-start | bytes 786432 | tf_op jit(solution)/shard_map/all_to_all | solution.py:489
  15.0 1.7 %collective-permute-start.5 = (s32[384]{0:T(512)}, s32[384]{0:T(512)S(1)}, u32[]{:S(2)}, u32[]{:S(2)}) collective-permute-start(s32[384]{0:T(512)} %param.4), channel_id=1, source_target_pairs={{0,1},{1,0},{2,3},{3,2},{4,5},{5,4},{6,7},{7,6},{8,9},{9,8},{10,11... | collective-permute-start | bytes 4616 | tf_op jit(solution)/shard_map/ppermute | solution.py:483
  24.2 16.8 %collective-permute-start.3 = (f32[192,256]{1,0:T(8,128)S(1)}, f32[192,256]{1,0:T(8,128)S(1)}, u32[]{:S(2)}, u32[]{:S(2)}) collective-permute-start(f32[192,256]{1,0:T(8,128)S(1)} %slice.9), channel_id=1, source_target_pairs={{0,6},{1,7},{2,0},{3,1},{4,2},{5,3},{6,4},{7,5},{8,14},{9,15},{10,... | collective-permute-start | bytes 589832 | tf_op jit(solution)/shard_map/ppermute | solution.py:480
  28.9 5.6 %copy-start.1 = (s32[2,32]{1,0:T(2,128)S(1)}, s32[2,32]{1,0:T(2,128)}, u32[]{:S(2)}) copy-start(s32[2,32]{1,0:T(2,128)} %pairing_ref.1) | copy-start | bytes 772
  28.9 12.1 %collective-permute-start.2 = (f32[192,256]{1,0:T(8,128)S(1)}, f32[192,256]{1,0:T(8,128)S(1)}, u32[]{:S(2)}, u32[]{:S(2)}) collective-permute-start(f32[192,256]{1,0:T(8,128)S(1)} %slice.8), channel_id=1, source_target_pairs={{0,2},{1,3},{2,4},{3,5},{4,6},{5,7},{6,0},{7,1},{8,10},{9,11},{10,... | collective-permute-start | bytes 589832 | tf_op jit(solution)/shard_map/ppermute | solution.py:480
  30.4 10.6 %copy-start = (f32[384,256]{1,0:T(8,128)S(1)}, f32[384,256]{1,0:T(8,128)}, u32[]{:S(2)}) copy-start(f32[384,256]{1,0:T(8,128)} %emb_ref.1) | copy-start | bytes 1179652
  36.1 17.8 %all-to-all-start.1 = ((f32[32,48,128]{2,1,0:T(8,128)}), f32[32,48,128]{2,1,0:T(8,128)S(1)}, u32[]{:S(2)}, u32[]{:S(2)}) async-start(f32[32,48,128]{2,1,0:T(8,128)} %pick.1), calls=%async_computation.1 | async-start | bytes 1572864 | tf_op jit(solution)/shard_map/all_to_all | solution.py:492
  53.9 2.3 %collective-permute-start.6 = (f32[32,48,128]{2,1,0:T(8,128)S(1)}, f32[32,48,128]{2,1,0:T(8,128)S(1)}, u32[]{:S(2)}, u32[]{:S(2)}) collective-permute-start(f32[32,48,128]{2,1,0:T(8,128)S(1)} %all-to-all-done.1.got), channel_id=1, source_target_pairs={{0,1},{1,0},{2,3},{3,2},{4,5},{5,4},{6,7},{7,6},{8,9},{9,8},{10,11... | collective-permute-start | bytes 2359304 | tf_op jit(solution)/shard_map/ppermute | solution.py:483
  95.8 14.7 %collective-permute-start.7 = (f32[192,256]{1,0:T(8,128)S(1)}, f32[192,256]{1,0:T(8,128)S(1)}, u32[]{:S(2)}, u32[]{:S(2)}) collective-permute-start(f32[192,256]{1,0:T(8,128)S(1)} %get-tuple-element.42), channel_id=1, source_target_pairs={{0,2},{1,3},{2,4},{3,5},{4,6},{5,7},{6,0},{7,1},{8,10},{9,11},{10,... | collective-permute-start | bytes 589832 | tf_op jit(solution)/shard_map/ppermute | solution.py:480
  96.4 14.1 %collective-permute-start.8 = (f32[192,256]{1,0:T(8,128)S(1)}, f32[192,256]{1,0:T(8,128)S(1)}, u32[]{:S(2)}, u32[]{:S(2)}) collective-permute-start(f32[192,256]{1,0:T(8,128)S(1)} %get-tuple-element.44), channel_id=1, source_target_pairs={{0,6},{1,7},{2,0},{3,1},{4,2},{5,3},{6,4},{7,5},{8,14},{9,15},{10,... | collective-permute-start | bytes 589832 | tf_op jit(solution)/shard_map/ppermute | solution.py:480
  107.3 15.8 %collective-permute-start.10 = (f32[192,256]{1,0:T(8,128)S(1)}, f32[192,256]{1,0:T(8,128)S(1)}, u32[]{:S(2)}, u32[]{:S(2)}) collective-permute-start(f32[192,256]{1,0:T(8,128)S(1)} %get-tuple-element.46), channel_id=1, source_target_pairs={{0,6},{1,7},{2,0},{3,1},{4,2},{5,3},{6,4},{7,5},{8,14},{9,15},{10,... | collective-permute-start | bytes 589832 | tf_op jit(solution)/shard_map/ppermute | solution.py:480
  107.6 15.5 %collective-permute-start.11 = (f32[192,256]{1,0:T(8,128)S(1)}, f32[192,256]{1,0:T(8,128)S(1)}, u32[]{:S(2)}, u32[]{:S(2)}) collective-permute-start(f32[192,256]{1,0:T(8,128)S(1)} %get-tuple-element.47), channel_id=1, source_target_pairs={{0,2},{1,3},{2,4},{3,5},{4,6},{5,7},{6,0},{7,1},{8,10},{9,11},{10,... | collective-permute-start | bytes 589832 | tf_op jit(solution)/shard_map/ppermute | solution.py:480
  110.6 15.0 %collective-permute-start.9 = (f32[192,256]{1,0:T(8,128)S(1)}, f32[192,256]{1,0:T(8,128)S(1)}, u32[]{:S(2)}, u32[]{:S(2)}) collective-permute-start(f32[192,256]{1,0:T(8,128)S(1)} %get-tuple-element.45), channel_id=1, source_target_pairs={{0,2},{1,3},{2,4},{3,5},{4,6},{5,7},{6,0},{7,1},{8,10},{9,11},{10,... | collective-permute-start | bytes 589832 | tf_op jit(solution)/shard_map/ppermute | solution.py:480
  111.1 14.5 %collective-permute-start.12 = (f32[192,256]{1,0:T(8,128)S(1)}, f32[192,256]{1,0:T(8,128)S(1)}, u32[]{:S(2)}, u32[]{:S(2)}) collective-permute-start(f32[192,256]{1,0:T(8,128)S(1)} %get-tuple-element.48), channel_id=1, source_target_pairs={{0,6},{1,7},{2,0},{3,1},{4,2},{5,3},{6,4},{7,5},{8,14},{9,15},{10,... | collective-permute-start | bytes 589832 | tf_op jit(solution)/shard_map/ppermute | solution.py:480
